TPU v7x, 32 devices: a whole 2x2x4 slice. The times are simulated.
32 devices in a mesh: dp: 32 (over z, y, x, core).
Axes of the slice: x: 2, y: 2, z: 4, core: 2. Of those that a mesh axis runs over, the one named last changes fastest.
Arguments:
- tokens: bfloat16 [32, 512, 640], P('dp'), may hold values from -27 to 27
- segment_ids: int32 [32, 512], P('dp'), may hold values from 0 to 3, never falling along the last dimension, each value on 1 to 256 neighbouring positions
- cotangent: bfloat16 [32, 512, 640], P('dp'), may hold values from -6 to 6
- query_weight: float32 [640, 1024], P('dp'), may hold values from -0.25 to 0.25
- keyval_weight: float32 [640, 512], P('dp'), may hold values from -0.25 to 0.25
- output_weight: float32 [1024, 640], P('dp'), may hold values from -0.1875 to 0.1875
- gateup_weight: float32 [640, 2, 2048], P('dp'), may hold values from -0.25 to 0.25
- down_weight: float32 [2048, 640], P('dp'), may hold values from -0.125 to 0.125
- norm_gains: float32 [4, 640], P(None, 'dp'), may hold values from -0.12 to 0.12
- qknorm_gains: float32 [2, 256], P(None, 'dp'), may hold values from -0.12 to 0.12
- query_mean: float32 [640, 1024], P('dp'), may hold values from -80 to 80
- keyval_mean: float32 [640, 512], P('dp'), may hold values from -80 to 80
- output_mean: float32 [1024, 640], P('dp'), may hold values from -80 to 80
- gateup_mean: float32 [640, 2, 2048], P('dp'), may hold values from -80 to 80
- down_mean: float32 [2048, 640], P('dp'), may hold values from -80 to 80
- norm_mean: float32 [4, 640], P(None, 'dp'), may hold values from -80 to 80
- qknorm_mean: float32 [2, 256], P(None, 'dp'), may hold values from -80 to 80
- query_square: float32 [640, 1024], P('dp'), may hold values from 16.384 to 65.536
- keyval_square: float32 [640, 512], P('dp'), may hold values from 16.384 to 65.536
- output_square: float32 [1024, 640], P('dp'), may hold values from 16.384 to 65.536
- gateup_square: float32 [640, 2, 2048], P('dp'), may hold values from 16.384 to 65.536
- down_square: float32 [2048, 640], P('dp'), may hold values from 16.384 to 65.536
- norm_square: float32 [4, 640], P(None, 'dp'), may hold values from 16.384 to 65.536
- qknorm_square: float32 [2, 256], P(None, 'dp'), may hold values from 16.384 to 65.536
Outputs:
- result: bfloat16 [32, 512, 640], P('dp')
- input_grad: float32 [32, 512, 640], P('dp')
- query_grad: float32 [640, 1024], P('dp')
- keyval_grad: float32 [640, 512], P('dp')
- output_grad: float32 [1024, 640], P('dp')
- gateup_grad: float32 [640, 2, 2048], P('dp')
- down_grad: float32 [2048, 640], P('dp')
- norm_grad: float32 [4, 640], P(None, 'dp')
- qknorm_grad: float32 [2, 256], P(None, 'dp')
- query_new: float32 [640, 1024], P('dp')
- keyval_new: float32 [640, 512], P('dp')
- output_new: float32 [1024, 640], P('dp')
- gateup_new: float32 [640, 2, 2048], P('dp')
- down_new: float32 [2048, 640], P('dp')
- norm_new: float32 [4, 640], P(None, 'dp')
- qknorm_new: float32 [2, 256], P(None, 'dp')
- query_mean_new: float32 [640, 1024], P('dp')
- keyval_mean_new: float32 [640, 512], P('dp')
- output_mean_new: float32 [1024, 640], P('dp')
- gateup_mean_new: float32 [640, 2, 2048], P('dp')
- down_mean_new: float32 [2048, 640], P('dp')
- norm_mean_new: float32 [4, 640], P(None, 'dp')
- qknorm_mean_new: float32 [2, 256], P(None, 'dp')
- query_square_new: float32 [640, 1024], P('dp')
- keyval_square_new: float32 [640, 512], P('dp')
- output_square_new: float32 [1024, 640], P('dp')
- gateup_square_new: float32 [640, 2, 2048], P('dp')
- down_square_new: float32 [2048, 640], P('dp')
- norm_square_new: float32 [4, 640], P(None, 'dp')
- qknorm_square_new: float32 [2, 256], P(None, 'dp')
Inputs may be any that keep to these rules, and one draw needn't show every extreme that they name: `segment_ids`: segment numbers never fall along a sequence; a document holds 1 to 256 tokens.
All inputs are finite; a program needn't handle non-finite values.
Results may differ from a plain program's by a relative error of at most 0.025.
Values may be sent and summed in bfloat16 or wider, within the bound.
No kernel may reach another device: no remote copies, remote signals or barrier semaphores. Data moves between devices by JAX's collectives and lax.ppermute only.
A program may use at most 128 MiB of HBM per device.

v0:
```python
import jax
import jax.numpy as jnp
from jax import lax
from jax.sharding import PartitionSpec as P

STEP = 3


norm_epsilon = 1e-06
beta_one = 0.9
beta_two = 0.999
learn_rate = 0.03
decay_coef = 0.1
adam_epsilon = 1e-08


def norm_apply(values, gain_vector):
    inverse = lax.rsqrt(jnp.mean(values * values, axis=-1, keepdims=True) + norm_epsilon)
    return values * inverse * (1.0 + gain_vector)


def gelu_product(gate_part, up_part):
    return jax.nn.gelu(gate_part, approximate=True) * up_part


def block_scores(query_normed, key_normed, segments, row_start, row_stop, score_scale):
    positions = jnp.arange(row_stop)
    same_doc = segments[row_start:row_stop, None] == segments[None, :row_stop]
    causal = positions[None, :] <= positions[row_start:row_stop, None]
    allowed = (same_doc & causal)[None]
    scores = (
        jnp.einsum("qhd,kd->hqk", query_normed, key_normed, preferred_element_type=jnp.float32)
        * score_scale
    )
    return (jnp.where(allowed, scores, -1e30), allowed)


def attend_forward(query_normed, key_normed, value_round, segments, score_scale):
    length = query_normed.shape[0]
    block_rows = min(512, length)
    masked, allowed = block_scores(query_normed, key_normed, segments, 0, block_rows, score_scale)
    row_max = jnp.max(masked, axis=-1, keepdims=True)
    row_total = jnp.sum(jnp.where(allowed, jnp.exp(masked - row_max), 0.0), axis=-1, keepdims=True)
    log_total = row_max + jnp.log(row_total)
    soft_round = jnp.where(allowed, jnp.exp(masked - log_total), 0.0).astype(jnp.bfloat16)
    attended_block = jnp.einsum(
        "hqk,kd->qhd", soft_round, value_round, preferred_element_type=jnp.float32
    )
    attended_parts = attended_block.astype(jnp.bfloat16)
    total_parts = log_total[:, :, 0]
    return (attended_parts, total_parts)


def attend_backward(
    query_normed,
    key_normed,
    value_round,
    segments,
    log_totals,
    attended,
    grad_attended,
    score_scale,
):
    length = query_normed.shape[0]
    head_dim = key_normed.shape[1]
    block_rows = min(512, length)
    row_delta = jnp.sum(grad_attended.astype(jnp.float32) * attended.astype(jnp.float32), axis=-1)
    grad_key_sum = jnp.zeros((length, head_dim), jnp.float32)
    grad_value_sum = jnp.zeros((length, head_dim), jnp.float32)
    masked, allowed = block_scores(query_normed, key_normed, segments, 0, block_rows, score_scale)
    soft_weights = jnp.where(allowed, jnp.exp(masked - log_totals[:, 0:block_rows, None]), 0.0)
    soft_round = soft_weights.astype(jnp.bfloat16)
    grad_value_sum = grad_value_sum.at[:block_rows].add(
        jnp.einsum("hqk,qhd->kd", soft_round, grad_attended, preferred_element_type=jnp.float32)
    )
    grad_soft = jnp.einsum(
        "qhd,kd->hqk", grad_attended, value_round, preferred_element_type=jnp.float32
    )
    delta_block = row_delta.T[:, :, None]
    grad_scores = (soft_weights * (grad_soft - delta_block) * score_scale).astype(jnp.bfloat16)
    grad_query_parts = jnp.einsum(
        "hqk,kd->qhd", grad_scores, key_normed, preferred_element_type=jnp.float32
    )
    grad_key_sum = grad_key_sum.at[:block_rows].add(
        jnp.einsum("hqk,qhd->kd", grad_scores, query_normed, preferred_element_type=jnp.float32)
    )
    return (grad_query_parts, grad_key_sum, grad_value_sum)


def adam_update(parameter, gradient, first_moment, second_moment, decay_value):
    first_new = beta_one * first_moment + (1.0 - beta_one) * gradient
    second_new = beta_two * second_moment + (1.0 - beta_two) * gradient * gradient
    first_hat = first_new / (1.0 - beta_one**STEP)
    second_hat = second_new / (1.0 - beta_two**STEP)
    parameter_new = (
        parameter
        - learn_rate * first_hat / (jnp.sqrt(second_hat) + adam_epsilon)
        - learn_rate * decay_value * parameter
    )
    return (parameter_new, first_new, second_new)


def per_device(
    tokens,
    segment_ids,
    cotangent,
    query_weight,
    keyval_weight,
    output_weight,
    gateup_weight,
    down_weight,
    norm_gains,
    qknorm_gains,
    query_mean,
    keyval_mean,
    output_mean,
    gateup_mean,
    down_mean,
    norm_mean,
    qknorm_mean,
    query_square,
    keyval_square,
    output_square,
    gateup_square,
    down_square,
    norm_square,
    qknorm_square,
):
    query_round = query_weight.astype(jnp.bfloat16)
    keyval_round = keyval_weight.astype(jnp.bfloat16)
    output_round = output_weight.astype(jnp.bfloat16)
    gateup_round = gateup_weight.astype(jnp.bfloat16)
    down_round = down_weight.astype(jnp.bfloat16)
    gains_round = norm_gains.astype(jnp.bfloat16)
    headgain_round = qknorm_gains.astype(jnp.bfloat16)
    query_full, keyval_full, output_full, gateup_full, down_full, gains_full, headgain_full = (
        lax.all_gather(query_round, "dp", axis=0, tiled=True),
        lax.all_gather(keyval_round, "dp", axis=0, tiled=True),
        lax.all_gather(output_round, "dp", axis=0, tiled=True),
        lax.all_gather(gateup_round, "dp", axis=0, tiled=True),
        lax.all_gather(down_round, "dp", axis=0, tiled=True),
        lax.all_gather(gains_round, "dp", axis=1, tiled=True),
        lax.all_gather(headgain_round, "dp", axis=1, tiled=True),
    )
    seq_count, length, model_width = tokens.shape
    row_count = seq_count * length
    head_dim = headgain_full.shape[1]
    head_count = query_full.shape[1] // head_dim
    hidden_units = gateup_full.shape[2]
    score_scale = head_dim ** (-0.5)
    main_gains = gains_full.astype(jnp.float32)
    head_gains = headgain_full.astype(jnp.float32)
    inputs = tokens.reshape(row_count, model_width).astype(jnp.float32)
    normed_in = norm_apply(inputs, main_gains[0]).astype(jnp.bfloat16)
    queries = jnp.dot(normed_in, query_full, preferred_element_type=jnp.float32).reshape(
        row_count, head_count, head_dim
    )
    keyvals = jnp.dot(normed_in, keyval_full, preferred_element_type=jnp.float32)
    key_rows = keyvals[:, :head_dim]
    value_rows = keyvals[:, head_dim:]
    query_normed = norm_apply(queries, head_gains[0]).astype(jnp.bfloat16)
    key_normed = norm_apply(key_rows, head_gains[1]).astype(jnp.bfloat16)
    value_round = value_rows.astype(jnp.bfloat16)
    seq_index = 0
    attended_seq, totals_seq = attend_forward(
        query_normed, key_normed, value_round, segment_ids[seq_index], score_scale
    )
    total_parts = [totals_seq]
    attended_flat = attended_seq.reshape(row_count, head_count * head_dim)
    branch = jnp.dot(attended_flat, output_full, preferred_element_type=jnp.float32)
    middle = inputs + norm_apply(branch, main_gains[1])
    normed_mid = norm_apply(middle, main_gains[2]).astype(jnp.bfloat16)
    gate_up = jnp.dot(
        normed_mid,
        gateup_full.reshape(model_width, 2 * hidden_units),
        preferred_element_type=jnp.float32,
    )
    gate_part = gate_up[:, :hidden_units]
    up_part = gate_up[:, hidden_units:]
    hidden = gelu_product(gate_part, up_part).astype(jnp.bfloat16)
    down_out = jnp.dot(hidden, down_full, preferred_element_type=jnp.float32)
    result = (middle + norm_apply(down_out, main_gains[3])).astype(jnp.bfloat16)
    query_back, keyval_back, output_back, gateup_back, down_back = (
        query_full,
        keyval_full,
        output_full,
        gateup_full,
        down_full,
    )
    gateup_flat = gateup_back.reshape(model_width, 2 * hidden_units)
    grad_out = cotangent.reshape(row_count, model_width).astype(jnp.float32)
    _, pull_back = jax.vjp(norm_apply, down_out, main_gains[3])
    grad_down_out, grad_gain_three = pull_back(grad_out)
    grad_down_round = grad_down_out.astype(jnp.bfloat16)
    grad_down = jnp.dot(hidden.T, grad_down_round, preferred_element_type=jnp.float32)
    grad_hidden = jnp.dot(grad_down_round, down_back.T, preferred_element_type=jnp.float32)
    _, pull_back = jax.vjp(gelu_product, gate_part, up_part)
    grad_gate, grad_up = pull_back(grad_hidden)
    grad_gate_up = jnp.concatenate([grad_gate, grad_up], axis=1).astype(jnp.bfloat16)
    grad_gateup = jnp.dot(normed_mid.T, grad_gate_up, preferred_element_type=jnp.float32).reshape(
        model_width, 2, hidden_units
    )
    grad_normed_mid = jnp.dot(grad_gate_up, gateup_flat.T, preferred_element_type=jnp.float32)
    _, pull_back = jax.vjp(norm_apply, middle, main_gains[2])
    grad_mid_norm, grad_gain_two = pull_back(grad_normed_mid)
    grad_middle = grad_out + grad_mid_norm
    _, pull_back = jax.vjp(norm_apply, branch, main_gains[1])
    grad_branch, grad_gain_one = pull_back(grad_middle)
    grad_branch_round = grad_branch.astype(jnp.bfloat16)
    grad_output = jnp.dot(attended_flat.T, grad_branch_round, preferred_element_type=jnp.float32)
    grad_attended = (
        jnp.dot(grad_branch_round, output_back.T, preferred_element_type=jnp.float32)
        .reshape(row_count, head_count, head_dim)
        .astype(jnp.bfloat16)
    )
    seq_index = 0
    grad_query_seq, grad_key_seq, grad_value_seq = attend_backward(
        query_normed,
        key_normed,
        value_round,
        segment_ids[seq_index],
        total_parts[seq_index],
        attended_seq,
        grad_attended,
        score_scale,
    )
    _, pull_back = jax.vjp(norm_apply, queries, head_gains[0])
    grad_queries, grad_head_zero = pull_back(grad_query_seq)
    _, pull_back = jax.vjp(norm_apply, key_rows, head_gains[1])
    grad_keys, grad_head_one = pull_back(grad_key_seq)
    grad_query_round = grad_queries.reshape(row_count, head_count * head_dim).astype(jnp.bfloat16)
    grad_keyval_round = jnp.concatenate([grad_keys, grad_value_seq], axis=1).astype(jnp.bfloat16)
    grad_query = jnp.dot(normed_in.T, grad_query_round, preferred_element_type=jnp.float32)
    grad_keyval = jnp.dot(normed_in.T, grad_keyval_round, preferred_element_type=jnp.float32)
    grad_normed_in = jnp.dot(
        grad_query_round, query_back.T, preferred_element_type=jnp.float32
    ) + jnp.dot(grad_keyval_round, keyval_back.T, preferred_element_type=jnp.float32)
    _, pull_back = jax.vjp(norm_apply, inputs, main_gains[0])
    grad_in_norm, grad_gain_zero = pull_back(grad_normed_in)
    input_grad = grad_middle + grad_in_norm
    grad_gains = jnp.stack([grad_gain_zero, grad_gain_one, grad_gain_two, grad_gain_three])
    grad_heads = jnp.stack([grad_head_zero, grad_head_one])
    query_grad, keyval_grad, output_grad, gateup_grad, down_grad, norm_grad, qknorm_grad = (
        lax.psum_scatter(grad_query, "dp", scatter_dimension=0, tiled=True),
        lax.psum_scatter(grad_keyval, "dp", scatter_dimension=0, tiled=True),
        lax.psum_scatter(grad_output, "dp", scatter_dimension=0, tiled=True),
        lax.psum_scatter(grad_gateup, "dp", scatter_dimension=0, tiled=True),
        lax.psum_scatter(grad_down, "dp", scatter_dimension=0, tiled=True),
        lax.psum_scatter(grad_gains, "dp", scatter_dimension=1, tiled=True),
        lax.psum_scatter(grad_heads, "dp", scatter_dimension=1, tiled=True),
    )
    parameters = (
        query_weight,
        keyval_weight,
        output_weight,
        gateup_weight,
        down_weight,
        norm_gains,
        qknorm_gains,
    )
    gradients = (
        query_grad,
        keyval_grad,
        output_grad,
        gateup_grad,
        down_grad,
        norm_grad,
        qknorm_grad,
    )
    firsts = (query_mean, keyval_mean, output_mean, gateup_mean, down_mean, norm_mean, qknorm_mean)
    seconds = (
        query_square,
        keyval_square,
        output_square,
        gateup_square,
        down_square,
        norm_square,
        qknorm_square,
    )
    decays = (decay_coef, decay_coef, decay_coef, decay_coef, decay_coef, 0.0, 0.0)
    updates = [
        adam_update(
            parameters[place], gradients[place], firsts[place], seconds[place], decays[place]
        )
        for place in range(7)
    ]
    news = tuple((update[0] for update in updates))
    first_news = tuple((update[1] for update in updates))
    second_news = tuple((update[2] for update in updates))
    result_out = result.reshape(seq_count, length, model_width)
    input_out = input_grad.reshape(seq_count, length, model_width)
    return (result_out, input_out) + gradients + news + first_news + second_news


def solution(mesh):
    in_specs = (
        P("dp", None, None),
        P("dp", None),
        P("dp", None, None),
        P("dp", None),
        P("dp", None),
        P("dp", None),
        P("dp", None, None),
        P("dp", None),
        P(None, "dp"),
        P(None, "dp"),
        P("dp", None),
        P("dp", None),
        P("dp", None),
        P("dp", None, None),
        P("dp", None),
        P(None, "dp"),
        P(None, "dp"),
        P("dp", None),
        P("dp", None),
        P("dp", None),
        P("dp", None, None),
        P("dp", None),
        P(None, "dp"),
        P(None, "dp"),
    )
    out_specs = (
        P("dp", None, None),
        P("dp", None, None),
        P("dp", None),
        P("dp", None),
        P("dp", None),
        P("dp", None, None),
        P("dp", None),
        P(None, "dp"),
        P(None, "dp"),
        P("dp", None),
        P("dp", None),
        P("dp", None),
        P("dp", None, None),
        P("dp", None),
        P(None, "dp"),
        P(None, "dp"),
        P("dp", None),
        P("dp", None),
        P("dp", None),
        P("dp", None, None),
        P("dp", None),
        P(None, "dp"),
        P(None, "dp"),
        P("dp", None),
        P("dp", None),
        P("dp", None),
        P("dp", None, None),
        P("dp", None),
        P(None, "dp"),
        P(None, "dp"),
    )
    return jax.shard_map(
        per_device, mesh=mesh, in_specs=in_specs, out_specs=out_specs, check_vma=False
    )
```

profile of v0, /device:TPU:1, one launch (start us, length us, event | category | flops | bytes accessed | tf_op | source)
XLA Modules:
  0.0 802.2 jit_solution(10100386324379047528)
XLA Ops:
  14.7 43.1 %all-gather = bf16[32,20,4]{1,2,0:T(4,128)(2,1)S(1)} all-gather(bf16[1,20,4]{1,2,0:T(4,128)(2,1)S(1)} %convert_bitcast_fusion.3), channel_id=1, replica_groups=mesh['dp'=32] {'dp'}, dimensions={0}, use_global_device_ids=true | all-gather | bytes 5280 | tf_op jit(solution)/shard_map/all_gather | solution.py:142
  59.0 38.9 %all-gather.1 = bf16[32,20,512]{2,1,0:T(8,128)(2,1)S(1)} all-gather(bf16[1,20,512]{2,1,0:T(8,128)(2,1)S(1)} %convert_bitcast_fusion.2), channel_id=1, replica_groups=mesh['dp'=32] {'dp'}, dimensions={0}, use_global_device_ids=true | all-gather | bytes 675840 | tf_op jit(solution)/shard_map/all_gather | solution.py:138
  98.3 37.9 %all-gather.2 = bf16[32,8,2]{1,2,0:T(2,128)(2,1)S(1)} all-gather(bf16[1,8,2]{1,2,0:T(2,128)(2,1)S(1)} %convert_bitcast_fusion.4), channel_id=1, replica_groups=mesh['dp'=32] {'dp'}, dimensions={0}, use_global_device_ids=true | all-gather | bytes 1056 | tf_op jit(solution)/shard_map/all_gather | solution.py:143
  142.5 2.5 multiply_reduce_fusion.2
  149.8 2.8 multiply_reduce_fusion.9
  153.7 40.7 %all-gather.11.cloned.1.call-done = bf16[640,2,2048]{2,1,0:T(2,128)(2,1)} async-done(((bf16[20,2,2048]{2,1,0:T(2,128)(2,1)}), bf16[640,2,2048]{2,1,0:T(2,128)(2,1)}) %all-gather.11.cloned.1.call-update) | async-done | bytes 5242896 | tf_op jit(solution)/shard_map/all_gather | solution.py:140
  194.4 5.8 copy.116
  200.2 3.5 fusion.83
  203.8 3.3 copy-done
  207.0 2.7 multiply_convert_fusion.1
  209.7 44.8 %all-gather.13.cloned.1.call-done = bf16[2048,640]{1,0:T(8,128)(2,1)} async-done(((bf16[64,640]{1,0:T(8,128)(2,1)}), bf16[2048,640]{1,0:T(8,128)(2,1)}) %all-gather.13.cloned.1.call-update) | async-done | bytes 2621456 | tf_op jit(solution)/shard_map/all_gather | solution.py:141
  254.5 4.4 multiply_reduce_fusion.7
  261.5 4.6 fusion.8
  268.1 5.9 fusion.14
  274.0 14.3 %reshape.356 = f32[640,2,2048]{2,1,0:T(2,128)} reshape(f32[640,4096]{1,0:T(8,128)} %fusion.14) | data formatting | bytes 20971520 | tf_op jit(solution)/shard_map/reshape | solution.py:200
  288.4 7.7 multiply_reduce_fusion.3
  298.6 2.5 fusion.95
  302.2 5.8 fusion.96
  308.0 3.3 convolution_convert_fusion.1
  315.8 4.0 fusion.11
  327.9 2.5 fusion.44
  330.5 86.9 %fusion.86 = (f32[24,1024]{1,0:T(8,128)S(1)}, f32[24,512]{1,0:T(8,128)S(1)}) fusion(f32[640,1024]{1,0:T(8,128)} %fusion.44, f32[640,512]{1,0:T(8,128)S(1)} %copy-done.32), kind=kCustom, calls=%all-reduce-scatter.2 | all-reduce-scatter fusion | flops 1179649 | bytes 4079616
  428.5 45.1 %all-reduce.7 = (f32[4,640]{1,0:T(4,128)S(1)}, f32[2,256]{1,0:T(2,128)S(1)}) all-reduce(f32[4,640]{1,0:T(4,128)S(1)} %pad_maximum_fusion.6, f32[2,256]{1,0:T(2,128)S(1)} %pad_maximum_fusion.7), channel_id=7, replica_groups=mesh['dp'=32] {'dp'}, use_global_device_ids=true, to_apply=%region_24.25.clone | all-reduce | flops 3072 | bytes 24576
  473.7 2.9 fusion.37
  477.4 4.4 collective-permute-start.6
  484.0 3.1 collective-permute-start.4
  487.1 2.8 collective-permute-start.3
  490.0 4.2 collective-permute-start.2
  497.8 4.0 collective-permute-start
  506.1 3.2 multiply_subtract_fusion
  509.3 142.4 %reduce-scatter.9.cloned.1.call-done = f32[32,640]{1,0:T(8,128)} async-done(((f32[1024,640]{1,0:T(8,128)}), f32[32,640]{1,0:T(8,128)}) %reduce-scatter.9.cloned.1.call-update) | async-done | bytes 81936 | tf_op jit(solution)/shard_map/reduce_scatter | solution.py:246
  653.3 140.1 %reduce-scatter.11.cloned.1.call-done = f32[64,640]{1,0:T(8,128)} async-done(((f32[2048,640]{1,0:T(8,128)}), f32[64,640]{1,0:T(8,128)}) %reduce-scatter.11.cloned.1.call-update) | async-done | bytes 163856 | tf_op jit(solution)/shard_map/reduce_scatter | solution.py:248
  (230 shorter events, 66.6 us)
Async XLA Ops:
  7.2 90.8 %copy-start.5 = (bf16[1,512,640]{2,1,0:T(8,128)(2,1)S(1)}, bf16[1,512,640]{2,1,0:T(8,128)(2,1)}, u32[]{:S(2)}) copy-start(bf16[1,512,640]{2,1,0:T(8,128)(2,1)} %param.32) | copy-start | bytes 1966084
  7.2 131.3 %all-gather.15.cloned.1.call-start = ((), (), s32[]{:S(2)}) async-start(), calls=%async_computation.7 | async-start | bytes 1622016 | tf_op jit(solution)/shard_map/all_gather | solution.py:137
  8.9 140.9 %all-gather.9.cloned.1.call-start = ((), (), s32[]{:S(2)}) async-start(), calls=%async_computation.2 | async-start | bytes 1351680 | tf_op jit(solution)/shard_map/all_gather | solution.py:139
  10.4 87.8 %copy-start.58 = (f32[2,8]{1,0:T(2,128)S(1)}, f32[2,8]{1,0:T(2,128)}, u32[]{:S(2)}) copy-start(f32[2,8]{1,0:T(2,128)} %param.41) | copy-start | bytes 196
  10.5 184.0 %all-gather.11.cloned.1.call-start = ((), (), s32[]{:S(2)}) async-start(), calls=%async_computation.3 | async-start | bytes 5406720 | tf_op jit(solution)/shard_map/all_gather | solution.py:140
  12.3 242.2 %all-gather.13.cloned.1.call-start = ((), (), s32[]{:S(2)}) async-start(), calls=%async_computation.4 | async-start | bytes 2703360 | tf_op jit(solution)/shard_map/all_gather | solution.py:141
  13.9 492.2 %all-reduce.11.cloned.1.call-start = ((), (), s32[]{:S(2)}) async-start(), calls=%async_computation.8 | async-start | bytes 20971520
  288.3 363.4 %reduce-scatter.9.cloned.1.call-start = ((), (), s32[]{:S(2)}) async-start(), calls=%async_computation.5 | async-start | bytes 2703360 | tf_op jit(solution)/shard_map/reduce_scatter | solution.py:246
  301.1 492.3 %reduce-scatter.11.cloned.1.call-start = ((), (), s32[]{:S(2)}) async-start(), calls=%async_computation.6 | async-start | bytes 5406720 | tf_op jit(solution)/shard_map/reduce_scatter | solution.py:248
  330.4 95.0 %copy-start.55 = (f32[640]{0:T(1024)S(1)}, f32[640]{0:T(1024)}, u32[]{:S(2)}) copy-start(f32[640]{0:T(1024)} %get-tuple-element.74) | copy-start | bytes 7684
  330.4 95.0 %copy-start.20 = (bf16[640,512]{1,0:T(8,128)(2,1)S(1)}, bf16[640,512]{1,0:T(8,128)(2,1)}, u32[]{:S(2)}) copy-start(bf16[640,512]{1,0:T(8,128)(2,1)} %copy-done.19) | copy-start | bytes 1966084
  330.4 95.0 %copy-start.35 = (bf16[512,256]{0,1:T(8,128)(2,1)S(1)}, bf16[512,256]{0,1:T(8,128)(2,1)}, u32[]{:S(2)}) copy-start(bf16[512,256]{0,1:T(8,128)(2,1)} %copy-done.34) | copy-start | bytes 786436
  330.4 95.0 %copy-start.42 = (bf16[512,256]{0,1:T(8,128)(2,1)S(1)}, bf16[512,256]{0,1:T(8,128)(2,1)}, u32[]{:S(2)}) copy-start(bf16[512,256]{0,1:T(8,128)(2,1)} %copy-done.41) | copy-start | bytes 786436
  417.4 64.4 %collective-permute-start.10 = (f32[24,512]{1,0:T(8,128)S(1)}, f32[24,512]{1,0:T(8,128)S(1)}, u32[]{:S(2)}, u32[]{:S(2)}) collective-permute-start(f32[24,512]{1,0:T(8,128)S(1)} %get-tuple-element.91), channel_id=1, source_target_pairs={{0,5},{1,6},{2,7},{3,8},{4,9},{5,10},{6,11},{7,12},{8,13},{9,14},{... | collective-permute-start | bytes 147464
  418.8 65.2 %collective-permute-start.9 = (f32[24,512]{1,0:T(8,128)S(1)}, f32[24,512]{1,0:T(8,128)S(1)}, u32[]{:S(2)}, u32[]{:S(2)}) collective-permute-start(f32[24,512]{1,0:T(8,128)S(1)} %get-tuple-element.91), channel_id=1, source_target_pairs={{0,4},{1,5},{2,6},{3,7},{4,8},{5,9},{6,10},{7,11},{8,12},{9,13},{1... | collective-permute-start | bytes 147464
  420.1 67.0 %collective-permute-start.8 = (f32[24,512]{1,0:T(8,128)S(1)}, f32[24,512]{1,0:T(8,128)}, u32[]{:S(2)}, u32[]{:S(2)}) collective-permute-start(f32[24,512]{1,0:T(8,128)S(1)} %get-tuple-element.91), channel_id=1, source_target_pairs={{0,3},{1,4},{2,5},{3,6},{4,7},{5,8},{6,9},{7,10},{8,11},{9,12},{10... | collective-permute-start | bytes 147464
  422.0 67.9 %collective-permute-start.7 = (f32[24,512]{1,0:T(8,128)S(1)}, f32[24,512]{1,0:T(8,128)}, u32[]{:S(2)}, u32[]{:S(2)}) collective-permute-start(f32[24,512]{1,0:T(8,128)S(1)} %get-tuple-element.91), channel_id=1, source_target_pairs={{0,2},{1,3},{2,4},{3,5},{4,6},{5,7},{6,8},{7,9},{8,10},{9,11},{10,... | collective-permute-start | bytes 147464
  423.9 53.5 %collective-permute-start.11 = (f32[4,512]{1,0:T(4,128)S(1)}, f32[4,512]{1,0:T(4,128)S(1)}, u32[]{:S(2)}, u32[]{:S(2)}) collective-permute-start(f32[4,512]{1,0:T(4,128)S(1)} %slice.86), channel_id=1, source_target_pairs={{0,6},{1,7},{2,8},{3,9},{4,10},{5,11},{6,12},{7,13},{8,14},{9,15},... | collective-permute-start | bytes 24584
  426.1 47.5 %copy-start.14 = (f32[512,640]{1,0:T(8,128)S(1)}, f32[512,640]{1,0:T(8,128)}, u32[]{:S(2)}) copy-start(f32[512,640]{1,0:T(8,128)} %copy-done.13) | copy-start | bytes 3932164
  477.4 16.7 %collective-permute-start.6 = (f32[24,512]{1,0:T(8,128)S(1)}, f32[24,512]{1,0:T(8,128)S(1)}, u32[]{:S(2)}, u32[]{:S(2)}) collective-permute-start(f32[24,512]{1,0:T(8,128)S(1)} %get-tuple-element.91), channel_id=1, source_target_pairs={{0,1},{1,2},{2,3},{3,4},{4,5},{5,6},{6,7},{7,8},{8,9},{9,10},{10,1... | collective-permute-start | bytes 147464
  481.8 15.9 %collective-permute-start.5 = (f32[4,1024]{1,0:T(4,128)S(1)}, f32[4,1024]{1,0:T(4,128)S(1)}, u32[]{:S(2)}, u32[]{:S(2)}) collective-permute-start(f32[4,1024]{1,0:T(4,128)S(1)} %slice.85), channel_id=1, source_target_pairs={{0,6},{1,7},{2,8},{3,9},{4,10},{5,11},{6,12},{7,13},{8,14},{9,15},... | collective-permute-start | bytes 49160
  484.0 18.5 %collective-permute-start.4 = (f32[24,1024]{1,0:T(8,128)S(1)}, f32[24,1024]{1,0:T(8,128)S(1)}, u32[]{:S(2)}, u32[]{:S(2)}) collective-permute-start(f32[24,1024]{1,0:T(8,128)S(1)} %get-tuple-element.90), channel_id=1, source_target_pairs={{0,5},{1,6},{2,7},{3,8},{4,9},{5,10},{6,11},{7,12},{8,13},{9,14},{... | collective-permute-start | bytes 294920
  487.1 15.4 %collective-permute-start.3 = (f32[24,1024]{1,0:T(8,128)S(1)}, f32[24,1024]{1,0:T(8,128)S(1)}, u32[]{:S(2)}, u32[]{:S(2)}) collective-permute-start(f32[24,1024]{1,0:T(8,128)S(1)} %get-tuple-element.90), channel_id=1, source_target_pairs={{0,4},{1,5},{2,6},{3,7},{4,8},{5,9},{6,10},{7,11},{8,12},{9,13},{1... | collective-permute-start | bytes 294920
  490.0 12.6 %collective-permute-start.2 = (f32[24,1024]{1,0:T(8,128)S(1)}, f32[24,1024]{1,0:T(8,128)S(1)}, u32[]{:S(2)}, u32[]{:S(2)}) collective-permute-start(f32[24,1024]{1,0:T(8,128)S(1)} %get-tuple-element.90), channel_id=1, source_target_pairs={{0,3},{1,4},{2,5},{3,6},{4,7},{5,8},{6,9},{7,10},{8,11},{9,12},{10... | collective-permute-start | bytes 294920
  494.1 8.4 %collective-permute-start.1 = (f32[24,1024]{1,0:T(8,128)S(1)}, f32[24,1024]{1,0:T(8,128)S(1)}, u32[]{:S(2)}, u32[]{:S(2)}) collective-permute-start(f32[24,1024]{1,0:T(8,128)S(1)} %get-tuple-element.90), channel_id=1, source_target_pairs={{0,2},{1,3},{2,4},{3,5},{4,6},{5,7},{6,8},{7,9},{8,10},{9,11},{10,... | collective-permute-start | bytes 294920
  497.8 5.6 collective-permute-start
  502.5 149.2 %copy-start.38 = (f32[32,640]{1,0:T(8,128)S(1)}, f32[32,640]{1,0:T(8,128)}, u32[]{:S(2)}) copy-start(f32[32,640]{1,0:T(8,128)} %param.37) | copy-start | bytes 245764
  502.5 149.2 %copy-start.48 = (f32[32,640]{1,0:T(8,128)S(1)}, f32[32,640]{1,0:T(8,128)}, u32[]{:S(2)}) copy-start(f32[32,640]{1,0:T(8,128)} %param.44) | copy-start | bytes 245764
  502.5 149.2 %copy-start.49 = (f32[32,640]{1,0:T(8,128)S(1)}, f32[32,640]{1,0:T(8,128)}, u32[]{:S(2)}) copy-start(f32[32,640]{1,0:T(8,128)} %param.51) | copy-start | bytes 245764
  504.4 289.0 %copy-start.36 = (f32[64,640]{1,0:T(8,128)S(1)}, f32[64,640]{1,0:T(8,128)}, u32[]{:S(2)}) copy-start(f32[64,640]{1,0:T(8,128)} %param.39) | copy-start | bytes 491524
  504.4 289.0 %copy-start.44 = (f32[64,640]{1,0:T(8,128)S(1)}, f32[64,640]{1,0:T(8,128)}, u32[]{:S(2)}) copy-start(f32[64,640]{1,0:T(8,128)} %param.46) | copy-start | bytes 491524
  504.4 289.0 %copy-start.45 = (f32[64,640]{1,0:T(8,128)S(1)}, f32[64,640]{1,0:T(8,128)}, u32[]{:S(2)}) copy-start(f32[64,640]{1,0:T(8,128)} %param.53) | copy-start | bytes 491524
  (50 other events, 489.1 us)
Sparse Core Ops, SparseCore 0:
  11.5 58.5 all-gather.14
  73.5 53.1 all-gather.8
  130.2 64.2 all-gather.10
  197.7 56.7 all-gather.12
  288.4 217.6 all-reduce.10
  508.8 142.8 reduce-scatter.8
  654.5 138.8 reduce-scatter.10
where the time goes:
time: 813 us; the launch traced here: 802 us
  waiting for transfers between devices  370 us (46%)
  blocking collectives  252 us (31%)
  matrix products  61.4 us (8%)
  local copies, waits for them, and re-layouts  42.8 us (5%)
  other arithmetic  30.6 us (4%)
  starting transfers between devices  29.9 us (4%)
  between operations  15.5 us (2%)
    reduce_scatter x1, waiting for transfers between devices, per_device(): lax.psum_scatter(grad_output, 'dp', scatter_dimension=0, tiled=True)  142 us
    reduce_scatter x1, waiting for transfers between devices, per_device(): lax.psum_scatter(grad_down, 'dp', scatter_dimension=0, tiled=True)  140 us
    unnamed x2, blocking collectives  132 us
    all_gather x1, waiting for transfers between devices, per_device(): lax.all_gather(down_round, 'dp', axis=0, tiled=True)  44.8 us
    all_gather x1, blocking collectives, per_device(): lax.all_gather(gains_round, 'dp', axis=1, tiled=True)  43.1 us
    all_gather x1, waiting for transfers between devices, per_device(): lax.all_gather(gateup_round, 'dp', axis=0, tiled=True)  40.7 us
    all_gather x1, blocking collectives, per_device(): lax.all_gather(keyval_round, 'dp', axis=0, tiled=True)  38.9 us
    all_gather x1, blocking collectives, per_device(): lax.all_gather(headgain_round, 'dp', axis=1, tiled=True)  37.9 us
  transfers between devices with their start and end apart: 19, of which 6 were waited for; matrix products, arithmetic and copies ran while one was open for 22% of the time, Pallas kernels for 0%

commit v1 on v0

--- a/solution.py
+++ b/solution.py
@@ -1,9 +1,304 @@
 import jax
 import jax.numpy as jnp
+import numpy as np
 from jax import lax
+from jax.experimental import pallas as pl
+from jax.experimental.pallas import tpu as pltpu
 from jax.sharding import PartitionSpec as P
 
 STEP = 3
+DIMS = (4, 2, 2, 2)
+BF = jnp.bfloat16
+
+
+def shift_perm(axis, amount):
+    pairs = []
+    for place in range(int(np.prod(DIMS))):
+        spot = list(np.unravel_index(place, DIMS))
+        spot[axis] = (spot[axis] + amount) % DIMS[axis]
+        pairs.append((place, int(np.ravel_multi_index(spot, DIMS))))
+    return pairs
+
+
+def shift(values, axis, amount):
+    return lax.ppermute(values, "dp", shift_perm(axis, amount))
+
+
+def own_coords():
+    place = lax.axis_index("dp")
+    return place // 8, (place // 4) % 2, (place // 2) % 2, place % 2
+
+
+def gather_pieces(block):
+    near = [block] + [shift(block, 0, -step) for step in (1, 2, 3)]
+    first = jnp.stack([near[0], near[1]])
+    second = jnp.stack([near[2], near[3]])
+    pair_a = jnp.stack([first, shift(first, 2, 1)])
+    pair_b = jnp.stack([second, shift(second, 1, 1)])
+    across_a = shift(pair_a, 1, 1)
+    across_b = shift(pair_b, 2, 1)
+    mine = [pair_a, across_a, pair_b, across_b]
+    return mine + [shift(piece, 3, 1) for piece in mine]
+
+
+def piece_spots(coords_ref):
+    for group in range(8):
+        far_core, kind = group // 4, group % 4
+        for one in range(2):
+            for two in range(2):
+                if kind < 2:
+                    gap = (two, kind, one)
+                else:
+                    gap = (2 + two, one, kind - 2)
+                along = lax.rem(coords_ref[0] + gap[0], 4)
+                upward = lax.rem(coords_ref[1] + gap[1], 2)
+                sideways = lax.rem(coords_ref[2] + gap[2], 2)
+                core = lax.rem(coords_ref[3] + far_core, 2)
+                yield group, one, two, (along * 2 + upward) * 2 + sideways, core
+
+
+def fetch_pieces(coords_ref, piece_refs, room, arrived):
+    copies = []
+    for group, one, two, chip, core in piece_spots(coords_ref):
+        copies.append(
+            pltpu.make_async_copy(
+                piece_refs[group].at[one, two], room.at[core, chip], arrived
+            )
+        )
+    for copy in copies:
+        copy.start()
+    for copy in copies:
+        copy.wait()
+
+
+def assemble_attention(coords_ref, *refs):
+    piece_refs, (query_ref, keyval_ref, output_ref, gains_ref), (room, arrived) = (
+        refs[:8],
+        refs[8:12],
+        refs[12:],
+    )
+    fetch_pieces(coords_ref, piece_refs, room, arrived)
+    gains = jnp.zeros((8, 640), jnp.float32)
+    for core in range(2):
+        for chip in range(16):
+            rows = slice(40 * chip, 40 * chip + 40)
+            query_ref[rows, 512 * core : 512 * core + 512] = room[core, chip, :, 0:512]
+            keyval_ref[rows, 256 * core : 256 * core + 256] = room[core, chip, :, 512:768]
+            spot = 32 * (2 * chip + core)
+            output_ref[spot : spot + 32, :] = room[core, chip, 0:32, 768:1408]
+            gains = gains + room[core, chip, 32:40, 768:1408].astype(jnp.float32)
+    gains_ref[...] = gains
+
+
+def assemble_gateup(coords_ref, *refs):
+    piece_refs, gateup_ref, (room, arrived) = refs[:8], refs[8], refs[9:]
+    fetch_pieces(coords_ref, piece_refs, room, arrived)
+    for core in range(2):
+        for chip in range(16):
+            gateup_ref[40 * chip : 40 * chip + 40, 2048 * core : 2048 * core + 2048] = room[core, chip]
+
+
+def assemble_down(coords_ref, *refs):
+    piece_refs, down_ref, (room, arrived) = refs[:8], refs[8], refs[9:]
+    fetch_pieces(coords_ref, piece_refs, room, arrived)
+    for core in range(2):
+        for chip in range(16):
+            spot = 64 * (2 * chip + core)
+            down_ref[spot : spot + 64, :] = room[core, chip]
+
+
+def run_assemble(kernel, coords, pieces, outs):
+    return pl.pallas_call(
+        kernel,
+        out_shape=outs,
+        in_specs=[pl.BlockSpec(memory_space=pltpu.SMEM)] + [pl.BlockSpec(memory_space=pl.ANY)] * 8,
+        out_specs=jax.tree.map(lambda _: pl.BlockSpec(memory_space=pltpu.VMEM), outs),
+        scratch_shapes=[
+            pltpu.VMEM((2, 16) + pieces[0].shape[2:], BF),
+            pltpu.SemaphoreType.DMA,
+        ],
+        compiler_params=pltpu.CompilerParams(vmem_limit_bytes=48 * 1024 * 1024),
+    )(coords, *pieces)
+
+
+def send_spots(coords_ref):
+    for far_core in range(2):
+        core = lax.rem(coords_ref[3] + far_core, 2)
+        for group in range(2):
+            for one in range(2):
+                for two in range(2):
+                    for three in range(2):
+                        gap = (three, one, two) if group == 0 else (2 + three, two, one)
+                        along = lax.rem(coords_ref[0] + gap[0], 4)
+                        upward = lax.rem(coords_ref[1] + gap[1], 2)
+                        sideways = lax.rem(coords_ref[2] + gap[2], 2)
+                        chip = (along * 2 + upward) * 2 + sideways
+                        yield 2 * far_core + group, one, two, three, chip, core
+
+
+def post_pieces(coords_ref, room, out_refs, posted):
+    copies = []
+    for which, one, two, three, chip, core in send_spots(coords_ref):
+        copies.append(
+            pltpu.make_async_copy(
+                room.at[core, chip], out_refs[which].at[one, two, three], posted
+            )
+        )
+    for copy in copies:
+        copy.start()
+    for copy in copies:
+        copy.wait()
+
+
+def split_attention(coords_ref, query_ref, keyval_ref, output_ref, gains_ref, *refs):
+    out_refs, (room, posted) = refs[:4], refs[4:]
+    gains = gains_ref[...].astype(BF)
+    for core in range(2):
+        for chip in range(16):
+            rows = slice(40 * chip, 40 * chip + 40)
+            room[core, chip, :, 0:512] = query_ref[rows, 512 * core : 512 * core + 512].astype(BF)
+            room[core, chip, :, 512:768] = keyval_ref[rows, 256 * core : 256 * core + 256].astype(BF)
+            spot = 32 * (2 * chip + core)
+            room[core, chip, 0:32, 768:1408] = output_ref[spot : spot + 32, :].astype(BF)
+            room[core, chip, 32:40, 768:1408] = gains
+    post_pieces(coords_ref, room, out_refs, posted)
+
+
+def split_gateup(coords_ref, gateup_ref, *refs):
+    out_refs, (room, posted) = refs[:4], refs[4:]
+    for core in range(2):
+        for chip in range(16):
+            room[core, chip] = gateup_ref[
+                40 * chip : 40 * chip + 40, 2048 * core : 2048 * core + 2048
+            ].astype(BF)
+    post_pieces(coords_ref, room, out_refs, posted)
+
+
+def split_down(coords_ref, down_ref, *refs):
+    out_refs, (room, posted) = refs[:4], refs[4:]
+    for core in range(2):
+        for chip in range(16):
+            spot = 64 * (2 * chip + core)
+            room[core, chip] = down_ref[spot : spot + 64, :].astype(BF)
+    post_pieces(coords_ref, room, out_refs, posted)
+
+
+def run_split(kernel, coords, grads, rows, columns):
+    outs = [jax.ShapeDtypeStruct((2, 2, 2, rows, columns), BF)] * 4
+    return pl.pallas_call(
+        kernel,
+        out_shape=outs,
+        in_specs=[pl.BlockSpec(memory_space=pltpu.SMEM)]
+        + [pl.BlockSpec(memory_space=pltpu.VMEM)] * len(grads),
+        out_specs=[pl.BlockSpec(memory_space=pl.ANY)] * 4,
+        scratch_shapes=[pltpu.VMEM((2, 16, rows, columns), BF), pltpu.SemaphoreType.DMA],
+        compiler_params=pltpu.CompilerParams(vmem_limit_bytes=48 * 1024 * 1024),
+    )(coords, *grads)
+
+
+def wide(values):
+    return values.astype(jnp.float32)
+
+
+def scatter_pieces(keep_a, keep_b, send_a, send_b):
+    got_a, got_b = shift(send_a, 3, 1), shift(send_b, 3, 1)
+    far_a = shift((wide(keep_a[1]) + wide(got_a[1])).astype(BF), 1, 1)
+    far_b = shift((wide(keep_b[1]) + wide(got_b[1])).astype(BF), 2, 1)
+    sum_a = wide(keep_a[0]) + wide(got_a[0]) + wide(far_a)
+    sum_b = wide(keep_b[0]) + wide(got_b[0]) + wide(far_b)
+    side_a = shift(sum_a[1].astype(BF), 2, 1)
+    side_b = shift(sum_b[1].astype(BF), 1, 1)
+    last_a = sum_a[0] + wide(side_a)
+    last_b = sum_b[0] + wide(side_b)
+    total = last_a[0]
+    total = total + wide(shift(last_a[1].astype(BF), 0, 1))
+    total = total + wide(shift(last_b[0].astype(BF), 0, 2))
+    total = total + wide(shift(last_b[1].astype(BF), 0, 3))
+    return total
+
+
+def swap_halves(core, low, high):
+    return jnp.where(core == 0, high, low), jnp.where(core == 0, low, high)
+
+
+def gather_all(query_round, keyval_round, output_round, gateup_round, down_round, gains, heads):
+    along, upward, sideways, core = own_coords()
+    coords = jnp.stack([along, upward, sideways, core]).astype(jnp.int32)
+    low = jnp.concatenate([query_round[:, :512], keyval_round[:, :256], gateup_round[:, 0]], axis=1)
+    high = jnp.concatenate([query_round[:, 512:], keyval_round[:, 256:], gateup_round[:, 1]], axis=1)
+    away, keep = swap_halves(core, low, high)
+    got = shift(away, 3, 1)
+    both = jnp.concatenate(
+        [jnp.where(core == 0, keep, got), jnp.where(core == 0, got, keep)], axis=0
+    )
+    place = lax.axis_index("dp")
+    spread = jnp.zeros((8, 640), BF)
+    spread = lax.dynamic_update_slice(spread, gains, (0, place * gains.shape[1]))
+    spread = lax.dynamic_update_slice(spread, heads, (4, place * heads.shape[1]))
+    block_a = jnp.concatenate([both[:, :768], jnp.concatenate([output_round, spread], axis=0)], axis=1)
+    block_g = both[:, 768:]
+    pieces_a = gather_pieces(block_a)
+    pieces_g = gather_pieces(block_g)
+    pieces_w = gather_pieces(down_round)
+    shape = jax.ShapeDtypeStruct
+    query_full, keyval_full, output_full, gains_full = run_assemble(
+        assemble_attention,
+        coords,
+        pieces_a,
+        [shape((640, 1024), BF), shape((640, 512), BF), shape((1024, 640), BF), shape((8, 640), jnp.float32)],
+    )
+    gateup_full = run_assemble(assemble_gateup, coords, pieces_g, shape((640, 4096), BF))
+    down_full = run_assemble(assemble_down, coords, pieces_w, shape((2048, 640), BF))
+    return query_full, keyval_full, output_full, gateup_full, down_full, gains_full[:4], gains_full[4:6, :256]
+
+
+def scatter_all(grad_query, grad_keyval, grad_output, grad_gateup, grad_down, grad_gains, grad_heads):
+    along, upward, sideways, core = own_coords()
+    place = lax.axis_index("dp")
+    coords = jnp.stack([along, upward, sideways, core]).astype(jnp.int32)
+    down_grad = scatter_pieces(*run_split(split_down, coords, [grad_down], 64, 640))
+    gateup_sum = scatter_pieces(*run_split(split_gateup, coords, [grad_gateup], 40, 2048))
+    small = jnp.concatenate(
+        [grad_gains, jnp.pad(grad_heads, ((0, 2), (0, 640 - grad_heads.shape[1])))], axis=0
+    )
+    rest = scatter_pieces(*run_split(split_attention, coords, [grad_query, grad_keyval, grad_output, small], 40, 1408))
+    output_grad = rest[:32, 768:]
+    norm_grad = lax.dynamic_slice(rest[32:36, 768:], (0, place * 20), (4, 20))
+    qknorm_grad = lax.dynamic_slice(rest[36:38, 768:], (0, place * 8), (2, 8))
+    both = jnp.concatenate([rest[:, :768], gateup_sum], axis=1)
+    away, keep = swap_halves(core, both[:20], both[20:])
+    got = shift(away, 3, 1)
+    low, high = jnp.where(core == 0, keep, got), jnp.where(core == 0, got, keep)
+    query_grad = jnp.concatenate([low[:, :512], high[:, :512]], axis=1)
+    keyval_grad = jnp.concatenate([low[:, 512:768], high[:, 512:768]], axis=1)
+    gateup_grad = jnp.stack([low[:, 768:], high[:, 768:]], axis=1)
+    return query_grad, keyval_grad, output_grad, gateup_grad, down_grad, norm_grad, qknorm_grad
+
+
+def gather_plain(query_round, keyval_round, output_round, gateup_round, down_round, gains_round, headgain_round):
+    gateup_full = lax.all_gather(gateup_round, "dp", axis=0, tiled=True)
+    return (
+        lax.all_gather(query_round, "dp", axis=0, tiled=True),
+        lax.all_gather(keyval_round, "dp", axis=0, tiled=True),
+        lax.all_gather(output_round, "dp", axis=0, tiled=True),
+        gateup_full.reshape(gateup_full.shape[0], -1),
+        lax.all_gather(down_round, "dp", axis=0, tiled=True),
+        lax.all_gather(gains_round, "dp", axis=1, tiled=True).astype(jnp.float32),
+        lax.all_gather(headgain_round, "dp", axis=1, tiled=True).astype(jnp.float32),
+    )
+
+
+def scatter_plain(grad_query, grad_keyval, grad_output, grad_gateup, grad_down, grad_gains, grad_heads):
+    rows = grad_gateup.shape[0]
+    return (
+        lax.psum_scatter(grad_query, "dp", scatter_dimension=0, tiled=True),
+        lax.psum_scatter(grad_keyval, "dp", scatter_dimension=0, tiled=True),
+        lax.psum_scatter(grad_output, "dp", scatter_dimension=0, tiled=True),
+        lax.psum_scatter(grad_gateup.reshape(rows, 2, -1), "dp", scatter_dimension=0, tiled=True),
+        lax.psum_scatter(grad_down, "dp", scatter_dimension=0, tiled=True),
+        lax.psum_scatter(grad_gains, "dp", scatter_dimension=1, tiled=True),
+        lax.psum_scatter(grad_heads, "dp", scatter_dimension=1, tiled=True),
+    )
 
 
 norm_epsilon = 1e-06
@@ -133,23 +428,23 @@
     down_round = down_weight.astype(jnp.bfloat16)
     gains_round = norm_gains.astype(jnp.bfloat16)
     headgain_round = qknorm_gains.astype(jnp.bfloat16)
-    query_full, keyval_full, output_full, gateup_full, down_full, gains_full, headgain_full = (
-        lax.all_gather(query_round, "dp", axis=0, tiled=True),
-        lax.all_gather(keyval_round, "dp", axis=0, tiled=True),
-        lax.all_gather(output_round, "dp", axis=0, tiled=True),
-        lax.all_gather(gateup_round, "dp", axis=0, tiled=True),
-        lax.all_gather(down_round, "dp", axis=0, tiled=True),
-        lax.all_gather(gains_round, "dp", axis=1, tiled=True),
-        lax.all_gather(headgain_round, "dp", axis=1, tiled=True),
+    fast = lax.axis_size("dp") == 32
+    gather, scatter = (gather_all, scatter_all) if fast else (gather_plain, scatter_plain)
+    query_full, keyval_full, output_full, gateup_full, down_full, main_gains, head_gains = gather(
+        query_round,
+        keyval_round,
+        output_round,
+        gateup_round,
+        down_round,
+        gains_round,
+        headgain_round,
     )
     seq_count, length, model_width = tokens.shape
     row_count = seq_count * length
-    head_dim = headgain_full.shape[1]
+    head_dim = head_gains.shape[1]
     head_count = query_full.shape[1] // head_dim
-    hidden_units = gateup_full.shape[2]
+    hidden_units = gateup_full.shape[1] // 2
     score_scale = head_dim ** (-0.5)
-    main_gains = gains_full.astype(jnp.float32)
-    head_gains = headgain_full.astype(jnp.float32)
     inputs = tokens.reshape(row_count, model_width).astype(jnp.float32)
     normed_in = norm_apply(inputs, main_gains[0]).astype(jnp.bfloat16)
     queries = jnp.dot(normed_in, query_full, preferred_element_type=jnp.float32).reshape(
@@ -172,7 +467,7 @@
     normed_mid = norm_apply(middle, main_gains[2]).astype(jnp.bfloat16)
     gate_up = jnp.dot(
         normed_mid,
-        gateup_full.reshape(model_width, 2 * hidden_units),
+        gateup_full,
         preferred_element_type=jnp.float32,
     )
     gate_part = gate_up[:, :hidden_units]
@@ -187,7 +482,7 @@
         gateup_full,
         down_full,
     )
-    gateup_flat = gateup_back.reshape(model_width, 2 * hidden_units)
+    gateup_flat = gateup_back
     grad_out = cotangent.reshape(row_count, model_width).astype(jnp.float32)
     _, pull_back = jax.vjp(norm_apply, down_out, main_gains[3])
     grad_down_out, grad_gain_three = pull_back(grad_out)
@@ -197,9 +492,7 @@
     _, pull_back = jax.vjp(gelu_product, gate_part, up_part)
     grad_gate, grad_up = pull_back(grad_hidden)
     grad_gate_up = jnp.concatenate([grad_gate, grad_up], axis=1).astype(jnp.bfloat16)
-    grad_gateup = jnp.dot(normed_mid.T, grad_gate_up, preferred_element_type=jnp.float32).reshape(
-        model_width, 2, hidden_units
-    )
+    grad_gateup = jnp.dot(normed_mid.T, grad_gate_up, preferred_element_type=jnp.float32)
     grad_normed_mid = jnp.dot(grad_gate_up, gateup_flat.T, preferred_element_type=jnp.float32)
     _, pull_back = jax.vjp(norm_apply, middle, main_gains[2])
     grad_mid_norm, grad_gain_two = pull_back(grad_normed_mid)
@@ -240,14 +533,8 @@
     input_grad = grad_middle + grad_in_norm
     grad_gains = jnp.stack([grad_gain_zero, grad_gain_one, grad_gain_two, grad_gain_three])
     grad_heads = jnp.stack([grad_head_zero, grad_head_one])
-    query_grad, keyval_grad, output_grad, gateup_grad, down_grad, norm_grad, qknorm_grad = (
-        lax.psum_scatter(grad_query, "dp", scatter_dimension=0, tiled=True),
-        lax.psum_scatter(grad_keyval, "dp", scatter_dimension=0, tiled=True),
-        lax.psum_scatter(grad_output, "dp", scatter_dimension=0, tiled=True),
-        lax.psum_scatter(grad_gateup, "dp", scatter_dimension=0, tiled=True),
-        lax.psum_scatter(grad_down, "dp", scatter_dimension=0, tiled=True),
-        lax.psum_scatter(grad_gains, "dp", scatter_dimension=1, tiled=True),
-        lax.psum_scatter(grad_heads, "dp", scatter_dimension=1, tiled=True),
+    gradients = scatter(
+        grad_query, grad_keyval, grad_output, grad_gateup, grad_down, grad_gains, grad_heads
     )
     parameters = (
         query_weight,
@@ -257,15 +544,6 @@
         down_weight,
         norm_gains,
         qknorm_gains,
-    )
-    gradients = (
-        query_grad,
-        keyval_grad,
-        output_grad,
-        gateup_grad,
-        down_grad,
-        norm_grad,
-        qknorm_grad,
     )
     firsts = (query_mean, keyval_mean, output_mean, gateup_mean, down_mean, norm_mean, qknorm_mean)
     seconds = (

time: 813 us -> 308 us (0.38)
  waiting for transfers between devices: 370 us -> 72.4 us
  blocking collectives: 252 us -> 0 us
  starting transfers between devices: 29.9 us -> 82 us
  Pallas kernels: 0 us -> 44.3 us
  local copies, waits for them, and re-layouts: 42.8 us -> 18.5 us
  between operations: 15.5 us -> 2.69 us
  matrix products: 61.4 us -> 51.8 us
    reduce_scatter x2 -> x0, waiting for transfers between devices: 283 us -> none  [the longest x1 142 us: per_device(): lax.psum_scatter(grad_output, 'dp', scatter_dimension=0, tiled=True)]
    unnamed x2 -> x0, blocking collectives: 132 us -> none
    all_gather x3 -> x0, blocking collectives: 120 us -> none  [the longest x1 43.1 us: per_device(): lax.all_gather(gains_round, 'dp', axis=1, tiled=True)]
    all_gather x4 -> x0, waiting for transfers between devices: 85.6 us -> none  [the longest x1 44.8 us: per_device(): lax.all_gather(down_round, 'dp', axis=0, tiled=True)]
    ppermute x0 -> x62, starting transfers between devices: none -> 82 us  [shift(): return lax.ppermute(values, 'dp', shift_perm(axis, amount))]
    ppermute x0 -> x62, waiting for transfers between devices: none -> 72.4 us  [shift(): return lax.ppermute(values, 'dp', shift_perm(axis, amount))]
    pallas_call x0 -> x6, Pallas kernels: none -> 44.3 us  [the longest x3 26 us: run_split(): pl.pallas_call(kernel, out_shape=outs, in_specs=[pl.BlockSpec(memory_spac...]
    unnamed x13 -> x0, starting transfers between devices: 29.3 us -> none
  transfers between devices with their start and end apart: 19 -> 62, of which waited for: 6 -> 21; matrix products, arithmetic and copies ran while one was open for 22% -> 11% of each run, Pallas kernels for 0% -> 11%
where the time goes in v1:
time: 308 us; the launch traced here: 303 us
  starting transfers between devices  82 us (27%)
  waiting for transfers between devices  72.4 us (24%)
  matrix products  51.8 us (17%)
  Pallas kernels  44.3 us (14%)
  other arithmetic  31.6 us (10%)
  local copies, waits for them, and re-layouts  18.5 us (6%)
    ppermute x62, starting transfers between devices, shift(): return lax.ppermute(values, 'dp', shift_perm(axis, amount))  82 us
    ppermute x62, waiting for transfers between devices, shift(): return lax.ppermute(values, 'dp', shift_perm(axis, amount))  72.4 us
    pallas_call x3, Pallas kernels, run_split(): pl.pallas_call(kernel, out_shape=outs, in_specs=[pl.BlockSpec(memory_spac...  26 us
    pallas_call x3, Pallas kernels, run_assemble(): pl.pallas_call(kernel, out_shape=outs, in_specs=[pl.BlockSpec(memory_spac...  18.3 us
    unnamed x179, local copies, waits for them, and re-layouts  12.6 us
  transfers between devices with their start and end apart: 62, of which 21 were waited for; matrix products, arithmetic and copies ran while one was open for 11% of the time, Pallas kernels for 11%

profile of v1, /device:TPU:1, one launch (start us, length us, event | category | flops | bytes accessed | tf_op | source)
XLA Modules:
  0.0 303.3 jit_solution(6672353383597807429)
XLA Ops:
  1.7 3.2 %collective-permute-start.26 = (bf16[64,640]{1,0:T(8,128)(2,1)S(1)}, bf16[64,640]{1,0:T(8,128)(2,1)S(1)}, u32[]{:S(2)}, u32[]{:S(2)}) collective-permute-start(bf16[64,640]{1,0:T(8,128)(2,1)S(1)} %convert_element_type.378), channel_id=1, source_target_pairs={{0,16},{1,17},{2,18},{3,19},{4,20},{5,21},{6,22},{7,23},{8,24},{9,... | collective-permute-start | bytes 245768 | tf_op jit(solution)/shard_map/ppermute | solution.py:24
  15.8 2.9 collective-permute-start.1
  24.7 6.8 %collective-permute-done.4 = bf16[40,1408]{1,0:T(8,128)(2,1)S(1)} collective-permute-done((bf16[40,1408]{1,0:T(8,128)(2,1)S(1)}, bf16[40,1408]{1,0:T(8,128)(2,1)S(1)}, u32[]{:S(2)}, u32[]{:S(2)}) %collective-permute-start.4) | collective-permute-done | bytes 112672 | tf_op jit(solution)/shard_map/ppermute | solution.py:24
  31.5 3.6 %collective-permute-start.16 = (bf16[40,2048]{1,0:T(8,128)(2,1)S(1)}, bf16[40,2048]{1,0:T(8,128)(2,1)S(1)}, u32[]{:S(2)}, u32[]{:S(2)}) collective-permute-start(bf16[40,2048]{1,0:T(8,128)(2,1)S(1)} %pad_maximum_fusion.18), channel_id=1, source_target_pairs={{0,8},{1,9},{2,10},{3,11},{4,12},{5,13},{6,14},{7,15},{8,16},{9,17... | collective-permute-start | bytes 491528 | tf_op jit(solution)/shard_map/ppermute | solution.py:24
  42.9 3.4 %collective-permute-start.30 = (bf16[2,2,64,640]{3,2,1,0:T(8,128)(2,1)S(1)}, bf16[2,2,64,640]{3,2,1,0:T(8,128)(2,1)S(1)}, u32[]{:S(2)}, u32[]{:S(2)}) collective-permute-start(bf16[2,2,64,640]{3,2,1,0:T(8,128)(2,1)S(1)} %pad_maximum_fusion.13.refs_0_), channel_id=1, source_target_pairs={{0,1},{1,0},{2,3},{3,2},{4,5},{5,4},{6,7},{7,6},{8,9},{9,8},{10,11... | collective-permute-start | bytes 983048 | tf_op jit(solution)/shard_map/ppermute | solution.py:24
  47.9 6.8 %collective-permute-start.33 = (bf16[2,2,64,640]{3,2,1,0:T(8,128)(2,1)S(1)}, bf16[2,2,64,640]{3,2,1,0:T(8,128)(2,1)S(1)}, u32[]{:S(2)}, u32[]{:S(2)}) collective-permute-start(bf16[2,2,64,640]{3,2,1,0:T(8,128)(2,1)S(1)} %collective-permute-done.29.refs_3_), channel_id=1, source_target_pairs={{0,1},{1,0},{2,3},{3,2},{4,5},{5,4},{6,7},{7,6},{8,9},{9,8},{10,11... | collective-permute-start | bytes 983048 | tf_op jit(solution)/shard_map/ppermute | solution.py:24
  54.7 3.7 %collective-permute-start.31 = (bf16[2,2,64,640]{3,2,1,0:T(8,128)(2,1)S(1)}, bf16[2,2,64,640]{3,2,1,0:T(8,128)(2,1)S(1)}, u32[]{:S(2)}, u32[]{:S(2)}) collective-permute-start(bf16[2,2,64,640]{3,2,1,0:T(8,128)(2,1)S(1)} %collective-permute-done.25.refs_1_), channel_id=1, source_target_pairs={{0,1},{1,0},{2,3},{3,2},{4,5},{5,4},{6,7},{7,6},{8,9},{9,8},{10,11... | collective-permute-start | bytes 983048 | tf_op jit(solution)/shard_map/ppermute | solution.py:24
  65.1 5.7 %collective-permute-done.3.refs_1_ = bf16[2,2,40,1408]{3,2,1,0:T(8,128)(2,1)S(1)} collective-permute-done((bf16[2,2,40,1408]{3,2,1,0:T(8,128)(2,1)S(1)}, bf16[2,2,40,1408]{3,2,1,0:T(8,128)(2,1)S(1)}, u32[]{:S(2)}, u32[]{:S(2)}) %collective-permute-start.3) | collective-permute-done | bytes 450592 | tf_op jit(solution)/shard_map/ppermute | solution.py:24
  73.8 5.0 %shard_map.475 = bf16[2048,640]{1,0:T(8,128)(2,1)S(1)} custom-call(s32[4]{0:T(128)S(1)} %pad_add_fusion.coords_ref, bf16[2,2,64,640]{3,2,1,0:T(8,128)(2,1)S(1)} %pad_maximum_fusion.13.refs_0_, bf16[2,2,64,640]{3,2,1,0:T(8,128)(2,1)S(1)} %collective-permute-done.25.refs_1_, bf16[2,2,64,640]{3,2,1,0:T(8,128)(2,1)S(1)} %pad_maximum_fusion.14.refs_2_, ...), custom_call_target="tpu_custom_call" | custom-call | tf_op jit(solution)/shard_map/pallas_call | solution.py:111
  78.8 6.1 %collective-permute-done.14.refs_1_ = bf16[2,2,40,2048]{3,2,1,0:T(8,128)(2,1)} collective-permute-done((bf16[2,2,40,2048]{3,2,1,0:T(8,128)(2,1)}, bf16[2,2,40,2048]{3,2,1,0:T(8,128)(2,1)}, u32[]{:S(2)}, u32[]{:S(2)}) %collective-permute-start.14) | collective-permute-done | bytes 655392 | tf_op jit(solution)/shard_map/ppermute | solution.py:24
  86.8 7.5 %shard_map.473 = (bf16[640,1024]{1,0:T(8,128)(2,1)S(1)}, bf16[640,512]{1,0:T(8,128)(2,1)S(1)}, bf16[1024,640]{1,0:T(8,128)(2,1)}, f32[8,640]{1,0:T(8,128)S(1)}) custom-call(s32[4]{0:T(128)S(1)} %pad_add_fusion.coords_ref, bf16[2,2,40,1408]{3,2,1,0:T(8,128)(2,1)S(1)} %pad_maximum_fusion.6.refs_0_, ...), custom_call_target="tpu_custom_call" | custom-call | tf_op jit(solution)/shard_map/pallas_call | solution.py:111
  102.0 2.7 multiply_reduce_fusion.2
  112.0 5.8 %shard_map.474 = bf16[640,4096]{1,0:T(8,128)(2,1)} custom-call(s32[4]{0:T(128)S(1)} %pad_add_fusion.coords_ref, bf16[2,2,40,2048]{3,2,1,0:T(8,128)(2,1)} %pad_maximum_fusion.3.refs_0_, bf16[2,2,40,2048]{3,2,1,0:T(8,128)(2,1)} %collective-permute-done.14.refs_1_, bf16[2,2,40,2048]{3,2,1,0:T(8,128)(2,1)} %pad_maximum_fusion.4.refs_2_, ...), custom_call_target="tpu_custom_call" | custom-call | tf_op jit(solution)/shard_map/pallas_call | solution.py:111
  117.8 5.5 %fusion.123 = f32[512,4096]{1,0:T(8,128)S(1)} fusion(bf16[640,4096]{1,0:T(8,128)(2,1)} %shard_map.474, f32[512,640]{1,0:T(8,128)S(1)} %get-tuple-element.179, f32[640]{0:T(1024)S(1)} %get-tuple-element.145, f32[512]{0:T(512)S(1)} %fusion.110), kind=kOutput, calls=%fused_computation.282 | convolution fusion | flops 2685337600 | bytes 14946816 | tf_op jit(solution)/shard_map/dot_general | solution.py:468
  129.4 4.5 %fusion.6 = (bf16[512,2048]{1,0:T(8,128)(2,1)S(1)}, bf16[512,2048]{1,0:T(8,128)(2,1)S(1)}) fusion(f32[512,4096]{1,0:T(8,128)S(1)} %fusion.123, bf16[512,640]{1,0:T(8,128)(2,1)S(1)} %get-tuple-element.182, bf16[2048,640]{1,0:T(8,128)(2,1)S(1)} %shard_map.475), kind=kOutput, calls=%fused_computation.8 | convolution fusion | flops 1367343104 | bytes 15859712 | tf_op jit(solution)/shard_map/dot_general | solution.py:491
  134.1 4.1 %multiply_reduce_fusion.3 = (f32[640]{0:T(1024)}, f32[512]{0:T(512)S(1)}, f32[512,640]{1,0:T(8,128)S(1)}) fusion(f32[512,640]{1,0:T(8,128)S(1)} %get-tuple-element.179, f32[512]{0:T(512)S(1)} %fusion.110, f32[640]{0:T(1024)S(1)} %get-tuple-element.145, bf16[640,4096]{1,0:T(8,128)(2,1)S(1)} %bitcast.294, bf16[512,2048]{1,0:T(8,128)(2,1)S(1)} %get-tuple-element.181, ...), kind=kOutput, calls=%fused_computation.70 | convolution fusion | flops 2694708224 | bytes 12067840 | tf_op jit(solution)/shard_map/dot_general | solution.py:496
  145.7 3.8 %fusion.37 = bf16[512,256]{0,1:T(8,128)(2,1)S(1)} fusion(bf16[512,4,256]{0,2,1:T(8,128)(2,1)S(1)} %bitcast.299, f32[512,512,4]{1,0,2:T(8,128)} %copy-done.8, f32[4,512]{1,0:T(4,128)S(1)} %copy-done.73, pred[512,512]{0,1:T(8,128)(4,1)S(1)} %fusion.38), kind=kOutput, calls=%fused_computation.81 | convolution fusion | flops 542244864 | bytes 5775360 | tf_op jit(solution)/shard_map/hqk,qhd->kd/dot_general | solution.py:369
  157.8 4.2 %fusion.139.down_ref = f32[2048,640]{1,0:T(8,128)} fusion(bf16[512,2048]{1,0:T(8,128)(2,1)S(1)} %copy-done.19, bf16[512,640]{1,0:T(8,128)(2,1)S(1)} %copy-done.25), kind=kOutput, calls=%fused_computation.286 | convolution fusion | flops 1342177280 | bytes 7995392 | tf_op jit(solution)/shard_map/dot_general | solution.py:490
  162.0 6.0 %fusion.12.gateup_ref = f32[640,4096]{1,0:T(8,128)} fusion(bf16[512,2048]{1,0:T(8,128)(2,1)S(1)} %copy-done.31, bf16[512,2048]{1,0:T(8,128)(2,1)S(1)} %copy-done.29, f32[512,640]{1,0:T(8,128)S(1)} %copy-done.7, f32[640]{0:T(1024)S(1)} %get-tuple-element.145, f32[512]{0:T(512)S(1)} %fusion.110), kind=kOutput, calls=%fused_computation.23 | convolution fusion | flops 2693726208 | bytes 15995392 | tf_op jit(solution)/shard_map/dot_general | solution.py:495
  173.8 5.6 %shard_map.478 = (bf16[2,2,2,64,640]{4,3,2,1,0:T(8,128)(2,1)S(1)}, bf16[2,2,2,64,640]{4,3,2,1,0:T(8,128)(2,1)S(1)}, bf16[2,2,2,64,640]{4,3,2,1,0:T(8,128)(2,1)}, bf16[2,2,2,64,640]{4,3,2,1,0:T(8,128)(2,1)S(1)}) custom-call(s32[4]{0:T(128)S(1)} %pad_add_fusion.coords_ref, f32[2048,640]{1,0:T(8,128)} %fusion.139.down_ref), custom_call_target="tpu_custom_call" | custom-call | tf_op jit(solution)/shard_map/pallas_call | solution.py:188
  180.5 8.3 %shard_map.476 = (bf16[2,2,2,40,1408]{4,3,2,1,0:T(8,128)(2,1)S(1)}, bf16[2,2,2,40,1408]{4,3,2,1,0:T(8,128)(2,1)S(1)}, bf16[2,2,2,40,1408]{4,3,2,1,0:T(8,128)(2,1)S(1)}, bf16[2,2,2,40,1408]{4,3,2,1,0:T(8,128)(2,1)S(1)}) custom-call(s32[4]{0:T(128)S(1)} %pad_add_fusion.coords_ref, f32[640,1024]{1,0:T(8,128)} %fusion.47.query_ref, ...), custom_call_target="tpu_custom_call" | custom-call | tf_op jit(solution)/shard_map/pallas_call | solution.py:188
  189.8 12.2 %shard_map.477 = (bf16[2,2,2,40,2048]{4,3,2,1,0:T(8,128)(2,1)S(1)}, bf16[2,2,2,40,2048]{4,3,2,1,0:T(8,128)(2,1)S(1)}, bf16[2,2,2,40,2048]{4,3,2,1,0:T(8,128)(2,1)S(1)}, bf16[2,2,2,40,2048]{4,3,2,1,0:T(8,128)(2,1)S(1)}) custom-call(s32[4]{0:T(128)S(1)} %pad_add_fusion.coords_ref, f32[640,4096]{1,0:T(8,128)} %fusion.12.gateup_ref), custom_call_target="tpu_custom_call" | custom-call | tf_op jit(solution)/shard_map/pallas_call | solution.py:188
  209.7 4.5 %collective-permute-done.54 = bf16[2,2,64,640]{3,2,1,0:T(8,128)(2,1)S(1)} collective-permute-done((bf16[2,2,64,640]{3,2,1,0:T(8,128)(2,1)S(1)}, bf16[2,2,64,640]{3,2,1,0:T(8,128)(2,1)S(1)}, u32[]{:S(2)}, u32[]{:S(2)}) %collective-permute-start.54) | collective-permute-done | bytes 327712 | tf_op jit(solution)/shard_map/ppermute | solution.py:24
  222.1 3.4 %collective-permute-start.60 = (bf16[64,640]{1,0:T(8,128)(2,1)S(1)}, bf16[64,640]{1,0:T(8,128)(2,1)S(1)}, u32[]{:S(2)}, u32[]{:S(2)}) collective-permute-start(bf16[64,640]{1,0:T(8,128)(2,1)S(1)} %get-tuple-element.201), channel_id=1, source_target_pairs={{0,16},{1,17},{2,18},{3,19},{4,20},{5,21},{6,22},{7,23},{8,24},{9,... | collective-permute-start | bytes 245768 | tf_op jit(solution)/shard_map/ppermute | solution.py:24
  231.8 3.1 %collective-permute-done.35 = bf16[2,2,40,1408]{3,2,1,0:T(8,128)(2,1)S(1)} collective-permute-done((bf16[2,2,40,1408]{3,2,1,0:T(8,128)(2,1)S(1)}, bf16[2,2,40,1408]{3,2,1,0:T(8,128)(2,1)S(1)}, u32[]{:S(2)}, u32[]{:S(2)}) %collective-permute-start.35) | collective-permute-done | bytes 450592 | tf_op jit(solution)/shard_map/ppermute | solution.py:24
  238.1 5.7 %collective-permute-done.36 = bf16[2,40,1408]{2,1,0:T(8,128)(2,1)S(1)} collective-permute-done((bf16[2,40,1408]{2,1,0:T(8,128)(2,1)S(1)}, bf16[2,40,1408]{2,1,0:T(8,128)(2,1)S(1)}, u32[]{:S(2)}, u32[]{:S(2)}) %collective-permute-start.36) | collective-permute-done | bytes 225312 | tf_op jit(solution)/shard_map/ppermute | solution.py:24
  244.8 9.0 %collective-permute-done.40 = bf16[2,40,1408]{2,1,0:T(8,128)(2,1)S(1)} collective-permute-done((bf16[2,40,1408]{2,1,0:T(8,128)(2,1)S(1)}, bf16[2,40,1408]{2,1,0:T(8,128)(2,1)S(1)}, u32[]{:S(2)}, u32[]{:S(2)}) %collective-permute-start.40) | collective-permute-done | bytes 225312 | tf_op jit(solution)/shard_map/ppermute | solution.py:24
  254.3 3.4 %collective-permute-start.42 = (bf16[40,1408]{1,0:T(8,128)(2,1)S(1)}, bf16[40,1408]{1,0:T(8,128)(2,1)S(1)}, u32[]{:S(2)}, u32[]{:S(2)}) collective-permute-start(bf16[40,1408]{1,0:T(8,128)(2,1)S(1)} %get-tuple-element.194), channel_id=1, source_target_pairs={{0,24},{1,25},{2,26},{3,27},{4,28},{5,29},{6,30},{7,31},{8,0},{9,1... | collective-permute-start | bytes 337928 | tf_op jit(solution)/shard_map/ppermute | solution.py:24
  262.4 8.4 %collective-permute-done.48 = bf16[2,2,40,2048]{3,2,1,0:T(8,128)(2,1)S(1)} collective-permute-done((bf16[2,2,40,2048]{3,2,1,0:T(8,128)(2,1)S(1)}, bf16[2,2,40,2048]{3,2,1,0:T(8,128)(2,1)S(1)}, u32[]{:S(2)}, u32[]{:S(2)}) %collective-permute-start.48) | collective-permute-done | bytes 655392 | tf_op jit(solution)/shard_map/ppermute | solution.py:24
  271.3 6.5 %collective-permute-done.45 = bf16[2,40,2048]{2,1,0:T(8,128)(2,1)S(1)} collective-permute-done((bf16[2,40,2048]{2,1,0:T(8,128)(2,1)S(1)}, bf16[2,40,2048]{2,1,0:T(8,128)(2,1)S(1)}, u32[]{:S(2)}, u32[]{:S(2)}) %collective-permute-start.45) | collective-permute-done | bytes 327712 | tf_op jit(solution)/shard_map/ppermute | solution.py:24
  284.4 2.9 collective-permute-done.50
  287.5 7.7 %collective-permute-start.52 = (f32[20,2816]{1,0:T(8,128)S(1)}, f32[20,2816]{1,0:T(8,128)S(1)}, u32[]{:S(2)}, u32[]{:S(2)}) collective-permute-start(f32[20,2816]{1,0:T(8,128)S(1)} %broadcast_select_fusion.2), channel_id=1, source_target_pairs={{0,1},{1,0},{2,3},{3,2},{4,5},{5,4},{6,7},{7,6},{8,9},{9,8},{10,11... | collective-permute-start | bytes 675848 | tf_op jit(solution)/shard_map/ppermute | solution.py:24
  (418 shorter events, 128.5 us)
Async XLA Ops:
  1.7 12.6 %collective-permute-start.26 = (bf16[64,640]{1,0:T(8,128)(2,1)S(1)}, bf16[64,640]{1,0:T(8,128)(2,1)S(1)}, u32[]{:S(2)}, u32[]{:S(2)}) collective-permute-start(bf16[64,640]{1,0:T(8,128)(2,1)S(1)} %convert_element_type.378), channel_id=1, source_target_pairs={{0,16},{1,17},{2,18},{3,19},{4,20},{5,21},{6,22},{7,23},{8,24},{9,... | collective-permute-start | bytes 245768 | tf_op jit(solution)/shard_map/ppermute | solution.py:24
  13.0 22.1 %collective-permute-start.24 = (bf16[2,64,640]{2,1,0:T(8,128)(2,1)S(1)}, bf16[2,64,640]{2,1,0:T(8,128)(2,1)S(1)}, u32[]{:S(2)}, u32[]{:S(2)}) collective-permute-start(bf16[2,64,640]{2,1,0:T(8,128)(2,1)S(1)} %get-tuple-element.206), channel_id=1, source_target_pairs={{0,2},{1,3},{2,0},{3,1},{4,6},{5,7},{6,4},{7,5},{8,10},{9,11},{10,... | collective-permute-start | bytes 491528 | tf_op jit(solution)/shard_map/ppermute | solution.py:24
  14.3 21.1 %collective-permute-start.28 = (bf16[2,64,640]{2,1,0:T(8,128)(2,1)S(1)}, bf16[2,64,640]{2,1,0:T(8,128)(2,1)S(1)}, u32[]{:S(2)}, u32[]{:S(2)}) collective-permute-start(bf16[2,64,640]{2,1,0:T(8,128)(2,1)S(1)} %get-tuple-element.204), channel_id=1, source_target_pairs={{0,4},{1,5},{2,6},{3,7},{4,0},{5,1},{6,2},{7,3},{8,12},{9,13},{10,... | collective-permute-start | bytes 491528 | tf_op jit(solution)/shard_map/ppermute | solution.py:24
  18.8 12.7 %collective-permute-start.4 = (bf16[40,1408]{1,0:T(8,128)(2,1)S(1)}, bf16[40,1408]{1,0:T(8,128)(2,1)S(1)}, u32[]{:S(2)}, u32[]{:S(2)}) collective-permute-start(bf16[40,1408]{1,0:T(8,128)(2,1)S(1)} %fusion.93), channel_id=1, source_target_pairs={{0,16},{1,17},{2,18},{3,19},{4,20},{5,21},{6,22},{7,23},{8,24},{9,... | collective-permute-start | bytes 337928 | tf_op jit(solution)/shard_map/ppermute | solution.py:24
  20.4 15.4 %collective-permute-start.15 = (bf16[40,2048]{1,0:T(8,128)(2,1)S(1)}, bf16[40,2048]{1,0:T(8,128)(2,1)S(1)}, u32[]{:S(2)}, u32[]{:S(2)}) collective-permute-start(bf16[40,2048]{1,0:T(8,128)(2,1)S(1)} %pad_maximum_fusion.18), channel_id=1, source_target_pairs={{0,16},{1,17},{2,18},{3,19},{4,20},{5,21},{6,22},{7,23},{8,24},{9,... | collective-permute-start | bytes 491528 | tf_op jit(solution)/shard_map/ppermute | solution.py:24
  24.3 16.9 %collective-permute-start.12 = (bf16[40,2048]{1,0:T(8,128)(2,1)S(1)}, bf16[40,2048]{1,0:T(8,128)(2,1)S(1)}, u32[]{:S(2)}, u32[]{:S(2)}) collective-permute-start(bf16[40,2048]{1,0:T(8,128)(2,1)S(1)} %pad_maximum_fusion.18), channel_id=1, source_target_pairs={{0,24},{1,25},{2,26},{3,27},{4,28},{5,29},{6,30},{7,31},{8,0},{9,1... | collective-permute-start | bytes 491528 | tf_op jit(solution)/shard_map/ppermute | solution.py:24
  35.9 23.4 %collective-permute-start.32 = (bf16[2,2,64,640]{3,2,1,0:T(8,128)(2,1)S(1)}, bf16[2,2,64,640]{3,2,1,0:T(8,128)(2,1)S(1)}, u32[]{:S(2)}, u32[]{:S(2)}) collective-permute-start(bf16[2,2,64,640]{3,2,1,0:T(8,128)(2,1)S(1)} %pad_maximum_fusion.14.refs_2_), channel_id=1, source_target_pairs={{0,1},{1,0},{2,3},{3,2},{4,5},{5,4},{6,7},{7,6},{8,9},{9,8},{10,11... | collective-permute-start | bytes 983048 | tf_op jit(solution)/shard_map/ppermute | solution.py:24
  41.5 13.2 %collective-permute-start.17 = (bf16[2,40,2048]{2,1,0:T(8,128)(2,1)S(1)}, bf16[2,40,2048]{2,1,0:T(8,128)(2,1)S(1)}, u32[]{:S(2)}, u32[]{:S(2)}) collective-permute-start(bf16[2,40,2048]{2,1,0:T(8,128)(2,1)S(1)} %get-tuple-element.190), channel_id=1, source_target_pairs={{0,4},{1,5},{2,6},{3,7},{4,0},{5,1},{6,2},{7,3},{8,12},{9,13},{10,... | collective-permute-start | bytes 983048 | tf_op jit(solution)/shard_map/ppermute | solution.py:24
  42.9 16.4 %collective-permute-start.30 = (bf16[2,2,64,640]{3,2,1,0:T(8,128)(2,1)S(1)}, bf16[2,2,64,640]{3,2,1,0:T(8,128)(2,1)S(1)}, u32[]{:S(2)}, u32[]{:S(2)}) collective-permute-start(bf16[2,2,64,640]{3,2,1,0:T(8,128)(2,1)S(1)} %pad_maximum_fusion.13.refs_0_), channel_id=1, source_target_pairs={{0,1},{1,0},{2,3},{3,2},{4,5},{5,4},{6,7},{7,6},{8,9},{9,8},{10,11... | collective-permute-start | bytes 983048 | tf_op jit(solution)/shard_map/ppermute | solution.py:24
  47.6 12.0 %collective-permute-start.13 = (bf16[2,40,2048]{2,1,0:T(8,128)(2,1)S(1)}, bf16[2,40,2048]{2,1,0:T(8,128)(2,1)S(1)}, u32[]{:S(2)}, u32[]{:S(2)}) collective-permute-start(bf16[2,40,2048]{2,1,0:T(8,128)(2,1)S(1)} %get-tuple-element.192), channel_id=1, source_target_pairs={{0,2},{1,3},{2,0},{3,1},{4,6},{5,7},{6,4},{7,5},{8,10},{9,11},{10,... | collective-permute-start | bytes 983048 | tf_op jit(solution)/shard_map/ppermute | solution.py:24
  47.9 13.8 %collective-permute-start.33 = (bf16[2,2,64,640]{3,2,1,0:T(8,128)(2,1)S(1)}, bf16[2,2,64,640]{3,2,1,0:T(8,128)(2,1)S(1)}, u32[]{:S(2)}, u32[]{:S(2)}) collective-permute-start(bf16[2,2,64,640]{3,2,1,0:T(8,128)(2,1)S(1)} %collective-permute-done.29.refs_3_), channel_id=1, source_target_pairs={{0,1},{1,0},{2,3},{3,2},{4,5},{5,4},{6,7},{7,6},{8,9},{9,8},{10,11... | collective-permute-start | bytes 983048 | tf_op jit(solution)/shard_map/ppermute | solution.py:24
  59.6 13.4 %collective-permute-start.7 = (bf16[2,2,40,1408]{3,2,1,0:T(8,128)(2,1)S(1)}, bf16[2,2,40,1408]{3,2,1,0:T(8,128)(2,1)S(1)}, u32[]{:S(2)}, u32[]{:S(2)}) collective-permute-start(bf16[2,2,40,1408]{3,2,1,0:T(8,128)(2,1)S(1)} %pad_maximum_fusion.7.refs_2_), channel_id=1, source_target_pairs={{0,2},{1,3},{2,0},{3,1},{4,6},{5,7},{6,4},{7,5},{8,10},{9,11},{10,... | collective-permute-start | bytes 1351688 | tf_op jit(solution)/shard_map/ppermute | solution.py:24
  61.7 23.3 %collective-permute-start.14 = (bf16[2,2,40,2048]{3,2,1,0:T(8,128)(2,1)}, bf16[2,2,40,2048]{3,2,1,0:T(8,128)(2,1)}, u32[]{:S(2)}, u32[]{:S(2)}) collective-permute-start(bf16[2,2,40,2048]{3,2,1,0:T(8,128)(2,1)} %pad_maximum_fusion.3.refs_0_), channel_id=1, source_target_pairs={{0,4},{1,5},{2,6},{3,7},{4,0},{5,1},{6,2},{7,3},{8,12},{9,13},{10,... | collective-permute-start | bytes 1966088 | tf_op jit(solution)/shard_map/ppermute | solution.py:24
  62.9 23.3 %collective-permute-start.18 = (bf16[2,2,40,2048]{3,2,1,0:T(8,128)(2,1)}, bf16[2,2,40,2048]{3,2,1,0:T(8,128)(2,1)}, u32[]{:S(2)}, u32[]{:S(2)}) collective-permute-start(bf16[2,2,40,2048]{3,2,1,0:T(8,128)(2,1)} %pad_maximum_fusion.4.refs_2_), channel_id=1, source_target_pairs={{0,2},{1,3},{2,0},{3,1},{4,6},{5,7},{6,4},{7,5},{8,10},{9,11},{10,... | collective-permute-start | bytes 1966088 | tf_op jit(solution)/shard_map/ppermute | solution.py:24
  63.5 15.3 %collective-permute-start.10 = (bf16[2,2,40,1408]{3,2,1,0:T(8,128)(2,1)S(1)}, bf16[2,2,40,1408]{3,2,1,0:T(8,128)(2,1)S(1)}, u32[]{:S(2)}, u32[]{:S(2)}) collective-permute-start(bf16[2,2,40,1408]{3,2,1,0:T(8,128)(2,1)S(1)} %pad_maximum_fusion.7.refs_2_), channel_id=1, source_target_pairs={{0,1},{1,0},{2,3},{3,2},{4,5},{5,4},{6,7},{7,6},{8,9},{9,8},{10,11... | collective-permute-start | bytes 1351688 | tf_op jit(solution)/shard_map/ppermute | solution.py:24
  70.8 15.7 %collective-permute-start.9 = (bf16[2,2,40,1408]{3,2,1,0:T(8,128)(2,1)S(1)}, bf16[2,2,40,1408]{3,2,1,0:T(8,128)(2,1)S(1)}, u32[]{:S(2)}, u32[]{:S(2)}) collective-permute-start(bf16[2,2,40,1408]{3,2,1,0:T(8,128)(2,1)S(1)} %collective-permute-done.3.refs_1_), channel_id=1, source_target_pairs={{0,1},{1,0},{2,3},{3,2},{4,5},{5,4},{6,7},{7,6},{8,9},{9,8},{10,11... | collective-permute-start | bytes 1351688 | tf_op jit(solution)/shard_map/ppermute | solution.py:24
  73.0 13.8 %collective-permute-start.11 = (bf16[2,2,40,1408]{3,2,1,0:T(8,128)(2,1)S(1)}, bf16[2,2,40,1408]{3,2,1,0:T(8,128)(2,1)S(1)}, u32[]{:S(2)}, u32[]{:S(2)}) collective-permute-start(bf16[2,2,40,1408]{3,2,1,0:T(8,128)(2,1)S(1)} %collective-permute-done.7.refs_3_), channel_id=1, source_target_pairs={{0,1},{1,0},{2,3},{3,2},{4,5},{5,4},{6,7},{7,6},{8,9},{9,8},{10,11... | collective-permute-start | bytes 1351688 | tf_op jit(solution)/shard_map/ppermute | solution.py:24
  78.8 33.2 %collective-permute-start.19 = (bf16[2,2,40,2048]{3,2,1,0:T(8,128)(2,1)}, bf16[2,2,40,2048]{3,2,1,0:T(8,128)(2,1)}, u32[]{:S(2)}, u32[]{:S(2)}) collective-permute-start(bf16[2,2,40,2048]{3,2,1,0:T(8,128)(2,1)} %pad_maximum_fusion.3.refs_0_), channel_id=1, source_target_pairs={{0,1},{1,0},{2,3},{3,2},{4,5},{5,4},{6,7},{7,6},{8,9},{9,8},{10,11... | collective-permute-start | bytes 1966088 | tf_op jit(solution)/shard_map/ppermute | solution.py:24
  85.0 27.0 %collective-permute-start.21 = (bf16[2,2,40,2048]{3,2,1,0:T(8,128)(2,1)}, bf16[2,2,40,2048]{3,2,1,0:T(8,128)(2,1)}, u32[]{:S(2)}, u32[]{:S(2)}) collective-permute-start(bf16[2,2,40,2048]{3,2,1,0:T(8,128)(2,1)} %pad_maximum_fusion.4.refs_2_), channel_id=1, source_target_pairs={{0,1},{1,0},{2,3},{3,2},{4,5},{5,4},{6,7},{7,6},{8,9},{9,8},{10,11... | collective-permute-start | bytes 1966088 | tf_op jit(solution)/shard_map/ppermute | solution.py:24
  86.2 25.8 %collective-permute-start.20 = (bf16[2,2,40,2048]{3,2,1,0:T(8,128)(2,1)}, bf16[2,2,40,2048]{3,2,1,0:T(8,128)(2,1)}, u32[]{:S(2)}, u32[]{:S(2)}) collective-permute-start(bf16[2,2,40,2048]{3,2,1,0:T(8,128)(2,1)} %collective-permute-done.14.refs_1_), channel_id=1, source_target_pairs={{0,1},{1,0},{2,3},{3,2},{4,5},{5,4},{6,7},{7,6},{8,9},{9,8},{10,11... | collective-permute-start | bytes 1966088 | tf_op jit(solution)/shard_map/ppermute | solution.py:24
  86.5 25.5 %collective-permute-start.22 = (bf16[2,2,40,2048]{3,2,1,0:T(8,128)(2,1)}, bf16[2,2,40,2048]{3,2,1,0:T(8,128)(2,1)}, u32[]{:S(2)}, u32[]{:S(2)}) collective-permute-start(bf16[2,2,40,2048]{3,2,1,0:T(8,128)(2,1)} %collective-permute-done.18.refs_3_), channel_id=1, source_target_pairs={{0,1},{1,0},{2,3},{3,2},{4,5},{5,4},{6,7},{7,6},{8,9},{9,8},{10,11... | collective-permute-start | bytes 1966088 | tf_op jit(solution)/shard_map/ppermute | solution.py:24
  180.2 23.5 %collective-permute-start.53 = (bf16[2,2,2,64,640]{4,3,2,1,0:T(8,128)(2,1)}, bf16[2,2,2,64,640]{4,3,2,1,0:T(8,128)(2,1)}, u32[]{:S(2)}, u32[]{:S(2)}) collective-permute-start(bf16[2,2,2,64,640]{4,3,2,1,0:T(8,128)(2,1)} %get-tuple-element.99), channel_id=1, source_target_pairs={{0,1},{1,0},{2,3},{3,2},{4,5},{5,4},{6,7},{7,6},{8,9},{9,8},{10,11... | collective-permute-start | bytes 1966088 | tf_op jit(solution)/shard_map/ppermute | solution.py:24
  188.8 18.4 %collective-permute-start.34 = (bf16[2,2,2,40,1408]{4,3,2,1,0:T(8,128)(2,1)S(1)}, bf16[2,2,2,40,1408]{4,3,2,1,0:T(8,128)(2,1)}, u32[]{:S(2)}, u32[]{:S(2)}) collective-permute-start(bf16[2,2,2,40,1408]{4,3,2,1,0:T(8,128)(2,1)S(1)} %get-tuple-element.91), channel_id=1, source_target_pairs={{0,1},{1,0},{2,3},{3,2},{4,5},{5,4},{6,7},{7,6},{8,9},{9,8},{10,11... | collective-permute-start | bytes 2703368 | tf_op jit(solution)/shard_map/ppermute | solution.py:24
  189.2 15.9 %collective-permute-start.57 = (bf16[2,2,2,64,640]{4,3,2,1,0:T(8,128)(2,1)S(1)}, bf16[2,2,2,64,640]{4,3,2,1,0:T(8,128)(2,1)}, u32[]{:S(2)}, u32[]{:S(2)}) collective-permute-start(bf16[2,2,2,64,640]{4,3,2,1,0:T(8,128)(2,1)S(1)} %copy-done.3), channel_id=1, source_target_pairs={{0,1},{1,0},{2,3},{3,2},{4,5},{5,4},{6,7},{7,6},{8,9},{9,8},{10,11... | collective-permute-start | bytes 1966088 | tf_op jit(solution)/shard_map/ppermute | solution.py:24
  189.4 36.0 %collective-permute-start.38 = (bf16[2,2,2,40,1408]{4,3,2,1,0:T(8,128)(2,1)S(1)}, bf16[2,2,2,40,1408]{4,3,2,1,0:T(8,128)(2,1)S(1)}, u32[]{:S(2)}, u32[]{:S(2)}) collective-permute-start(bf16[2,2,2,40,1408]{4,3,2,1,0:T(8,128)(2,1)S(1)} %get-tuple-element.93), channel_id=1, source_target_pairs={{0,1},{1,0},{2,3},{3,2},{4,5},{5,4},{6,7},{7,6},{8,9},{9,8},{10,11... | collective-permute-start | bytes 2703368 | tf_op jit(solution)/shard_map/ppermute | solution.py:24
  201.9 29.0 %collective-permute-start.43 = (bf16[2,2,2,40,2048]{4,3,2,1,0:T(8,128)(2,1)S(1)}, bf16[2,2,2,40,2048]{4,3,2,1,0:T(8,128)(2,1)S(1)}, u32[]{:S(2)}, u32[]{:S(2)}) collective-permute-start(bf16[2,2,2,40,2048]{4,3,2,1,0:T(8,128)(2,1)S(1)} %get-tuple-element.95), channel_id=1, source_target_pairs={{0,1},{1,0},{2,3},{3,2},{4,5},{5,4},{6,7},{7,6},{8,9},{9,8},{10,11... | collective-permute-start | bytes 3932168 | tf_op jit(solution)/shard_map/ppermute | solution.py:24
  203.7 54.1 %collective-permute-start.47 = (bf16[2,2,2,40,2048]{4,3,2,1,0:T(8,128)(2,1)S(1)}, bf16[2,2,2,40,2048]{4,3,2,1,0:T(8,128)(2,1)S(1)}, u32[]{:S(2)}, u32[]{:S(2)}) collective-permute-start(bf16[2,2,2,40,2048]{4,3,2,1,0:T(8,128)(2,1)S(1)} %get-tuple-element.97), channel_id=1, source_target_pairs={{0,1},{1,0},{2,3},{3,2},{4,5},{5,4},{6,7},{7,6},{8,9},{9,8},{10,11... | collective-permute-start | bytes 3932168 | tf_op jit(solution)/shard_map/ppermute | solution.py:24
  231.2 29.1 %collective-permute-start.44 = (bf16[2,2,40,2048]{3,2,1,0:T(8,128)(2,1)S(1)}, bf16[2,2,40,2048]{3,2,1,0:T(8,128)(2,1)S(1)}, u32[]{:S(2)}, u32[]{:S(2)}) collective-permute-start(bf16[2,2,40,2048]{3,2,1,0:T(8,128)(2,1)S(1)} %fusion.40), channel_id=1, source_target_pairs={{0,4},{1,5},{2,6},{3,7},{4,0},{5,1},{6,2},{7,3},{8,12},{9,13},{10,... | collective-permute-start | bytes 1966088 | tf_op jit(solution)/shard_map/ppermute | solution.py:24
  238.0 15.8 %collective-permute-start.40 = (bf16[2,40,1408]{2,1,0:T(8,128)(2,1)S(1)}, bf16[2,40,1408]{2,1,0:T(8,128)(2,1)S(1)}, u32[]{:S(2)}, u32[]{:S(2)}) collective-permute-start(bf16[2,40,1408]{2,1,0:T(8,128)(2,1)S(1)} %fusion.74), channel_id=1, source_target_pairs={{0,4},{1,5},{2,6},{3,7},{4,0},{5,1},{6,2},{7,3},{8,12},{9,13},{10,... | collective-permute-start | bytes 675848 | tf_op jit(solution)/shard_map/ppermute | solution.py:24
  243.8 15.9 %collective-permute-start.37 = (bf16[40,1408]{1,0:T(8,128)(2,1)S(1)}, bf16[40,1408]{1,0:T(8,128)(2,1)S(1)}, u32[]{:S(2)}, u32[]{:S(2)}) collective-permute-start(bf16[40,1408]{1,0:T(8,128)(2,1)S(1)} %fusion.94), channel_id=1, source_target_pairs={{0,8},{1,9},{2,10},{3,11},{4,12},{5,13},{6,14},{7,15},{8,16},{9,17... | collective-permute-start | bytes 337928 | tf_op jit(solution)/shard_map/ppermute | solution.py:24
  258.0 12.8 %collective-permute-start.48 = (bf16[2,2,40,2048]{3,2,1,0:T(8,128)(2,1)S(1)}, bf16[2,2,40,2048]{3,2,1,0:T(8,128)(2,1)S(1)}, u32[]{:S(2)}, u32[]{:S(2)}) collective-permute-start(bf16[2,2,40,2048]{3,2,1,0:T(8,128)(2,1)S(1)} %fusion.41), channel_id=1, source_target_pairs={{0,2},{1,3},{2,0},{3,1},{4,6},{5,7},{6,4},{7,5},{8,10},{9,11},{10,... | collective-permute-start | bytes 1966088 | tf_op jit(solution)/shard_map/ppermute | solution.py:24
  260.6 17.2 %collective-permute-start.45 = (bf16[2,40,2048]{2,1,0:T(8,128)(2,1)S(1)}, bf16[2,40,2048]{2,1,0:T(8,128)(2,1)S(1)}, u32[]{:S(2)}, u32[]{:S(2)}) collective-permute-start(bf16[2,40,2048]{2,1,0:T(8,128)(2,1)S(1)} %fusion.62), channel_id=1, source_target_pairs={{0,2},{1,3},{2,0},{3,1},{4,6},{5,7},{6,4},{7,5},{8,10},{9,11},{10,... | collective-permute-start | bytes 983048 | tf_op jit(solution)/shard_map/ppermute | solution.py:24
  (119 other events, 798.6 us)

commit v2 on v0

v2 whole, which is shorter than its diff:
```python
import jax
import jax.numpy as jnp
import numpy as np
from jax import lax
from jax.experimental import pallas as pl
from jax.experimental.pallas import tpu as pltpu
from jax.sharding import PartitionSpec as P

STEP = 3
norm_epsilon = 1e-06
beta_one = 0.9
beta_two = 0.999
learn_rate = 0.03
decay_coef = 0.1
adam_epsilon = 1e-08

DIMS = (4, 2, 2, 2)
BF = jnp.bfloat16


def shift_perm(axis, amount):
    pairs = []
    for place in range(int(np.prod(DIMS))):
        spot = list(np.unravel_index(place, DIMS))
        spot[axis] = (spot[axis] + amount) % DIMS[axis]
        pairs.append((place, int(np.ravel_multi_index(spot, DIMS))))
    return pairs


def shift(values, axis, amount):
    return lax.ppermute(values, "dp", shift_perm(axis, amount))


def own_coords():
    place = lax.axis_index("dp")
    return place // 8, (place // 4) % 2, (place // 2) % 2, place % 2


def after(values, *others):
    return lax.optimization_barrier((values, others))[0]


def gather_along(block):
    return [block] + [shift(block, 0, -step) for step in (1, 2, 3)]


def gather_pair(near):
    first = jnp.stack([near[0], near[1]])
    second = jnp.stack([near[2], near[3]])
    return jnp.stack([first, shift(first, 2, 1)]), jnp.stack([second, shift(second, 1, 1)])


def gather_across(pair_a, pair_b):
    return [pair_a, shift(pair_a, 1, 1), pair_b, shift(pair_b, 2, 1)]


def gather_core(mine):
    return mine + [shift(piece, 3, 1) for piece in mine]


def wide(values):
    return values.astype(jnp.float32)


def swap_halves(core, low, high):
    return jnp.where(core == 0, high, low), jnp.where(core == 0, low, high)


def gather_plain(query_round, keyval_round, output_round, gateup_round, down_round, gains_round, headgain_round):
    gateup_full = lax.all_gather(gateup_round, "dp", axis=0, tiled=True)
    return (
        lax.all_gather(query_round, "dp", axis=0, tiled=True),
        lax.all_gather(keyval_round, "dp", axis=0, tiled=True),
        lax.all_gather(output_round, "dp", axis=0, tiled=True),
        gateup_full.reshape(gateup_full.shape[0], -1),
        lax.all_gather(down_round, "dp", axis=0, tiled=True),
        lax.all_gather(gains_round, "dp", axis=1, tiled=True).astype(jnp.float32),
        lax.all_gather(headgain_round, "dp", axis=1, tiled=True).astype(jnp.float32),
    )


def scatter_plain(grad_query, grad_keyval, grad_output, grad_gateup, grad_down, grad_gains, grad_heads):
    rows = grad_gateup.shape[0]
    return (
        lax.psum_scatter(grad_query, "dp", scatter_dimension=0, tiled=True),
        lax.psum_scatter(grad_keyval, "dp", scatter_dimension=0, tiled=True),
        lax.psum_scatter(grad_output, "dp", scatter_dimension=0, tiled=True),
        lax.psum_scatter(grad_gateup.reshape(rows, 2, -1), "dp", scatter_dimension=0, tiled=True),
        lax.psum_scatter(grad_down, "dp", scatter_dimension=0, tiled=True),
        lax.psum_scatter(grad_gains, "dp", scatter_dimension=1, tiled=True),
        lax.psum_scatter(grad_heads, "dp", scatter_dimension=1, tiled=True),
    )


HALF = 1024 // 2
SCALE = 256 ** (-0.5)
KEY_SPANS = ((0, 128), (0, 256), (0, 384), (128, 512))
TANH_SLOPE = (2.0 / np.pi) ** 0.5
TANH_CUBE = 0.044715


def dot(left, right):
    return jnp.dot(left, right, preferred_element_type=jnp.float32)


def dot_right_t(left, right):
    return lax.dot_general(left, right, (((1,), (1,)), ((), ())), preferred_element_type=jnp.float32)


def dot_left_t(left, right):
    return lax.dot_general(left, right, (((0,), (0,)), ((), ())), preferred_element_type=jnp.float32)


def inverse_rms(values):
    return lax.rsqrt(jnp.mean(values * values, axis=-1, keepdims=True) + norm_epsilon)


def pull_norm(values, gain_plus, grad):
    inverse = inverse_rms(values)
    unit = values * inverse
    scaled = grad * gain_plus
    return inverse * (scaled - unit * jnp.mean(scaled * unit, axis=-1, keepdims=True)), grad * unit


def fold_rows(values):
    rows, columns = values.shape
    return jnp.sum(values.reshape(rows // 8, 8, columns), axis=0)


def chunks(count, size, body, carry):
    def step(index, carried):
        return body(pl.ds(pl.multiple_of(index * size, size), size), carried)

    return lax.fori_loop(0, count // size, step, carry)


def group_rows(piece_ref, low, high):
    return piece_ref[:, :, :, low:high].reshape(160, high - low)


def chip_at(coords_ref, gap):
    along = lax.rem(coords_ref[0] + gap[0], 4)
    upward = lax.rem(coords_ref[1] + gap[1], 2)
    sideways = lax.rem(coords_ref[2] + gap[2], 2)
    return (along * 2 + upward) * 2 + sideways


def gap_of(group, one, two):
    return (two, group, one) if group < 2 else (2 + two, one, group - 2)


def slots(coords_ref):
    for far in range(2):
        core = lax.rem(coords_ref[3] + far, 2)
        for group in range(4):
            for one in range(2):
                for two in range(2):
                    yield far, group, one, two, 2 * chip_at(coords_ref, gap_of(group, one, two)) + core


def project_forward(coords_ref, index_ref, tokens_ref, *refs):
    piece_refs, refs = refs[:8], refs[8:]
    (
        h1_ref, q_ref, kv_ref, qn_ref, kn_ref, vb_ref, wo_ref, gains_ref, perm_ref, plain_ref
    ) = refs
    for far, group, one, two, place in slots(coords_ref):
        wo_ref[place] = piece_refs[4 * far + group][one, two, 0:32, 768:1408]
    gains = jnp.zeros((8, 640), jnp.float32)
    for far in range(2):
        for group in range(4):
            for one in range(2):
                for two in range(2):
                    gains = gains + piece_refs[4 * far + group][one, two, 32:40, 768:1408].astype(jnp.float32)
    gains_ref[...] = gains
    core = coords_ref[3]

    def make_perm(rows, carry):
        place = lax.broadcasted_iota(jnp.int32, (64, 1024), 0) + rows.start
        perm_ref[rows, :] = jnp.where(place == index_ref[...], 1.0, 0.0).astype(BF)
        return carry

    chunks(640, 64, make_perm, 0)
    gain_zero = 1.0 + gains_ref[0:1, :]

    def norm_in(rows, carry):
        values = tokens_ref[rows, :].astype(jnp.float32)
        plain_ref[rows, :] = (values * inverse_rms(values) * gain_zero).astype(BF)
        return carry

    chunks(512, 32, norm_in, 0)
    h1_ref[...] = dot(plain_ref[...], perm_ref[...]).astype(BF)
    for far in range(2):
        side = lax.rem(core + far, 2)
        for part in range(3):
            total = jnp.zeros((512, 256), jnp.float32)
            for group in range(4):
                total = total + dot(
                    h1_ref[:, 256 * group : 256 * group + 160],
                    group_rows(piece_refs[4 * far + group], 256 * part, 256 * part + 256),
                )
            if part < 2:
                q_ref[2 * side + part] = total
            else:
                kv_ref[side] = total
    query_gain, key_gain = 1.0 + gains_ref[4:5, 0:256], 1.0 + gains_ref[5:6, 0:256]

    def norm_heads(rows, carry):
        for head in range(4):
            values = q_ref[head, rows, :]
            qn_ref[head, rows, :] = (values * inverse_rms(values) * query_gain).astype(BF)
        values = kv_ref[0, rows, :]
        kn_ref[rows, :] = (values * inverse_rms(values) * key_gain).astype(BF)
        vb_ref[rows, :] = kv_ref[1, rows, :].astype(BF)
        return carry

    chunks(512, 64, norm_heads, 0)


def attention_forward(
    coords_ref, tokens_ref, segrow_ref, segcol_ref, qn_ref, kn_ref, vb_ref, wo_ref, gains_ref, perm_ref,
    prob_ref, o_ref, branch_ref, mid_ref, h3_ref, plain_ref, bias_ref,
):
    for block, (low, high) in enumerate(KEY_SPANS):
        rows, span = slice(128 * block, 128 * block + 128), high - low
        row_at = lax.broadcasted_iota(jnp.int32, (128, span), 0) + 128 * block
        key_at = lax.broadcasted_iota(jnp.int32, (128, span), 1) + low
        allowed = (segcol_ref[rows, :] == segrow_ref[:, low:high]) & (key_at <= row_at)
        bias_ref[:, 0:span] = jnp.where(allowed, 0.0, -1e30)
        for head in range(4):
            scores = dot_right_t(qn_ref[head, rows, :], kn_ref[low:high, :]) * SCALE + bias_ref[:, 0:span]
            powers = jnp.exp(scores - jnp.max(scores, axis=-1, keepdims=True))
            weights = (powers * (1.0 / jnp.sum(powers, axis=-1, keepdims=True))).astype(BF)
            prob_ref[block, 128 * head : 128 * head + 128, 0:span] = weights
            o_ref[head, rows, :] = dot(weights, vb_ref[low:high, :]).astype(BF)
    total = jnp.zeros((512, 640), jnp.float32)
    for head in range(4):
        total = total + dot(o_ref[head], wo_ref[8 * head : 8 * head + 8].reshape(256, 640))
    branch_ref[...] = total
    gain_one, gain_two = 1.0 + gains_ref[1:2, :], 1.0 + gains_ref[2:3, :]

    def norm_mid(rows, carry):
        values = branch_ref[rows, :]
        middle = tokens_ref[rows, :].astype(jnp.float32) + values * inverse_rms(values) * gain_one
        mid_ref[rows, :] = middle
        plain_ref[rows, :] = (middle * inverse_rms(middle) * gain_two).astype(BF)
        return carry

    chunks(512, 32, norm_mid, 0)
    h3_ref[...] = dot(plain_ref[...], perm_ref[...]).astype(BF)


def gateup_forward(coords_ref, h3_ref, *refs):
    piece_refs, (slope_ref, gelu_ref, hidden_ref, both_ref) = refs[:8], refs[8:]
    core = coords_ref[3]
    for block in range(4):
        low = 512 * block
        for far in range(2):
            side = lax.rem(core + far, 2)
            total = jnp.zeros((512, 512), jnp.float32)
            for group in range(4):
                total = total + dot(
                    h3_ref[:, 256 * group : 256 * group + 160],
                    group_rows(piece_refs[4 * far + group], low, low + 512),
                )
            both_ref[side] = total

        def activate(rows, carry, low=low):
            gate, up = both_ref[0, rows, :], both_ref[1, rows, :]
            square = gate * gate
            bend = jnp.tanh(gate * (TANH_SLOPE + (TANH_SLOPE * TANH_CUBE) * square))
            weight = 0.5 + 0.5 * bend
            gelu = gate * weight
            slope = weight + (0.5 * gate) * (1.0 - bend * bend) * (
                TANH_SLOPE + (3.0 * TANH_SLOPE * TANH_CUBE) * square
            )
            slope_ref[rows, low : low + 512] = (slope * up).astype(BF)
            gelu_ref[rows, low : low + 512] = gelu.astype(BF)
            hidden_ref[rows, low : low + 512] = (gelu * up).astype(BF)
            return carry

        chunks(512, 16, activate, 0)


def down_both(coords_ref, hidden_ref, mid_ref, cot_ref, gains_ref, *refs):
    piece_refs, refs = refs[:8], refs[8:]
    (result_ref, dm_ref, gain_ref, wd_ref), refs = refs[:4], refs[4:]
    out_refs, (product_ref, natural_ref) = refs[:4], refs[4:]
    for far, group, one, two, place in slots(coords_ref):
        wd_ref[place] = piece_refs[4 * far + group][one, two]
    total = jnp.zeros((512, 640), jnp.float32)
    for block in range(8):
        total = total + dot(
            hidden_ref[:, 256 * block : 256 * block + 256],
            wd_ref[4 * block : 4 * block + 4].reshape(256, 640),
        )
    product_ref[...] = total
    gain_three = 1.0 + gains_ref[3:4, :]

    def finish(rows, carry):
        values = product_ref[rows, :]
        grad = cot_ref[rows, :].astype(jnp.float32)
        result_ref[rows, :] = (mid_ref[rows, :] + values * inverse_rms(values) * gain_three).astype(BF)
        pulled, term = pull_norm(values, gain_three, grad)
        dm_ref[rows, :] = pulled.astype(BF)
        return carry + fold_rows(term)

    gain_ref[...] = chunks(512, 32, finish, jnp.zeros((8, 640), jnp.float32))
    for block in range(8):
        grad = dot_left_t(hidden_ref[:, 256 * block : 256 * block + 256], dm_ref[...])
        natural_ref[4 * block : 4 * block + 4] = grad.astype(BF).reshape(4, 64, 640)
    for far, group, one, two, place in slots(coords_ref):
        out_refs[2 * far + group // 2][group % 2, one, two] = natural_ref[place]


def gateup_backward(coords_ref, dm_ref, wd_ref, slope_ref, gelu_ref, h3_ref, *refs):
    dgu_ref, out_refs, (dhid_ref, h3t_ref) = refs[0], refs[1:5], refs[5:]
    for block in range(4):
        low = 512 * block
        dhid_ref[...] = dot_right_t(dm_ref[...], wd_ref[8 * block : 8 * block + 8].reshape(512, 640))

        def spread(rows, carry, low=low):
            grad = dhid_ref[rows, :]
            dgu_ref[0, rows, low : low + 512] = (
                grad * slope_ref[rows, low : low + 512].astype(jnp.float32)
            ).astype(BF)
            dgu_ref[1, rows, low : low + 512] = (
                grad * gelu_ref[rows, low : low + 512].astype(jnp.float32)
            ).astype(BF)
            return carry

        chunks(512, 16, spread, 0)
    for group in range(4):
        h3t_ref[160 * group : 160 * group + 160, :] = h3_ref[:, 256 * group : 256 * group + 160].T
    for far in (1, 0):
        side = lax.rem(coords_ref[3] + far, 2)
        for block in range(4):
            low = 512 * block
            grad = dot(h3t_ref[...], dgu_ref[side, :, low : low + 512]).astype(BF)
            for spot in range(16):
                group, one, two = spot // 4, (spot // 2) % 2, spot % 2
                out_refs[2 * far + group // 2][group % 2, one, two, :, low : low + 512] = grad[
                    40 * spot : 40 * spot + 40
                ]


def to_plain(rel_ref, perm_ref, out_ref):
    high = rel_ref[...].astype(BF)
    low = (rel_ref[...] - high.astype(jnp.float32)).astype(BF)
    out_ref[...] = dot_right_t(high, perm_ref[...]) + dot_right_t(low, perm_ref[...])


def middle_backward(
    coords_ref, dgu_ref, mid_ref, branch_ref, cot_ref, gains_ref, perm_ref, *refs
):
    piece_refs, refs = refs[:8], refs[8:]
    dmid_ref, da_ref, gain_ref, rel_ref, plain_ref = refs
    core = coords_ref[3]
    rel_ref[...] = jnp.zeros_like(rel_ref)
    for group in range(4):
        total = jnp.zeros((512, 160), jnp.float32)
        for far in range(2):
            side = lax.rem(core + far, 2)
            total = total + dot_right_t(
                dgu_ref[side], group_rows(piece_refs[4 * far + group], 0, 2048)
            )
        rel_ref[:, 256 * group : 256 * group + 160] = total
    to_plain(rel_ref, perm_ref, plain_ref)
    gain_one, gain_two = 1.0 + gains_ref[1:2, :], 1.0 + gains_ref[2:3, :]

    def pull(rows, carry):
        pulled, term_two = pull_norm(mid_ref[rows, :], gain_two, plain_ref[rows, :])
        grad = cot_ref[rows, :].astype(jnp.float32) + pulled
        dmid_ref[rows, :] = grad
        pulled, term_one = pull_norm(branch_ref[rows, :], gain_one, grad)
        da_ref[rows, :] = pulled.astype(BF)
        return carry[0] + fold_rows(term_one), carry[1] + fold_rows(term_two)

    zero = jnp.zeros((8, 640), jnp.float32)
    gain_ref[0], gain_ref[1] = chunks(512, 32, pull, (zero, zero))


def attention_backward(
    coords_ref, da_ref, wo_ref, o_ref, prob_ref, qn_ref, kn_ref, vb_ref, q_ref, kv_ref, gains_ref,
    dqkv_ref, gain_ref, dwo_ref, do_ref, dqn_ref, dkn_ref, dv_ref, ds_ref,
):
    for head in range(4):
        block = wo_ref[8 * head : 8 * head + 8].reshape(256, 640)
        do_ref[head] = dot_right_t(da_ref[...], block).astype(BF)
        grad = dot_left_t(o_ref[head], da_ref[...])
        dwo_ref[8 * head : 8 * head + 8] = grad.astype(BF).reshape(8, 32, 640)
    dkn_ref[...] = jnp.zeros_like(dkn_ref)
    dv_ref[...] = jnp.zeros_like(dv_ref)
    for block, (low, high) in enumerate(KEY_SPANS):
        rows, span = slice(128 * block, 128 * block + 128), high - low
        for head in range(4):
            grad = do_ref[head, rows, :]
            delta = jnp.sum(
                grad.astype(jnp.float32) * o_ref[head, rows, :].astype(jnp.float32), axis=-1, keepdims=True
            )
            soft = prob_ref[block, 128 * head : 128 * head + 128, 0:span].astype(jnp.float32)
            lifted = dot_right_t(grad, vb_ref[low:high, :])
            ds_ref[128 * head : 128 * head + 128, 0:span] = (soft * (lifted - delta) * SCALE).astype(BF)
        all_ds = ds_ref[:, 0:span]
        all_rows = qn_ref[:, rows, :].reshape(512, 256)
        dqn_ref[:, rows, :] = dot(all_ds, kn_ref[low:high, :]).reshape(4, 128, 256)
        dkn_ref[low:high, :] += dot_left_t(all_ds, all_rows)
        dv_ref[low:high, :] += dot_left_t(
            prob_ref[block, :, 0:span], do_ref[:, rows, :].reshape(512, 256)
        )
    query_gain, key_gain = 1.0 + gains_ref[4:5, 0:256], 1.0 + gains_ref[5:6, 0:256]

    def pull(rows, carry):
        query_sum, key_sum = carry
        for head in range(4):
            pulled, term = pull_norm(q_ref[head, rows, :], query_gain, dqn_ref[head, rows, :])
            dqkv_ref[head // 2, rows, 256 * (head % 2) : 256 * (head % 2) + 256] = pulled.astype(BF)
            query_sum = query_sum + fold_rows(term)
        pulled, term = pull_norm(kv_ref[0, rows, :], key_gain, dkn_ref[rows, :])
        dqkv_ref[0, rows, 512:768] = pulled.astype(BF)
        dqkv_ref[1, rows, 512:768] = dv_ref[rows, :].astype(BF)
        return query_sum, key_sum + fold_rows(term)

    zero = jnp.zeros((8, 256), jnp.float32)
    gain_ref[0], gain_ref[1] = chunks(512, 32, pull, (zero, zero))


def input_backward(
    coords_ref, dqkv_ref, h1_ref, dwo_ref, tokens_ref, dmid_ref, perm_ref, gains_ref, gain_mid_ref,
    gain_head_ref, gain_down_ref, *refs
):
    piece_refs, refs = refs[:8], refs[8:]
    (input_ref, *out_refs), (rel_ref, plain_ref, h1t_ref) = refs[:5], refs[5:]
    core = coords_ref[3]
    rel_ref[...] = jnp.zeros_like(rel_ref)
    for group in range(4):
        total = jnp.zeros((512, 160), jnp.float32)
        for far in range(2):
            side = lax.rem(core + far, 2)
            total = total + dot_right_t(
                dqkv_ref[side], group_rows(piece_refs[4 * far + group], 0, 768)
            )
        rel_ref[:, 256 * group : 256 * group + 160] = total
        h1t_ref[160 * group : 160 * group + 160, :] = h1_ref[:, 256 * group : 256 * group + 160].T
    to_plain(rel_ref, perm_ref, plain_ref)
    gain_zero = 1.0 + gains_ref[0:1, :]

    def pull(rows, carry):
        pulled, term = pull_norm(tokens_ref[rows, :].astype(jnp.float32), gain_zero, plain_ref[rows, :])
        input_ref[rows, :] = dmid_ref[rows, :] + pulled
        return carry + fold_rows(term)

    sums = [chunks(512, 32, pull, jnp.zeros((8, 640), jnp.float32))]
    sums += [gain_mid_ref[0], gain_mid_ref[1], gain_down_ref[...]]
    lines = [jnp.sum(part, axis=0, keepdims=True) for part in sums]
    for part in range(2):
        line = jnp.sum(gain_head_ref[part], axis=0, keepdims=True)
        lines.append(jnp.concatenate([line, jnp.zeros((1, 384), jnp.float32)], axis=1))
    lines.append(jnp.zeros((2, 640), jnp.float32))
    gain_block = jnp.concatenate(lines, axis=0).astype(BF)
    for far, group, one, two, place in slots(coords_ref):
        out = out_refs[2 * far + group // 2]
        out[group % 2, one, two, 0:32, 768:1408] = dwo_ref[place]
        out[group % 2, one, two, 32:40, 768:1408] = gain_block
    for far in range(2):
        side = lax.rem(core + far, 2)
        for part in range(3):
            low = 256 * part
            grad = dot(h1t_ref[...], dqkv_ref[side, :, low : low + 256]).astype(BF)
            for spot in range(16):
                group, one, two = spot // 4, (spot // 2) % 2, spot % 2
                out_refs[2 * far + group // 2][group % 2, one, two, :, low : low + 256] = grad[
                    40 * spot : 40 * spot + 40
                ]


def call(kernel, coords, inputs, outs, scratch=(), megabytes=32, cost=(1, 1), anys=0):
    whole = pl.BlockSpec(memory_space=pltpu.VMEM)
    return pl.pallas_call(
        kernel,
        out_shape=outs,
        in_specs=[pl.BlockSpec(memory_space=pltpu.SMEM)] + [whole] * len(inputs),
        out_specs=jax.tree.map(lambda _: whole, outs),
        scratch_shapes=list(scratch),
        cost_estimate=pl.CostEstimate(
            flops=int(cost[0] * 1e9), bytes_accessed=int(cost[1] * 1e6), transcendentals=0
        ),
        compiler_params=pltpu.CompilerParams(vmem_limit_bytes=megabytes * 1024 * 1024),
    )(coords, *inputs)


def rel_table():
    table = np.full((32, 1, 1024), -1, np.int32)
    for place in range(32):
        z, y, x, _ = np.unravel_index(place, DIMS)
        for group in range(4):
            for one in range(2):
                for two in range(2):
                    gap = gap_of(group, one, two)
                    chip = (((z + gap[0]) % 4) * 2 + (y + gap[1]) % 2) * 2 + (x + gap[2]) % 2
                    low = 256 * group + 80 * one + 40 * two
                    table[place, 0, low : low + 40] = 40 * chip + np.arange(40)
    return table


def shape(*sizes, kind=BF):
    return jax.ShapeDtypeStruct(sizes, kind)


def scatter_core(keep_a, keep_b, send_a, send_b):
    return keep_a, keep_b, shift(send_a, 3, 1), shift(send_b, 3, 1)


def scatter_across(keep_a, keep_b, got_a, got_b):
    far_a = shift((wide(keep_a[1]) + wide(got_a[1])).astype(BF), 1, 1)
    far_b = shift((wide(keep_b[1]) + wide(got_b[1])).astype(BF), 2, 1)
    return keep_a[0], keep_b[0], got_a[0], got_b[0], far_a, far_b


def scatter_pair(keep_a, keep_b, got_a, got_b, far_a, far_b):
    sum_a = wide(keep_a) + wide(got_a) + wide(far_a)
    sum_b = wide(keep_b) + wide(got_b) + wide(far_b)
    return sum_a[0], sum_b[0], shift(sum_a[1].astype(BF), 2, 1), shift(sum_b[1].astype(BF), 1, 1)


def scatter_along(sum_a, sum_b, side_a, side_b):
    last_a = sum_a + wide(side_a)
    last_b = sum_b + wide(side_b)
    return (
        last_a[0],
        shift(last_a[1].astype(BF), 0, 1),
        shift(last_b[0].astype(BF), 0, 2),
        shift(last_b[1].astype(BF), 0, 3),
    )


def scatter_end(own, *others):
    for other in others:
        own = own + wide(other)
    return own


def block_fast(tokens, segment_ids, cotangent, weights):
    query_round, keyval_round, output_round, gateup_round, down_round, gains, heads = weights
    f32 = jnp.float32
    along, upward, sideways, core = own_coords()
    place = lax.axis_index("dp")
    coords = jnp.stack([along, upward, sideways, core]).astype(jnp.int32)
    index = lax.dynamic_index_in_dim(jnp.asarray(rel_table()), place, keepdims=False)
    tokens, cotangent = tokens.reshape(512, 640), cotangent.reshape(512, 640)
    segcol = segment_ids.reshape(512, 1)

    low = jnp.concatenate([query_round[:, :512], keyval_round[:, :256], gateup_round[:, 0]], axis=1)
    high = jnp.concatenate([query_round[:, 512:], keyval_round[:, 256:], gateup_round[:, 1]], axis=1)
    away, keep = swap_halves(core, low, high)
    got = shift(away, 3, 1)
    both = jnp.concatenate([jnp.where(core == 0, keep, got), jnp.where(core == 0, got, keep)], axis=0)
    spread = jnp.zeros((8, 640), BF)
    spread = lax.dynamic_update_slice(spread, gains, (0, place * gains.shape[1]))
    spread = lax.dynamic_update_slice(spread, heads, (4, place * heads.shape[1]))
    block_a = jnp.concatenate([both[:, :768], jnp.concatenate([output_round, spread], axis=0)], axis=1)
    block_g = both[:, 768:]

    near_w = gather_along(down_round)
    near_a = gather_along(block_a)
    pairs_w = gather_pair(near_w)
    mine_w = gather_across(*pairs_w)
    pieces_w = gather_core(mine_w)
    near_g = gather_along(after(block_g, *near_a))
    pairs_a = gather_pair(after(near_a, *pairs_w))
    mine_a = gather_across(*pairs_a)
    pieces_a = gather_core(mine_a)
    pairs_g = gather_pair(after(near_g, *pairs_a))
    mine_g = gather_across(*after(pairs_g, *mine_a))
    pieces_g = gather_core(mine_g)

    h1, q, kv, qn, kn, vb, wo, gains_full, perm = call(
        project_forward,
        coords,
        [index, tokens, *after(pieces_a, *pairs_g)],
        [
            shape(512, 1024), shape(4, 512, 256, kind=f32), shape(2, 512, 256, kind=f32),
            shape(4, 512, 256), shape(512, 256), shape(512, 256),
            shape(32, 32, 640), shape(8, 640, kind=f32), shape(640, 1024),
        ],
        [pltpu.VMEM((512, 640), BF)],
        12,
        (5, 20),
    )
    prob, o, branch, mid, h3 = call(
        attention_forward,
        coords,
        [tokens, segment_ids, segcol, qn, kn, vb, wo, gains_full, perm],
        [
            shape(4, 512, 384), shape(4, 512, 256), shape(512, 640, kind=f32),
            shape(512, 640, kind=f32), shape(512, 1024),
        ],
        [pltpu.VMEM((512, 640), BF), pltpu.VMEM((128, 384), f32)],
        12,
        (5, 20),
    )
    slope, gelu, hidden = call(
        gateup_forward,
        coords,
        [h3, *pieces_g],
        [shape(512, 2048)] * 3,
        [pltpu.VMEM((2, 512, 512), f32)],
        12,
        (6, 20),
    )
    result, dm, gain_down, wd, *parts_w = call(
        down_both,
        coords,
        [hidden, mid, cotangent, gains_full, *pieces_w],
        [shape(512, 640), shape(512, 640), shape(8, 640, kind=f32), shape(32, 64, 640)]
        + [shape(2, 2, 2, 64, 640)] * 4,
        [pltpu.VMEM((512, 640), f32), pltpu.VMEM((32, 64, 640), BF)],
        12,
        (6, 20),
    )
    dgu, *parts_g = call(
        gateup_backward,
        coords,
        [dm, wd, slope, gelu, h3],
        [shape(2, 512, 2048)] + [shape(2, 2, 2, 40, 2048)] * 4,
        [pltpu.VMEM((512, 512), f32), pltpu.VMEM((640, 512), BF)],
        12,
        (8, 20),
    )
    got_w = scatter_core(*parts_w)
    dmid, da, gain_mid = call(
        middle_backward,
        coords,
        [after(dgu, *got_w), mid, branch, cotangent, gains_full, perm, *pieces_g],
        [shape(512, 640, kind=f32), shape(512, 640), shape(2, 8, 640, kind=f32)],
        [pltpu.VMEM((512, 1024), f32), pltpu.VMEM((512, 640), f32)],
        12,
        (8, 20),
    )
    far_w = scatter_across(*got_w)
    got_g = scatter_core(*parts_g)
    dqkv, gain_head, dwo = call(
        attention_backward,
        coords,
        [after(da, *far_w, *got_g), wo, o, prob, qn, kn, vb, q, kv, gains_full],
        [shape(2, 512, 768), shape(2, 8, 256, kind=f32), shape(32, 32, 640)],
        [
            pltpu.VMEM((4, 512, 256), BF),
            pltpu.VMEM((4, 512, 256), f32), pltpu.VMEM((512, 256), f32), pltpu.VMEM((512, 256), f32),
            pltpu.VMEM((512, 384), BF),
        ],
        12,
        (6, 20),
    )
    side_w = scatter_pair(*far_w)
    far_g = scatter_across(*got_g)
    input_grad, *parts_a = call(
        input_backward,
        coords,
        [after(dqkv, *side_w), h1, dwo, tokens, dmid, perm, gains_full, gain_mid, gain_head, gain_down, *pieces_a],
        [shape(512, 640, kind=f32)] + [shape(2, 2, 2, 40, 1408)] * 4,
        [pltpu.VMEM((512, 1024), f32), pltpu.VMEM((512, 640), f32), pltpu.VMEM((640, 512), BF)],
        12,
        (6, 20),
    )
    down_grad = scatter_end(*scatter_along(*side_w))
    side_g = scatter_pair(*far_g)
    got_a = scatter_core(*after(parts_a, *far_g))
    far_a = scatter_across(*after(got_a, *side_g))
    gateup_sum = scatter_end(*scatter_along(*side_g))
    rest = scatter_end(*scatter_along(*scatter_pair(*far_a)))
    output_grad = rest[:32, 768:]
    norm_grad = lax.dynamic_slice(rest[32:36, 768:], (0, place * 20), (4, 20))
    qknorm_grad = lax.dynamic_slice(rest[36:38, 768:], (0, place * 8), (2, 8))

    def own_rows(both):
        away, keep = swap_halves(core, both[:20], both[20:])
        got = shift(away, 3, 1)
        return jnp.where(core == 0, keep, got), jnp.where(core == 0, got, keep)

    low, high = own_rows(gateup_sum)
    gateup_grad = jnp.stack([low, high], axis=1)
    low, high = own_rows(rest[:, :768])
    query_grad = jnp.concatenate([low[:, :512], high[:, :512]], axis=1)
    keyval_grad = jnp.concatenate([low[:, 512:], high[:, 512:]], axis=1)
    grads = (query_grad, keyval_grad, output_grad, gateup_grad, down_grad, norm_grad, qknorm_grad)
    return result[None], input_grad[None], grads


def norm_apply(values, gain_vector):
    inverse = lax.rsqrt(jnp.mean(values * values, axis=-1, keepdims=True) + norm_epsilon)
    return values * inverse * (1.0 + gain_vector)


def gelu_product(gate_part, up_part):
    return jax.nn.gelu(gate_part, approximate=True) * up_part


def block_scores(query_normed, key_normed, segments, row_start, row_stop, score_scale):
    positions = jnp.arange(row_stop)
    same_doc = segments[row_start:row_stop, None] == segments[None, :row_stop]
    causal = positions[None, :] <= positions[row_start:row_stop, None]
    allowed = (same_doc & causal)[None]
    scores = (
        jnp.einsum("qhd,kd->hqk", query_normed, key_normed, preferred_element_type=jnp.float32)
        * score_scale
    )
    return (jnp.where(allowed, scores, -1e30), allowed)


def attend_forward(query_normed, key_normed, value_round, segments, score_scale):
    length = query_normed.shape[0]
    block_rows = min(512, length)
    masked, allowed = block_scores(query_normed, key_normed, segments, 0, block_rows, score_scale)
    row_max = jnp.max(masked, axis=-1, keepdims=True)
    row_total = jnp.sum(jnp.where(allowed, jnp.exp(masked - row_max), 0.0), axis=-1, keepdims=True)
    log_total = row_max + jnp.log(row_total)
    soft_round = jnp.where(allowed, jnp.exp(masked - log_total), 0.0).astype(jnp.bfloat16)
    attended_block = jnp.einsum(
        "hqk,kd->qhd", soft_round, value_round, preferred_element_type=jnp.float32
    )
    attended_parts = attended_block.astype(jnp.bfloat16)
    total_parts = log_total[:, :, 0]
    return (attended_parts, total_parts)


def attend_backward(
    query_normed,
    key_normed,
    value_round,
    segments,
    log_totals,
    attended,
    grad_attended,
    score_scale,
):
    length = query_normed.shape[0]
    head_dim = key_normed.shape[1]
    block_rows = min(512, length)
    row_delta = jnp.sum(grad_attended.astype(jnp.float32) * attended.astype(jnp.float32), axis=-1)
    grad_key_sum = jnp.zeros((length, head_dim), jnp.float32)
    grad_value_sum = jnp.zeros((length, head_dim), jnp.float32)
    masked, allowed = block_scores(query_normed, key_normed, segments, 0, block_rows, score_scale)
    soft_weights = jnp.where(allowed, jnp.exp(masked - log_totals[:, 0:block_rows, None]), 0.0)
    soft_round = soft_weights.astype(jnp.bfloat16)
    grad_value_sum = grad_value_sum.at[:block_rows].add(
        jnp.einsum("hqk,qhd->kd", soft_round, grad_attended, preferred_element_type=jnp.float32)
    )
    grad_soft = jnp.einsum(
        "qhd,kd->hqk", grad_attended, value_round, preferred_element_type=jnp.float32
    )
    delta_block = row_delta.T[:, :, None]
    grad_scores = (soft_weights * (grad_soft - delta_block) * score_scale).astype(jnp.bfloat16)
    grad_query_parts = jnp.einsum(
        "hqk,kd->qhd", grad_scores, key_normed, preferred_element_type=jnp.float32
    )
    grad_key_sum = grad_key_sum.at[:block_rows].add(
        jnp.einsum("hqk,qhd->kd", grad_scores, query_normed, preferred_element_type=jnp.float32)
    )
    return (grad_query_parts, grad_key_sum, grad_value_sum)


def adam_update(parameter, gradient, first_moment, second_moment, decay_value):
    first_new = beta_one * first_moment + (1.0 - beta_one) * gradient
    second_new = beta_two * second_moment + (1.0 - beta_two) * gradient * gradient
    first_hat = first_new / (1.0 - beta_one**STEP)
    second_hat = second_new / (1.0 - beta_two**STEP)
    parameter_new = (
        parameter
        - learn_rate * first_hat / (jnp.sqrt(second_hat) + adam_epsilon)
        - learn_rate * decay_value * parameter
    )
    return (parameter_new, first_new, second_new)


def block_plain(tokens, segment_ids, cotangent, weights):
    query_full, keyval_full, output_full, gateup_full, down_full, main_gains, head_gains = gather_plain(*weights)
    seq_count, length, model_width = tokens.shape
    row_count = seq_count * length
    head_dim = head_gains.shape[1]
    head_count = query_full.shape[1] // head_dim
    hidden_units = gateup_full.shape[1] // 2
    score_scale = head_dim ** (-0.5)
    inputs = tokens.reshape(row_count, model_width).astype(jnp.float32)
    normed_in = norm_apply(inputs, main_gains[0]).astype(jnp.bfloat16)
    queries = jnp.dot(normed_in, query_full, preferred_element_type=jnp.float32).reshape(
        row_count, head_count, head_dim
    )
    keyvals = jnp.dot(normed_in, keyval_full, preferred_element_type=jnp.float32)
    key_rows = keyvals[:, :head_dim]
    value_rows = keyvals[:, head_dim:]
    query_normed = norm_apply(queries, head_gains[0]).astype(jnp.bfloat16)
    key_normed = norm_apply(key_rows, head_gains[1]).astype(jnp.bfloat16)
    value_round = value_rows.astype(jnp.bfloat16)
    seq_index = 0
    attended_seq, totals_seq = attend_forward(
        query_normed, key_normed, value_round, segment_ids[seq_index], score_scale
    )
    total_parts = [totals_seq]
    attended_flat = attended_seq.reshape(row_count, head_count * head_dim)
    branch = jnp.dot(attended_flat, output_full, preferred_element_type=jnp.float32)
    middle = inputs + norm_apply(branch, main_gains[1])
    normed_mid = norm_apply(middle, main_gains[2]).astype(jnp.bfloat16)
    gate_up = jnp.dot(
        normed_mid,
        gateup_full,
        preferred_element_type=jnp.float32,
    )
    gate_part = gate_up[:, :hidden_units]
    up_part = gate_up[:, hidden_units:]
    hidden = gelu_product(gate_part, up_part).astype(jnp.bfloat16)
    down_out = jnp.dot(hidden, down_full, preferred_element_type=jnp.float32)
    result = (middle + norm_apply(down_out, main_gains[3])).astype(jnp.bfloat16)
    query_back, keyval_back, output_back, gateup_back, down_back = (
        query_full,
        keyval_full,
        output_full,
        gateup_full,
        down_full,
    )
    gateup_flat = gateup_back
    grad_out = cotangent.reshape(row_count, model_width).astype(jnp.float32)
    _, pull_back = jax.vjp(norm_apply, down_out, main_gains[3])
    grad_down_out, grad_gain_three = pull_back(grad_out)
    grad_down_round = grad_down_out.astype(jnp.bfloat16)
    grad_down = jnp.dot(hidden.T, grad_down_round, preferred_element_type=jnp.float32)
    grad_hidden = jnp.dot(grad_down_round, down_back.T, preferred_element_type=jnp.float32)
    _, pull_back = jax.vjp(gelu_product, gate_part, up_part)
    grad_gate, grad_up = pull_back(grad_hidden)
    grad_gate_up = jnp.concatenate([grad_gate, grad_up], axis=1).astype(jnp.bfloat16)
    grad_gateup = jnp.dot(normed_mid.T, grad_gate_up, preferred_element_type=jnp.float32)
    grad_normed_mid = jnp.dot(grad_gate_up, gateup_flat.T, preferred_element_type=jnp.float32)
    _, pull_back = jax.vjp(norm_apply, middle, main_gains[2])
    grad_mid_norm, grad_gain_two = pull_back(grad_normed_mid)
    grad_middle = grad_out + grad_mid_norm
    _, pull_back = jax.vjp(norm_apply, branch, main_gains[1])
    grad_branch, grad_gain_one = pull_back(grad_middle)
    grad_branch_round = grad_branch.astype(jnp.bfloat16)
    grad_output = jnp.dot(attended_flat.T, grad_branch_round, preferred_element_type=jnp.float32)
    grad_attended = (
        jnp.dot(grad_branch_round, output_back.T, preferred_element_type=jnp.float32)
        .reshape(row_count, head_count, head_dim)
        .astype(jnp.bfloat16)
    )
    seq_index = 0
    grad_query_seq, grad_key_seq, grad_value_seq = attend_backward(
        query_normed,
        key_normed,
        value_round,
        segment_ids[seq_index],
        total_parts[seq_index],
        attended_seq,
        grad_attended,
        score_scale,
    )
    _, pull_back = jax.vjp(norm_apply, queries, head_gains[0])
    grad_queries, grad_head_zero = pull_back(grad_query_seq)
    _, pull_back = jax.vjp(norm_apply, key_rows, head_gains[1])
    grad_keys, grad_head_one = pull_back(grad_key_seq)
    grad_query_round = grad_queries.reshape(row_count, head_count * head_dim).astype(jnp.bfloat16)
    grad_keyval_round = jnp.concatenate([grad_keys, grad_value_seq], axis=1).astype(jnp.bfloat16)
    grad_query = jnp.dot(normed_in.T, grad_query_round, preferred_element_type=jnp.float32)
    grad_keyval = jnp.dot(normed_in.T, grad_keyval_round, preferred_element_type=jnp.float32)
    grad_normed_in = jnp.dot(
        grad_query_round, query_back.T, preferred_element_type=jnp.float32
    ) + jnp.dot(grad_keyval_round, keyval_back.T, preferred_element_type=jnp.float32)
    _, pull_back = jax.vjp(norm_apply, inputs, main_gains[0])
    grad_in_norm, grad_gain_zero = pull_back(grad_normed_in)
    input_grad = grad_middle + grad_in_norm
    grad_gains = jnp.stack([grad_gain_zero, grad_gain_one, grad_gain_two, grad_gain_three])
    grad_heads = jnp.stack([grad_head_zero, grad_head_one])
    gradients = scatter_plain(
        grad_query, grad_keyval, grad_output, grad_gateup, grad_down, grad_gains, grad_heads
    )
    result_out = result.reshape(seq_count, length, model_width)
    input_out = input_grad.reshape(seq_count, length, model_width)
    return result_out, input_out, gradients


def per_device(
    tokens,
    segment_ids,
    cotangent,
    query_weight,
    keyval_weight,
    output_weight,
    gateup_weight,
    down_weight,
    norm_gains,
    qknorm_gains,
    query_mean,
    keyval_mean,
    output_mean,
    gateup_mean,
    down_mean,
    norm_mean,
    qknorm_mean,
    query_square,
    keyval_square,
    output_square,
    gateup_square,
    down_square,
    norm_square,
    qknorm_square,
):
    query_round = query_weight.astype(jnp.bfloat16)
    keyval_round = keyval_weight.astype(jnp.bfloat16)
    output_round = output_weight.astype(jnp.bfloat16)
    gateup_round = gateup_weight.astype(jnp.bfloat16)
    down_round = down_weight.astype(jnp.bfloat16)
    gains_round = norm_gains.astype(jnp.bfloat16)
    headgain_round = qknorm_gains.astype(jnp.bfloat16)
    weights = (
        query_round, keyval_round, output_round, gateup_round, down_round, gains_round, headgain_round
    )
    block = block_fast if lax.axis_size("dp") == 32 else block_plain
    result_out, input_out, gradients = block(tokens, segment_ids, cotangent, weights)
    parameters = (
        query_weight,
        keyval_weight,
        output_weight,
        gateup_weight,
        down_weight,
        norm_gains,
        qknorm_gains,
    )
    firsts = (query_mean, keyval_mean, output_mean, gateup_mean, down_mean, norm_mean, qknorm_mean)
    seconds = (
        query_square,
        keyval_square,
        output_square,
        gateup_square,
        down_square,
        norm_square,
        qknorm_square,
    )
    decays = (decay_coef, decay_coef, decay_coef, decay_coef, decay_coef, 0.0, 0.0)
    updates = [
        adam_update(
            parameters[place], gradients[place], firsts[place], seconds[place], decays[place]
        )
        for place in range(7)
    ]
    news = tuple((update[0] for update in updates))
    first_news = tuple((update[1] for update in updates))
    second_news = tuple((update[2] for update in updates))
    return (result_out, input_out) + gradients + news + first_news + second_news


def solution(mesh):
    in_specs = (
        P("dp", None, None),
        P("dp", None),
        P("dp", None, None),
        P("dp", None),
        P("dp", None),
        P("dp", None),
        P("dp", None, None),
        P("dp", None),
        P(None, "dp"),
        P(None, "dp"),
        P("dp", None),
        P("dp", None),
        P("dp", None),
        P("dp", None, None),
        P("dp", None),
        P(None, "dp"),
        P(None, "dp"),
        P("dp", None),
        P("dp", None),
        P("dp", None),
        P("dp", None, None),
        P("dp", None),
        P(None, "dp"),
        P(None, "dp"),
    )
    out_specs = (
        P("dp", None, None),
        P("dp", None, None),
        P("dp", None),
        P("dp", None),
        P("dp", None),
        P("dp", None, None),
        P("dp", None),
        P(None, "dp"),
        P(None, "dp"),
        P("dp", None),
        P("dp", None),
        P("dp", None),
        P("dp", None, None),
        P("dp", None),
        P(None, "dp"),
        P(None, "dp"),
        P("dp", None),
        P("dp", None),
        P("dp", None),
        P("dp", None, None),
        P("dp", None),
        P(None, "dp"),
        P(None, "dp"),
        P("dp", None),
        P("dp", None),
        P("dp", None),
        P("dp", None, None),
        P("dp", None),
        P(None, "dp"),
        P(None, "dp"),
    )
    return jax.shard_map(
        per_device, mesh=mesh, in_specs=in_specs, out_specs=out_specs, check_vma=False
    )
```

time: 813 us -> 249 us (0.31)
  waiting for transfers between devices: 370 us -> 74.3 us
  blocking collectives: 252 us -> 0 us
  Pallas kernels: 0 us -> 76.7 us
  matrix products: 61.4 us -> 0 us
  starting transfers between devices: 29.9 us -> 71.6 us
  local copies, waits for them, and re-layouts: 42.8 us -> 10.2 us
  other arithmetic: 30.6 us -> 10.2 us
  between operations: 15.5 us -> 1.75 us
    reduce_scatter x2 -> x0, waiting for transfers between devices: 283 us -> none  [the longest x1 142 us: per_device(): lax.psum_scatter(grad_output, 'dp', scatter_dimension=0, tiled=True)]
    unnamed x2 -> x0, blocking collectives: 132 us -> none
    all_gather x3 -> x0, blocking collectives: 120 us -> none  [the longest x1 43.1 us: per_device(): lax.all_gather(gains_round, 'dp', axis=1, tiled=True)]
    all_gather x4 -> x0, waiting for transfers between devices: 85.6 us -> none  [the longest x1 44.8 us: per_device(): lax.all_gather(down_round, 'dp', axis=0, tiled=True)]
    pallas_call x0 -> x8, Pallas kernels: none -> 76.7 us  [call(): pl.pallas_call(kernel, out_shape=outs, in_specs=[pl.BlockSpec(memory_spac...]
    ppermute x0 -> x63, waiting for transfers between devices: none -> 74.3 us  [shift(): return lax.ppermute(values, 'dp', shift_perm(axis, amount))]
    ppermute x0 -> x63, starting transfers between devices: none -> 71.6 us  [shift(): return lax.ppermute(values, 'dp', shift_perm(axis, amount))]
    dot_general x21 -> x0, matrix products: 61.4 us -> none  [the longest x1 7.72 us: per_device(): jnp.dot(grad_gate_up, gateup_flat.T, preferred_element_type=jnp.float32)]
  transfers between devices with their start and end apart: 19 -> 63, of which waited for: 6 -> 18; matrix products, arithmetic and copies ran while one was open for 22% -> 6% of each run, Pallas kernels for 0% -> 27%
where the time goes in v2:
time: 249 us; the launch traced here: 245 us
  Pallas kernels  76.7 us (31%)
  waiting for transfers between devices  74.3 us (30%)
  starting transfers between devices  71.6 us (29%)
  local copies, waits for them, and re-layouts  10.2 us (4%)
  other arithmetic  10.2 us (4%)
    pallas_call x8, Pallas kernels, call(): pl.pallas_call(kernel, out_shape=outs, in_specs=[pl.BlockSpec(memory_spac...  76.7 us
    ppermute x63, waiting for transfers between devices, shift(): return lax.ppermute(values, 'dp', shift_perm(axis, amount))  74.3 us
    ppermute x63, starting transfers between devices, shift(): return lax.ppermute(values, 'dp', shift_perm(axis, amount))  71.6 us
    unnamed x61, local copies, waits for them, and re-layouts  8.05 us
    sub x7, other arithmetic, adam_update(): parameter - learn_rate * first_hat / (jnp.sqrt(second_hat) + adam_epsilon)  5.18 us
  transfers between devices with their start and end apart: 63, of which 18 were waited for; matrix products, arithmetic and copies ran while one was open for 6% of the time, Pallas kernels for 27%

profile of v2, /device:TPU:1, one launch (start us, length us, event | category | flops | bytes accessed | tf_op | source)
XLA Modules:
  0.0 244.8 jit_solution(14935503288888547244)
XLA Ops:
  1.7 4.2 %collective-permute-start.4 = (bf16[64,640]{1,0:T(8,128)(2,1)S(1)}, bf16[64,640]{1,0:T(8,128)(2,1)S(1)}, u32[]{:S(2)}, u32[]{:S(2)}) collective-permute-start(bf16[64,640]{1,0:T(8,128)(2,1)S(1)} %convert_element_type.274), channel_id=1, source_target_pairs={{0,24},{1,25},{2,26},{3,27},{4,28},{5,29},{6,30},{7,31},{8,0},{9,1... | collective-permute-start | bytes 245768 | tf_op jit(solution)/shard_map/ppermute | solution.py:31
  8.4 1.6 collective-permute-start
  13.9 3.5 %collective-permute-start.1 = (bf16[40,1408]{1,0:T(8,128)(2,1)S(1)}, bf16[40,1408]{1,0:T(8,128)(2,1)S(1)}, u32[]{:S(2)}, u32[]{:S(2)}) collective-permute-start(bf16[40,1408]{1,0:T(8,128)(2,1)S(1)} %fusion.32), channel_id=1, source_target_pairs={{0,24},{1,25},{2,26},{3,27},{4,28},{5,29},{6,30},{7,31},{8,0},{9,1... | collective-permute-start | bytes 337928 | tf_op jit(solution)/shard_map/ppermute | solution.py:31
  19.5 8.6 %collective-permute-done.2 = bf16[40,1408]{1,0:T(8,128)(2,1)S(1)} collective-permute-done((bf16[40,1408]{1,0:T(8,128)(2,1)S(1)}, bf16[40,1408]{1,0:T(8,128)(2,1)S(1)}, u32[]{:S(2)}, u32[]{:S(2)}) %collective-permute-start.2) | collective-permute-done | bytes 112672 | tf_op jit(solution)/shard_map/ppermute | solution.py:31
  32.1 3.3 %collective-permute-done.9 = bf16[2,40,1408]{2,1,0:T(8,128)(2,1)S(1)} collective-permute-done((bf16[2,40,1408]{2,1,0:T(8,128)(2,1)S(1)}, bf16[2,40,1408]{2,1,0:T(8,128)(2,1)S(1)}, u32[]{:S(2)}, u32[]{:S(2)}) %collective-permute-start.9) | collective-permute-done | bytes 225312 | tf_op jit(solution)/shard_map/ppermute | solution.py:31
  35.5 1.6 collective-permute-done.11
  37.1 5.5 %collective-permute-done.18 = bf16[40,2048]{1,0:T(8,128)(2,1)S(1)} collective-permute-done((bf16[40,2048]{1,0:T(8,128)(2,1)S(1)}, bf16[40,2048]{1,0:T(8,128)(2,1)S(1)}, u32[]{:S(2)}, u32[]{:S(2)}) %collective-permute-start.18) | collective-permute-done | bytes 163872 | tf_op jit(solution)/shard_map/ppermute | solution.py:31
  45.7 3.1 %collective-permute-start.13 = (bf16[2,2,40,1408]{3,2,1,0:T(8,128)(2,1)S(1)}, bf16[2,2,40,1408]{3,2,1,0:T(8,128)(2,1)S(1)}, u32[]{:S(2)}, u32[]{:S(2)}) collective-permute-start(bf16[2,2,40,1408]{3,2,1,0:T(8,128)(2,1)S(1)} %pad_maximum_fusion.2.refs_0_), channel_id=1, source_target_pairs={{0,1},{1,0},{2,3},{3,2},{4,5},{5,4},{6,7},{7,6},{8,9},{9,8},{10,11... | collective-permute-start | bytes 1351688 | tf_op jit(solution)/shard_map/ppermute | solution.py:31
  51.0 9.7 %collective-permute-done.10.refs_1_ = bf16[2,2,40,1408]{3,2,1,0:T(8,128)(2,1)} collective-permute-done((bf16[2,2,40,1408]{3,2,1,0:T(8,128)(2,1)S(1)}, bf16[2,2,40,1408]{3,2,1,0:T(8,128)(2,1)}, u32[]{:S(2)}, u32[]{:S(2)}) %collective-permute-start.10) | collective-permute-done | bytes 450592 | tf_op jit(solution)/shard_map/ppermute | solution.py:31
  61.2 3.8 %collective-permute-start.15 = (bf16[2,2,40,1408]{3,2,1,0:T(8,128)(2,1)S(1)}, bf16[2,2,40,1408]{3,2,1,0:T(8,128)(2,1)}, u32[]{:S(2)}, u32[]{:S(2)}) collective-permute-start(bf16[2,2,40,1408]{3,2,1,0:T(8,128)(2,1)S(1)} %pad_maximum_fusion.3.refs_2_), channel_id=1, source_target_pairs={{0,1},{1,0},{2,3},{3,2},{4,5},{5,4},{6,7},{7,6},{8,9},{9,8},{10,11... | collective-permute-start | bytes 1351688 | tf_op jit(solution)/shard_map/ppermute | solution.py:31
  69.1 4.7 %collective-permute-done.22.refs_1_ = bf16[2,2,40,2048]{3,2,1,0:T(8,128)(2,1)} collective-permute-done((bf16[2,2,40,2048]{3,2,1,0:T(8,128)(2,1)S(1)}, bf16[2,2,40,2048]{3,2,1,0:T(8,128)(2,1)}, u32[]{:S(2)}, u32[]{:S(2)}) %collective-permute-start.22) | collective-permute-done | bytes 655392 | tf_op jit(solution)/shard_map/ppermute | solution.py:31
  73.8 7.6 %collective-permute-start.25 = (bf16[2,2,40,2048]{3,2,1,0:T(8,128)(2,1)}, bf16[2,2,40,2048]{3,2,1,0:T(8,128)(2,1)S(1)}, u32[]{:S(2)}, u32[]{:S(2)}) collective-permute-start(bf16[2,2,40,2048]{3,2,1,0:T(8,128)(2,1)} %collective-permute-done.22.refs_1_), channel_id=1, source_target_pairs={{0,1},{1,0},{2,3},{3,2},{4,5},{5,4},{6,7},{7,6},{8,9},{9,8},{10,11... | collective-permute-start | bytes 1966088 | tf_op jit(solution)/shard_map/ppermute | solution.py:31
  83.6 7.5 %shard_map.472 = (bf16[512,1024]{1,0:T(8,128)(2,1)S(1)}, f32[4,512,256]{2,1,0:T(8,128)S(1)}, f32[2,512,256]{2,1,0:T(8,128)S(1)}, bf16[4,512,256]{2,1,0:T(8,128)(...) custom-call(s32[4]{0:T(128)S(1)} %pad_add_fusion.coords_ref, ...), custom_call_target="tpu_custom_call" | custom-call | flops 5000000000 | bytes 20000000 | tf_op jit(solution)/shard_map/pallas_call | solution.py:478
  91.4 11.0 %shard_map.473 = (bf16[4,512,384]{2,1,0:T(8,128)(2,1)S(1)}, bf16[4,512,256]{2,1,0:T(8,128)(2,1)S(1)}, f32[512,640]{1,0:T(8,128)S(1)}, f32[512,640]{1,0:T(8,128)S(1)}, bf16[512,1024]{1,0:T(8,128)(2,1)S(1)}) custom-call(s32[4]{0:T(128)S(1)} %pad_add_fusion.coords_ref, bf16[512,640]{1,0:T(8,128)(2,1)S(1)} %bitcast.183, s32[1,512]{1,0:T(1,128)S(1)} %copy-done, ...), custom_call_target="tpu_custom_call" | custom-call | flops 5000000000 | bytes 20000000 | tf_op jit(solution)/shard_map/pallas_call | solution.py:478
  103.9 9.9 %shard_map.474 = (bf16[512,2048]{1,0:T(8,128)(2,1)S(1)}, bf16[512,2048]{1,0:T(8,128)(2,1)S(1)}, bf16[512,2048]{1,0:T(8,128)(2,1)S(1)}) custom-call(s32[4]{0:T(128)S(1)} %pad_add_fusion.coords_ref, bf16[512,1024]{1,0:T(8,128)(2,1)S(1)} %get-tuple-element.124.h3_ref, bf16[2,2,40,2048]{3,2,1,0:T(8,128)(2,1)S(1)} %pad_maximum_fusion.refs_0_, ...), custom_call_target="tpu_custom_call" | custom-call | flops 6000000000 | bytes 20000000 | tf_op jit(solution)/shard_map/pallas_call | solution.py:478
  113.9 9.9 %shard_map.475 = (bf16[512,640]{1,0:T(8,128)(2,1)}, bf16[512,640]{1,0:T(8,128)(2,1)S(1)}, f32[8,640]{1,0:T(8,128)S(1)}, bf16[32,64,640]{2,1,0:T(8,128)(2,1)S(1)}...) custom-call(s32[4]{0:T(128)S(1)} %pad_add_fusion.coords_ref, ...), custom_call_target="tpu_custom_call" | custom-call | flops 6000000000 | bytes 20000000 | tf_op jit(solution)/shard_map/pallas_call | solution.py:478
  124.3 7.2 %shard_map.476 = (bf16[2,512,2048]{2,1,0:T(8,128)(2,1)S(1)}, bf16[2,2,2,40,2048]{4,3,2,1,0:T(8,128)(2,1)S(1)}, bf16[2,2,2,40,2048]{4,3,2,1,0:T(8,128)(2,1)S(1)},...) custom-call(s32[4]{0:T(128)S(1)} %pad_add_fusion.coords_ref, ...), custom_call_target="tpu_custom_call" | custom-call | flops 8000000000 | bytes 20000000 | tf_op jit(solution)/shard_map/pallas_call | solution.py:478
  133.8 12.8 %shard_map.477 = (f32[512,640]{1,0:T(8,128)S(1)}, bf16[512,640]{1,0:T(8,128)(2,1)S(1)}, f32[2,8,640]{2,1,0:T(8,128)S(1)}) custom-call(s32[4]{0:T(128)S(1)} %pad_add_fusion.coords_ref, bf16[2,512,2048]{2,1,0:T(8,128)(2,1)S(1)} %get-tuple-element.139.dgu_ref, f32[512,640]{1,0:T(8,128)S(1)} %get-tuple-element.128.mid_ref, ...), custom_call_target="tpu_custom_call" | custom-call | flops 8000000000 | bytes 20000000 | tf_op jit(solution)/shard_map/pallas_call | solution.py:478
  148.5 3.0 %collective-permute-done.41 = bf16[2,64,640]{2,1,0:T(8,128)(2,1)S(1)} collective-permute-done((bf16[2,64,640]{2,1,0:T(8,128)(2,1)S(1)}, bf16[2,64,640]{2,1,0:T(8,128)(2,1)S(1)}, u32[]{:S(2)}, u32[]{:S(2)}) %collective-permute-start.41) | collective-permute-done | bytes 163872 | tf_op jit(solution)/shard_map/ppermute | solution.py:31
  152.2 2.7 %collective-permute-start.61 = (bf16[64,640]{1,0:T(8,128)(2,1)S(1)}, bf16[64,640]{1,0:T(8,128)(2,1)S(1)}, u32[]{:S(2)}, u32[]{:S(2)}) collective-permute-start(bf16[64,640]{1,0:T(8,128)(2,1)S(1)} %get-tuple-element.280), channel_id=1, source_target_pairs={{0,16},{1,17},{2,18},{3,19},{4,20},{5,21},{6,22},{7,23},{8,24},{9,... | collective-permute-start | bytes 245768 | tf_op jit(solution)/shard_map/ppermute | solution.py:31
  156.0 7.8 %shard_map.478 = (bf16[2,512,768]{2,1,0:T(8,128)(2,1)S(1)}, f32[2,8,256]{2,1,0:T(8,128)S(1)}, bf16[32,32,640]{2,1,0:T(8,128)(2,1)S(1)}) custom-call(s32[4]{0:T(128)S(1)} %pad_add_fusion.coords_ref, bf16[512,640]{1,0:T(8,128)(2,1)S(1)} %get-tuple-element.146.da_ref, bf16[32,32,640]{2,1,0:T(8,128)(2,1)S(1)} %get-tuple-element.121.wo_ref, ...), custom_call_target="tpu_custom_call" | custom-call | flops 6000000000 | bytes 20000000 | tf_op jit(solution)/shard_map/pallas_call | solution.py:478
  165.4 3.9 %collective-permute-done.43 = bf16[2,2,40,2048]{3,2,1,0:T(8,128)(2,1)S(1)} collective-permute-done((bf16[2,2,40,2048]{3,2,1,0:T(8,128)(2,1)S(1)}, bf16[2,2,40,2048]{3,2,1,0:T(8,128)(2,1)S(1)}, u32[]{:S(2)}, u32[]{:S(2)}) %collective-permute-start.43) | collective-permute-done | bytes 655392 | tf_op jit(solution)/shard_map/ppermute | solution.py:31
  170.9 7.0 %collective-permute-done.42 = bf16[2,2,40,2048]{3,2,1,0:T(8,128)(2,1)S(1)} collective-permute-done((bf16[2,2,40,2048]{3,2,1,0:T(8,128)(2,1)S(1)}, bf16[2,2,40,2048]{3,2,1,0:T(8,128)(2,1)S(1)}, u32[]{:S(2)}, u32[]{:S(2)}) %collective-permute-start.42) | collective-permute-done | bytes 655392 | tf_op jit(solution)/shard_map/ppermute | solution.py:31
  178.9 6.0 %collective-permute-done.47 = bf16[2,40,2048]{2,1,0:T(8,128)(2,1)S(1)} collective-permute-done((bf16[2,40,2048]{2,1,0:T(8,128)(2,1)S(1)}, bf16[2,40,2048]{2,1,0:T(8,128)(2,1)S(1)}, u32[]{:S(2)}, u32[]{:S(2)}) %collective-permute-start.47) | collective-permute-done | bytes 327712 | tf_op jit(solution)/shard_map/ppermute | solution.py:31
  187.6 10.6 %shard_map.479 = (f32[512,640]{1,0:T(8,128)}, bf16[2,2,2,40,1408]{4,3,2,1,0:T(8,128)(2,1)S(1)}, bf16[2,2,2,40,1408]{4,3,2,1,0:T(8,128)(2,1)S(1)}, bf16[2,2,2,40,...) custom-call(s32[4]{0:T(128)S(1)} %pad_add_fusion.coords_ref, ...), custom_call_target="tpu_custom_call" | custom-call | flops 6000000000 | bytes 20000000 | tf_op jit(solution)/shard_map/pallas_call | solution.py:478
  198.2 1.5 collective-permute-start.60
  200.3 4.4 %collective-permute-start.44 = (bf16[2,2,2,40,1408]{4,3,2,1,0:T(8,128)(2,1)S(1)}, bf16[2,2,2,40,1408]{4,3,2,1,0:T(8,128)(2,1)S(1)}, u32[]{:S(2)}, u32[]{:S(2)}) collective-permute-start(bf16[2,2,2,40,1408]{4,3,2,1,0:T(8,128)(2,1)S(1)} %get-tuple-element.166), channel_id=1, source_target_pairs={{0,1},{1,0},{2,3},{3,2},{4,5},{5,4},{6,7},{7,6},{8,9},{9,8},{10,11... | collective-permute-start | bytes 2703368 | tf_op jit(solution)/shard_map/ppermute | solution.py:31
  206.3 2.0 collective-permute-done.59
  210.6 6.4 %collective-permute-done.51 = bf16[2,2,40,1408]{3,2,1,0:T(8,128)(2,1)S(1)} collective-permute-done((bf16[2,2,40,1408]{3,2,1,0:T(8,128)(2,1)S(1)}, bf16[2,2,40,1408]{3,2,1,0:T(8,128)(2,1)S(1)}, u32[]{:S(2)}, u32[]{:S(2)}) %collective-permute-start.51) | collective-permute-done | bytes 450592 | tf_op jit(solution)/shard_map/ppermute | solution.py:31
  219.4 4.4 %collective-permute-done.52 = bf16[2,40,1408]{2,1,0:T(8,128)(2,1)S(1)} collective-permute-done((bf16[2,40,1408]{2,1,0:T(8,128)(2,1)S(1)}, bf16[2,40,1408]{2,1,0:T(8,128)(2,1)S(1)}, u32[]{:S(2)}, u32[]{:S(2)}) %collective-permute-start.52) | collective-permute-done | bytes 225312 | tf_op jit(solution)/shard_map/ppermute | solution.py:31
  224.0 5.8 %collective-permute-start.54 = (bf16[40,1408]{1,0:T(8,128)(2,1)S(1)}, bf16[40,1408]{1,0:T(8,128)(2,1)S(1)}, u32[]{:S(2)}, u32[]{:S(2)}) collective-permute-start(bf16[40,1408]{1,0:T(8,128)(2,1)S(1)} %get-tuple-element.273), channel_id=1, source_target_pairs={{0,24},{1,25},{2,26},{3,27},{4,28},{5,29},{6,30},{7,31},{8,0},{9,1... | collective-permute-start | bytes 337928 | tf_op jit(solution)/shard_map/ppermute | solution.py:31
  235.2 4.5 %collective-permute-done.53 = bf16[40,1408]{1,0:T(8,128)(2,1)S(1)} collective-permute-done((bf16[40,1408]{1,0:T(8,128)(2,1)S(1)}, bf16[40,1408]{1,0:T(8,128)(2,1)S(1)}, u32[]{:S(2)}, u32[]{:S(2)}) %collective-permute-start.53) | collective-permute-done | bytes 112672 | tf_op jit(solution)/shard_map/ppermute | solution.py:31
  (244 shorter events, 57.6 us)
Async XLA Ops:
  11.2 19.2 %collective-permute-start.5 = (bf16[2,64,640]{2,1,0:T(8,128)(2,1)S(1)}, bf16[2,64,640]{2,1,0:T(8,128)(2,1)S(1)}, u32[]{:S(2)}, u32[]{:S(2)}) collective-permute-start(bf16[2,64,640]{2,1,0:T(8,128)(2,1)S(1)} %get-tuple-element.285), channel_id=1, source_target_pairs={{0,2},{1,3},{2,0},{3,1},{4,6},{5,7},{6,4},{7,5},{8,10},{9,11},{10,... | collective-permute-start | bytes 491528 | tf_op jit(solution)/shard_map/ppermute | solution.py:31
  12.5 17.9 %collective-permute-start.8 = (bf16[2,64,640]{2,1,0:T(8,128)(2,1)S(1)}, bf16[2,64,640]{2,1,0:T(8,128)(2,1)S(1)}, u32[]{:S(2)}, u32[]{:S(2)}) collective-permute-start(bf16[2,64,640]{2,1,0:T(8,128)(2,1)S(1)} %get-tuple-element.283), channel_id=1, source_target_pairs={{0,4},{1,5},{2,6},{3,7},{4,0},{5,1},{6,2},{7,3},{8,12},{9,13},{10,... | collective-permute-start | bytes 491528 | tf_op jit(solution)/shard_map/ppermute | solution.py:31
  17.4 10.7 %collective-permute-start.2 = (bf16[40,1408]{1,0:T(8,128)(2,1)S(1)}, bf16[40,1408]{1,0:T(8,128)(2,1)S(1)}, u32[]{:S(2)}, u32[]{:S(2)}) collective-permute-start(bf16[40,1408]{1,0:T(8,128)(2,1)S(1)} %fusion.32), channel_id=1, source_target_pairs={{0,16},{1,17},{2,18},{3,19},{4,20},{5,21},{6,22},{7,23},{8,24},{9,... | collective-permute-start | bytes 337928 | tf_op jit(solution)/shard_map/ppermute | solution.py:31
  28.1 14.4 %collective-permute-start.18 = (bf16[40,2048]{1,0:T(8,128)(2,1)S(1)}, bf16[40,2048]{1,0:T(8,128)(2,1)S(1)}, u32[]{:S(2)}, u32[]{:S(2)}) collective-permute-start(bf16[40,2048]{1,0:T(8,128)(2,1)S(1)} %pad_maximum_fusion.11), channel_id=1, source_target_pairs={{0,16},{1,17},{2,18},{3,19},{4,20},{5,21},{6,22},{7,23},{8,24},{9,... | collective-permute-start | bytes 491528 | tf_op jit(solution)/shard_map/ppermute | solution.py:31
  28.9 13.7 %collective-permute-start.19 = (bf16[40,2048]{1,0:T(8,128)(2,1)S(1)}, bf16[40,2048]{1,0:T(8,128)(2,1)S(1)}, u32[]{:S(2)}, u32[]{:S(2)}) collective-permute-start(bf16[40,2048]{1,0:T(8,128)(2,1)S(1)} %pad_maximum_fusion.11), channel_id=1, source_target_pairs={{0,8},{1,9},{2,10},{3,11},{4,12},{5,13},{6,14},{7,15},{8,16},{9,17... | collective-permute-start | bytes 491528 | tf_op jit(solution)/shard_map/ppermute | solution.py:31
  44.2 16.4 %collective-permute-start.10 = (bf16[2,2,40,1408]{3,2,1,0:T(8,128)(2,1)S(1)}, bf16[2,2,40,1408]{3,2,1,0:T(8,128)(2,1)}, u32[]{:S(2)}, u32[]{:S(2)}) collective-permute-start(bf16[2,2,40,1408]{3,2,1,0:T(8,128)(2,1)S(1)} %pad_maximum_fusion.2.refs_0_), channel_id=1, source_target_pairs={{0,4},{1,5},{2,6},{3,7},{4,0},{5,1},{6,2},{7,3},{8,12},{9,13},{10,... | collective-permute-start | bytes 1351688 | tf_op jit(solution)/shard_map/ppermute | solution.py:31
  45.5 15.2 %collective-permute-start.12 = (bf16[2,2,40,1408]{3,2,1,0:T(8,128)(2,1)S(1)}, bf16[2,2,40,1408]{3,2,1,0:T(8,128)(2,1)}, u32[]{:S(2)}, u32[]{:S(2)}) collective-permute-start(bf16[2,2,40,1408]{3,2,1,0:T(8,128)(2,1)S(1)} %pad_maximum_fusion.3.refs_2_), channel_id=1, source_target_pairs={{0,2},{1,3},{2,0},{3,1},{4,6},{5,7},{6,4},{7,5},{8,10},{9,11},{10,... | collective-permute-start | bytes 1351688 | tf_op jit(solution)/shard_map/ppermute | solution.py:31
  45.7 19.2 %collective-permute-start.13 = (bf16[2,2,40,1408]{3,2,1,0:T(8,128)(2,1)S(1)}, bf16[2,2,40,1408]{3,2,1,0:T(8,128)(2,1)S(1)}, u32[]{:S(2)}, u32[]{:S(2)}) collective-permute-start(bf16[2,2,40,1408]{3,2,1,0:T(8,128)(2,1)S(1)} %pad_maximum_fusion.2.refs_0_), channel_id=1, source_target_pairs={{0,1},{1,0},{2,3},{3,2},{4,5},{5,4},{6,7},{7,6},{8,9},{9,8},{10,11... | collective-permute-start | bytes 1351688 | tf_op jit(solution)/shard_map/ppermute | solution.py:31
  60.7 13.1 %collective-permute-start.22 = (bf16[2,2,40,2048]{3,2,1,0:T(8,128)(2,1)S(1)}, bf16[2,2,40,2048]{3,2,1,0:T(8,128)(2,1)}, u32[]{:S(2)}, u32[]{:S(2)}) collective-permute-start(bf16[2,2,40,2048]{3,2,1,0:T(8,128)(2,1)S(1)} %pad_maximum_fusion.refs_0_), channel_id=1, source_target_pairs={{0,4},{1,5},{2,6},{3,7},{4,0},{5,1},{6,2},{7,3},{8,12},{9,13},{10,... | collective-permute-start | bytes 1966088 | tf_op jit(solution)/shard_map/ppermute | solution.py:31
  60.9 20.6 %collective-permute-start.23 = (bf16[2,2,40,2048]{3,2,1,0:T(8,128)(2,1)S(1)}, bf16[2,2,40,2048]{3,2,1,0:T(8,128)(2,1)}, u32[]{:S(2)}, u32[]{:S(2)}) collective-permute-start(bf16[2,2,40,2048]{3,2,1,0:T(8,128)(2,1)S(1)} %pad_maximum_fusion.1.refs_2_), channel_id=1, source_target_pairs={{0,2},{1,3},{2,0},{3,1},{4,6},{5,7},{6,4},{7,5},{8,10},{9,11},{10,... | collective-permute-start | bytes 1966088 | tf_op jit(solution)/shard_map/ppermute | solution.py:31
  67.2 23.9 %collective-permute-start.28 = (bf16[2,2,64,640]{3,2,1,0:T(8,128)(2,1)S(1)}, bf16[2,2,64,640]{3,2,1,0:T(8,128)(2,1)S(1)}, u32[]{:S(2)}, u32[]{:S(2)}) collective-permute-start(bf16[2,2,64,640]{3,2,1,0:T(8,128)(2,1)S(1)} %pad_maximum_fusion.5.refs_0_), channel_id=1, source_target_pairs={{0,4},{1,5},{2,6},{3,7},{4,0},{5,1},{6,2},{7,3},{8,12},{9,13},{10,... | collective-permute-start | bytes 983048 | tf_op jit(solution)/shard_map/ppermute | solution.py:31
  68.4 34.9 %collective-permute-start.24 = (bf16[2,2,40,2048]{3,2,1,0:T(8,128)(2,1)S(1)}, bf16[2,2,40,2048]{3,2,1,0:T(8,128)(2,1)S(1)}, u32[]{:S(2)}, u32[]{:S(2)}) collective-permute-start(bf16[2,2,40,2048]{3,2,1,0:T(8,128)(2,1)S(1)} %pad_maximum_fusion.refs_0_), channel_id=1, source_target_pairs={{0,1},{1,0},{2,3},{3,2},{4,5},{5,4},{6,7},{7,6},{8,9},{9,8},{10,11... | collective-permute-start | bytes 1966088 | tf_op jit(solution)/shard_map/ppermute | solution.py:31
  69.0 34.4 %collective-permute-start.26 = (bf16[2,2,40,2048]{3,2,1,0:T(8,128)(2,1)S(1)}, bf16[2,2,40,2048]{3,2,1,0:T(8,128)(2,1)S(1)}, u32[]{:S(2)}, u32[]{:S(2)}) collective-permute-start(bf16[2,2,40,2048]{3,2,1,0:T(8,128)(2,1)S(1)} %pad_maximum_fusion.1.refs_2_), channel_id=1, source_target_pairs={{0,1},{1,0},{2,3},{3,2},{4,5},{5,4},{6,7},{7,6},{8,9},{9,8},{10,11... | collective-permute-start | bytes 1966088 | tf_op jit(solution)/shard_map/ppermute | solution.py:31
  73.8 30.0 %collective-permute-start.25 = (bf16[2,2,40,2048]{3,2,1,0:T(8,128)(2,1)}, bf16[2,2,40,2048]{3,2,1,0:T(8,128)(2,1)S(1)}, u32[]{:S(2)}, u32[]{:S(2)}) collective-permute-start(bf16[2,2,40,2048]{3,2,1,0:T(8,128)(2,1)} %collective-permute-done.22.refs_1_), channel_id=1, source_target_pairs={{0,1},{1,0},{2,3},{3,2},{4,5},{5,4},{6,7},{7,6},{8,9},{9,8},{10,11... | collective-permute-start | bytes 1966088 | tf_op jit(solution)/shard_map/ppermute | solution.py:31
  81.5 22.5 %collective-permute-start.27 = (bf16[2,2,40,2048]{3,2,1,0:T(8,128)(2,1)}, bf16[2,2,40,2048]{3,2,1,0:T(8,128)(2,1)S(1)}, u32[]{:S(2)}, u32[]{:S(2)}) collective-permute-start(bf16[2,2,40,2048]{3,2,1,0:T(8,128)(2,1)} %collective-permute-done.23.refs_3_), channel_id=1, source_target_pairs={{0,1},{1,0},{2,3},{3,2},{4,5},{5,4},{6,7},{7,6},{8,9},{9,8},{10,11... | collective-permute-start | bytes 1966088 | tf_op jit(solution)/shard_map/ppermute | solution.py:31
  91.1 11.3 %collective-permute-start.29 = (bf16[2,2,64,640]{3,2,1,0:T(8,128)(2,1)S(1)}, bf16[2,2,64,640]{3,2,1,0:T(8,128)(2,1)S(1)}, u32[]{:S(2)}, u32[]{:S(2)}) collective-permute-start(bf16[2,2,64,640]{3,2,1,0:T(8,128)(2,1)S(1)} %pad_maximum_fusion.6.refs_2_), channel_id=1, source_target_pairs={{0,2},{1,3},{2,0},{3,1},{4,6},{5,7},{6,4},{7,5},{8,10},{9,11},{10,... | collective-permute-start | bytes 983048 | tf_op jit(solution)/shard_map/ppermute | solution.py:31
  102.4 11.4 %collective-permute-start.30 = (bf16[2,2,64,640]{3,2,1,0:T(8,128)(2,1)S(1)}, bf16[2,2,64,640]{3,2,1,0:T(8,128)(2,1)S(1)}, u32[]{:S(2)}, u32[]{:S(2)}) collective-permute-start(bf16[2,2,64,640]{3,2,1,0:T(8,128)(2,1)S(1)} %pad_maximum_fusion.5.refs_0_), channel_id=1, source_target_pairs={{0,1},{1,0},{2,3},{3,2},{4,5},{5,4},{6,7},{7,6},{8,9},{9,8},{10,11... | collective-permute-start | bytes 983048 | tf_op jit(solution)/shard_map/ppermute | solution.py:31
  103.3 10.5 %collective-permute-start.32 = (bf16[2,2,64,640]{3,2,1,0:T(8,128)(2,1)S(1)}, bf16[2,2,64,640]{3,2,1,0:T(8,128)(2,1)S(1)}, u32[]{:S(2)}, u32[]{:S(2)}) collective-permute-start(bf16[2,2,64,640]{3,2,1,0:T(8,128)(2,1)S(1)} %pad_maximum_fusion.6.refs_2_), channel_id=1, source_target_pairs={{0,1},{1,0},{2,3},{3,2},{4,5},{5,4},{6,7},{7,6},{8,9},{9,8},{10,11... | collective-permute-start | bytes 983048 | tf_op jit(solution)/shard_map/ppermute | solution.py:31
  131.5 23.5 %collective-permute-start.38 = (bf16[2,2,2,40,2048]{4,3,2,1,0:T(8,128)(2,1)S(1)}, bf16[2,2,2,40,2048]{4,3,2,1,0:T(8,128)(2,1)S(1)}, u32[]{:S(2)}, u32[]{:S(2)}) collective-permute-start(bf16[2,2,2,40,2048]{4,3,2,1,0:T(8,128)(2,1)S(1)} %get-tuple-element.144), channel_id=1, source_target_pairs={{0,1},{1,0},{2,3},{3,2},{4,5},{5,4},{6,7},{7,6},{8,9},{9,8},{10,11... | collective-permute-start | bytes 3932168 | tf_op jit(solution)/shard_map/ppermute | solution.py:31
  131.9 23.0 %collective-permute-start.39 = (bf16[2,2,2,40,2048]{4,3,2,1,0:T(8,128)(2,1)S(1)}, bf16[2,2,2,40,2048]{4,3,2,1,0:T(8,128)(2,1)S(1)}, u32[]{:S(2)}, u32[]{:S(2)}) collective-permute-start(bf16[2,2,2,40,2048]{4,3,2,1,0:T(8,128)(2,1)S(1)} %get-tuple-element.145), channel_id=1, source_target_pairs={{0,1},{1,0},{2,3},{3,2},{4,5},{5,4},{6,7},{7,6},{8,9},{9,8},{10,11... | collective-permute-start | bytes 3932168 | tf_op jit(solution)/shard_map/ppermute | solution.py:31
  132.1 15.9 %collective-permute-start.36 = (bf16[2,2,64,640]{3,2,1,0:T(8,128)(2,1)S(1)}, bf16[2,2,64,640]{3,2,1,0:T(8,128)(2,1)S(1)}, u32[]{:S(2)}, u32[]{:S(2)}) collective-permute-start(bf16[2,2,64,640]{3,2,1,0:T(8,128)(2,1)S(1)} %fusion.10), channel_id=1, source_target_pairs={{0,4},{1,5},{2,6},{3,7},{4,0},{5,1},{6,2},{7,3},{8,12},{9,13},{10,... | collective-permute-start | bytes 983048 | tf_op jit(solution)/shard_map/ppermute | solution.py:31
  132.5 14.1 %collective-permute-start.37 = (bf16[2,2,64,640]{3,2,1,0:T(8,128)(2,1)S(1)}, bf16[2,2,64,640]{3,2,1,0:T(8,128)(2,1)S(1)}, u32[]{:S(2)}, u32[]{:S(2)}) collective-permute-start(bf16[2,2,64,640]{3,2,1,0:T(8,128)(2,1)S(1)} %fusion.11), channel_id=1, source_target_pairs={{0,2},{1,3},{2,0},{3,1},{4,6},{5,7},{6,4},{7,5},{8,10},{9,11},{10,... | collective-permute-start | bytes 983048 | tf_op jit(solution)/shard_map/ppermute | solution.py:31
  151.6 53.3 %collective-permute-start.62 = (bf16[64,640]{1,0:T(8,128)(2,1)S(1)}, bf16[64,640]{1,0:T(8,128)(2,1)S(1)}, u32[]{:S(2)}, u32[]{:S(2)}) collective-permute-start(bf16[64,640]{1,0:T(8,128)(2,1)S(1)} %get-tuple-element.281), channel_id=1, source_target_pairs={{0,24},{1,25},{2,26},{3,27},{4,28},{5,29},{6,30},{7,31},{8,0},{9,1... | collective-permute-start | bytes 245768 | tf_op jit(solution)/shard_map/ppermute | solution.py:31
  152.2 53.2 %collective-permute-start.61 = (bf16[64,640]{1,0:T(8,128)(2,1)S(1)}, bf16[64,640]{1,0:T(8,128)(2,1)S(1)}, u32[]{:S(2)}, u32[]{:S(2)}) collective-permute-start(bf16[64,640]{1,0:T(8,128)(2,1)S(1)} %get-tuple-element.280), channel_id=1, source_target_pairs={{0,16},{1,17},{2,18},{3,19},{4,20},{5,21},{6,22},{7,23},{8,24},{9,... | collective-permute-start | bytes 245768 | tf_op jit(solution)/shard_map/ppermute | solution.py:31
  155.1 14.1 %collective-permute-start.43 = (bf16[2,2,40,2048]{3,2,1,0:T(8,128)(2,1)S(1)}, bf16[2,2,40,2048]{3,2,1,0:T(8,128)(2,1)S(1)}, u32[]{:S(2)}, u32[]{:S(2)}) collective-permute-start(bf16[2,2,40,2048]{3,2,1,0:T(8,128)(2,1)S(1)} %fusion.1), channel_id=1, source_target_pairs={{0,2},{1,3},{2,0},{3,1},{4,6},{5,7},{6,4},{7,5},{8,10},{9,11},{10,... | collective-permute-start | bytes 1966088 | tf_op jit(solution)/shard_map/ppermute | solution.py:31
  164.1 13.8 %collective-permute-start.42 = (bf16[2,2,40,2048]{3,2,1,0:T(8,128)(2,1)S(1)}, bf16[2,2,40,2048]{3,2,1,0:T(8,128)(2,1)S(1)}, u32[]{:S(2)}, u32[]{:S(2)}) collective-permute-start(bf16[2,2,40,2048]{3,2,1,0:T(8,128)(2,1)S(1)} %fusion), channel_id=1, source_target_pairs={{0,4},{1,5},{2,6},{3,7},{4,0},{5,1},{6,2},{7,3},{8,12},{9,13},{10,... | collective-permute-start | bytes 1966088 | tf_op jit(solution)/shard_map/ppermute | solution.py:31
  169.6 15.3 %collective-permute-start.47 = (bf16[2,40,2048]{2,1,0:T(8,128)(2,1)S(1)}, bf16[2,40,2048]{2,1,0:T(8,128)(2,1)S(1)}, u32[]{:S(2)}, u32[]{:S(2)}) collective-permute-start(bf16[2,40,2048]{2,1,0:T(8,128)(2,1)S(1)} %fusion.13), channel_id=1, source_target_pairs={{0,4},{1,5},{2,6},{3,7},{4,0},{5,1},{6,2},{7,3},{8,12},{9,13},{10,... | collective-permute-start | bytes 983048 | tf_op jit(solution)/shard_map/ppermute | solution.py:31
  185.0 13.2 %collective-permute-start.58 = (bf16[40,2048]{1,0:T(8,128)(2,1)S(1)}, bf16[40,2048]{1,0:T(8,128)(2,1)S(1)}, u32[]{:S(2)}, u32[]{:S(2)}) collective-permute-start(bf16[40,2048]{1,0:T(8,128)(2,1)S(1)} %get-tuple-element.265), channel_id=1, source_target_pairs={{0,24},{1,25},{2,26},{3,27},{4,28},{5,29},{6,30},{7,31},{8,0},{9,1... | collective-permute-start | bytes 491528 | tf_op jit(solution)/shard_map/ppermute | solution.py:31
  186.2 14.1 %collective-permute-start.57 = (bf16[40,2048]{1,0:T(8,128)(2,1)S(1)}, bf16[40,2048]{1,0:T(8,128)(2,1)S(1)}, u32[]{:S(2)}, u32[]{:S(2)}) collective-permute-start(bf16[40,2048]{1,0:T(8,128)(2,1)S(1)} %get-tuple-element.264), channel_id=1, source_target_pairs={{0,16},{1,17},{2,18},{3,19},{4,20},{5,21},{6,22},{7,23},{8,24},{9,... | collective-permute-start | bytes 491528 | tf_op jit(solution)/shard_map/ppermute | solution.py:31
  187.5 17.2 %collective-permute-start.56 = (bf16[40,2048]{1,0:T(8,128)(2,1)S(1)}, bf16[40,2048]{1,0:T(8,128)(2,1)S(1)}, u32[]{:S(2)}, u32[]{:S(2)}) collective-permute-start(bf16[40,2048]{1,0:T(8,128)(2,1)S(1)} %fusion.27), channel_id=1, source_target_pairs={{0,8},{1,9},{2,10},{3,11},{4,12},{5,13},{6,14},{7,15},{8,16},{9,17... | collective-permute-start | bytes 491528 | tf_op jit(solution)/shard_map/ppermute | solution.py:31
  218.7 11.1 %collective-permute-start.49 = (bf16[2,40,1408]{2,1,0:T(8,128)(2,1)S(1)}, bf16[2,40,1408]{2,1,0:T(8,128)(2,1)S(1)}, u32[]{:S(2)}, u32[]{:S(2)}) collective-permute-start(bf16[2,40,1408]{2,1,0:T(8,128)(2,1)S(1)} %fusion.17), channel_id=1, source_target_pairs={{0,2},{1,3},{2,0},{3,1},{4,6},{5,7},{6,4},{7,5},{8,10},{9,11},{10,... | collective-permute-start | bytes 675848 | tf_op jit(solution)/shard_map/ppermute | solution.py:31
  224.0 11.2 %collective-permute-start.54 = (bf16[40,1408]{1,0:T(8,128)(2,1)S(1)}, bf16[40,1408]{1,0:T(8,128)(2,1)S(1)}, u32[]{:S(2)}, u32[]{:S(2)}) collective-permute-start(bf16[40,1408]{1,0:T(8,128)(2,1)S(1)} %get-tuple-element.273), channel_id=1, source_target_pairs={{0,24},{1,25},{2,26},{3,27},{4,28},{5,29},{6,30},{7,31},{8,0},{9,1... | collective-permute-start | bytes 337928 | tf_op jit(solution)/shard_map/ppermute | solution.py:31
  (59 other events, 426.5 us)

commit v3 on v2

--- a/solution.py
+++ b/solution.py
@@ -3,6 +3,7 @@
 import numpy as np
 from jax import lax
 from jax.experimental import pallas as pl
+from jax.experimental.layout import Layout, with_layout_constraint
 from jax.experimental.pallas import tpu as pltpu
 from jax.sharding import PartitionSpec as P
 
@@ -28,7 +29,8 @@
 
 
 def shift(values, axis, amount):
-    return lax.ppermute(values, "dp", shift_perm(axis, amount))
+    with jax.named_scope("zyxc"[axis] + str(amount % DIMS[axis])):
+        return lax.ppermute(values, "dp", shift_perm(axis, amount))
 
 
 def own_coords():
@@ -92,6 +94,8 @@
     )
 
 
+BYTES = 1e6
+COST = 1.0
 HALF = 1024 // 2
 SCALE = 256 ** (-0.5)
 KEY_SPANS = ((0, 128), (0, 256), (0, 384), (128, 512))
@@ -128,10 +132,17 @@
 
 
 def chunks(count, size, body, carry):
+    for low in range(0, count, size):
+        carry = body(slice(low, low + size), carry)
+    return carry
+
+
+def looped(count, size, body, unroll):
     def step(index, carried):
-        return body(pl.ds(pl.multiple_of(index * size, size), size), carried)
-
-    return lax.fori_loop(0, count // size, step, carry)
+        body(pl.ds(pl.multiple_of(index * size, size), size))
+        return carried
+
+    lax.fori_loop(0, count // size, step, 0, unroll=unroll)
 
 
 def group_rows(piece_ref, low, high):
@@ -158,10 +169,18 @@
                     yield far, group, one, two, 2 * chip_at(coords_ref, gap_of(group, one, two)) + core
 
 
+def place_rows(out_ref, piece_refs, low, high):
+    for group in range(4):
+        for one in range(2):
+            for two in range(2):
+                row = 160 * group + 80 * one + 40 * two
+                out_ref[row : row + 40, :] = piece_refs[group][one, two, :, low:high]
+
+
 def project_forward(coords_ref, index_ref, tokens_ref, *refs):
     piece_refs, refs = refs[:8], refs[8:]
     (
-        h1_ref, q_ref, kv_ref, qn_ref, kn_ref, vb_ref, wo_ref, gains_ref, perm_ref, plain_ref
+        h1_ref, q_ref, kv_ref, qn_ref, kn_ref, vb_ref, wo_ref, gains_ref, perm_ref, own_ref, far_ref, plain_ref
     ) = refs
     for far, group, one, two, place in slots(coords_ref):
         wo_ref[place] = piece_refs[4 * far + group][one, two, 0:32, 768:1408]
@@ -175,7 +194,7 @@
     core = coords_ref[3]
 
     def make_perm(rows, carry):
-        place = lax.broadcasted_iota(jnp.int32, (64, 1024), 0) + rows.start
+        place = lax.broadcasted_iota(jnp.int32, (64, 640), 0) + rows.start
         perm_ref[rows, :] = jnp.where(place == index_ref[...], 1.0, 0.0).astype(BF)
         return carry
 
@@ -189,15 +208,11 @@
 
     chunks(512, 32, norm_in, 0)
     h1_ref[...] = dot(plain_ref[...], perm_ref[...]).astype(BF)
-    for far in range(2):
+    for far, weight_ref in enumerate((own_ref, far_ref)):
+        place_rows(weight_ref, piece_refs[4 * far : 4 * far + 4], 0, 768)
         side = lax.rem(core + far, 2)
         for part in range(3):
-            total = jnp.zeros((512, 256), jnp.float32)
-            for group in range(4):
-                total = total + dot(
-                    h1_ref[:, 256 * group : 256 * group + 160],
-                    group_rows(piece_refs[4 * far + group], 256 * part, 256 * part + 256),
-                )
+            total = dot(h1_ref[...], weight_ref[:, 256 * part : 256 * part + 256])
             if part < 2:
                 q_ref[2 * side + part] = total
             else:
@@ -218,7 +233,7 @@
 
 def attention_forward(
     coords_ref, tokens_ref, segrow_ref, segcol_ref, qn_ref, kn_ref, vb_ref, wo_ref, gains_ref, perm_ref,
-    prob_ref, o_ref, branch_ref, mid_ref, h3_ref, plain_ref, bias_ref,
+    prob_ref, o_ref, branch_ref, mid_ref, h3_ref, plain_ref, bias_ref, score_ref,
 ):
     for block, (low, high) in enumerate(KEY_SPANS):
         rows, span = slice(128 * block, 128 * block + 128), high - low
@@ -226,12 +241,19 @@
         key_at = lax.broadcasted_iota(jnp.int32, (128, span), 1) + low
         allowed = (segcol_ref[rows, :] == segrow_ref[:, low:high]) & (key_at <= row_at)
         bias_ref[:, 0:span] = jnp.where(allowed, 0.0, -1e30)
-        for head in range(4):
-            scores = dot_right_t(qn_ref[head, rows, :], kn_ref[low:high, :]) * SCALE + bias_ref[:, 0:span]
+        score_ref[:, 0:span] = dot_right_t(qn_ref[:, rows, :].reshape(512, 256), kn_ref[low:high, :])
+
+        def soften(part, carry, block=block, span=span):
+            near = slice(part.start % 128, part.start % 128 + 32)
+            scores = score_ref[part, 0:span] * SCALE + bias_ref[near, 0:span]
             powers = jnp.exp(scores - jnp.max(scores, axis=-1, keepdims=True))
-            weights = (powers * (1.0 / jnp.sum(powers, axis=-1, keepdims=True))).astype(BF)
-            prob_ref[block, 128 * head : 128 * head + 128, 0:span] = weights
-            o_ref[head, rows, :] = dot(weights, vb_ref[low:high, :]).astype(BF)
+            inverse = 1.0 / jnp.sum(powers, axis=-1, keepdims=True)
+            prob_ref[block, part, 0:span] = (powers * inverse).astype(BF)
+            return carry
+
+        chunks(512, 32, soften, 0)
+        mixed = dot(prob_ref[block, :, 0:span], vb_ref[low:high, :])
+        o_ref[:, rows, :] = mixed.astype(BF).reshape(4, 128, 256)
     total = jnp.zeros((512, 640), jnp.float32)
     for head in range(4):
         total = total + dot(o_ref[head], wo_ref[8 * head : 8 * head + 8].reshape(256, 640))
@@ -249,23 +271,25 @@
     h3_ref[...] = dot(plain_ref[...], perm_ref[...]).astype(BF)
 
 
-def gateup_forward(coords_ref, h3_ref, *refs):
-    piece_refs, (slope_ref, gelu_ref, hidden_ref, both_ref) = refs[:8], refs[8:]
-    core = coords_ref[3]
+def gateup_own(coords_ref, h3_ref, *refs):
+    piece_refs, (own_ref, weight_ref) = refs[:4], refs[4:]
+    place_rows(weight_ref, piece_refs, 0, 2048)
     for block in range(4):
         low = 512 * block
-        for far in range(2):
-            side = lax.rem(core + far, 2)
-            total = jnp.zeros((512, 512), jnp.float32)
-            for group in range(4):
-                total = total + dot(
-                    h3_ref[:, 256 * group : 256 * group + 160],
-                    group_rows(piece_refs[4 * far + group], low, low + 512),
-                )
-            both_ref[side] = total
-
-        def activate(rows, carry, low=low):
-            gate, up = both_ref[0, rows, :], both_ref[1, rows, :]
+        own_ref[:, low : low + 512] = dot(h3_ref[...], weight_ref[:, low : low + 512])
+
+
+def gateup_forward(coords_ref, h3_ref, own_ref, *refs):
+    piece_refs, (slope_ref, gelu_ref, hidden_ref, weight_ref, far_ref) = refs[:4], refs[4:]
+    core = coords_ref[3]
+    place_rows(weight_ref, piece_refs, 0, 2048)
+    for block in range(4):
+        low = 512 * block
+        far_ref[...] = dot(h3_ref[...], weight_ref[:, low : low + 512])
+
+        def activate(rows, low=low):
+            own, far = own_ref[rows, low : low + 512], far_ref[rows, :]
+            gate, up = jnp.where(core == 0, own, far), jnp.where(core == 0, far, own)
             square = gate * gate
             bend = jnp.tanh(gate * (TANH_SLOPE + (TANH_SLOPE * TANH_CUBE) * square))
             weight = 0.5 + 0.5 * bend
@@ -276,15 +300,14 @@
             slope_ref[rows, low : low + 512] = (slope * up).astype(BF)
             gelu_ref[rows, low : low + 512] = gelu.astype(BF)
             hidden_ref[rows, low : low + 512] = (gelu * up).astype(BF)
-            return carry
-
-        chunks(512, 16, activate, 0)
+
+        looped(512, 16, activate, 4)
 
 
 def down_both(coords_ref, hidden_ref, mid_ref, cot_ref, gains_ref, *refs):
     piece_refs, refs = refs[:8], refs[8:]
     (result_ref, dm_ref, gain_ref, wd_ref), refs = refs[:4], refs[4:]
-    out_refs, (product_ref, natural_ref) = refs[:4], refs[4:]
+    out_refs, (product_ref, natural_ref) = refs[:2], refs[2:]
     for far, group, one, two, place in slots(coords_ref):
         wd_ref[place] = piece_refs[4 * far + group][one, two]
     total = jnp.zeros((512, 640), jnp.float32)
@@ -309,16 +332,16 @@
         grad = dot_left_t(hidden_ref[:, 256 * block : 256 * block + 256], dm_ref[...])
         natural_ref[4 * block : 4 * block + 4] = grad.astype(BF).reshape(4, 64, 640)
     for far, group, one, two, place in slots(coords_ref):
-        out_refs[2 * far + group // 2][group % 2, one, two] = natural_ref[place]
+        out_refs[far][group, one, two] = natural_ref[place]
 
 
 def gateup_backward(coords_ref, dm_ref, wd_ref, slope_ref, gelu_ref, h3_ref, *refs):
-    dgu_ref, out_refs, (dhid_ref, h3t_ref) = refs[0], refs[1:5], refs[5:]
+    dgu_ref, out_refs, (dhid_ref, h3t_ref) = refs[0], refs[1:3], refs[3:]
     for block in range(4):
         low = 512 * block
         dhid_ref[...] = dot_right_t(dm_ref[...], wd_ref[8 * block : 8 * block + 8].reshape(512, 640))
 
-        def spread(rows, carry, low=low):
+        def spread(rows, low=low):
             grad = dhid_ref[rows, :]
             dgu_ref[0, rows, low : low + 512] = (
                 grad * slope_ref[rows, low : low + 512].astype(jnp.float32)
@@ -326,11 +349,9 @@
             dgu_ref[1, rows, low : low + 512] = (
                 grad * gelu_ref[rows, low : low + 512].astype(jnp.float32)
             ).astype(BF)
-            return carry
-
-        chunks(512, 16, spread, 0)
-    for group in range(4):
-        h3t_ref[160 * group : 160 * group + 160, :] = h3_ref[:, 256 * group : 256 * group + 160].T
+
+        looped(512, 16, spread, 4)
+    h3t_ref[...] = h3_ref[...].T
     for far in (1, 0):
         side = lax.rem(coords_ref[3] + far, 2)
         for block in range(4):
@@ -338,33 +359,22 @@
             grad = dot(h3t_ref[...], dgu_ref[side, :, low : low + 512]).astype(BF)
             for spot in range(16):
                 group, one, two = spot // 4, (spot // 2) % 2, spot % 2
-                out_refs[2 * far + group // 2][group % 2, one, two, :, low : low + 512] = grad[
+                out_refs[far][group, one, two, :, low : low + 512] = grad[
                     40 * spot : 40 * spot + 40
                 ]
 
 
-def to_plain(rel_ref, perm_ref, out_ref):
-    high = rel_ref[...].astype(BF)
-    low = (rel_ref[...] - high.astype(jnp.float32)).astype(BF)
-    out_ref[...] = dot_right_t(high, perm_ref[...]) + dot_right_t(low, perm_ref[...])
-
-
 def middle_backward(
-    coords_ref, dgu_ref, mid_ref, branch_ref, cot_ref, gains_ref, perm_ref, *refs
+    coords_ref, dgu_ref, mid_ref, branch_ref, cot_ref, gains_ref, perm_ref, own_ref, far_ref,
+    dmid_ref, da_ref, gain_ref, rel_ref, plain_ref,
 ):
-    piece_refs, refs = refs[:8], refs[8:]
-    dmid_ref, da_ref, gain_ref, rel_ref, plain_ref = refs
     core = coords_ref[3]
-    rel_ref[...] = jnp.zeros_like(rel_ref)
-    for group in range(4):
-        total = jnp.zeros((512, 160), jnp.float32)
-        for far in range(2):
-            side = lax.rem(core + far, 2)
-            total = total + dot_right_t(
-                dgu_ref[side], group_rows(piece_refs[4 * far + group], 0, 2048)
-            )
-        rel_ref[:, 256 * group : 256 * group + 160] = total
-    to_plain(rel_ref, perm_ref, plain_ref)
+    for low in (0, 256):
+        rows = slice(low, low + 256)
+        total = dot_right_t(dgu_ref[core, rows, :], own_ref[...])
+        total = total + dot_right_t(dgu_ref[1 - core, rows, :], far_ref[...])
+        rel_ref[rows, :] = total.astype(BF)
+    plain_ref[...] = dot_right_t(rel_ref[...], perm_ref[...])
     gain_one, gain_two = 1.0 + gains_ref[1:2, :], 1.0 + gains_ref[2:3, :]
 
     def pull(rows, carry):
@@ -381,7 +391,7 @@
 
 def attention_backward(
     coords_ref, da_ref, wo_ref, o_ref, prob_ref, qn_ref, kn_ref, vb_ref, q_ref, kv_ref, gains_ref,
-    dqkv_ref, gain_ref, dwo_ref, do_ref, dqn_ref, dkn_ref, dv_ref, ds_ref,
+    dqkv_ref, gain_ref, dwo_ref, do_ref, dqn_ref, dkn_ref, dv_ref, ds_ref, lifted_ref,
 ):
     for head in range(4):
         block = wo_ref[8 * head : 8 * head + 8].reshape(256, 640)
@@ -392,14 +402,21 @@
     dv_ref[...] = jnp.zeros_like(dv_ref)
     for block, (low, high) in enumerate(KEY_SPANS):
         rows, span = slice(128 * block, 128 * block + 128), high - low
-        for head in range(4):
-            grad = do_ref[head, rows, :]
+        lifted_ref[:, 0:span] = dot_right_t(do_ref[:, rows, :].reshape(512, 256), vb_ref[low:high, :])
+
+        def soften(part, carry, block=block, span=span):
+            head, near = part.start // 128, 128 * block + part.start % 128
+            near = slice(near, near + 32)
             delta = jnp.sum(
-                grad.astype(jnp.float32) * o_ref[head, rows, :].astype(jnp.float32), axis=-1, keepdims=True
+                do_ref[head, near, :].astype(jnp.float32) * o_ref[head, near, :].astype(jnp.float32),
+                axis=-1,
+                keepdims=True,
             )
-            soft = prob_ref[block, 128 * head : 128 * head + 128, 0:span].astype(jnp.float32)
-            lifted = dot_right_t(grad, vb_ref[low:high, :])
-            ds_ref[128 * head : 128 * head + 128, 0:span] = (soft * (lifted - delta) * SCALE).astype(BF)
+            soft = prob_ref[block, part, 0:span].astype(jnp.float32)
+            ds_ref[part, 0:span] = (soft * (lifted_ref[part, 0:span] - delta) * SCALE).astype(BF)
+            return carry
+
+        chunks(512, 32, soften, 0)
         all_ds = ds_ref[:, 0:span]
         all_rows = qn_ref[:, rows, :].reshape(512, 256)
         dqn_ref[:, rows, :] = dot(all_ds, kn_ref[low:high, :]).reshape(4, 128, 256)
@@ -426,22 +443,14 @@
 
 def input_backward(
     coords_ref, dqkv_ref, h1_ref, dwo_ref, tokens_ref, dmid_ref, perm_ref, gains_ref, gain_mid_ref,
-    gain_head_ref, gain_down_ref, *refs
+    gain_head_ref, gain_down_ref, own_ref, far_ref, input_ref, *refs
 ):
-    piece_refs, refs = refs[:8], refs[8:]
-    (input_ref, *out_refs), (rel_ref, plain_ref, h1t_ref) = refs[:5], refs[5:]
+    out_refs, (rel_ref, plain_ref, h1t_ref) = refs[:2], refs[2:]
     core = coords_ref[3]
-    rel_ref[...] = jnp.zeros_like(rel_ref)
-    for group in range(4):
-        total = jnp.zeros((512, 160), jnp.float32)
-        for far in range(2):
-            side = lax.rem(core + far, 2)
-            total = total + dot_right_t(
-                dqkv_ref[side], group_rows(piece_refs[4 * far + group], 0, 768)
-            )
-        rel_ref[:, 256 * group : 256 * group + 160] = total
-        h1t_ref[160 * group : 160 * group + 160, :] = h1_ref[:, 256 * group : 256 * group + 160].T
-    to_plain(rel_ref, perm_ref, plain_ref)
+    total = dot_right_t(dqkv_ref[core], own_ref[...]) + dot_right_t(dqkv_ref[1 - core], far_ref[...])
+    rel_ref[...] = total.astype(BF)
+    h1t_ref[...] = h1_ref[...].T
+    plain_ref[...] = dot_right_t(rel_ref[...], perm_ref[...])
     gain_zero = 1.0 + gains_ref[0:1, :]
 
     def pull(rows, carry):
@@ -458,9 +467,8 @@
     lines.append(jnp.zeros((2, 640), jnp.float32))
     gain_block = jnp.concatenate(lines, axis=0).astype(BF)
     for far, group, one, two, place in slots(coords_ref):
-        out = out_refs[2 * far + group // 2]
-        out[group % 2, one, two, 0:32, 768:1408] = dwo_ref[place]
-        out[group % 2, one, two, 32:40, 768:1408] = gain_block
+        out_refs[far][group, one, two, 0:32, 768:1408] = dwo_ref[place]
+        out_refs[far][group, one, two, 32:40, 768:1408] = gain_block
     for far in range(2):
         side = lax.rem(core + far, 2)
         for part in range(3):
@@ -468,7 +476,7 @@
             grad = dot(h1t_ref[...], dqkv_ref[side, :, low : low + 256]).astype(BF)
             for spot in range(16):
                 group, one, two = spot // 4, (spot // 2) % 2, spot % 2
-                out_refs[2 * far + group // 2][group % 2, one, two, :, low : low + 256] = grad[
+                out_refs[far][group, one, two, :, low : low + 256] = grad[
                     40 * spot : 40 * spot + 40
                 ]
 
@@ -482,14 +490,14 @@
         out_specs=jax.tree.map(lambda _: whole, outs),
         scratch_shapes=list(scratch),
         cost_estimate=pl.CostEstimate(
-            flops=int(cost[0] * 1e9), bytes_accessed=int(cost[1] * 1e6), transcendentals=0
+            flops=int(cost[0] * COST * 1e9), bytes_accessed=int(cost[1] * BYTES), transcendentals=0
         ),
         compiler_params=pltpu.CompilerParams(vmem_limit_bytes=megabytes * 1024 * 1024),
     )(coords, *inputs)
 
 
 def rel_table():
-    table = np.full((32, 1, 1024), -1, np.int32)
+    table = np.zeros((32, 1, 640), np.int32)
     for place in range(32):
         z, y, x, _ = np.unravel_index(place, DIMS)
         for group in range(4):
@@ -497,7 +505,7 @@
                 for two in range(2):
                     gap = gap_of(group, one, two)
                     chip = (((z + gap[0]) % 4) * 2 + (y + gap[1]) % 2) * 2 + (x + gap[2]) % 2
-                    low = 256 * group + 80 * one + 40 * two
+                    low = 160 * group + 80 * one + 40 * two
                     table[place, 0, low : low + 40] = 40 * chip + np.arange(40)
     return table
 
@@ -506,31 +514,33 @@
     return jax.ShapeDtypeStruct(sizes, kind)
 
 
-def scatter_core(keep_a, keep_b, send_a, send_b):
-    return keep_a, keep_b, shift(send_a, 3, 1), shift(send_b, 3, 1)
-
-
-def scatter_across(keep_a, keep_b, got_a, got_b):
-    far_a = shift((wide(keep_a[1]) + wide(got_a[1])).astype(BF), 1, 1)
-    far_b = shift((wide(keep_b[1]) + wide(got_b[1])).astype(BF), 2, 1)
-    return keep_a[0], keep_b[0], got_a[0], got_b[0], far_a, far_b
-
-
-def scatter_pair(keep_a, keep_b, got_a, got_b, far_a, far_b):
-    sum_a = wide(keep_a) + wide(got_a) + wide(far_a)
-    sum_b = wide(keep_b) + wide(got_b) + wide(far_b)
-    return sum_a[0], sum_b[0], shift(sum_a[1].astype(BF), 2, 1), shift(sum_b[1].astype(BF), 1, 1)
+def join(*values):
+    return lax.optimization_barrier(values)
+
+
+def narrow(left, right):
+    return (wide(left) + wide(right)).astype(BF)
+
+
+def scatter_across(keep, got):
+    return shift(narrow(keep[1], got[1]), 1, 1), shift(narrow(keep[3], got[3]), 2, 1)
+
+
+def scatter_sums(keep, got, far_a, far_b):
+    sum_a = wide(keep[0]) + wide(got[0]) + wide(far_a)
+    sum_b = wide(keep[2]) + wide(got[2]) + wide(far_b)
+    return sum_a[0], sum_b[0], sum_a[1].astype(BF), sum_b[1].astype(BF)
+
+
+def scatter_pair(keep, got, far_a, far_b):
+    first, second, side_a, side_b = scatter_sums(keep, got, far_a, far_b)
+    return first, second, shift(side_a, 2, 1), shift(side_b, 1, 1)
 
 
 def scatter_along(sum_a, sum_b, side_a, side_b):
     last_a = sum_a + wide(side_a)
     last_b = sum_b + wide(side_b)
-    return (
-        last_a[0],
-        shift(last_a[1].astype(BF), 0, 1),
-        shift(last_b[0].astype(BF), 0, 2),
-        shift(last_b[1].astype(BF), 0, 3),
-    )
+    return last_a[0], [last_a[1].astype(BF), last_b[0].astype(BF), last_b[1].astype(BF)]
 
 
 def scatter_end(own, *others):
@@ -539,7 +549,7 @@
     return own
 
 
-def block_fast(tokens, segment_ids, cotangent, weights):
+def block_fast(tokens, segment_ids, cotangent, weights, update_gateup):
     query_round, keyval_round, output_round, gateup_round, down_round, gains, heads = weights
     f32 = jnp.float32
     along, upward, sideways, core = own_coords()
@@ -560,117 +570,152 @@
     block_a = jnp.concatenate([both[:, :768], jnp.concatenate([output_round, spread], axis=0)], axis=1)
     block_g = both[:, 768:]
 
-    near_w = gather_along(down_round)
     near_a = gather_along(block_a)
+    near_a, block_w, block_g = join(near_a, down_round, block_g)
+    first, second = jnp.stack([near_a[0], near_a[1]]), jnp.stack([near_a[2], near_a[3]])
+    first, second, block_w, block_g = join(first, second, block_w, block_g)
+    pairs_a = [jnp.stack([first, shift(first, 2, 1)]), jnp.stack([second, shift(second, 1, 1)])]
+    near_w = gather_along(block_w)
+    pairs_a, near_w, block_g = join(pairs_a, near_w, block_g)
+    mine_a = gather_across(*pairs_a)
+    near_g = gather_along(block_g)
     pairs_w = gather_pair(near_w)
-    mine_w = gather_across(*pairs_w)
-    pieces_w = gather_core(mine_w)
-    near_g = gather_along(after(block_g, *near_a))
-    pairs_a = gather_pair(after(near_a, *pairs_w))
-    mine_a = gather_across(*pairs_a)
+    mine_a, near_g = join(mine_a, near_g)
     pieces_a = gather_core(mine_a)
-    pairs_g = gather_pair(after(near_g, *pairs_a))
-    mine_g = gather_across(*after(pairs_g, *mine_a))
-    pieces_g = gather_core(mine_g)
-
-    h1, q, kv, qn, kn, vb, wo, gains_full, perm = call(
+    pairs_g = gather_pair(near_g)
+    pairs_g, pairs_w = join(pairs_g, pairs_w)
+    mine_g = gather_across(*pairs_g)
+    early_g = [shift(pair, 3, 1) for pair in pairs_g]
+    h1, q, kv, qn, kn, vb, wo, gains_full, perm, own_qkv, far_qkv = call(
         project_forward,
         coords,
-        [index, tokens, *after(pieces_a, *pairs_g)],
+        [index, tokens, *pieces_a],
         [
-            shape(512, 1024), shape(4, 512, 256, kind=f32), shape(2, 512, 256, kind=f32),
+            shape(512, 640), shape(4, 512, 256, kind=f32), shape(2, 512, 256, kind=f32),
             shape(4, 512, 256), shape(512, 256), shape(512, 256),
-            shape(32, 32, 640), shape(8, 640, kind=f32), shape(640, 1024),
+            shape(32, 32, 640), shape(8, 640, kind=f32), shape(640, 640), shape(640, 768), shape(640, 768),
         ],
         [pltpu.VMEM((512, 640), BF)],
         12,
         (5, 20),
     )
+    qn, pairs_w = join(qn, pairs_w)
+    mine_w = gather_across(*pairs_w)
+    early_w = [shift(pair, 3, 1) for pair in pairs_w]
     prob, o, branch, mid, h3 = call(
         attention_forward,
         coords,
         [tokens, segment_ids, segcol, qn, kn, vb, wo, gains_full, perm],
         [
             shape(4, 512, 384), shape(4, 512, 256), shape(512, 640, kind=f32),
-            shape(512, 640, kind=f32), shape(512, 1024),
+            shape(512, 640, kind=f32), shape(512, 640),
         ],
-        [pltpu.VMEM((512, 640), BF), pltpu.VMEM((128, 384), f32)],
+        [pltpu.VMEM((512, 640), BF), pltpu.VMEM((128, 384), f32), pltpu.VMEM((512, 384), f32)],
         12,
         (5, 20),
     )
-    slope, gelu, hidden = call(
+    mine_g, h3, early_g = join(mine_g, h3, early_g)
+    far_g = [early_g[0], shift(mine_g[1], 3, 1), early_g[1], shift(mine_g[3], 3, 1)]
+    own, own_gu = call(
+        gateup_own,
+        coords,
+        [h3, *mine_g],
+        [shape(512, 2048, kind=f32), shape(640, 2048)],
+        [],
+        12,
+        (6, 20),
+    )
+    far_g, own = join(far_g, own)
+    slope, gelu, hidden, far_gu = call(
         gateup_forward,
         coords,
-        [h3, *pieces_g],
-        [shape(512, 2048)] * 3,
-        [pltpu.VMEM((2, 512, 512), f32)],
+        [h3, own, *far_g],
+        [shape(512, 2048)] * 3 + [shape(640, 2048)],
+        [pltpu.VMEM((512, 512), f32)],
         12,
         (6, 20),
     )
-    result, dm, gain_down, wd, *parts_w = call(
+    hidden, mine_w = join(hidden, mine_w)
+    pieces_w = mine_w + [early_w[0], shift(mine_w[1], 3, 1), early_w[1], shift(mine_w[3], 3, 1)]
+    result, dm, gain_down, wd, keep_w, send_w = call(
         down_both,
         coords,
         [hidden, mid, cotangent, gains_full, *pieces_w],
         [shape(512, 640), shape(512, 640), shape(8, 640, kind=f32), shape(32, 64, 640)]
-        + [shape(2, 2, 2, 64, 640)] * 4,
+        + [shape(4, 2, 2, 64, 640)] * 2,
         [pltpu.VMEM((512, 640), f32), pltpu.VMEM((32, 64, 640), BF)],
         12,
         (6, 20),
     )
-    dgu, *parts_g = call(
+    got_w = shift(send_w, 3, 1)
+    dgu, keep_g, send_g = call(
         gateup_backward,
         coords,
         [dm, wd, slope, gelu, h3],
-        [shape(2, 512, 2048)] + [shape(2, 2, 2, 40, 2048)] * 4,
+        [shape(2, 512, 2048)] + [shape(4, 2, 2, 40, 2048)] * 2,
         [pltpu.VMEM((512, 512), f32), pltpu.VMEM((640, 512), BF)],
         12,
         (8, 20),
     )
-    got_w = scatter_core(*parts_w)
+    dgu, got_w, send_g = join(dgu, got_w, send_g)
+    far_w = scatter_across(keep_w, got_w)
+    got_g = shift(send_g, 3, 1)
     dmid, da, gain_mid = call(
         middle_backward,
         coords,
-        [after(dgu, *got_w), mid, branch, cotangent, gains_full, perm, *pieces_g],
+        [dgu, mid, branch, cotangent, gains_full, perm, own_gu, far_gu],
         [shape(512, 640, kind=f32), shape(512, 640), shape(2, 8, 640, kind=f32)],
-        [pltpu.VMEM((512, 1024), f32), pltpu.VMEM((512, 640), f32)],
+        [pltpu.VMEM((512, 640), BF), pltpu.VMEM((512, 640), f32)],
         12,
         (8, 20),
     )
-    far_w = scatter_across(*got_w)
-    got_g = scatter_core(*parts_g)
+    da, got_g, far_w = join(da, got_g, far_w)
+    side_w = scatter_pair(keep_w, got_w, *far_w)
+    far_g = scatter_across(keep_g, got_g)
     dqkv, gain_head, dwo = call(
         attention_backward,
         coords,
-        [after(da, *far_w, *got_g), wo, o, prob, qn, kn, vb, q, kv, gains_full],
+        [da, wo, o, prob, qn, kn, vb, q, kv, gains_full],
         [shape(2, 512, 768), shape(2, 8, 256, kind=f32), shape(32, 32, 640)],
         [
             pltpu.VMEM((4, 512, 256), BF),
             pltpu.VMEM((4, 512, 256), f32), pltpu.VMEM((512, 256), f32), pltpu.VMEM((512, 256), f32),
-            pltpu.VMEM((512, 384), BF),
+            pltpu.VMEM((512, 384), BF), pltpu.VMEM((512, 384), f32),
         ],
         12,
         (6, 20),
     )
-    side_w = scatter_pair(*far_w)
-    far_g = scatter_across(*got_g)
-    input_grad, *parts_a = call(
+    dqkv, side_w = join(dqkv, side_w)
+    own_w, along_w = scatter_along(*side_w)
+    along_w = [shift(part, 0, step + 1) for step, part in enumerate(along_w)]
+    input_grad, keep_a, send_a = call(
         input_backward,
         coords,
-        [after(dqkv, *side_w), h1, dwo, tokens, dmid, perm, gains_full, gain_mid, gain_head, gain_down, *pieces_a],
-        [shape(512, 640, kind=f32)] + [shape(2, 2, 2, 40, 1408)] * 4,
-        [pltpu.VMEM((512, 1024), f32), pltpu.VMEM((512, 640), f32), pltpu.VMEM((640, 512), BF)],
+        [dqkv, h1, dwo, tokens, dmid, perm, gains_full, gain_mid, gain_head, gain_down, own_qkv, far_qkv],
+        [shape(512, 640, kind=f32)] + [shape(4, 2, 2, 40, 1408)] * 2,
+        [pltpu.VMEM((512, 640), BF), pltpu.VMEM((512, 640), f32), pltpu.VMEM((640, 512), BF)],
         12,
         (6, 20),
     )
-    down_grad = scatter_end(*scatter_along(*side_w))
-    side_g = scatter_pair(*far_g)
-    got_a = scatter_core(*after(parts_a, *far_g))
-    far_a = scatter_across(*after(got_a, *side_g))
-    gateup_sum = scatter_end(*scatter_along(*side_g))
-    rest = scatter_end(*scatter_along(*scatter_pair(*far_a)))
-    output_grad = rest[:32, 768:]
-    norm_grad = lax.dynamic_slice(rest[32:36, 768:], (0, place * 20), (4, 20))
-    qknorm_grad = lax.dynamic_slice(rest[36:38, 768:], (0, place * 8), (2, 8))
+    send_a, far_g, along_w = join(send_a, far_g, along_w)
+    down_grad = scatter_end(own_w, *along_w)
+    got_a = shift(send_a, 3, 1)
+    side_g = scatter_pair(keep_g, got_g, *far_g)
+    got_a, side_g = join(got_a, side_g)
+    first, second = narrow(keep_a[1], got_a[1]), narrow(keep_a[3], got_a[3])
+    first, second, side_g = join(first, second, side_g)
+    far_a = shift(first, 1, 1), shift(second, 2, 1)
+    own_g, along_g = scatter_along(*side_g)
+    ends_g = [shift(along_g[0], 0, 1), shift(along_g[2], 0, 3)]
+    far_a, ends_g, across_g = join(far_a, ends_g, along_g[1])
+    first, second, *side_a = scatter_sums(keep_a, got_a, *far_a)
+    side_a, across_g = join(side_a, across_g)
+    side_a = shift(side_a[0], 2, 1), shift(side_a[1], 1, 1)
+    across_g = shift(across_g, 0, 2)
+    side_a, across_g = join(side_a, across_g)
+    own_a, along_a = scatter_along(first, second, *side_a)
+    along_a = [shift(part, 0, step + 1) for step, part in enumerate(along_a)]
+    gateup_sum = scatter_end(own_g, across_g, *ends_g)
 
     def own_rows(both):
         away, keep = swap_halves(core, both[:20], both[20:])
@@ -678,12 +723,19 @@
         return jnp.where(core == 0, keep, got), jnp.where(core == 0, got, keep)
 
     low, high = own_rows(gateup_sum)
-    gateup_grad = jnp.stack([low, high], axis=1)
+    gateup_grad = with_layout_constraint(jnp.stack([low, high], axis=1), Layout((0, 1, 2)))
+    gateup_done = (gateup_grad, *update_gateup(gateup_grad))
+    along_a, gateup_done = join(along_a, gateup_done)
+    rest = scatter_end(own_a, *along_a)
+    output_grad = rest[:32, 768:]
+    norm_grad = lax.dynamic_slice(rest[32:36, 768:], (0, place * 20), (4, 20))
+    qknorm_grad = lax.dynamic_slice(rest[36:38, 768:], (0, place * 8), (2, 8))
+
     low, high = own_rows(rest[:, :768])
     query_grad = jnp.concatenate([low[:, :512], high[:, :512]], axis=1)
     keyval_grad = jnp.concatenate([low[:, 512:], high[:, 512:]], axis=1)
-    grads = (query_grad, keyval_grad, output_grad, gateup_grad, down_grad, norm_grad, qknorm_grad)
-    return result[None], input_grad[None], grads
+    grads = (query_grad, keyval_grad, output_grad, gateup_done[0], down_grad, norm_grad, qknorm_grad)
+    return result[None], input_grad[None], grads, gateup_done[1:]
 
 
 def norm_apply(values, gain_vector):
@@ -772,7 +824,7 @@
     return (parameter_new, first_new, second_new)
 
 
-def block_plain(tokens, segment_ids, cotangent, weights):
+def block_plain(tokens, segment_ids, cotangent, weights, update_gateup):
     query_full, keyval_full, output_full, gateup_full, down_full, main_gains, head_gains = gather_plain(*weights)
     seq_count, length, model_width = tokens.shape
     row_count = seq_count * length
@@ -873,7 +925,7 @@
     )
     result_out = result.reshape(seq_count, length, model_width)
     input_out = input_grad.reshape(seq_count, length, model_width)
-    return result_out, input_out, gradients
+    return result_out, input_out, gradients, update_gateup(gradients[3])
 
 
 def per_device(
@@ -912,8 +964,14 @@
     weights = (
         query_round, keyval_round, output_round, gateup_round, down_round, gains_round, headgain_round
     )
+
+    def update_gateup(gradient):
+        return adam_update(gateup_weight, gradient, gateup_mean, gateup_square, decay_coef)
+
     block = block_fast if lax.axis_size("dp") == 32 else block_plain
-    result_out, input_out, gradients = block(tokens, segment_ids, cotangent, weights)
+    result_out, input_out, gradients, gateup_done = block(
+        tokens, segment_ids, cotangent, weights, update_gateup
+    )
     parameters = (
         query_weight,
         keyval_weight,
@@ -938,6 +996,8 @@
         adam_update(
             parameters[place], gradients[place], firsts[place], seconds[place], decays[place]
         )
+        if place != 3
+        else gateup_done
         for place in range(7)
     ]
     news = tuple((update[0] for update in updates))

time: 249 us -> 200 us (0.80)
  Pallas kernels: 76.7 us -> 49.2 us
  starting transfers between devices: 71.6 us -> 58.4 us
  local copies, waits for them, and re-layouts: 10.2 us -> 4.38 us
  waiting for transfers between devices: 74.3 us -> 71.8 us
    pallas_call x8 -> x9, Pallas kernels: 76.7 us -> 49.2 us  [call(): pl.pallas_call(kernel, out_shape=outs, in_specs=[pl.BlockSpec(memory_spac...]
    ppermute x63 -> x60, starting transfers between devices: 71.6 us -> 58.4 us  [shift(): return lax.ppermute(values, 'dp', shift_perm(axis, amount))]
    unnamed x61 -> x53, local copies, waits for them, and re-layouts: 8.05 us -> 1.78 us
    ppermute x63 -> x60, waiting for transfers between devices: 74.3 us -> 71.8 us  [shift(): return lax.ppermute(values, 'dp', shift_perm(axis, amount))]
  transfers between devices with their start and end apart: 63 -> 60, of which waited for: 18 -> 23; matrix products, arithmetic and copies ran while one was open for 6% -> 5% of each run, Pallas kernels for 27% -> 21%
where the time goes in v3:
time: 200 us; the launch traced here: 197 us
  waiting for transfers between devices  71.8 us (36%)
  starting transfers between devices  58.4 us (29%)
  Pallas kernels  49.2 us (25%)
  other arithmetic  11.8 us (6%)
  local copies, waits for them, and re-layouts  4.38 us (2%)
    ppermute x60, waiting for transfers between devices, shift(): return lax.ppermute(values, 'dp', shift_perm(axis, amount))  71.8 us
    ppermute x60, starting transfers between devices, shift(): return lax.ppermute(values, 'dp', shift_perm(axis, amount))  58.4 us
    pallas_call x9, Pallas kernels, call(): pl.pallas_call(kernel, out_shape=outs, in_specs=[pl.BlockSpec(memory_spac...  49.2 us
    sub x7, other arithmetic, adam_update(): parameter - learn_rate * first_hat / (jnp.sqrt(second_hat) + adam_epsilon)  6.71 us
  transfers between devices with their start and end apart: 60, of which 23 were waited for; matrix products, arithmetic and copies ran while one was open for 5% of the time, Pallas kernels for 21%

profile of v3, /device:TPU:1, one launch (start us, length us, event | category | flops | bytes accessed | tf_op | source)
XLA Modules:
  0.0 197.4 jit_solution(8908509918853622368)
XLA Ops:
  5.3 2.6 %collective-permute-start.3 = (bf16[40,1408]{1,0:T(8,128)(2,1)S(1)}, bf16[40,1408]{1,0:T(8,128)(2,1)S(1)}, u32[]{:S(2)}, u32[]{:S(2)}) collective-permute-start(bf16[40,1408]{1,0:T(8,128)(2,1)S(1)} %fusion.30), channel_id=1, source_target_pairs={{0,8},{1,9},{2,10},{3,11},{4,12},{5,13},{6,14},{7,15},{8,16},{9,17... | collective-permute-start | bytes 337928 | tf_op jit(solution)/shard_map/z1/ppermute | solution.py:33
  7.9 2.3 %collective-permute-start.2 = (bf16[40,1408]{1,0:T(8,128)(2,1)S(1)}, bf16[40,1408]{1,0:T(8,128)(2,1)S(1)}, u32[]{:S(2)}, u32[]{:S(2)}) collective-permute-start(bf16[40,1408]{1,0:T(8,128)(2,1)S(1)} %fusion.30), channel_id=1, source_target_pairs={{0,16},{1,17},{2,18},{3,19},{4,20},{5,21},{6,22},{7,23},{8,24},{9,... | collective-permute-start | bytes 337928 | tf_op jit(solution)/shard_map/z2/ppermute | solution.py:33
  11.3 2.0 collective-permute-done.3
  13.3 5.0 %collective-permute-done.2 = bf16[40,1408]{1,0:T(8,128)(2,1)S(1)} collective-permute-done((bf16[40,1408]{1,0:T(8,128)(2,1)S(1)}, bf16[40,1408]{1,0:T(8,128)(2,1)S(1)}, u32[]{:S(2)}, u32[]{:S(2)}) %collective-permute-start.2) | collective-permute-done | bytes 112672 | tf_op jit(solution)/shard_map/z2/ppermute | solution.py:33
  19.6 2.7 %collective-permute-start.8 = (bf16[64,640]{1,0:T(8,128)(2,1)S(1)}, bf16[64,640]{1,0:T(8,128)(2,1)S(1)}, u32[]{:S(2)}, u32[]{:S(2)}) collective-permute-start(bf16[64,640]{1,0:T(8,128)(2,1)S(1)} %convert_element_type.282), channel_id=1, source_target_pairs={{0,8},{1,9},{2,10},{3,11},{4,12},{5,13},{6,14},{7,15},{8,16},{9,17... | collective-permute-start | bytes 245768 | tf_op jit(solution)/shard_map/z1/ppermute | solution.py:33
  25.7 4.4 %collective-permute-done.5 = bf16[2,40,1408]{2,1,0:T(8,128)(2,1)S(1)} collective-permute-done((bf16[2,40,1408]{2,1,0:T(8,128)(2,1)S(1)}, bf16[2,40,1408]{2,1,0:T(8,128)(2,1)S(1)}, u32[]{:S(2)}, u32[]{:S(2)}) %collective-permute-start.5) | collective-permute-done | bytes 225312 | tf_op jit(solution)/shard_map/y1/ppermute | solution.py:33
  35.7 2.6 %collective-permute-start.11 = (bf16[40,2048]{1,0:T(8,128)(2,1)S(1)}, bf16[40,2048]{1,0:T(8,128)(2,1)S(1)}, u32[]{:S(2)}, u32[]{:S(2)}) collective-permute-start(bf16[40,2048]{1,0:T(8,128)(2,1)S(1)} %pad_maximum_fusion.11), channel_id=1, source_target_pairs={{0,24},{1,25},{2,26},{3,27},{4,28},{5,29},{6,30},{7,31},{8,0},{9,1... | collective-permute-start | bytes 491528 | tf_op jit(solution)/shard_map/z3/ppermute | solution.py:33
  40.3 8.6 %collective-permute-done.12 = bf16[40,2048]{1,0:T(8,128)(2,1)S(1)} collective-permute-done((bf16[40,2048]{1,0:T(8,128)(2,1)S(1)}, bf16[40,2048]{1,0:T(8,128)(2,1)S(1)}, u32[]{:S(2)}, u32[]{:S(2)}) %collective-permute-start.12) | collective-permute-done | bytes 163872 | tf_op jit(solution)/shard_map/z2/ppermute | solution.py:33
  51.9 5.8 %collective-permute-done.14 = bf16[2,40,2048]{2,1,0:T(8,128)(2,1)S(1)} collective-permute-done((bf16[2,40,2048]{2,1,0:T(8,128)(2,1)S(1)}, bf16[2,40,2048]{2,1,0:T(8,128)(2,1)S(1)}, u32[]{:S(2)}, u32[]{:S(2)}) %collective-permute-start.14) | collective-permute-done | bytes 327712 | tf_op jit(solution)/shard_map/x1/ppermute | solution.py:33
  61.4 3.7 %shard_map.472 = (bf16[512,640]{1,0:T(8,128)(2,1)S(1)}, f32[4,512,256]{2,1,0:T(8,128)S(1)}, f32[2,512,256]{2,1,0:T(8,128)S(1)}, bf16[4,512,256]{2,1,0:T(8,128)(2...) custom-call(s32[4]{0:T(128)S(1)} %pad_add_fusion.coords_ref, ...), custom_call_target="tpu_custom_call" | custom-call | flops 5000000000 | bytes 20000000 | tf_op jit(solution)/shard_map/pallas_call | solution.py:486
  65.2 5.0 %shard_map.473 = (bf16[4,512,384]{2,1,0:T(8,128)(2,1)S(1)}, bf16[4,512,256]{2,1,0:T(8,128)(2,1)S(1)}, f32[512,640]{1,0:T(8,128)S(1)}, f32[512,640]{1,0:T(8,128)S(1)}, bf16[512,640]{1,0:T(8,128)(2,1)S(1)}) custom-call(s32[4]{0:T(128)S(1)} %pad_add_fusion.coords_ref, bf16[512,640]{1,0:T(8,128)(2,1)S(1)} %bitcast.146, s32[1,512]{1,0:T(1,128)S(1)} %copy-done, ...), custom_call_target="tpu_custom_call" | custom-call | flops 5000000000 | bytes 20000000 | tf_op jit(solution)/shard_map/pallas_call | solution.py:486
  70.2 5.6 %collective-permute-done.18.refs_1_ = bf16[2,2,40,2048]{3,2,1,0:T(8,128)(2,1)S(1)} collective-permute-done((bf16[2,2,40,2048]{3,2,1,0:T(8,128)(2,1)S(1)}, bf16[2,2,40,2048]{3,2,1,0:T(8,128)(2,1)S(1)}, u32[]{:S(2)}, u32[]{:S(2)}) %collective-permute-start.18) | collective-permute-done | bytes 655392 | tf_op jit(solution)/shard_map/y1/ppermute | solution.py:33
  79.6 2.3 %shard_map.474 = (f32[512,2048]{1,0:T(8,128)S(1)}, bf16[640,2048]{1,0:T(8,128)(2,1)S(1)}) custom-call(s32[4]{0:T(128)S(1)} %pad_add_fusion.coords_ref, bf16[512,640]{1,0:T(8,128)(2,1)S(1)} %get-tuple-element.203.h3_ref, bf16[2,2,40,2048]{3,2,1,0:T(8,128)(2,1)S(1)} %pad_maximum_fusion.refs_0_, bf16[2,2,40,2048]{3,2,1,0:T(8,128)(2,1)S(1)} %collective-permute-done.18.refs_1_, ...), custom_call_target="tpu_custom_call" | custom-call | flops 6000000000 | bytes 20000000 | tf_op jit(solution)/shard_map/pallas_call | solution.py:486
  83.1 6.4 %shard_map.475 = (bf16[512,2048]{1,0:T(8,128)(2,1)S(1)}, bf16[512,2048]{1,0:T(8,128)(2,1)S(1)}, bf16[512,2048]{1,0:T(8,128)(2,1)S(1)}, bf16[640,2048]{1,0:T(8,128)(2,1)S(1)}) custom-call(s32[4]{0:T(128)S(1)} %pad_add_fusion.coords_ref, bf16[512,640]{1,0:T(8,128)(2,1)S(1)} %get-tuple-element.203.h3_ref, f32[512,2048]{1,0:T(8,128)S(1)} %get-tuple-element.211.own_ref, ...), custom_call_target="tpu_custom_call" | custom-call | flops 6000000000 | bytes 20000000 | tf_op jit(solution)/shard_map/pallas_call | solution.py:486
  93.8 7.1 %shard_map.476 = (bf16[512,640]{1,0:T(8,128)(2,1)}, bf16[512,640]{1,0:T(8,128)(2,1)S(1)}, f32[8,640]{1,0:T(8,128)S(1)}, bf16[32,64,640]{2,1,0:T(8,128)(2,1)S(1)}...) custom-call(s32[4]{0:T(128)S(1)} %pad_add_fusion.coords_ref, ...), custom_call_target="tpu_custom_call" | custom-call | flops 6000000000 | bytes 20000000 | tf_op jit(solution)/shard_map/pallas_call | solution.py:486
  101.4 7.1 %shard_map.477 = (bf16[2,512,2048]{2,1,0:T(8,128)(2,1)S(1)}, bf16[4,2,2,40,2048]{4,3,2,1,0:T(8,128)(2,1)S(1)}, bf16[4,2,2,40,2048]{4,3,2,1,0:T(8,128)(2,1)S(1)}) custom-call(s32[4]{0:T(128)S(1)} %pad_add_fusion.coords_ref, bf16[512,640]{1,0:T(8,128)(2,1)S(1)} %get-tuple-element.226.dm_ref, bf16[32,64,640]{2,1,0:T(8,128)(2,1)S(1)} %get-tuple-element.227.wd_ref, ...), custom_call_target="tpu_custom_call" | custom-call | flops 8000000000 | bytes 20000000 | tf_op jit(solution)/shard_map/pallas_call | solution.py:486
  110.1 5.5 %shard_map.478 = (f32[512,640]{1,0:T(8,128)S(1)}, bf16[512,640]{1,0:T(8,128)(2,1)S(1)}, f32[2,8,640]{2,1,0:T(8,128)S(1)}) custom-call(s32[4]{0:T(128)S(1)} %pad_add_fusion.coords_ref, bf16[2,512,2048]{2,1,0:T(8,128)(2,1)S(1)} %get-tuple-element.233.dgu_ref, f32[512,640]{1,0:T(8,128)S(1)} %get-tuple-element.220.mid_ref, ...), custom_call_target="tpu_custom_call" | custom-call | flops 8000000000 | bytes 20000000 | tf_op jit(solution)/shard_map/pallas_call | solution.py:486
  115.6 2.1 %collective-permute-done.37 = bf16[2,2,64,640]{3,2,1,0:T(8,128)(2,1)S(1)} collective-permute-done((bf16[2,2,64,640]{3,2,1,0:T(8,128)(2,1)S(1)}, bf16[2,2,64,640]{3,2,1,0:T(8,128)(2,1)S(1)}, u32[]{:S(2)}, u32[]{:S(2)}) %collective-permute-start.37) | collective-permute-done | bytes 327712 | tf_op jit(solution)/shard_map/x1/ppermute | solution.py:33
  122.4 7.4 %shard_map.479 = (bf16[2,512,768]{2,1,0:T(8,128)(2,1)S(1)}, f32[2,8,256]{2,1,0:T(8,128)S(1)}, bf16[32,32,640]{2,1,0:T(8,128)(2,1)S(1)}) custom-call(s32[4]{0:T(128)S(1)} %pad_add_fusion.coords_ref, bf16[512,640]{1,0:T(8,128)(2,1)S(1)} %get-tuple-element.241.da_ref, bf16[32,32,640]{2,1,0:T(8,128)(2,1)S(1)} %get-tuple-element.199.wo_ref, ...), custom_call_target="tpu_custom_call" | custom-call | flops 6000000000 | bytes 20000000 | tf_op jit(solution)/shard_map/pallas_call | solution.py:486
  129.9 1.9 collective-permute-start.44
  131.8 3.2 %collective-permute-start.43 = (bf16[64,640]{1,0:T(8,128)(2,1)S(1)}, bf16[64,640]{1,0:T(8,128)(2,1)S(1)}, u32[]{:S(2)}, u32[]{:S(2)}) collective-permute-start(bf16[64,640]{1,0:T(8,128)(2,1)S(1)} %get-tuple-element.359), channel_id=1, source_target_pairs={{0,16},{1,17},{2,18},{3,19},{4,20},{5,21},{6,22},{7,23},{8,24},{9,... | collective-permute-start | bytes 245768 | tf_op jit(solution)/shard_map/z2/ppermute | solution.py:33
  135.0 4.6 %shard_map.480 = (f32[512,640]{1,0:T(8,128)}, bf16[4,2,2,40,1408]{4,3,2,1,0:T(8,128)(2,1)S(1)}, bf16[4,2,2,40,1408]{4,3,2,1,0:T(8,128)(2,1)S(1)}) custom-call(s32[4]{0:T(128)S(1)} %pad_add_fusion.coords_ref, bf16[2,512,768]{2,1,0:T(8,128)(2,1)S(1)} %get-tuple-element.249.dqkv_ref, bf16[512,640]{1,0:T(8,128)(2,1)S(1)} %get-tuple-element.250.h1_ref, ...), custom_call_target="tpu_custom_call" | custom-call | flops 6000000000 | bytes 20000000 | tf_op jit(solution)/shard_map/pallas_call | solution.py:486
  140.4 4.1 %collective-permute-start.45 = (bf16[4,2,2,40,1408]{4,3,2,1,0:T(8,128)(2,1)S(1)}, bf16[4,2,2,40,1408]{4,3,2,1,0:T(8,128)(2,1)S(1)}, u32[]{:S(2)}, u32[]{:S(2)}) collective-permute-start(bf16[4,2,2,40,1408]{4,3,2,1,0:T(8,128)(2,1)S(1)} %get-tuple-element.267), channel_id=1, source_target_pairs={{0,1},{1,0},{2,3},{3,2},{4,5},{5,4},{6,7},{7,6},{8,9},{9,8},{10,11... | collective-permute-start | bytes 5406728 | tf_op jit(solution)/shard_map/c1/ppermute | solution.py:33
  146.1 8.6 %collective-permute-done.46 = bf16[2,40,2048]{2,1,0:T(8,128)(2,1)S(1)} collective-permute-done((bf16[2,40,2048]{2,1,0:T(8,128)(2,1)S(1)}, bf16[2,40,2048]{2,1,0:T(8,128)(2,1)S(1)}, u32[]{:S(2)}, u32[]{:S(2)}) %collective-permute-start.46) | collective-permute-done | bytes 327712 | tf_op jit(solution)/shard_map/x1/ppermute | solution.py:33
  155.1 2.1 %collective-permute-start.51 = (bf16[40,2048]{1,0:T(8,128)(2,1)S(1)}, bf16[40,2048]{1,0:T(8,128)(2,1)S(1)}, u32[]{:S(2)}, u32[]{:S(2)}) collective-permute-start(bf16[40,2048]{1,0:T(8,128)(2,1)S(1)} %get-tuple-element.347), channel_id=1, source_target_pairs={{0,24},{1,25},{2,26},{3,27},{4,28},{5,29},{6,30},{7,31},{8,0},{9,1... | collective-permute-start | bytes 491528 | tf_op jit(solution)/shard_map/z3/ppermute | solution.py:33
  159.7 4.8 %collective-permute-done.50 = bf16[40,2048]{1,0:T(8,128)(2,1)S(1)} collective-permute-done((bf16[40,2048]{1,0:T(8,128)(2,1)S(1)}, bf16[40,2048]{1,0:T(8,128)(2,1)S(1)}, u32[]{:S(2)}, u32[]{:S(2)}) %collective-permute-start.50) | collective-permute-done | bytes 163872 | tf_op jit(solution)/shard_map/z1/ppermute | solution.py:33
  164.6 3.0 %collective-permute-done.48 = bf16[2,2,40,1408]{3,2,1,0:T(8,128)(2,1)S(1)} collective-permute-done((bf16[2,2,40,1408]{3,2,1,0:T(8,128)(2,1)S(1)}, bf16[2,2,40,1408]{3,2,1,0:T(8,128)(2,1)S(1)}, u32[]{:S(2)}, u32[]{:S(2)}) %collective-permute-start.48) | collective-permute-done | bytes 450592 | tf_op jit(solution)/shard_map/y1/ppermute | solution.py:33
  171.3 5.2 %collective-permute-done.54 = bf16[40,2048]{1,0:T(8,128)(2,1)S(1)} collective-permute-done((bf16[40,2048]{1,0:T(8,128)(2,1)S(1)}, bf16[40,2048]{1,0:T(8,128)(2,1)S(1)}, u32[]{:S(2)}, u32[]{:S(2)}) %collective-permute-start.54) | collective-permute-done | bytes 163872 | tf_op jit(solution)/shard_map/z2/ppermute | solution.py:33
  176.8 1.8 collective-permute-start.58
  179.0 3.0 %collective-permute-start.57 = (bf16[40,1408]{1,0:T(8,128)(2,1)S(1)}, bf16[40,1408]{1,0:T(8,128)(2,1)S(1)}, u32[]{:S(2)}, u32[]{:S(2)}) collective-permute-start(bf16[40,1408]{1,0:T(8,128)(2,1)S(1)} %get-tuple-element.354), channel_id=1, source_target_pairs={{0,24},{1,25},{2,26},{3,27},{4,28},{5,29},{6,30},{7,31},{8,0},{9,1... | collective-permute-start | bytes 337928 | tf_op jit(solution)/shard_map/z3/ppermute | solution.py:33
  182.8 2.3 %multiply_subtract_fusion = (f32[20,2,2048]{2,1,0:T(2,128)}, f32[20,2,2048]{2,1,0:T(2,128)}, f32[20,2,2048]{2,1,0:T(2,128)}, f32[20,2,2048]{2,1,0:T(2,128)}) fusion(f32[20,2,2048]{2,1,0:T(2,128)S(1)} %copy-done.5, f32[20,1,2048]{2,1,0:T(1,128)S(1)} %stack.174, f32[20,1,2048]{2,1,0:T(1,128)S(1)} %copy.59, f32[20,2,2048]{2,1,0:T(2,128)S(1)} %copy-done.8, ...), kind=kLoop, calls=%fused_computation.54 | loop fusion | flops 1228800 | bytes 2621440 | tf_op jit(solution)/shard_map/sub | solution.py:820
  186.9 5.9 %collective-permute-done.56 = bf16[40,1408]{1,0:T(8,128)(2,1)S(1)} collective-permute-done((bf16[40,1408]{1,0:T(8,128)(2,1)S(1)}, bf16[40,1408]{1,0:T(8,128)(2,1)S(1)}, u32[]{:S(2)}, u32[]{:S(2)}) %collective-permute-start.56) | collective-permute-done | bytes 112672 | tf_op jit(solution)/shard_map/z2/ppermute | solution.py:33
  (229 shorter events, 56.8 us)
Async XLA Ops:
  7.9 10.4 %collective-permute-start.2 = (bf16[40,1408]{1,0:T(8,128)(2,1)S(1)}, bf16[40,1408]{1,0:T(8,128)(2,1)S(1)}, u32[]{:S(2)}, u32[]{:S(2)}) collective-permute-start(bf16[40,1408]{1,0:T(8,128)(2,1)S(1)} %fusion.30), channel_id=1, source_target_pairs={{0,16},{1,17},{2,18},{3,19},{4,20},{5,21},{6,22},{7,23},{8,24},{9,... | collective-permute-start | bytes 337928 | tf_op jit(solution)/shard_map/z2/ppermute | solution.py:33
  19.6 10.5 %collective-permute-start.8 = (bf16[64,640]{1,0:T(8,128)(2,1)S(1)}, bf16[64,640]{1,0:T(8,128)(2,1)S(1)}, u32[]{:S(2)}, u32[]{:S(2)}) collective-permute-start(bf16[64,640]{1,0:T(8,128)(2,1)S(1)} %convert_element_type.282), channel_id=1, source_target_pairs={{0,8},{1,9},{2,10},{3,11},{4,12},{5,13},{6,14},{7,15},{8,16},{9,17... | collective-permute-start | bytes 245768 | tf_op jit(solution)/shard_map/z1/ppermute | solution.py:33
  30.6 18.3 %collective-permute-start.9 = (bf16[2,2,40,1408]{3,2,1,0:T(8,128)(2,1)S(1)}, bf16[2,2,40,1408]{3,2,1,0:T(8,128)(2,1)S(1)}, u32[]{:S(2)}, u32[]{:S(2)}) collective-permute-start(bf16[2,2,40,1408]{3,2,1,0:T(8,128)(2,1)S(1)} %pad_maximum_fusion.2.refs_0_), channel_id=1, source_target_pairs={{0,4},{1,5},{2,6},{3,7},{4,0},{5,1},{6,2},{7,3},{8,12},{9,13},{10,... | collective-permute-start | bytes 1351688 | tf_op jit(solution)/shard_map/y1/ppermute | solution.py:33
  31.8 17.1 %collective-permute-start.10 = (bf16[2,2,40,1408]{3,2,1,0:T(8,128)(2,1)S(1)}, bf16[2,2,40,1408]{3,2,1,0:T(8,128)(2,1)S(1)}, u32[]{:S(2)}, u32[]{:S(2)}) collective-permute-start(bf16[2,2,40,1408]{3,2,1,0:T(8,128)(2,1)S(1)} %pad_maximum_fusion.3.refs_2_), channel_id=1, source_target_pairs={{0,2},{1,3},{2,0},{3,1},{4,6},{5,7},{6,4},{7,5},{8,10},{9,11},{10,... | collective-permute-start | bytes 1351688 | tf_op jit(solution)/shard_map/x1/ppermute | solution.py:33
  35.7 13.2 %collective-permute-start.12 = (bf16[40,2048]{1,0:T(8,128)(2,1)S(1)}, bf16[40,2048]{1,0:T(8,128)(2,1)S(1)}, u32[]{:S(2)}, u32[]{:S(2)}) collective-permute-start(bf16[40,2048]{1,0:T(8,128)(2,1)S(1)} %pad_maximum_fusion.11), channel_id=1, source_target_pairs={{0,16},{1,17},{2,18},{3,19},{4,20},{5,21},{6,22},{7,23},{8,24},{9,... | collective-permute-start | bytes 491528 | tf_op jit(solution)/shard_map/z2/ppermute | solution.py:33
  35.7 13.2 %collective-permute-start.11 = (bf16[40,2048]{1,0:T(8,128)(2,1)S(1)}, bf16[40,2048]{1,0:T(8,128)(2,1)S(1)}, u32[]{:S(2)}, u32[]{:S(2)}) collective-permute-start(bf16[40,2048]{1,0:T(8,128)(2,1)S(1)} %pad_maximum_fusion.11), channel_id=1, source_target_pairs={{0,24},{1,25},{2,26},{3,27},{4,28},{5,29},{6,30},{7,31},{8,0},{9,1... | collective-permute-start | bytes 491528 | tf_op jit(solution)/shard_map/z3/ppermute | solution.py:33
  40.1 9.5 %collective-permute-start.17 = (bf16[2,64,640]{2,1,0:T(8,128)(2,1)S(1)}, bf16[2,64,640]{2,1,0:T(8,128)(2,1)S(1)}, u32[]{:S(2)}, u32[]{:S(2)}) collective-permute-start(bf16[2,64,640]{2,1,0:T(8,128)(2,1)S(1)} %get-tuple-element.361), channel_id=1, source_target_pairs={{0,4},{1,5},{2,6},{3,7},{4,0},{5,1},{6,2},{7,3},{8,12},{9,13},{10,... | collective-permute-start | bytes 491528 | tf_op jit(solution)/shard_map/y1/ppermute | solution.py:33
  49.0 8.7 %collective-permute-start.14 = (bf16[2,40,2048]{2,1,0:T(8,128)(2,1)S(1)}, bf16[2,40,2048]{2,1,0:T(8,128)(2,1)S(1)}, u32[]{:S(2)}, u32[]{:S(2)}) collective-permute-start(bf16[2,40,2048]{2,1,0:T(8,128)(2,1)S(1)} %get-tuple-element.351), channel_id=1, source_target_pairs={{0,2},{1,3},{2,0},{3,1},{4,6},{5,7},{6,4},{7,5},{8,10},{9,11},{10,... | collective-permute-start | bytes 983048 | tf_op jit(solution)/shard_map/x1/ppermute | solution.py:33
  49.3 9.9 %collective-permute-start.15 = (bf16[2,40,2048]{2,1,0:T(8,128)(2,1)S(1)}, bf16[2,40,2048]{2,1,0:T(8,128)(2,1)S(1)}, u32[]{:S(2)}, u32[]{:S(2)}) collective-permute-start(bf16[2,40,2048]{2,1,0:T(8,128)(2,1)S(1)} %get-tuple-element.349), channel_id=1, source_target_pairs={{0,4},{1,5},{2,6},{3,7},{4,0},{5,1},{6,2},{7,3},{8,12},{9,13},{10,... | collective-permute-start | bytes 983048 | tf_op jit(solution)/shard_map/y1/ppermute | solution.py:33
  49.6 10.0 %collective-permute-start.20 = (bf16[2,2,40,1408]{3,2,1,0:T(8,128)(2,1)S(1)}, bf16[2,2,40,1408]{3,2,1,0:T(8,128)(2,1)S(1)}, u32[]{:S(2)}, u32[]{:S(2)}) collective-permute-start(bf16[2,2,40,1408]{3,2,1,0:T(8,128)(2,1)S(1)} %pad_maximum_fusion.2.refs_0_), channel_id=1, source_target_pairs={{0,1},{1,0},{2,3},{3,2},{4,5},{5,4},{6,7},{7,6},{8,9},{9,8},{10,11... | collective-permute-start | bytes 1351688 | tf_op jit(solution)/shard_map/c1/ppermute | solution.py:33
  51.4 8.9 %collective-permute-start.22 = (bf16[2,2,40,1408]{3,2,1,0:T(8,128)(2,1)S(1)}, bf16[2,2,40,1408]{3,2,1,0:T(8,128)(2,1)S(1)}, u32[]{:S(2)}, u32[]{:S(2)}) collective-permute-start(bf16[2,2,40,1408]{3,2,1,0:T(8,128)(2,1)S(1)} %pad_maximum_fusion.3.refs_2_), channel_id=1, source_target_pairs={{0,1},{1,0},{2,3},{3,2},{4,5},{5,4},{6,7},{7,6},{8,9},{9,8},{10,11... | collective-permute-start | bytes 1351688 | tf_op jit(solution)/shard_map/c1/ppermute | solution.py:33
  59.3 10.8 %collective-permute-start.24 = (bf16[2,2,40,2048]{3,2,1,0:T(8,128)(2,1)S(1)}, bf16[2,2,40,2048]{3,2,1,0:T(8,128)(2,1)S(1)}, u32[]{:S(2)}, u32[]{:S(2)}) collective-permute-start(bf16[2,2,40,2048]{3,2,1,0:T(8,128)(2,1)S(1)} %pad_maximum_fusion.refs_0_), channel_id=1, source_target_pairs={{0,1},{1,0},{2,3},{3,2},{4,5},{5,4},{6,7},{7,6},{8,9},{9,8},{10,11... | collective-permute-start | bytes 1966088 | tf_op jit(solution)/shard_map/c1/ppermute | solution.py:33
  59.7 16.1 %collective-permute-start.18 = (bf16[2,2,40,2048]{3,2,1,0:T(8,128)(2,1)S(1)}, bf16[2,2,40,2048]{3,2,1,0:T(8,128)(2,1)S(1)}, u32[]{:S(2)}, u32[]{:S(2)}) collective-permute-start(bf16[2,2,40,2048]{3,2,1,0:T(8,128)(2,1)S(1)} %pad_maximum_fusion.refs_0_), channel_id=1, source_target_pairs={{0,4},{1,5},{2,6},{3,7},{4,0},{5,1},{6,2},{7,3},{8,12},{9,13},{10,... | collective-permute-start | bytes 1966088 | tf_op jit(solution)/shard_map/y1/ppermute | solution.py:33
  59.9 15.9 %collective-permute-start.25 = (bf16[2,2,40,2048]{3,2,1,0:T(8,128)(2,1)S(1)}, bf16[2,2,40,2048]{3,2,1,0:T(8,128)(2,1)S(1)}, u32[]{:S(2)}, u32[]{:S(2)}) collective-permute-start(bf16[2,2,40,2048]{3,2,1,0:T(8,128)(2,1)S(1)} %pad_maximum_fusion.1.refs_2_), channel_id=1, source_target_pairs={{0,1},{1,0},{2,3},{3,2},{4,5},{5,4},{6,7},{7,6},{8,9},{9,8},{10,11... | collective-permute-start | bytes 1966088 | tf_op jit(solution)/shard_map/c1/ppermute | solution.py:33
  60.4 16.3 %collective-permute-start.19 = (bf16[2,2,40,2048]{3,2,1,0:T(8,128)(2,1)S(1)}, bf16[2,2,40,2048]{3,2,1,0:T(8,128)(2,1)S(1)}, u32[]{:S(2)}, u32[]{:S(2)}) collective-permute-start(bf16[2,2,40,2048]{3,2,1,0:T(8,128)(2,1)S(1)} %pad_maximum_fusion.1.refs_2_), channel_id=1, source_target_pairs={{0,2},{1,3},{2,0},{3,1},{4,6},{5,7},{6,4},{7,5},{8,10},{9,11},{10,... | collective-permute-start | bytes 1966088 | tf_op jit(solution)/shard_map/x1/ppermute | solution.py:33
  77.5 14.6 %collective-permute-start.30 = (bf16[2,2,64,640]{3,2,1,0:T(8,128)(2,1)S(1)}, bf16[2,2,64,640]{3,2,1,0:T(8,128)(2,1)S(1)}, u32[]{:S(2)}, u32[]{:S(2)}) collective-permute-start(bf16[2,2,64,640]{3,2,1,0:T(8,128)(2,1)S(1)} %pad_maximum_fusion.6.refs_0_), channel_id=1, source_target_pairs={{0,1},{1,0},{2,3},{3,2},{4,5},{5,4},{6,7},{7,6},{8,9},{9,8},{10,11... | collective-permute-start | bytes 983048 | tf_op jit(solution)/shard_map/c1/ppermute | solution.py:33
  78.0 11.5 %collective-permute-start.28 = (bf16[2,2,64,640]{3,2,1,0:T(8,128)(2,1)S(1)}, bf16[2,2,64,640]{3,2,1,0:T(8,128)(2,1)S(1)}, u32[]{:S(2)}, u32[]{:S(2)}) collective-permute-start(bf16[2,2,64,640]{3,2,1,0:T(8,128)(2,1)S(1)} %pad_maximum_fusion.6.refs_0_), channel_id=1, source_target_pairs={{0,4},{1,5},{2,6},{3,7},{4,0},{5,1},{6,2},{7,3},{8,12},{9,13},{10,... | collective-permute-start | bytes 983048 | tf_op jit(solution)/shard_map/y1/ppermute | solution.py:33
  79.3 12.8 %collective-permute-start.32 = (bf16[2,2,64,640]{3,2,1,0:T(8,128)(2,1)S(1)}, bf16[2,2,64,640]{3,2,1,0:T(8,128)(2,1)S(1)}, u32[]{:S(2)}, u32[]{:S(2)}) collective-permute-start(bf16[2,2,64,640]{3,2,1,0:T(8,128)(2,1)S(1)} %pad_maximum_fusion.7.refs_2_), channel_id=1, source_target_pairs={{0,1},{1,0},{2,3},{3,2},{4,5},{5,4},{6,7},{7,6},{8,9},{9,8},{10,11... | collective-permute-start | bytes 983048 | tf_op jit(solution)/shard_map/c1/ppermute | solution.py:33
  81.9 9.1 %collective-permute-start.29 = (bf16[2,2,64,640]{3,2,1,0:T(8,128)(2,1)S(1)}, bf16[2,2,64,640]{3,2,1,0:T(8,128)(2,1)S(1)}, u32[]{:S(2)}, u32[]{:S(2)}) collective-permute-start(bf16[2,2,64,640]{3,2,1,0:T(8,128)(2,1)S(1)} %pad_maximum_fusion.7.refs_2_), channel_id=1, source_target_pairs={{0,2},{1,3},{2,0},{3,1},{4,6},{5,7},{6,4},{7,5},{8,10},{9,11},{10,... | collective-permute-start | bytes 983048 | tf_op jit(solution)/shard_map/x1/ppermute | solution.py:33
  108.4 10.1 %collective-permute-start.35 = (bf16[4,2,2,40,2048]{4,3,2,1,0:T(8,128)(2,1)S(1)}, bf16[4,2,2,40,2048]{4,3,2,1,0:T(8,128)(2,1)S(1)}, u32[]{:S(2)}, u32[]{:S(2)}) collective-permute-start(bf16[4,2,2,40,2048]{4,3,2,1,0:T(8,128)(2,1)S(1)} %get-tuple-element.238), channel_id=1, source_target_pairs={{0,1},{1,0},{2,3},{3,2},{4,5},{5,4},{6,7},{7,6},{8,9},{9,8},{10,11... | collective-permute-start | bytes 7864328 | tf_op jit(solution)/shard_map/c1/ppermute | solution.py:33
  108.8 9.0 %collective-permute-start.37 = (bf16[2,2,64,640]{3,2,1,0:T(8,128)(2,1)S(1)}, bf16[2,2,64,640]{3,2,1,0:T(8,128)(2,1)S(1)}, u32[]{:S(2)}, u32[]{:S(2)}) collective-permute-start(bf16[2,2,64,640]{3,2,1,0:T(8,128)(2,1)S(1)} %get-tuple-element.339), channel_id=1, source_target_pairs={{0,2},{1,3},{2,0},{3,1},{4,6},{5,7},{6,4},{7,5},{8,10},{9,11},{10,... | collective-permute-start | bytes 983048 | tf_op jit(solution)/shard_map/x1/ppermute | solution.py:33
  118.9 11.0 %collective-permute-start.38 = (bf16[2,64,640]{2,1,0:T(8,128)(2,1)S(1)}, bf16[2,64,640]{2,1,0:T(8,128)(2,1)S(1)}, u32[]{:S(2)}, u32[]{:S(2)}) collective-permute-start(bf16[2,64,640]{2,1,0:T(8,128)(2,1)S(1)} %fusion.23), channel_id=1, source_target_pairs={{0,2},{1,3},{2,0},{3,1},{4,6},{5,7},{6,4},{7,5},{8,10},{9,11},{10,... | collective-permute-start | bytes 491528 | tf_op jit(solution)/shard_map/x1/ppermute | solution.py:33
  119.3 10.5 %collective-permute-start.39 = (bf16[2,64,640]{2,1,0:T(8,128)(2,1)S(1)}, bf16[2,64,640]{2,1,0:T(8,128)(2,1)S(1)}, u32[]{:S(2)}, u32[]{:S(2)}) collective-permute-start(bf16[2,64,640]{2,1,0:T(8,128)(2,1)S(1)} %fusion.24), channel_id=1, source_target_pairs={{0,4},{1,5},{2,6},{3,7},{4,0},{5,1},{6,2},{7,3},{8,12},{9,13},{10,... | collective-permute-start | bytes 491528 | tf_op jit(solution)/shard_map/y1/ppermute | solution.py:33
  120.4 20.0 %collective-permute-start.41 = (bf16[2,2,40,2048]{3,2,1,0:T(8,128)(2,1)S(1)}, bf16[2,2,40,2048]{3,2,1,0:T(8,128)(2,1)S(1)}, u32[]{:S(2)}, u32[]{:S(2)}) collective-permute-start(bf16[2,2,40,2048]{3,2,1,0:T(8,128)(2,1)S(1)} %get-tuple-element.331), channel_id=1, source_target_pairs={{0,2},{1,3},{2,0},{3,1},{4,6},{5,7},{6,4},{7,5},{8,10},{9,11},{10,... | collective-permute-start | bytes 1966088 | tf_op jit(solution)/shard_map/x1/ppermute | solution.py:33
  121.1 19.4 %collective-permute-start.40 = (bf16[2,2,40,2048]{3,2,1,0:T(8,128)(2,1)S(1)}, bf16[2,2,40,2048]{3,2,1,0:T(8,128)(2,1)S(1)}, u32[]{:S(2)}, u32[]{:S(2)}) collective-permute-start(bf16[2,2,40,2048]{3,2,1,0:T(8,128)(2,1)S(1)} %get-tuple-element.332), channel_id=1, source_target_pairs={{0,4},{1,5},{2,6},{3,7},{4,0},{5,1},{6,2},{7,3},{8,12},{9,13},{10,... | collective-permute-start | bytes 1966088 | tf_op jit(solution)/shard_map/y1/ppermute | solution.py:33
  129.9 9.8 %collective-permute-start.44 = (bf16[64,640]{1,0:T(8,128)(2,1)S(1)}, bf16[64,640]{1,0:T(8,128)(2,1)S(1)}, u32[]{:S(2)}, u32[]{:S(2)}) collective-permute-start(bf16[64,640]{1,0:T(8,128)(2,1)S(1)} %get-tuple-element.358), channel_id=1, source_target_pairs={{0,24},{1,25},{2,26},{3,27},{4,28},{5,29},{6,30},{7,31},{8,0},{9,1... | collective-permute-start | bytes 245768 | tf_op jit(solution)/shard_map/z3/ppermute | solution.py:33
  140.4 14.4 %collective-permute-start.45 = (bf16[4,2,2,40,1408]{4,3,2,1,0:T(8,128)(2,1)S(1)}, bf16[4,2,2,40,1408]{4,3,2,1,0:T(8,128)(2,1)S(1)}, u32[]{:S(2)}, u32[]{:S(2)}) collective-permute-start(bf16[4,2,2,40,1408]{4,3,2,1,0:T(8,128)(2,1)S(1)} %get-tuple-element.267), channel_id=1, source_target_pairs={{0,1},{1,0},{2,3},{3,2},{4,5},{5,4},{6,7},{7,6},{8,9},{9,8},{10,11... | collective-permute-start | bytes 5406728 | tf_op jit(solution)/shard_map/c1/ppermute | solution.py:33
  145.2 9.4 %collective-permute-start.46 = (bf16[2,40,2048]{2,1,0:T(8,128)(2,1)S(1)}, bf16[2,40,2048]{2,1,0:T(8,128)(2,1)S(1)}, u32[]{:S(2)}, u32[]{:S(2)}) collective-permute-start(bf16[2,40,2048]{2,1,0:T(8,128)(2,1)S(1)} %fusion.10), channel_id=1, source_target_pairs={{0,2},{1,3},{2,0},{3,1},{4,6},{5,7},{6,4},{7,5},{8,10},{9,11},{10,... | collective-permute-start | bytes 983048 | tf_op jit(solution)/shard_map/x1/ppermute | solution.py:33
  145.7 9.1 %collective-permute-start.47 = (bf16[2,40,2048]{2,1,0:T(8,128)(2,1)S(1)}, bf16[2,40,2048]{2,1,0:T(8,128)(2,1)S(1)}, u32[]{:S(2)}, u32[]{:S(2)}) collective-permute-start(bf16[2,40,2048]{2,1,0:T(8,128)(2,1)S(1)} %fusion.11), channel_id=1, source_target_pairs={{0,4},{1,5},{2,6},{3,7},{4,0},{5,1},{6,2},{7,3},{8,12},{9,13},{10,... | collective-permute-start | bytes 983048 | tf_op jit(solution)/shard_map/y1/ppermute | solution.py:33
  157.2 10.4 %collective-permute-start.48 = (bf16[2,2,40,1408]{3,2,1,0:T(8,128)(2,1)S(1)}, bf16[2,2,40,1408]{3,2,1,0:T(8,128)(2,1)S(1)}, u32[]{:S(2)}, u32[]{:S(2)}) collective-permute-start(bf16[2,2,40,1408]{3,2,1,0:T(8,128)(2,1)S(1)} %get-tuple-element.275), channel_id=1, source_target_pairs={{0,4},{1,5},{2,6},{3,7},{4,0},{5,1},{6,2},{7,3},{8,12},{9,13},{10,... | collective-permute-start | bytes 1351688 | tf_op jit(solution)/shard_map/y1/ppermute | solution.py:33
  157.4 10.3 %collective-permute-start.49 = (bf16[2,2,40,1408]{3,2,1,0:T(8,128)(2,1)S(1)}, bf16[2,2,40,1408]{3,2,1,0:T(8,128)(2,1)S(1)}, u32[]{:S(2)}, u32[]{:S(2)}) collective-permute-start(bf16[2,2,40,1408]{3,2,1,0:T(8,128)(2,1)S(1)} %get-tuple-element.276), channel_id=1, source_target_pairs={{0,2},{1,3},{2,0},{3,1},{4,6},{5,7},{6,4},{7,5},{8,10},{9,11},{10,... | collective-permute-start | bytes 1351688 | tf_op jit(solution)/shard_map/x1/ppermute | solution.py:33
  182.0 10.8 %collective-permute-start.56 = (bf16[40,1408]{1,0:T(8,128)(2,1)S(1)}, bf16[40,1408]{1,0:T(8,128)(2,1)S(1)}, u32[]{:S(2)}, u32[]{:S(2)}) collective-permute-start(bf16[40,1408]{1,0:T(8,128)(2,1)S(1)} %get-tuple-element.355), channel_id=1, source_target_pairs={{0,16},{1,17},{2,18},{3,19},{4,20},{5,21},{6,22},{7,23},{8,24},{9,... | collective-permute-start | bytes 337928 | tf_op jit(solution)/shard_map/z2/ppermute | solution.py:33
  (54 other events, 346.9 us)

commit v4 on v3

--- a/solution.py
+++ b/solution.py
@@ -135,14 +135,6 @@
     for low in range(0, count, size):
         carry = body(slice(low, low + size), carry)
     return carry
-
-
-def looped(count, size, body, unroll):
-    def step(index, carried):
-        body(pl.ds(pl.multiple_of(index * size, size), size))
-        return carried
-
-    lax.fori_loop(0, count // size, step, 0, unroll=unroll)
 
 
 def group_rows(piece_ref, low, high):
@@ -281,27 +273,28 @@
 
 def gateup_forward(coords_ref, h3_ref, own_ref, *refs):
     piece_refs, (slope_ref, gelu_ref, hidden_ref, weight_ref, far_ref) = refs[:4], refs[4:]
-    core = coords_ref[3]
+    first = jnp.full((16, 512), coords_ref[3]) == 0
     place_rows(weight_ref, piece_refs, 0, 2048)
     for block in range(4):
         low = 512 * block
-        far_ref[...] = dot(h3_ref[...], weight_ref[:, low : low + 512])
-
-        def activate(rows, low=low):
-            own, far = own_ref[rows, low : low + 512], far_ref[rows, :]
-            gate, up = jnp.where(core == 0, own, far), jnp.where(core == 0, far, own)
+        spot = block % 2
+        far_ref[spot] = dot(h3_ref[...], weight_ref[:, low : low + 512])
+
+        def activate(rows, low=low, spot=spot):
+            own, far = own_ref[rows, low : low + 512], far_ref[spot, rows, :]
+            gate, up = jnp.where(first, own, far), jnp.where(first, far, own)
             square = gate * gate
             bend = jnp.tanh(gate * (TANH_SLOPE + (TANH_SLOPE * TANH_CUBE) * square))
             weight = 0.5 + 0.5 * bend
+            rise = gate * (2.0 * TANH_SLOPE + (6.0 * TANH_SLOPE * TANH_CUBE) * square)
             gelu = gate * weight
-            slope = weight + (0.5 * gate) * (1.0 - bend * bend) * (
-                TANH_SLOPE + (3.0 * TANH_SLOPE * TANH_CUBE) * square
-            )
+            slope = weight + (weight * rise) * (1.0 - weight)
             slope_ref[rows, low : low + 512] = (slope * up).astype(BF)
             gelu_ref[rows, low : low + 512] = gelu.astype(BF)
             hidden_ref[rows, low : low + 512] = (gelu * up).astype(BF)
 
-        looped(512, 16, activate, 4)
+        for start in range(0, 512, 16):
+            activate(slice(start, start + 16))
 
 
 def down_both(coords_ref, hidden_ref, mid_ref, cot_ref, gains_ref, *refs):
@@ -310,13 +303,9 @@
     out_refs, (product_ref, natural_ref) = refs[:2], refs[2:]
     for far, group, one, two, place in slots(coords_ref):
         wd_ref[place] = piece_refs[4 * far + group][one, two]
-    total = jnp.zeros((512, 640), jnp.float32)
-    for block in range(8):
-        total = total + dot(
-            hidden_ref[:, 256 * block : 256 * block + 256],
-            wd_ref[4 * block : 4 * block + 4].reshape(256, 640),
-        )
-    product_ref[...] = total
+    weights = wd_ref[...].reshape(2048, 640)
+    for low in (0, 256):
+        product_ref[low : low + 256, :] = dot(hidden_ref[low : low + 256, :], weights)
     gain_three = 1.0 + gains_ref[3:4, :]
 
     def finish(rows, carry):
@@ -339,10 +328,11 @@
     dgu_ref, out_refs, (dhid_ref, h3t_ref) = refs[0], refs[1:3], refs[3:]
     for block in range(4):
         low = 512 * block
-        dhid_ref[...] = dot_right_t(dm_ref[...], wd_ref[8 * block : 8 * block + 8].reshape(512, 640))
-
-        def spread(rows, low=low):
-            grad = dhid_ref[rows, :]
+        spot = block % 2
+        dhid_ref[spot] = dot_right_t(dm_ref[...], wd_ref[8 * block : 8 * block + 8].reshape(512, 640))
+
+        def spread(rows, low=low, spot=spot):
+            grad = dhid_ref[spot, rows, :]
             dgu_ref[0, rows, low : low + 512] = (
                 grad * slope_ref[rows, low : low + 512].astype(jnp.float32)
             ).astype(BF)
@@ -350,7 +340,8 @@
                 grad * gelu_ref[rows, low : low + 512].astype(jnp.float32)
             ).astype(BF)
 
-        looped(512, 16, spread, 4)
+        for start in range(0, 512, 16):
+            spread(slice(start, start + 16))
     h3t_ref[...] = h3_ref[...].T
     for far in (1, 0):
         side = lax.rem(coords_ref[3] + far, 2)
@@ -631,9 +622,9 @@
         coords,
         [h3, own, *far_g],
         [shape(512, 2048)] * 3 + [shape(640, 2048)],
-        [pltpu.VMEM((512, 512), f32)],
+        [pltpu.VMEM((2, 512, 512), f32)],
         12,
-        (6, 20),
+        (3, 10),
     )
     hidden, mine_w = join(hidden, mine_w)
     pieces_w = mine_w + [early_w[0], shift(mine_w[1], 3, 1), early_w[1], shift(mine_w[3], 3, 1)]
@@ -653,7 +644,7 @@
         coords,
         [dm, wd, slope, gelu, h3],
         [shape(2, 512, 2048)] + [shape(4, 2, 2, 40, 2048)] * 2,
-        [pltpu.VMEM((512, 512), f32), pltpu.VMEM((640, 512), BF)],
+        [pltpu.VMEM((2, 512, 512), f32), pltpu.VMEM((640, 512), BF)],
         12,
         (8, 20),
     )

time: 200 us -> 195 us (0.975)
  Pallas kernels: 49.2 us -> 45 us
    pallas_call x9, Pallas kernels: 49.2 us -> 45 us  [call(): pl.pallas_call(kernel, out_shape=outs, in_specs=[pl.BlockSpec(memory_spac...]
  transfers between devices with their start and end apart: 60 -> 60, of which waited for: 23 -> 23; matrix products, arithmetic and copies ran while one was open for 5% -> 5% of each run, Pallas kernels for 21% -> 20%
where the time goes in v4:
time: 195 us; the launch traced here: 192 us
  waiting for transfers between devices  70.4 us (36%)
  starting transfers between devices  59.2 us (30%)
  Pallas kernels  45 us (23%)
  other arithmetic  11.9 us (6%)
  local copies, waits for them, and re-layouts  3.87 us (2%)
    ppermute x60, waiting for transfers between devices, shift(): return lax.ppermute(values, 'dp', shift_perm(axis, amount))  70.4 us
    ppermute x60, starting transfers between devices, shift(): return lax.ppermute(values, 'dp', shift_perm(axis, amount))  59.2 us
    pallas_call x9, Pallas kernels, call(): pl.pallas_call(kernel, out_shape=outs, in_specs=[pl.BlockSpec(memory_spac...  45 us
    sub x7, other arithmetic, adam_update(): parameter - learn_rate * first_hat / (jnp.sqrt(second_hat) + adam_epsilon)  6.7 us
  transfers between devices with their start and end apart: 60, of which 23 were waited for; matrix products, arithmetic and copies ran while one was open for 5% of the time, Pallas kernels for 20%

profile of v4, /device:TPU:1, one launch (start us, length us, event | category | flops | bytes accessed | tf_op | source)
XLA Modules:
  0.0 192.0 jit_solution(18166820987334750906)
XLA Ops:
  5.3 2.6 %collective-permute-start.3 = (bf16[40,1408]{1,0:T(8,128)(2,1)S(1)}, bf16[40,1408]{1,0:T(8,128)(2,1)S(1)}, u32[]{:S(2)}, u32[]{:S(2)}) collective-permute-start(bf16[40,1408]{1,0:T(8,128)(2,1)S(1)} %fusion.30), channel_id=1, source_target_pairs={{0,8},{1,9},{2,10},{3,11},{4,12},{5,13},{6,14},{7,15},{8,16},{9,17... | collective-permute-start | bytes 337928 | tf_op jit(solution)/shard_map/z1/ppermute | solution.py:33
  7.9 2.3 %collective-permute-start.2 = (bf16[40,1408]{1,0:T(8,128)(2,1)S(1)}, bf16[40,1408]{1,0:T(8,128)(2,1)S(1)}, u32[]{:S(2)}, u32[]{:S(2)}) collective-permute-start(bf16[40,1408]{1,0:T(8,128)(2,1)S(1)} %fusion.30), channel_id=1, source_target_pairs={{0,16},{1,17},{2,18},{3,19},{4,20},{5,21},{6,22},{7,23},{8,24},{9,... | collective-permute-start | bytes 337928 | tf_op jit(solution)/shard_map/z2/ppermute | solution.py:33
  11.3 2.0 %collective-permute-done.3 = bf16[40,1408]{1,0:T(8,128)(2,1)S(1)} collective-permute-done((bf16[40,1408]{1,0:T(8,128)(2,1)S(1)}, bf16[40,1408]{1,0:T(8,128)(2,1)S(1)}, u32[]{:S(2)}, u32[]{:S(2)}) %collective-permute-start.3) | collective-permute-done | bytes 112672 | tf_op jit(solution)/shard_map/z1/ppermute | solution.py:33
  13.3 5.0 %collective-permute-done.2 = bf16[40,1408]{1,0:T(8,128)(2,1)S(1)} collective-permute-done((bf16[40,1408]{1,0:T(8,128)(2,1)S(1)}, bf16[40,1408]{1,0:T(8,128)(2,1)S(1)}, u32[]{:S(2)}, u32[]{:S(2)}) %collective-permute-start.2) | collective-permute-done | bytes 112672 | tf_op jit(solution)/shard_map/z2/ppermute | solution.py:33
  19.6 2.7 %collective-permute-start.8 = (bf16[64,640]{1,0:T(8,128)(2,1)S(1)}, bf16[64,640]{1,0:T(8,128)(2,1)S(1)}, u32[]{:S(2)}, u32[]{:S(2)}) collective-permute-start(bf16[64,640]{1,0:T(8,128)(2,1)S(1)} %convert_element_type.282), channel_id=1, source_target_pairs={{0,8},{1,9},{2,10},{3,11},{4,12},{5,13},{6,14},{7,15},{8,16},{9,17... | collective-permute-start | bytes 245768 | tf_op jit(solution)/shard_map/z1/ppermute | solution.py:33
  25.7 4.4 %collective-permute-done.5 = bf16[2,40,1408]{2,1,0:T(8,128)(2,1)S(1)} collective-permute-done((bf16[2,40,1408]{2,1,0:T(8,128)(2,1)S(1)}, bf16[2,40,1408]{2,1,0:T(8,128)(2,1)S(1)}, u32[]{:S(2)}, u32[]{:S(2)}) %collective-permute-start.5) | collective-permute-done | bytes 225312 | tf_op jit(solution)/shard_map/y1/ppermute | solution.py:33
  35.7 2.6 %collective-permute-start.11 = (bf16[40,2048]{1,0:T(8,128)(2,1)S(1)}, bf16[40,2048]{1,0:T(8,128)(2,1)S(1)}, u32[]{:S(2)}, u32[]{:S(2)}) collective-permute-start(bf16[40,2048]{1,0:T(8,128)(2,1)S(1)} %pad_maximum_fusion.11), channel_id=1, source_target_pairs={{0,24},{1,25},{2,26},{3,27},{4,28},{5,29},{6,30},{7,31},{8,0},{9,1... | collective-permute-start | bytes 491528 | tf_op jit(solution)/shard_map/z3/ppermute | solution.py:33
  40.3 8.6 %collective-permute-done.12 = bf16[40,2048]{1,0:T(8,128)(2,1)S(1)} collective-permute-done((bf16[40,2048]{1,0:T(8,128)(2,1)S(1)}, bf16[40,2048]{1,0:T(8,128)(2,1)S(1)}, u32[]{:S(2)}, u32[]{:S(2)}) %collective-permute-start.12) | collective-permute-done | bytes 163872 | tf_op jit(solution)/shard_map/z2/ppermute | solution.py:33
  51.9 5.8 %collective-permute-done.14 = bf16[2,40,2048]{2,1,0:T(8,128)(2,1)S(1)} collective-permute-done((bf16[2,40,2048]{2,1,0:T(8,128)(2,1)S(1)}, bf16[2,40,2048]{2,1,0:T(8,128)(2,1)S(1)}, u32[]{:S(2)}, u32[]{:S(2)}) %collective-permute-start.14) | collective-permute-done | bytes 327712 | tf_op jit(solution)/shard_map/x1/ppermute | solution.py:33
  61.4 3.8 %shard_map.472 = (bf16[512,640]{1,0:T(8,128)(2,1)S(1)}, f32[4,512,256]{2,1,0:T(8,128)S(1)}, f32[2,512,256]{2,1,0:T(8,128)S(1)}, bf16[4,512,256]{2,1,0:T(8,128)(2...) custom-call(s32[4]{0:T(128)S(1)} %pad_add_fusion.coords_ref, ...), custom_call_target="tpu_custom_call" | custom-call | flops 5000000000 | bytes 20000000 | tf_op jit(solution)/shard_map/pallas_call | solution.py:477
  65.2 5.0 %shard_map.473 = (bf16[4,512,384]{2,1,0:T(8,128)(2,1)S(1)}, bf16[4,512,256]{2,1,0:T(8,128)(2,1)S(1)}, f32[512,640]{1,0:T(8,128)S(1)}, f32[512,640]{1,0:T(8,128)S(1)}, bf16[512,640]{1,0:T(8,128)(2,1)S(1)}) custom-call(s32[4]{0:T(128)S(1)} %pad_add_fusion.coords_ref, bf16[512,640]{1,0:T(8,128)(2,1)S(1)} %bitcast.146, s32[1,512]{1,0:T(1,128)S(1)} %copy-done, ...), custom_call_target="tpu_custom_call" | custom-call | flops 5000000000 | bytes 20000000 | tf_op jit(solution)/shard_map/pallas_call | solution.py:477
  70.2 5.6 %collective-permute-done.18.refs_1_ = bf16[2,2,40,2048]{3,2,1,0:T(8,128)(2,1)S(1)} collective-permute-done((bf16[2,2,40,2048]{3,2,1,0:T(8,128)(2,1)S(1)}, bf16[2,2,40,2048]{3,2,1,0:T(8,128)(2,1)S(1)}, u32[]{:S(2)}, u32[]{:S(2)}) %collective-permute-start.18) | collective-permute-done | bytes 655392 | tf_op jit(solution)/shard_map/y1/ppermute | solution.py:33
  80.4 2.3 %shard_map.474 = (f32[512,2048]{1,0:T(8,128)S(1)}, bf16[640,2048]{1,0:T(8,128)(2,1)S(1)}) custom-call(s32[4]{0:T(128)S(1)} %pad_add_fusion.coords_ref, bf16[512,640]{1,0:T(8,128)(2,1)S(1)} %get-tuple-element.203.h3_ref, bf16[2,2,40,2048]{3,2,1,0:T(8,128)(2,1)S(1)} %pad_maximum_fusion.refs_0_, bf16[2,2,40,2048]{3,2,1,0:T(8,128)(2,1)S(1)} %collective-permute-done.18.refs_1_, ...), custom_call_target="tpu_custom_call" | custom-call | flops 6000000000 | bytes 20000000 | tf_op jit(solution)/shard_map/pallas_call | solution.py:477
  83.4 4.9 %shard_map.475 = (bf16[512,2048]{1,0:T(8,128)(2,1)S(1)}, bf16[512,2048]{1,0:T(8,128)(2,1)S(1)}, bf16[512,2048]{1,0:T(8,128)(2,1)S(1)}, bf16[640,2048]{1,0:T(8,128)(2,1)S(1)}) custom-call(s32[4]{0:T(128)S(1)} %pad_add_fusion.coords_ref, bf16[512,640]{1,0:T(8,128)(2,1)S(1)} %get-tuple-element.203.h3_ref, f32[512,2048]{1,0:T(8,128)S(1)} %get-tuple-element.211.own_ref, ...), custom_call_target="tpu_custom_call" | custom-call | flops 3000000000 | bytes 10000000 | tf_op jit(solution)/shard_map/pallas_call | solution.py:477
  91.1 6.1 %shard_map.476 = (bf16[512,640]{1,0:T(8,128)(2,1)}, bf16[512,640]{1,0:T(8,128)(2,1)S(1)}, f32[8,640]{1,0:T(8,128)S(1)}, bf16[32,64,640]{2,1,0:T(8,128)(2,1)S(1)}...) custom-call(s32[4]{0:T(128)S(1)} %pad_add_fusion.coords_ref, ...), custom_call_target="tpu_custom_call" | custom-call | flops 6000000000 | bytes 20000000 | tf_op jit(solution)/shard_map/pallas_call | solution.py:477
  97.6 5.4 %shard_map.477 = (bf16[2,512,2048]{2,1,0:T(8,128)(2,1)S(1)}, bf16[4,2,2,40,2048]{4,3,2,1,0:T(8,128)(2,1)S(1)}, bf16[4,2,2,40,2048]{4,3,2,1,0:T(8,128)(2,1)S(1)}) custom-call(s32[4]{0:T(128)S(1)} %pad_add_fusion.coords_ref, bf16[512,640]{1,0:T(8,128)(2,1)S(1)} %get-tuple-element.226.dm_ref, bf16[32,64,640]{2,1,0:T(8,128)(2,1)S(1)} %get-tuple-element.227.wd_ref, ...), custom_call_target="tpu_custom_call" | custom-call | flops 8000000000 | bytes 20000000 | tf_op jit(solution)/shard_map/pallas_call | solution.py:477
  104.7 5.7 %shard_map.478 = (f32[512,640]{1,0:T(8,128)S(1)}, bf16[512,640]{1,0:T(8,128)(2,1)S(1)}, f32[2,8,640]{2,1,0:T(8,128)S(1)}) custom-call(s32[4]{0:T(128)S(1)} %pad_add_fusion.coords_ref, bf16[2,512,2048]{2,1,0:T(8,128)(2,1)S(1)} %get-tuple-element.233.dgu_ref, f32[512,640]{1,0:T(8,128)S(1)} %get-tuple-element.220.mid_ref, ...), custom_call_target="tpu_custom_call" | custom-call | flops 8000000000 | bytes 20000000 | tf_op jit(solution)/shard_map/pallas_call | solution.py:477
  110.5 1.9 collective-permute-done.37
  117.0 7.2 %shard_map.479 = (bf16[2,512,768]{2,1,0:T(8,128)(2,1)S(1)}, f32[2,8,256]{2,1,0:T(8,128)S(1)}, bf16[32,32,640]{2,1,0:T(8,128)(2,1)S(1)}) custom-call(s32[4]{0:T(128)S(1)} %pad_add_fusion.coords_ref, bf16[512,640]{1,0:T(8,128)(2,1)S(1)} %get-tuple-element.241.da_ref, bf16[32,32,640]{2,1,0:T(8,128)(2,1)S(1)} %get-tuple-element.199.wo_ref, ...), custom_call_target="tpu_custom_call" | custom-call | flops 6000000000 | bytes 20000000 | tf_op jit(solution)/shard_map/pallas_call | solution.py:477
  124.3 1.9 collective-permute-start.44
  126.2 3.1 %collective-permute-start.43 = (bf16[64,640]{1,0:T(8,128)(2,1)S(1)}, bf16[64,640]{1,0:T(8,128)(2,1)S(1)}, u32[]{:S(2)}, u32[]{:S(2)}) collective-permute-start(bf16[64,640]{1,0:T(8,128)(2,1)S(1)} %get-tuple-element.359), channel_id=1, source_target_pairs={{0,16},{1,17},{2,18},{3,19},{4,20},{5,21},{6,22},{7,23},{8,24},{9,... | collective-permute-start | bytes 245768 | tf_op jit(solution)/shard_map/z2/ppermute | solution.py:33
  129.7 4.6 %shard_map.480 = (f32[512,640]{1,0:T(8,128)}, bf16[4,2,2,40,1408]{4,3,2,1,0:T(8,128)(2,1)S(1)}, bf16[4,2,2,40,1408]{4,3,2,1,0:T(8,128)(2,1)S(1)}) custom-call(s32[4]{0:T(128)S(1)} %pad_add_fusion.coords_ref, bf16[2,512,768]{2,1,0:T(8,128)(2,1)S(1)} %get-tuple-element.249.dqkv_ref, bf16[512,640]{1,0:T(8,128)(2,1)S(1)} %get-tuple-element.250.h1_ref, ...), custom_call_target="tpu_custom_call" | custom-call | flops 6000000000 | bytes 20000000 | tf_op jit(solution)/shard_map/pallas_call | solution.py:477
  135.4 3.8 %collective-permute-start.45 = (bf16[4,2,2,40,1408]{4,3,2,1,0:T(8,128)(2,1)S(1)}, bf16[4,2,2,40,1408]{4,3,2,1,0:T(8,128)(2,1)S(1)}, u32[]{:S(2)}, u32[]{:S(2)}) collective-permute-start(bf16[4,2,2,40,1408]{4,3,2,1,0:T(8,128)(2,1)S(1)} %get-tuple-element.267), channel_id=1, source_target_pairs={{0,1},{1,0},{2,3},{3,2},{4,5},{5,4},{6,7},{7,6},{8,9},{9,8},{10,11... | collective-permute-start | bytes 5406728 | tf_op jit(solution)/shard_map/c1/ppermute | solution.py:33
  140.7 8.6 %collective-permute-done.46 = bf16[2,40,2048]{2,1,0:T(8,128)(2,1)S(1)} collective-permute-done((bf16[2,40,2048]{2,1,0:T(8,128)(2,1)S(1)}, bf16[2,40,2048]{2,1,0:T(8,128)(2,1)S(1)}, u32[]{:S(2)}, u32[]{:S(2)}) %collective-permute-start.46) | collective-permute-done | bytes 327712 | tf_op jit(solution)/shard_map/x1/ppermute | solution.py:33
  149.8 2.1 %collective-permute-start.51 = (bf16[40,2048]{1,0:T(8,128)(2,1)S(1)}, bf16[40,2048]{1,0:T(8,128)(2,1)S(1)}, u32[]{:S(2)}, u32[]{:S(2)}) collective-permute-start(bf16[40,2048]{1,0:T(8,128)(2,1)S(1)} %get-tuple-element.347), channel_id=1, source_target_pairs={{0,24},{1,25},{2,26},{3,27},{4,28},{5,29},{6,30},{7,31},{8,0},{9,1... | collective-permute-start | bytes 491528 | tf_op jit(solution)/shard_map/z3/ppermute | solution.py:33
  154.4 4.8 %collective-permute-done.50 = bf16[40,2048]{1,0:T(8,128)(2,1)S(1)} collective-permute-done((bf16[40,2048]{1,0:T(8,128)(2,1)S(1)}, bf16[40,2048]{1,0:T(8,128)(2,1)S(1)}, u32[]{:S(2)}, u32[]{:S(2)}) %collective-permute-start.50) | collective-permute-done | bytes 163872 | tf_op jit(solution)/shard_map/z1/ppermute | solution.py:33
  159.3 3.1 %collective-permute-done.48 = bf16[2,2,40,1408]{3,2,1,0:T(8,128)(2,1)S(1)} collective-permute-done((bf16[2,2,40,1408]{3,2,1,0:T(8,128)(2,1)S(1)}, bf16[2,2,40,1408]{3,2,1,0:T(8,128)(2,1)S(1)}, u32[]{:S(2)}, u32[]{:S(2)}) %collective-permute-start.48) | collective-permute-done | bytes 450592 | tf_op jit(solution)/shard_map/y1/ppermute | solution.py:33
  166.0 5.2 %collective-permute-done.54 = bf16[40,2048]{1,0:T(8,128)(2,1)S(1)} collective-permute-done((bf16[40,2048]{1,0:T(8,128)(2,1)S(1)}, bf16[40,2048]{1,0:T(8,128)(2,1)S(1)}, u32[]{:S(2)}, u32[]{:S(2)}) %collective-permute-start.54) | collective-permute-done | bytes 163872 | tf_op jit(solution)/shard_map/z2/ppermute | solution.py:33
  171.5 1.8 collective-permute-start.58
  173.7 3.0 %collective-permute-start.57 = (bf16[40,1408]{1,0:T(8,128)(2,1)S(1)}, bf16[40,1408]{1,0:T(8,128)(2,1)S(1)}, u32[]{:S(2)}, u32[]{:S(2)}) collective-permute-start(bf16[40,1408]{1,0:T(8,128)(2,1)S(1)} %get-tuple-element.354), channel_id=1, source_target_pairs={{0,24},{1,25},{2,26},{3,27},{4,28},{5,29},{6,30},{7,31},{8,0},{9,1... | collective-permute-start | bytes 337928 | tf_op jit(solution)/shard_map/z3/ppermute | solution.py:33
  177.5 2.3 %multiply_subtract_fusion = (f32[20,2,2048]{2,1,0:T(2,128)}, f32[20,2,2048]{2,1,0:T(2,128)}, f32[20,2,2048]{2,1,0:T(2,128)}, f32[20,2,2048]{2,1,0:T(2,128)}) fusion(f32[20,2,2048]{2,1,0:T(2,128)S(1)} %copy-done.3, f32[20,1,2048]{2,1,0:T(1,128)S(1)} %stack.174, f32[20,1,2048]{2,1,0:T(1,128)S(1)} %copy.59, f32[20,2,2048]{2,1,0:T(2,128)S(1)} %copy-done.6, ...), kind=kLoop, calls=%fused_computation.54 | loop fusion | flops 1228800 | bytes 2621440 | tf_op jit(solution)/shard_map/sub | solution.py:811
  181.6 5.9 %collective-permute-done.56 = bf16[40,1408]{1,0:T(8,128)(2,1)S(1)} collective-permute-done((bf16[40,1408]{1,0:T(8,128)(2,1)S(1)}, bf16[40,1408]{1,0:T(8,128)(2,1)S(1)}, u32[]{:S(2)}, u32[]{:S(2)}) %collective-permute-start.56) | collective-permute-done | bytes 112672 | tf_op jit(solution)/shard_map/z2/ppermute | solution.py:33
  (225 shorter events, 56.3 us)
Async XLA Ops:
  7.9 10.4 %collective-permute-start.2 = (bf16[40,1408]{1,0:T(8,128)(2,1)S(1)}, bf16[40,1408]{1,0:T(8,128)(2,1)S(1)}, u32[]{:S(2)}, u32[]{:S(2)}) collective-permute-start(bf16[40,1408]{1,0:T(8,128)(2,1)S(1)} %fusion.30), channel_id=1, source_target_pairs={{0,16},{1,17},{2,18},{3,19},{4,20},{5,21},{6,22},{7,23},{8,24},{9,... | collective-permute-start | bytes 337928 | tf_op jit(solution)/shard_map/z2/ppermute | solution.py:33
  19.6 10.5 %collective-permute-start.8 = (bf16[64,640]{1,0:T(8,128)(2,1)S(1)}, bf16[64,640]{1,0:T(8,128)(2,1)S(1)}, u32[]{:S(2)}, u32[]{:S(2)}) collective-permute-start(bf16[64,640]{1,0:T(8,128)(2,1)S(1)} %convert_element_type.282), channel_id=1, source_target_pairs={{0,8},{1,9},{2,10},{3,11},{4,12},{5,13},{6,14},{7,15},{8,16},{9,17... | collective-permute-start | bytes 245768 | tf_op jit(solution)/shard_map/z1/ppermute | solution.py:33
  30.6 18.3 %collective-permute-start.9 = (bf16[2,2,40,1408]{3,2,1,0:T(8,128)(2,1)S(1)}, bf16[2,2,40,1408]{3,2,1,0:T(8,128)(2,1)S(1)}, u32[]{:S(2)}, u32[]{:S(2)}) collective-permute-start(bf16[2,2,40,1408]{3,2,1,0:T(8,128)(2,1)S(1)} %pad_maximum_fusion.2.refs_0_), channel_id=1, source_target_pairs={{0,4},{1,5},{2,6},{3,7},{4,0},{5,1},{6,2},{7,3},{8,12},{9,13},{10,... | collective-permute-start | bytes 1351688 | tf_op jit(solution)/shard_map/y1/ppermute | solution.py:33
  31.8 17.1 %collective-permute-start.10 = (bf16[2,2,40,1408]{3,2,1,0:T(8,128)(2,1)S(1)}, bf16[2,2,40,1408]{3,2,1,0:T(8,128)(2,1)S(1)}, u32[]{:S(2)}, u32[]{:S(2)}) collective-permute-start(bf16[2,2,40,1408]{3,2,1,0:T(8,128)(2,1)S(1)} %pad_maximum_fusion.3.refs_2_), channel_id=1, source_target_pairs={{0,2},{1,3},{2,0},{3,1},{4,6},{5,7},{6,4},{7,5},{8,10},{9,11},{10,... | collective-permute-start | bytes 1351688 | tf_op jit(solution)/shard_map/x1/ppermute | solution.py:33
  35.7 13.2 %collective-permute-start.12 = (bf16[40,2048]{1,0:T(8,128)(2,1)S(1)}, bf16[40,2048]{1,0:T(8,128)(2,1)S(1)}, u32[]{:S(2)}, u32[]{:S(2)}) collective-permute-start(bf16[40,2048]{1,0:T(8,128)(2,1)S(1)} %pad_maximum_fusion.11), channel_id=1, source_target_pairs={{0,16},{1,17},{2,18},{3,19},{4,20},{5,21},{6,22},{7,23},{8,24},{9,... | collective-permute-start | bytes 491528 | tf_op jit(solution)/shard_map/z2/ppermute | solution.py:33
  35.7 13.2 %collective-permute-start.11 = (bf16[40,2048]{1,0:T(8,128)(2,1)S(1)}, bf16[40,2048]{1,0:T(8,128)(2,1)S(1)}, u32[]{:S(2)}, u32[]{:S(2)}) collective-permute-start(bf16[40,2048]{1,0:T(8,128)(2,1)S(1)} %pad_maximum_fusion.11), channel_id=1, source_target_pairs={{0,24},{1,25},{2,26},{3,27},{4,28},{5,29},{6,30},{7,31},{8,0},{9,1... | collective-permute-start | bytes 491528 | tf_op jit(solution)/shard_map/z3/ppermute | solution.py:33
  40.1 9.5 %collective-permute-start.17 = (bf16[2,64,640]{2,1,0:T(8,128)(2,1)S(1)}, bf16[2,64,640]{2,1,0:T(8,128)(2,1)S(1)}, u32[]{:S(2)}, u32[]{:S(2)}) collective-permute-start(bf16[2,64,640]{2,1,0:T(8,128)(2,1)S(1)} %get-tuple-element.361), channel_id=1, source_target_pairs={{0,4},{1,5},{2,6},{3,7},{4,0},{5,1},{6,2},{7,3},{8,12},{9,13},{10,... | collective-permute-start | bytes 491528 | tf_op jit(solution)/shard_map/y1/ppermute | solution.py:33
  49.0 8.7 %collective-permute-start.14 = (bf16[2,40,2048]{2,1,0:T(8,128)(2,1)S(1)}, bf16[2,40,2048]{2,1,0:T(8,128)(2,1)S(1)}, u32[]{:S(2)}, u32[]{:S(2)}) collective-permute-start(bf16[2,40,2048]{2,1,0:T(8,128)(2,1)S(1)} %get-tuple-element.351), channel_id=1, source_target_pairs={{0,2},{1,3},{2,0},{3,1},{4,6},{5,7},{6,4},{7,5},{8,10},{9,11},{10,... | collective-permute-start | bytes 983048 | tf_op jit(solution)/shard_map/x1/ppermute | solution.py:33
  49.3 9.9 %collective-permute-start.15 = (bf16[2,40,2048]{2,1,0:T(8,128)(2,1)S(1)}, bf16[2,40,2048]{2,1,0:T(8,128)(2,1)S(1)}, u32[]{:S(2)}, u32[]{:S(2)}) collective-permute-start(bf16[2,40,2048]{2,1,0:T(8,128)(2,1)S(1)} %get-tuple-element.349), channel_id=1, source_target_pairs={{0,4},{1,5},{2,6},{3,7},{4,0},{5,1},{6,2},{7,3},{8,12},{9,13},{10,... | collective-permute-start | bytes 983048 | tf_op jit(solution)/shard_map/y1/ppermute | solution.py:33
  49.6 10.0 %collective-permute-start.20 = (bf16[2,2,40,1408]{3,2,1,0:T(8,128)(2,1)S(1)}, bf16[2,2,40,1408]{3,2,1,0:T(8,128)(2,1)S(1)}, u32[]{:S(2)}, u32[]{:S(2)}) collective-permute-start(bf16[2,2,40,1408]{3,2,1,0:T(8,128)(2,1)S(1)} %pad_maximum_fusion.2.refs_0_), channel_id=1, source_target_pairs={{0,1},{1,0},{2,3},{3,2},{4,5},{5,4},{6,7},{7,6},{8,9},{9,8},{10,11... | collective-permute-start | bytes 1351688 | tf_op jit(solution)/shard_map/c1/ppermute | solution.py:33
  51.4 8.9 %collective-permute-start.22 = (bf16[2,2,40,1408]{3,2,1,0:T(8,128)(2,1)S(1)}, bf16[2,2,40,1408]{3,2,1,0:T(8,128)(2,1)S(1)}, u32[]{:S(2)}, u32[]{:S(2)}) collective-permute-start(bf16[2,2,40,1408]{3,2,1,0:T(8,128)(2,1)S(1)} %pad_maximum_fusion.3.refs_2_), channel_id=1, source_target_pairs={{0,1},{1,0},{2,3},{3,2},{4,5},{5,4},{6,7},{7,6},{8,9},{9,8},{10,11... | collective-permute-start | bytes 1351688 | tf_op jit(solution)/shard_map/c1/ppermute | solution.py:33
  59.3 10.9 %collective-permute-start.24 = (bf16[2,2,40,2048]{3,2,1,0:T(8,128)(2,1)S(1)}, bf16[2,2,40,2048]{3,2,1,0:T(8,128)(2,1)S(1)}, u32[]{:S(2)}, u32[]{:S(2)}) collective-permute-start(bf16[2,2,40,2048]{3,2,1,0:T(8,128)(2,1)S(1)} %pad_maximum_fusion.refs_0_), channel_id=1, source_target_pairs={{0,1},{1,0},{2,3},{3,2},{4,5},{5,4},{6,7},{7,6},{8,9},{9,8},{10,11... | collective-permute-start | bytes 1966088 | tf_op jit(solution)/shard_map/c1/ppermute | solution.py:33
  59.7 16.1 %collective-permute-start.18 = (bf16[2,2,40,2048]{3,2,1,0:T(8,128)(2,1)S(1)}, bf16[2,2,40,2048]{3,2,1,0:T(8,128)(2,1)S(1)}, u32[]{:S(2)}, u32[]{:S(2)}) collective-permute-start(bf16[2,2,40,2048]{3,2,1,0:T(8,128)(2,1)S(1)} %pad_maximum_fusion.refs_0_), channel_id=1, source_target_pairs={{0,4},{1,5},{2,6},{3,7},{4,0},{5,1},{6,2},{7,3},{8,12},{9,13},{10,... | collective-permute-start | bytes 1966088 | tf_op jit(solution)/shard_map/y1/ppermute | solution.py:33
  59.9 15.9 %collective-permute-start.25 = (bf16[2,2,40,2048]{3,2,1,0:T(8,128)(2,1)S(1)}, bf16[2,2,40,2048]{3,2,1,0:T(8,128)(2,1)S(1)}, u32[]{:S(2)}, u32[]{:S(2)}) collective-permute-start(bf16[2,2,40,2048]{3,2,1,0:T(8,128)(2,1)S(1)} %pad_maximum_fusion.1.refs_2_), channel_id=1, source_target_pairs={{0,1},{1,0},{2,3},{3,2},{4,5},{5,4},{6,7},{7,6},{8,9},{9,8},{10,11... | collective-permute-start | bytes 1966088 | tf_op jit(solution)/shard_map/c1/ppermute | solution.py:33
  60.4 16.3 %collective-permute-start.19 = (bf16[2,2,40,2048]{3,2,1,0:T(8,128)(2,1)S(1)}, bf16[2,2,40,2048]{3,2,1,0:T(8,128)(2,1)S(1)}, u32[]{:S(2)}, u32[]{:S(2)}) collective-permute-start(bf16[2,2,40,2048]{3,2,1,0:T(8,128)(2,1)S(1)} %pad_maximum_fusion.1.refs_2_), channel_id=1, source_target_pairs={{0,2},{1,3},{2,0},{3,1},{4,6},{5,7},{6,4},{7,5},{8,10},{9,11},{10,... | collective-permute-start | bytes 1966088 | tf_op jit(solution)/shard_map/x1/ppermute | solution.py:33
  77.5 11.9 %collective-permute-start.30 = (bf16[2,2,64,640]{3,2,1,0:T(8,128)(2,1)S(1)}, bf16[2,2,64,640]{3,2,1,0:T(8,128)(2,1)S(1)}, u32[]{:S(2)}, u32[]{:S(2)}) collective-permute-start(bf16[2,2,64,640]{3,2,1,0:T(8,128)(2,1)S(1)} %pad_maximum_fusion.6.refs_0_), channel_id=1, source_target_pairs={{0,1},{1,0},{2,3},{3,2},{4,5},{5,4},{6,7},{7,6},{8,9},{9,8},{10,11... | collective-permute-start | bytes 983048 | tf_op jit(solution)/shard_map/c1/ppermute | solution.py:33
  78.0 10.2 %collective-permute-start.28 = (bf16[2,2,64,640]{3,2,1,0:T(8,128)(2,1)S(1)}, bf16[2,2,64,640]{3,2,1,0:T(8,128)(2,1)S(1)}, u32[]{:S(2)}, u32[]{:S(2)}) collective-permute-start(bf16[2,2,64,640]{3,2,1,0:T(8,128)(2,1)S(1)} %pad_maximum_fusion.6.refs_0_), channel_id=1, source_target_pairs={{0,4},{1,5},{2,6},{3,7},{4,0},{5,1},{6,2},{7,3},{8,12},{9,13},{10,... | collective-permute-start | bytes 983048 | tf_op jit(solution)/shard_map/y1/ppermute | solution.py:33
  79.3 9.0 %collective-permute-start.29 = (bf16[2,2,64,640]{3,2,1,0:T(8,128)(2,1)S(1)}, bf16[2,2,64,640]{3,2,1,0:T(8,128)(2,1)S(1)}, u32[]{:S(2)}, u32[]{:S(2)}) collective-permute-start(bf16[2,2,64,640]{3,2,1,0:T(8,128)(2,1)S(1)} %pad_maximum_fusion.7.refs_2_), channel_id=1, source_target_pairs={{0,2},{1,3},{2,0},{3,1},{4,6},{5,7},{6,4},{7,5},{8,10},{9,11},{10,... | collective-permute-start | bytes 983048 | tf_op jit(solution)/shard_map/x1/ppermute | solution.py:33
  103.0 10.1 %collective-permute-start.35 = (bf16[4,2,2,40,2048]{4,3,2,1,0:T(8,128)(2,1)S(1)}, bf16[4,2,2,40,2048]{4,3,2,1,0:T(8,128)(2,1)S(1)}, u32[]{:S(2)}, u32[]{:S(2)}) collective-permute-start(bf16[4,2,2,40,2048]{4,3,2,1,0:T(8,128)(2,1)S(1)} %get-tuple-element.238), channel_id=1, source_target_pairs={{0,1},{1,0},{2,3},{3,2},{4,5},{5,4},{6,7},{7,6},{8,9},{9,8},{10,11... | collective-permute-start | bytes 7864328 | tf_op jit(solution)/shard_map/c1/ppermute | solution.py:33
  103.4 9.0 %collective-permute-start.37 = (bf16[2,2,64,640]{3,2,1,0:T(8,128)(2,1)S(1)}, bf16[2,2,64,640]{3,2,1,0:T(8,128)(2,1)S(1)}, u32[]{:S(2)}, u32[]{:S(2)}) collective-permute-start(bf16[2,2,64,640]{3,2,1,0:T(8,128)(2,1)S(1)} %get-tuple-element.339), channel_id=1, source_target_pairs={{0,2},{1,3},{2,0},{3,1},{4,6},{5,7},{6,4},{7,5},{8,10},{9,11},{10,... | collective-permute-start | bytes 983048 | tf_op jit(solution)/shard_map/x1/ppermute | solution.py:33
  104.5 8.6 %collective-permute-start.36 = (bf16[2,2,64,640]{3,2,1,0:T(8,128)(2,1)S(1)}, bf16[2,2,64,640]{3,2,1,0:T(8,128)(2,1)S(1)}, u32[]{:S(2)}, u32[]{:S(2)}) collective-permute-start(bf16[2,2,64,640]{3,2,1,0:T(8,128)(2,1)S(1)} %get-tuple-element.340), channel_id=1, source_target_pairs={{0,4},{1,5},{2,6},{3,7},{4,0},{5,1},{6,2},{7,3},{8,12},{9,13},{10,... | collective-permute-start | bytes 983048 | tf_op jit(solution)/shard_map/y1/ppermute | solution.py:33
  113.5 10.8 %collective-permute-start.38 = (bf16[2,64,640]{2,1,0:T(8,128)(2,1)S(1)}, bf16[2,64,640]{2,1,0:T(8,128)(2,1)S(1)}, u32[]{:S(2)}, u32[]{:S(2)}) collective-permute-start(bf16[2,64,640]{2,1,0:T(8,128)(2,1)S(1)} %fusion.23), channel_id=1, source_target_pairs={{0,2},{1,3},{2,0},{3,1},{4,6},{5,7},{6,4},{7,5},{8,10},{9,11},{10,... | collective-permute-start | bytes 491528 | tf_op jit(solution)/shard_map/x1/ppermute | solution.py:33
  113.9 10.3 %collective-permute-start.39 = (bf16[2,64,640]{2,1,0:T(8,128)(2,1)S(1)}, bf16[2,64,640]{2,1,0:T(8,128)(2,1)S(1)}, u32[]{:S(2)}, u32[]{:S(2)}) collective-permute-start(bf16[2,64,640]{2,1,0:T(8,128)(2,1)S(1)} %fusion.24), channel_id=1, source_target_pairs={{0,4},{1,5},{2,6},{3,7},{4,0},{5,1},{6,2},{7,3},{8,12},{9,13},{10,... | collective-permute-start | bytes 491528 | tf_op jit(solution)/shard_map/y1/ppermute | solution.py:33
  114.6 20.8 %collective-permute-start.41 = (bf16[2,2,40,2048]{3,2,1,0:T(8,128)(2,1)S(1)}, bf16[2,2,40,2048]{3,2,1,0:T(8,128)(2,1)S(1)}, u32[]{:S(2)}, u32[]{:S(2)}) collective-permute-start(bf16[2,2,40,2048]{3,2,1,0:T(8,128)(2,1)S(1)} %get-tuple-element.331), channel_id=1, source_target_pairs={{0,2},{1,3},{2,0},{3,1},{4,6},{5,7},{6,4},{7,5},{8,10},{9,11},{10,... | collective-permute-start | bytes 1966088 | tf_op jit(solution)/shard_map/x1/ppermute | solution.py:33
  115.7 19.7 %collective-permute-start.40 = (bf16[2,2,40,2048]{3,2,1,0:T(8,128)(2,1)S(1)}, bf16[2,2,40,2048]{3,2,1,0:T(8,128)(2,1)S(1)}, u32[]{:S(2)}, u32[]{:S(2)}) collective-permute-start(bf16[2,2,40,2048]{3,2,1,0:T(8,128)(2,1)S(1)} %get-tuple-element.332), channel_id=1, source_target_pairs={{0,4},{1,5},{2,6},{3,7},{4,0},{5,1},{6,2},{7,3},{8,12},{9,13},{10,... | collective-permute-start | bytes 1966088 | tf_op jit(solution)/shard_map/y1/ppermute | solution.py:33
  124.3 10.0 %collective-permute-start.44 = (bf16[64,640]{1,0:T(8,128)(2,1)S(1)}, bf16[64,640]{1,0:T(8,128)(2,1)S(1)}, u32[]{:S(2)}, u32[]{:S(2)}) collective-permute-start(bf16[64,640]{1,0:T(8,128)(2,1)S(1)} %get-tuple-element.358), channel_id=1, source_target_pairs={{0,24},{1,25},{2,26},{3,27},{4,28},{5,29},{6,30},{7,31},{8,0},{9,1... | collective-permute-start | bytes 245768 | tf_op jit(solution)/shard_map/z3/ppermute | solution.py:33
  135.4 14.1 %collective-permute-start.45 = (bf16[4,2,2,40,1408]{4,3,2,1,0:T(8,128)(2,1)S(1)}, bf16[4,2,2,40,1408]{4,3,2,1,0:T(8,128)(2,1)S(1)}, u32[]{:S(2)}, u32[]{:S(2)}) collective-permute-start(bf16[4,2,2,40,1408]{4,3,2,1,0:T(8,128)(2,1)S(1)} %get-tuple-element.267), channel_id=1, source_target_pairs={{0,1},{1,0},{2,3},{3,2},{4,5},{5,4},{6,7},{7,6},{8,9},{9,8},{10,11... | collective-permute-start | bytes 5406728 | tf_op jit(solution)/shard_map/c1/ppermute | solution.py:33
  139.9 9.4 %collective-permute-start.46 = (bf16[2,40,2048]{2,1,0:T(8,128)(2,1)S(1)}, bf16[2,40,2048]{2,1,0:T(8,128)(2,1)S(1)}, u32[]{:S(2)}, u32[]{:S(2)}) collective-permute-start(bf16[2,40,2048]{2,1,0:T(8,128)(2,1)S(1)} %fusion.10), channel_id=1, source_target_pairs={{0,2},{1,3},{2,0},{3,1},{4,6},{5,7},{6,4},{7,5},{8,10},{9,11},{10,... | collective-permute-start | bytes 983048 | tf_op jit(solution)/shard_map/x1/ppermute | solution.py:33
  140.4 9.1 %collective-permute-start.47 = (bf16[2,40,2048]{2,1,0:T(8,128)(2,1)S(1)}, bf16[2,40,2048]{2,1,0:T(8,128)(2,1)S(1)}, u32[]{:S(2)}, u32[]{:S(2)}) collective-permute-start(bf16[2,40,2048]{2,1,0:T(8,128)(2,1)S(1)} %fusion.11), channel_id=1, source_target_pairs={{0,4},{1,5},{2,6},{3,7},{4,0},{5,1},{6,2},{7,3},{8,12},{9,13},{10,... | collective-permute-start | bytes 983048 | tf_op jit(solution)/shard_map/y1/ppermute | solution.py:33
  151.9 10.4 %collective-permute-start.48 = (bf16[2,2,40,1408]{3,2,1,0:T(8,128)(2,1)S(1)}, bf16[2,2,40,1408]{3,2,1,0:T(8,128)(2,1)S(1)}, u32[]{:S(2)}, u32[]{:S(2)}) collective-permute-start(bf16[2,2,40,1408]{3,2,1,0:T(8,128)(2,1)S(1)} %get-tuple-element.275), channel_id=1, source_target_pairs={{0,4},{1,5},{2,6},{3,7},{4,0},{5,1},{6,2},{7,3},{8,12},{9,13},{10,... | collective-permute-start | bytes 1351688 | tf_op jit(solution)/shard_map/y1/ppermute | solution.py:33
  152.0 10.3 %collective-permute-start.49 = (bf16[2,2,40,1408]{3,2,1,0:T(8,128)(2,1)S(1)}, bf16[2,2,40,1408]{3,2,1,0:T(8,128)(2,1)S(1)}, u32[]{:S(2)}, u32[]{:S(2)}) collective-permute-start(bf16[2,2,40,1408]{3,2,1,0:T(8,128)(2,1)S(1)} %get-tuple-element.276), channel_id=1, source_target_pairs={{0,2},{1,3},{2,0},{3,1},{4,6},{5,7},{6,4},{7,5},{8,10},{9,11},{10,... | collective-permute-start | bytes 1351688 | tf_op jit(solution)/shard_map/x1/ppermute | solution.py:33
  176.7 10.8 %collective-permute-start.56 = (bf16[40,1408]{1,0:T(8,128)(2,1)S(1)}, bf16[40,1408]{1,0:T(8,128)(2,1)S(1)}, u32[]{:S(2)}, u32[]{:S(2)}) collective-permute-start(bf16[40,1408]{1,0:T(8,128)(2,1)S(1)} %get-tuple-element.355), channel_id=1, source_target_pairs={{0,16},{1,17},{2,18},{3,19},{4,20},{5,21},{6,22},{7,23},{8,24},{9,... | collective-permute-start | bytes 337928 | tf_op jit(solution)/shard_map/z2/ppermute | solution.py:33
  (52 other events, 331.3 us)

commit v5 on v4

--- a/solution.py
+++ b/solution.py
@@ -47,8 +47,8 @@
 
 
 def gather_pair(near):
-    first = jnp.stack([near[0], near[1]])
-    second = jnp.stack([near[2], near[3]])
+    first = jnp.stack([near[0], near[2]])
+    second = jnp.stack([near[1], near[3]])
     return jnp.stack([first, shift(first, 2, 1)]), jnp.stack([second, shift(second, 1, 1)])
 
 
@@ -149,7 +149,7 @@
 
 
 def gap_of(group, one, two):
-    return (two, group, one) if group < 2 else (2 + two, one, group - 2)
+    return (2 * two, group, one) if group < 2 else (1 + 2 * two, one, group - 2)
 
 
 def slots(coords_ref):
@@ -297,6 +297,14 @@
             activate(slice(start, start + 16))
 
 
+def plane_slots(coords_ref):
+    for far in range(2):
+        core = lax.rem(coords_ref[3] + far, 2)
+        for step in range(4):
+            for spot in range(4):
+                yield far, step, spot, 2 * chip_at(coords_ref, (step, spot // 2, spot % 2)) + core
+
+
 def down_both(coords_ref, hidden_ref, mid_ref, cot_ref, gains_ref, *refs):
     piece_refs, refs = refs[:8], refs[8:]
     (result_ref, dm_ref, gain_ref, wd_ref), refs = refs[:4], refs[4:]
@@ -320,8 +328,8 @@
     for block in range(8):
         grad = dot_left_t(hidden_ref[:, 256 * block : 256 * block + 256], dm_ref[...])
         natural_ref[4 * block : 4 * block + 4] = grad.astype(BF).reshape(4, 64, 640)
-    for far, group, one, two, place in slots(coords_ref):
-        out_refs[far][group, one, two] = natural_ref[place]
+    for far, step, spot, place in plane_slots(coords_ref):
+        out_refs[far][step, spot] = natural_ref[place]
 
 
 def gateup_backward(coords_ref, dm_ref, wd_ref, slope_ref, gelu_ref, h3_ref, *refs):
@@ -513,6 +521,16 @@
     return (wide(left) + wide(right)).astype(BF)
 
 
+def diagonal(values):
+    pairs = []
+    for place in range(int(np.prod(DIMS))):
+        spot = list(np.unravel_index(place, DIMS))
+        spot[1], spot[2] = (spot[1] + 1) % DIMS[1], (spot[2] + 1) % DIMS[2]
+        pairs.append((place, int(np.ravel_multi_index(spot, DIMS))))
+    with jax.named_scope("xy"):
+        return lax.ppermute(values, "dp", pairs)
+
+
 def scatter_across(keep, got):
     return shift(narrow(keep[1], got[1]), 1, 1), shift(narrow(keep[3], got[3]), 2, 1)
 
@@ -531,7 +549,7 @@
 def scatter_along(sum_a, sum_b, side_a, side_b):
     last_a = sum_a + wide(side_a)
     last_b = sum_b + wide(side_b)
-    return last_a[0], [last_a[1].astype(BF), last_b[0].astype(BF), last_b[1].astype(BF)]
+    return last_a[0], [last_b[0].astype(BF), last_a[1].astype(BF), last_b[1].astype(BF)]
 
 
 def scatter_end(own, *others):
@@ -563,7 +581,7 @@
 
     near_a = gather_along(block_a)
     near_a, block_w, block_g = join(near_a, down_round, block_g)
-    first, second = jnp.stack([near_a[0], near_a[1]]), jnp.stack([near_a[2], near_a[3]])
+    first, second = jnp.stack([near_a[0], near_a[2]]), jnp.stack([near_a[1], near_a[3]])
     first, second, block_w, block_g = join(first, second, block_w, block_g)
     pairs_a = [jnp.stack([first, shift(first, 2, 1)]), jnp.stack([second, shift(second, 1, 1)])]
     near_w = gather_along(block_w)
@@ -633,7 +651,7 @@
         coords,
         [hidden, mid, cotangent, gains_full, *pieces_w],
         [shape(512, 640), shape(512, 640), shape(8, 640, kind=f32), shape(32, 64, 640)]
-        + [shape(4, 2, 2, 64, 640)] * 2,
+        + [shape(4, 4, 64, 640)] * 2,
         [pltpu.VMEM((512, 640), f32), pltpu.VMEM((32, 64, 640), BF)],
         12,
         (6, 20),
@@ -649,7 +667,8 @@
         (8, 20),
     )
     dgu, got_w, send_g = join(dgu, got_w, send_g)
-    far_w = scatter_across(keep_w, got_w)
+    near_w, far_w, across_w = [narrow(keep_w[step], got_w[step]) for step in (1, 3, 2)]
+    near_w = shift(near_w, 0, 1)
     got_g = shift(send_g, 3, 1)
     dmid, da, gain_mid = call(
         middle_backward,
@@ -660,9 +679,9 @@
         12,
         (8, 20),
     )
-    da, got_g, far_w = join(da, got_g, far_w)
-    side_w = scatter_pair(keep_w, got_w, *far_w)
+    da, got_g, near_w, far_w = join(da, got_g, near_w, far_w)
     far_g = scatter_across(keep_g, got_g)
+    far_w = shift(far_w, 0, 3)
     dqkv, gain_head, dwo = call(
         attention_backward,
         coords,
@@ -676,9 +695,8 @@
         12,
         (6, 20),
     )
-    dqkv, side_w = join(dqkv, side_w)
-    own_w, along_w = scatter_along(*side_w)
-    along_w = [shift(part, 0, step + 1) for step, part in enumerate(along_w)]
+    dqkv, far_w, across_w = join(dqkv, far_w, across_w)
+    across_w = shift(across_w, 0, 2)
     input_grad, keep_a, send_a = call(
         input_backward,
         coords,
@@ -688,8 +706,7 @@
         12,
         (6, 20),
     )
-    send_a, far_g, along_w = join(send_a, far_g, along_w)
-    down_grad = scatter_end(own_w, *along_w)
+    send_a, far_g = join(send_a, far_g)
     got_a = shift(send_a, 3, 1)
     side_g = scatter_pair(keep_g, got_g, *far_g)
     got_a, side_g = join(got_a, side_g)
@@ -698,11 +715,14 @@
     far_a = shift(first, 1, 1), shift(second, 2, 1)
     own_g, along_g = scatter_along(*side_g)
     ends_g = [shift(along_g[0], 0, 1), shift(along_g[2], 0, 3)]
-    far_a, ends_g, across_g = join(far_a, ends_g, along_g[1])
+    far_a, ends_g, across_g, across_w = join(far_a, ends_g, along_g[1], across_w)
     first, second, *side_a = scatter_sums(keep_a, got_a, *far_a)
     side_a, across_g = join(side_a, across_g)
     side_a = shift(side_a[0], 2, 1), shift(side_a[1], 1, 1)
     across_g = shift(across_g, 0, 2)
+    plane = scatter_end(wide(keep_w[0]) + wide(got_w[0]), near_w, far_w, across_w)
+    sent = plane.astype(BF)
+    plane_w = [shift(sent[1], 2, 1), shift(sent[2], 1, 1), diagonal(sent[3])]
     side_a, across_g = join(side_a, across_g)
     own_a, along_a = scatter_along(first, second, *side_a)
     along_a = [shift(part, 0, step + 1) for step, part in enumerate(along_a)]
@@ -716,7 +736,8 @@
     low, high = own_rows(gateup_sum)
     gateup_grad = with_layout_constraint(jnp.stack([low, high], axis=1), Layout((0, 1, 2)))
     gateup_done = (gateup_grad, *update_gateup(gateup_grad))
-    along_a, gateup_done = join(along_a, gateup_done)
+    along_a, gateup_done, plane_w = join(along_a, gateup_done, plane_w)
+    down_grad = scatter_end(plane[0], *plane_w)
     rest = scatter_end(own_a, *along_a)
     output_grad = rest[:32, 768:]
     norm_grad = lax.dynamic_slice(rest[32:36, 768:], (0, place * 20), (4, 20))

time: 195 us -> 192 us (0.985)
  waiting for transfers between devices: 70.4 us -> 63 us
  starting transfers between devices: 59.2 us -> 63.4 us
    ppermute x60 -> x58, waiting for transfers between devices: 70.4 us -> 63 us  [shift(): return lax.ppermute(values, 'dp', shift_perm(axis, amount))]
    ppermute x60 -> x58, starting transfers between devices: 59.2 us -> 62.9 us  [shift(): return lax.ppermute(values, 'dp', shift_perm(axis, amount))]
  transfers between devices with their start and end apart: 60 -> 59, of which waited for: 23 -> 22; matrix products, arithmetic and copies ran while one was open for 5% -> 6% of each run, Pallas kernels for 20% -> 21%
where the time goes in v5:
time: 192 us; the launch traced here: 189 us
  starting transfers between devices  63.4 us (33%)
  waiting for transfers between devices  63 us (33%)
  Pallas kernels  44.9 us (23%)
  other arithmetic  11.9 us (6%)
  local copies, waits for them, and re-layouts  3.79 us (2%)
    ppermute x58, waiting for transfers between devices, shift(): return lax.ppermute(values, 'dp', shift_perm(axis, amount))  63 us
    ppermute x58, starting transfers between devices, shift(): return lax.ppermute(values, 'dp', shift_perm(axis, amount))  62.9 us
    pallas_call x9, Pallas kernels, call(): pl.pallas_call(kernel, out_shape=outs, in_specs=[pl.BlockSpec(memory_spac...  44.9 us
    sub x7, other arithmetic, adam_update(): parameter - learn_rate * first_hat / (jnp.sqrt(second_hat) + adam_epsilon)  6.71 us
  transfers between devices with their start and end apart: 59, of which 22 were waited for; matrix products, arithmetic and copies ran while one was open for 6% of the time, Pallas kernels for 21%

profile of v5, /device:TPU:1, one launch (start us, length us, event | category | flops | bytes accessed | tf_op | source)
XLA Modules:
  0.0 188.6 jit_solution(2215842842264078335)
XLA Ops:
  5.3 2.6 %collective-permute-start.3 = (bf16[40,1408]{1,0:T(8,128)(2,1)S(1)}, bf16[40,1408]{1,0:T(8,128)(2,1)S(1)}, u32[]{:S(2)}, u32[]{:S(2)}) collective-permute-start(bf16[40,1408]{1,0:T(8,128)(2,1)S(1)} %fusion.31), channel_id=1, source_target_pairs={{0,8},{1,9},{2,10},{3,11},{4,12},{5,13},{6,14},{7,15},{8,16},{9,17... | collective-permute-start | bytes 337928 | tf_op jit(solution)/shard_map/z1/ppermute | solution.py:33
  7.9 2.3 %collective-permute-start.2 = (bf16[40,1408]{1,0:T(8,128)(2,1)S(1)}, bf16[40,1408]{1,0:T(8,128)(2,1)S(1)}, u32[]{:S(2)}, u32[]{:S(2)}) collective-permute-start(bf16[40,1408]{1,0:T(8,128)(2,1)S(1)} %fusion.31), channel_id=1, source_target_pairs={{0,16},{1,17},{2,18},{3,19},{4,20},{5,21},{6,22},{7,23},{8,24},{9,... | collective-permute-start | bytes 337928 | tf_op jit(solution)/shard_map/z2/ppermute | solution.py:33
  11.3 2.0 %collective-permute-done.3 = bf16[40,1408]{1,0:T(8,128)(2,1)S(1)} collective-permute-done((bf16[40,1408]{1,0:T(8,128)(2,1)S(1)}, bf16[40,1408]{1,0:T(8,128)(2,1)S(1)}, u32[]{:S(2)}, u32[]{:S(2)}) %collective-permute-start.3) | collective-permute-done | bytes 112672 | tf_op jit(solution)/shard_map/z1/ppermute | solution.py:33
  13.3 5.0 %collective-permute-done.2 = bf16[40,1408]{1,0:T(8,128)(2,1)S(1)} collective-permute-done((bf16[40,1408]{1,0:T(8,128)(2,1)S(1)}, bf16[40,1408]{1,0:T(8,128)(2,1)S(1)}, u32[]{:S(2)}, u32[]{:S(2)}) %collective-permute-start.2) | collective-permute-done | bytes 112672 | tf_op jit(solution)/shard_map/z2/ppermute | solution.py:33
  19.6 2.7 %collective-permute-start.8 = (bf16[64,640]{1,0:T(8,128)(2,1)S(1)}, bf16[64,640]{1,0:T(8,128)(2,1)S(1)}, u32[]{:S(2)}, u32[]{:S(2)}) collective-permute-start(bf16[64,640]{1,0:T(8,128)(2,1)S(1)} %convert_element_type.268), channel_id=1, source_target_pairs={{0,8},{1,9},{2,10},{3,11},{4,12},{5,13},{6,14},{7,15},{8,16},{9,17... | collective-permute-start | bytes 245768 | tf_op jit(solution)/shard_map/z1/ppermute | solution.py:33
  25.7 4.4 %collective-permute-done.5 = bf16[2,40,1408]{2,1,0:T(8,128)(2,1)S(1)} collective-permute-done((bf16[2,40,1408]{2,1,0:T(8,128)(2,1)S(1)}, bf16[2,40,1408]{2,1,0:T(8,128)(2,1)S(1)}, u32[]{:S(2)}, u32[]{:S(2)}) %collective-permute-start.5) | collective-permute-done | bytes 225312 | tf_op jit(solution)/shard_map/y1/ppermute | solution.py:33
  35.7 2.2 %collective-permute-start.11 = (bf16[40,2048]{1,0:T(8,128)(2,1)S(1)}, bf16[40,2048]{1,0:T(8,128)(2,1)S(1)}, u32[]{:S(2)}, u32[]{:S(2)}) collective-permute-start(bf16[40,2048]{1,0:T(8,128)(2,1)S(1)} %pad_maximum_fusion.11), channel_id=1, source_target_pairs={{0,24},{1,25},{2,26},{3,27},{4,28},{5,29},{6,30},{7,31},{8,0},{9,1... | collective-permute-start | bytes 491528 | tf_op jit(solution)/shard_map/z3/ppermute | solution.py:33
  38.0 2.1 %collective-permute-done.13 = bf16[40,2048]{1,0:T(8,128)(2,1)S(1)} collective-permute-done((bf16[40,2048]{1,0:T(8,128)(2,1)S(1)}, bf16[40,2048]{1,0:T(8,128)(2,1)S(1)}, u32[]{:S(2)}, u32[]{:S(2)}) %collective-permute-start.13) | collective-permute-done | bytes 163872 | tf_op jit(solution)/shard_map/z1/ppermute | solution.py:33
  40.3 8.6 %collective-permute-done.12 = bf16[40,2048]{1,0:T(8,128)(2,1)S(1)} collective-permute-done((bf16[40,2048]{1,0:T(8,128)(2,1)S(1)}, bf16[40,2048]{1,0:T(8,128)(2,1)S(1)}, u32[]{:S(2)}, u32[]{:S(2)}) %collective-permute-start.12) | collective-permute-done | bytes 163872 | tf_op jit(solution)/shard_map/z2/ppermute | solution.py:33
  51.9 5.8 %collective-permute-done.14 = bf16[2,40,2048]{2,1,0:T(8,128)(2,1)S(1)} collective-permute-done((bf16[2,40,2048]{2,1,0:T(8,128)(2,1)S(1)}, bf16[2,40,2048]{2,1,0:T(8,128)(2,1)S(1)}, u32[]{:S(2)}, u32[]{:S(2)}) %collective-permute-start.14) | collective-permute-done | bytes 327712 | tf_op jit(solution)/shard_map/x1/ppermute | solution.py:33
  61.4 3.7 %shard_map.472 = (bf16[512,640]{1,0:T(8,128)(2,1)S(1)}, f32[4,512,256]{2,1,0:T(8,128)S(1)}, f32[2,512,256]{2,1,0:T(8,128)S(1)}, bf16[4,512,256]{2,1,0:T(8,128)(2...) custom-call(s32[4]{0:T(128)S(1)} %pad_add_fusion.coords_ref, ...), custom_call_target="tpu_custom_call" | custom-call | flops 5000000000 | bytes 20000000 | tf_op jit(solution)/shard_map/pallas_call | solution.py:485
  65.2 5.0 %shard_map.473 = (bf16[4,512,384]{2,1,0:T(8,128)(2,1)S(1)}, bf16[4,512,256]{2,1,0:T(8,128)(2,1)S(1)}, f32[512,640]{1,0:T(8,128)S(1)}, f32[512,640]{1,0:T(8,128)S(1)}, bf16[512,640]{1,0:T(8,128)(2,1)S(1)}) custom-call(s32[4]{0:T(128)S(1)} %pad_add_fusion.coords_ref, bf16[512,640]{1,0:T(8,128)(2,1)S(1)} %bitcast.143, s32[1,512]{1,0:T(1,128)S(1)} %copy-done, ...), custom_call_target="tpu_custom_call" | custom-call | flops 5000000000 | bytes 20000000 | tf_op jit(solution)/shard_map/pallas_call | solution.py:485
  70.2 5.6 %collective-permute-done.18.refs_1_ = bf16[2,2,40,2048]{3,2,1,0:T(8,128)(2,1)S(1)} collective-permute-done((bf16[2,2,40,2048]{3,2,1,0:T(8,128)(2,1)S(1)}, bf16[2,2,40,2048]{3,2,1,0:T(8,128)(2,1)S(1)}, u32[]{:S(2)}, u32[]{:S(2)}) %collective-permute-start.18) | collective-permute-done | bytes 655392 | tf_op jit(solution)/shard_map/y1/ppermute | solution.py:33
  80.4 2.3 %shard_map.474 = (f32[512,2048]{1,0:T(8,128)S(1)}, bf16[640,2048]{1,0:T(8,128)(2,1)S(1)}) custom-call(s32[4]{0:T(128)S(1)} %pad_add_fusion.coords_ref, bf16[512,640]{1,0:T(8,128)(2,1)S(1)} %get-tuple-element.202.h3_ref, bf16[2,2,40,2048]{3,2,1,0:T(8,128)(2,1)S(1)} %pad_maximum_fusion.refs_0_, bf16[2,2,40,2048]{3,2,1,0:T(8,128)(2,1)S(1)} %collective-permute-done.18.refs_1_, ...), custom_call_target="tpu_custom_call" | custom-call | flops 6000000000 | bytes 20000000 | tf_op jit(solution)/shard_map/pallas_call | solution.py:485
  83.4 5.1 %shard_map.475 = (bf16[512,2048]{1,0:T(8,128)(2,1)S(1)}, bf16[512,2048]{1,0:T(8,128)(2,1)S(1)}, bf16[512,2048]{1,0:T(8,128)(2,1)S(1)}, bf16[640,2048]{1,0:T(8,128)(2,1)S(1)}) custom-call(s32[4]{0:T(128)S(1)} %pad_add_fusion.coords_ref, bf16[512,640]{1,0:T(8,128)(2,1)S(1)} %get-tuple-element.202.h3_ref, f32[512,2048]{1,0:T(8,128)S(1)} %get-tuple-element.210.own_ref, ...), custom_call_target="tpu_custom_call" | custom-call | flops 3000000000 | bytes 10000000 | tf_op jit(solution)/shard_map/pallas_call | solution.py:485
  91.1 6.1 %shard_map.476 = (bf16[512,640]{1,0:T(8,128)(2,1)}, bf16[512,640]{1,0:T(8,128)(2,1)S(1)}, f32[8,640]{1,0:T(8,128)S(1)}, bf16[32,64,640]{2,1,0:T(8,128)(2,1)S(1)}...) custom-call(s32[4]{0:T(128)S(1)} %pad_add_fusion.coords_ref, ...), custom_call_target="tpu_custom_call" | custom-call | flops 6000000000 | bytes 20000000 | tf_op jit(solution)/shard_map/pallas_call | solution.py:485
  97.6 5.4 %shard_map.477 = (bf16[2,512,2048]{2,1,0:T(8,128)(2,1)S(1)}, bf16[4,2,2,40,2048]{4,3,2,1,0:T(8,128)(2,1)S(1)}, bf16[4,2,2,40,2048]{4,3,2,1,0:T(8,128)(2,1)S(1)}) custom-call(s32[4]{0:T(128)S(1)} %pad_add_fusion.coords_ref, bf16[512,640]{1,0:T(8,128)(2,1)S(1)} %get-tuple-element.225.dm_ref, bf16[32,64,640]{2,1,0:T(8,128)(2,1)S(1)} %get-tuple-element.226.wd_ref, ...), custom_call_target="tpu_custom_call" | custom-call | flops 8000000000 | bytes 20000000 | tf_op jit(solution)/shard_map/pallas_call | solution.py:485
  103.5 3.8 %collective-permute-start.36 = (bf16[4,64,640]{2,1,0:T(8,128)(2,1)S(1)}, bf16[4,64,640]{2,1,0:T(8,128)(2,1)S(1)}, u32[]{:S(2)}, u32[]{:S(2)}) collective-permute-start(bf16[4,64,640]{2,1,0:T(8,128)(2,1)S(1)} %get-tuple-element.339), channel_id=1, source_target_pairs={{0,8},{1,9},{2,10},{3,11},{4,12},{5,13},{6,14},{7,15},{8,16},{9,17... | collective-permute-start | bytes 983048 | tf_op jit(solution)/shard_map/z1/ppermute | solution.py:33
  107.3 5.5 %shard_map.478 = (f32[512,640]{1,0:T(8,128)S(1)}, bf16[512,640]{1,0:T(8,128)(2,1)S(1)}, f32[2,8,640]{2,1,0:T(8,128)S(1)}) custom-call(s32[4]{0:T(128)S(1)} %pad_add_fusion.coords_ref, bf16[2,512,2048]{2,1,0:T(8,128)(2,1)S(1)} %get-tuple-element.232.dgu_ref, f32[512,640]{1,0:T(8,128)S(1)} %get-tuple-element.219.mid_ref, ...), custom_call_target="tpu_custom_call" | custom-call | flops 8000000000 | bytes 20000000 | tf_op jit(solution)/shard_map/pallas_call | solution.py:485
  114.3 1.9 %collective-permute-start.37 = (bf16[4,64,640]{2,1,0:T(8,128)(2,1)S(1)}, bf16[4,64,640]{2,1,0:T(8,128)(2,1)S(1)}, u32[]{:S(2)}, u32[]{:S(2)}) collective-permute-start(bf16[4,64,640]{2,1,0:T(8,128)(2,1)S(1)} %get-tuple-element.246), channel_id=1, source_target_pairs={{0,24},{1,25},{2,26},{3,27},{4,28},{5,29},{6,30},{7,31},{8,0},{9,1... | collective-permute-start | bytes 983048 | tf_op jit(solution)/shard_map/z3/ppermute | solution.py:33
  117.3 7.2 %shard_map.479 = (bf16[2,512,768]{2,1,0:T(8,128)(2,1)S(1)}, f32[2,8,256]{2,1,0:T(8,128)S(1)}, bf16[32,32,640]{2,1,0:T(8,128)(2,1)S(1)}) custom-call(s32[4]{0:T(128)S(1)} %pad_add_fusion.coords_ref, bf16[512,640]{1,0:T(8,128)(2,1)S(1)} %get-tuple-element.240.da_ref, bf16[32,32,640]{2,1,0:T(8,128)(2,1)S(1)} %get-tuple-element.198.wo_ref, ...), custom_call_target="tpu_custom_call" | custom-call | flops 6000000000 | bytes 20000000 | tf_op jit(solution)/shard_map/pallas_call | solution.py:485
  124.5 2.2 %collective-permute-start.47 = (bf16[4,64,640]{2,1,0:T(8,128)(2,1)S(1)}, bf16[4,64,640]{2,1,0:T(8,128)(2,1)S(1)}, u32[]{:S(2)}, u32[]{:S(2)}) collective-permute-start(bf16[4,64,640]{2,1,0:T(8,128)(2,1)S(1)} %get-tuple-element.275), channel_id=1, source_target_pairs={{0,16},{1,17},{2,18},{3,19},{4,20},{5,21},{6,22},{7,23},{8,24},{9,... | collective-permute-start | bytes 983048 | tf_op jit(solution)/shard_map/z2/ppermute | solution.py:33
  126.7 4.6 %shard_map.480 = (f32[512,640]{1,0:T(8,128)}, bf16[4,2,2,40,1408]{4,3,2,1,0:T(8,128)(2,1)S(1)}, bf16[4,2,2,40,1408]{4,3,2,1,0:T(8,128)(2,1)S(1)}) custom-call(s32[4]{0:T(128)S(1)} %pad_add_fusion.coords_ref, bf16[2,512,768]{2,1,0:T(8,128)(2,1)S(1)} %get-tuple-element.247.dqkv_ref, bf16[512,640]{1,0:T(8,128)(2,1)S(1)} %get-tuple-element.248.h1_ref, ...), custom_call_target="tpu_custom_call" | custom-call | flops 6000000000 | bytes 20000000 | tf_op jit(solution)/shard_map/pallas_call | solution.py:485
  131.8 2.4 %collective-permute-start.40 = (bf16[4,2,2,40,1408]{4,3,2,1,0:T(8,128)(2,1)S(1)}, bf16[4,2,2,40,1408]{4,3,2,1,0:T(8,128)(2,1)S(1)}, u32[]{:S(2)}, u32[]{:S(2)}) collective-permute-start(bf16[4,2,2,40,1408]{4,3,2,1,0:T(8,128)(2,1)S(1)} %get-tuple-element.261), channel_id=1, source_target_pairs={{0,1},{1,0},{2,3},{3,2},{4,5},{5,4},{6,7},{7,6},{8,9},{9,8},{10,11... | collective-permute-start | bytes 5406728 | tf_op jit(solution)/shard_map/c1/ppermute | solution.py:33
  136.6 7.8 %collective-permute-done.41 = bf16[2,40,2048]{2,1,0:T(8,128)(2,1)S(1)} collective-permute-done((bf16[2,40,2048]{2,1,0:T(8,128)(2,1)S(1)}, bf16[2,40,2048]{2,1,0:T(8,128)(2,1)S(1)}, u32[]{:S(2)}, u32[]{:S(2)}) %collective-permute-start.41) | collective-permute-done | bytes 327712 | tf_op jit(solution)/shard_map/x1/ppermute | solution.py:33
  150.2 4.7 %collective-permute-done.45 = bf16[40,2048]{1,0:T(8,128)(2,1)S(1)} collective-permute-done((bf16[40,2048]{1,0:T(8,128)(2,1)S(1)}, bf16[40,2048]{1,0:T(8,128)(2,1)S(1)}, u32[]{:S(2)}, u32[]{:S(2)}) %collective-permute-start.45) | collective-permute-done | bytes 163872 | tf_op jit(solution)/shard_map/z1/ppermute | solution.py:33
  154.9 2.4 %collective-permute-done.43 = bf16[2,2,40,1408]{3,2,1,0:T(8,128)(2,1)S(1)} collective-permute-done((bf16[2,2,40,1408]{3,2,1,0:T(8,128)(2,1)S(1)}, bf16[2,2,40,1408]{3,2,1,0:T(8,128)(2,1)S(1)}, u32[]{:S(2)}, u32[]{:S(2)}) %collective-permute-start.43) | collective-permute-done | bytes 450592 | tf_op jit(solution)/shard_map/y1/ppermute | solution.py:33
  165.1 3.4 %collective-permute-start.55 = (bf16[64,640]{1,0:T(8,128)(2,1)S(1)}, bf16[64,640]{1,0:T(8,128)(2,1)S(1)}, u32[]{:S(2)}, u32[]{:S(2)}) collective-permute-start(bf16[64,640]{1,0:T(8,128)(2,1)S(1)} %get-tuple-element.346), channel_id=1, source_target_pairs={{0,2},{1,3},{2,0},{3,1},{4,6},{5,7},{6,4},{7,5},{8,10},{9,11},{10,... | collective-permute-start | bytes 245768 | tf_op jit(solution)/shard_map/x1/ppermute | solution.py:33
  168.7 2.0 %collective-permute-start.54 = (f32[20,2048]{1,0:T(8,128)S(1)}, f32[20,2048]{1,0:T(8,128)S(1)}, u32[]{:S(2)}, u32[]{:S(2)}) collective-permute-start(f32[20,2048]{1,0:T(8,128)S(1)} %slice_select_fusion), channel_id=1, source_target_pairs={{0,1},{1,0},{2,3},{3,2},{4,5},{5,4},{6,7},{7,6},{8,9},{9,8},{10,11... | collective-permute-start | bytes 491528 | tf_op jit(solution)/shard_map/c1/ppermute | solution.py:33
  171.8 3.0 %collective-permute-start.53 = (bf16[40,1408]{1,0:T(8,128)(2,1)S(1)}, bf16[40,1408]{1,0:T(8,128)(2,1)S(1)}, u32[]{:S(2)}, u32[]{:S(2)}) collective-permute-start(bf16[40,1408]{1,0:T(8,128)(2,1)S(1)} %get-tuple-element.356), channel_id=1, source_target_pairs={{0,24},{1,25},{2,26},{3,27},{4,28},{5,29},{6,30},{7,31},{8,0},{9,1... | collective-permute-start | bytes 337928 | tf_op jit(solution)/shard_map/z3/ppermute | solution.py:33
  175.3 2.3 %multiply_subtract_fusion = (f32[20,2,2048]{2,1,0:T(2,128)}, f32[20,2,2048]{2,1,0:T(2,128)}, f32[20,2,2048]{2,1,0:T(2,128)}, f32[20,2,2048]{2,1,0:T(2,128)}) fusion(f32[20,2,2048]{2,1,0:T(2,128)S(1)} %copy-done.3, f32[20,1,2048]{2,1,0:T(1,128)S(1)} %stack.174, f32[20,1,2048]{2,1,0:T(1,128)S(1)} %copy.59, f32[20,2,2048]{2,1,0:T(2,128)S(1)} %copy-done.6, ...), kind=kLoop, calls=%fused_computation.53 | loop fusion | flops 1228800 | bytes 2621440 | tf_op jit(solution)/shard_map/sub | solution.py:832
  178.9 3.9 %collective-permute-done.51 = bf16[40,1408]{1,0:T(8,128)(2,1)S(1)} collective-permute-done((bf16[40,1408]{1,0:T(8,128)(2,1)S(1)}, bf16[40,1408]{1,0:T(8,128)(2,1)S(1)}, u32[]{:S(2)}, u32[]{:S(2)}) %collective-permute-start.51) | collective-permute-done | bytes 112672 | tf_op jit(solution)/shard_map/z1/ppermute | solution.py:33
  (216 shorter events, 58.9 us)
Async XLA Ops:
  7.9 10.4 %collective-permute-start.2 = (bf16[40,1408]{1,0:T(8,128)(2,1)S(1)}, bf16[40,1408]{1,0:T(8,128)(2,1)S(1)}, u32[]{:S(2)}, u32[]{:S(2)}) collective-permute-start(bf16[40,1408]{1,0:T(8,128)(2,1)S(1)} %fusion.31), channel_id=1, source_target_pairs={{0,16},{1,17},{2,18},{3,19},{4,20},{5,21},{6,22},{7,23},{8,24},{9,... | collective-permute-start | bytes 337928 | tf_op jit(solution)/shard_map/z2/ppermute | solution.py:33
  19.6 10.5 %collective-permute-start.8 = (bf16[64,640]{1,0:T(8,128)(2,1)S(1)}, bf16[64,640]{1,0:T(8,128)(2,1)S(1)}, u32[]{:S(2)}, u32[]{:S(2)}) collective-permute-start(bf16[64,640]{1,0:T(8,128)(2,1)S(1)} %convert_element_type.268), channel_id=1, source_target_pairs={{0,8},{1,9},{2,10},{3,11},{4,12},{5,13},{6,14},{7,15},{8,16},{9,17... | collective-permute-start | bytes 245768 | tf_op jit(solution)/shard_map/z1/ppermute | solution.py:33
  30.6 18.3 %collective-permute-start.9 = (bf16[2,2,40,1408]{3,2,1,0:T(8,128)(2,1)S(1)}, bf16[2,2,40,1408]{3,2,1,0:T(8,128)(2,1)S(1)}, u32[]{:S(2)}, u32[]{:S(2)}) collective-permute-start(bf16[2,2,40,1408]{3,2,1,0:T(8,128)(2,1)S(1)} %pad_maximum_fusion.2.refs_0_), channel_id=1, source_target_pairs={{0,4},{1,5},{2,6},{3,7},{4,0},{5,1},{6,2},{7,3},{8,12},{9,13},{10,... | collective-permute-start | bytes 1351688 | tf_op jit(solution)/shard_map/y1/ppermute | solution.py:33
  31.8 17.1 %collective-permute-start.10 = (bf16[2,2,40,1408]{3,2,1,0:T(8,128)(2,1)S(1)}, bf16[2,2,40,1408]{3,2,1,0:T(8,128)(2,1)S(1)}, u32[]{:S(2)}, u32[]{:S(2)}) collective-permute-start(bf16[2,2,40,1408]{3,2,1,0:T(8,128)(2,1)S(1)} %pad_maximum_fusion.3.refs_2_), channel_id=1, source_target_pairs={{0,2},{1,3},{2,0},{3,1},{4,6},{5,7},{6,4},{7,5},{8,10},{9,11},{10,... | collective-permute-start | bytes 1351688 | tf_op jit(solution)/shard_map/x1/ppermute | solution.py:33
  35.7 13.2 %collective-permute-start.12 = (bf16[40,2048]{1,0:T(8,128)(2,1)S(1)}, bf16[40,2048]{1,0:T(8,128)(2,1)S(1)}, u32[]{:S(2)}, u32[]{:S(2)}) collective-permute-start(bf16[40,2048]{1,0:T(8,128)(2,1)S(1)} %pad_maximum_fusion.11), channel_id=1, source_target_pairs={{0,16},{1,17},{2,18},{3,19},{4,20},{5,21},{6,22},{7,23},{8,24},{9,... | collective-permute-start | bytes 491528 | tf_op jit(solution)/shard_map/z2/ppermute | solution.py:33
  35.7 13.2 %collective-permute-start.11 = (bf16[40,2048]{1,0:T(8,128)(2,1)S(1)}, bf16[40,2048]{1,0:T(8,128)(2,1)S(1)}, u32[]{:S(2)}, u32[]{:S(2)}) collective-permute-start(bf16[40,2048]{1,0:T(8,128)(2,1)S(1)} %pad_maximum_fusion.11), channel_id=1, source_target_pairs={{0,24},{1,25},{2,26},{3,27},{4,28},{5,29},{6,30},{7,31},{8,0},{9,1... | collective-permute-start | bytes 491528 | tf_op jit(solution)/shard_map/z3/ppermute | solution.py:33
  40.1 9.5 %collective-permute-start.17 = (bf16[2,64,640]{2,1,0:T(8,128)(2,1)S(1)}, bf16[2,64,640]{2,1,0:T(8,128)(2,1)S(1)}, u32[]{:S(2)}, u32[]{:S(2)}) collective-permute-start(bf16[2,64,640]{2,1,0:T(8,128)(2,1)S(1)} %get-tuple-element.361), channel_id=1, source_target_pairs={{0,4},{1,5},{2,6},{3,7},{4,0},{5,1},{6,2},{7,3},{8,12},{9,13},{10,... | collective-permute-start | bytes 491528 | tf_op jit(solution)/shard_map/y1/ppermute | solution.py:33
  49.3 9.9 %collective-permute-start.15 = (bf16[2,40,2048]{2,1,0:T(8,128)(2,1)S(1)}, bf16[2,40,2048]{2,1,0:T(8,128)(2,1)S(1)}, u32[]{:S(2)}, u32[]{:S(2)}) collective-permute-start(bf16[2,40,2048]{2,1,0:T(8,128)(2,1)S(1)} %get-tuple-element.351), channel_id=1, source_target_pairs={{0,4},{1,5},{2,6},{3,7},{4,0},{5,1},{6,2},{7,3},{8,12},{9,13},{10,... | collective-permute-start | bytes 983048 | tf_op jit(solution)/shard_map/y1/ppermute | solution.py:33
  49.6 10.0 %collective-permute-start.20 = (bf16[2,2,40,1408]{3,2,1,0:T(8,128)(2,1)S(1)}, bf16[2,2,40,1408]{3,2,1,0:T(8,128)(2,1)S(1)}, u32[]{:S(2)}, u32[]{:S(2)}) collective-permute-start(bf16[2,2,40,1408]{3,2,1,0:T(8,128)(2,1)S(1)} %pad_maximum_fusion.2.refs_0_), channel_id=1, source_target_pairs={{0,1},{1,0},{2,3},{3,2},{4,5},{5,4},{6,7},{7,6},{8,9},{9,8},{10,11... | collective-permute-start | bytes 1351688 | tf_op jit(solution)/shard_map/c1/ppermute | solution.py:33
  51.4 8.9 %collective-permute-start.22 = (bf16[2,2,40,1408]{3,2,1,0:T(8,128)(2,1)S(1)}, bf16[2,2,40,1408]{3,2,1,0:T(8,128)(2,1)S(1)}, u32[]{:S(2)}, u32[]{:S(2)}) collective-permute-start(bf16[2,2,40,1408]{3,2,1,0:T(8,128)(2,1)S(1)} %pad_maximum_fusion.3.refs_2_), channel_id=1, source_target_pairs={{0,1},{1,0},{2,3},{3,2},{4,5},{5,4},{6,7},{7,6},{8,9},{9,8},{10,11... | collective-permute-start | bytes 1351688 | tf_op jit(solution)/shard_map/c1/ppermute | solution.py:33
  59.3 10.8 %collective-permute-start.24 = (bf16[2,2,40,2048]{3,2,1,0:T(8,128)(2,1)S(1)}, bf16[2,2,40,2048]{3,2,1,0:T(8,128)(2,1)S(1)}, u32[]{:S(2)}, u32[]{:S(2)}) collective-permute-start(bf16[2,2,40,2048]{3,2,1,0:T(8,128)(2,1)S(1)} %pad_maximum_fusion.refs_0_), channel_id=1, source_target_pairs={{0,1},{1,0},{2,3},{3,2},{4,5},{5,4},{6,7},{7,6},{8,9},{9,8},{10,11... | collective-permute-start | bytes 1966088 | tf_op jit(solution)/shard_map/c1/ppermute | solution.py:33
  59.7 16.1 %collective-permute-start.18 = (bf16[2,2,40,2048]{3,2,1,0:T(8,128)(2,1)S(1)}, bf16[2,2,40,2048]{3,2,1,0:T(8,128)(2,1)S(1)}, u32[]{:S(2)}, u32[]{:S(2)}) collective-permute-start(bf16[2,2,40,2048]{3,2,1,0:T(8,128)(2,1)S(1)} %pad_maximum_fusion.refs_0_), channel_id=1, source_target_pairs={{0,4},{1,5},{2,6},{3,7},{4,0},{5,1},{6,2},{7,3},{8,12},{9,13},{10,... | collective-permute-start | bytes 1966088 | tf_op jit(solution)/shard_map/y1/ppermute | solution.py:33
  59.9 15.9 %collective-permute-start.25 = (bf16[2,2,40,2048]{3,2,1,0:T(8,128)(2,1)S(1)}, bf16[2,2,40,2048]{3,2,1,0:T(8,128)(2,1)S(1)}, u32[]{:S(2)}, u32[]{:S(2)}) collective-permute-start(bf16[2,2,40,2048]{3,2,1,0:T(8,128)(2,1)S(1)} %pad_maximum_fusion.1.refs_2_), channel_id=1, source_target_pairs={{0,1},{1,0},{2,3},{3,2},{4,5},{5,4},{6,7},{7,6},{8,9},{9,8},{10,11... | collective-permute-start | bytes 1966088 | tf_op jit(solution)/shard_map/c1/ppermute | solution.py:33
  60.4 16.3 %collective-permute-start.19 = (bf16[2,2,40,2048]{3,2,1,0:T(8,128)(2,1)S(1)}, bf16[2,2,40,2048]{3,2,1,0:T(8,128)(2,1)S(1)}, u32[]{:S(2)}, u32[]{:S(2)}) collective-permute-start(bf16[2,2,40,2048]{3,2,1,0:T(8,128)(2,1)S(1)} %pad_maximum_fusion.1.refs_2_), channel_id=1, source_target_pairs={{0,2},{1,3},{2,0},{3,1},{4,6},{5,7},{6,4},{7,5},{8,10},{9,11},{10,... | collective-permute-start | bytes 1966088 | tf_op jit(solution)/shard_map/x1/ppermute | solution.py:33
  77.5 11.9 %collective-permute-start.30 = (bf16[2,2,64,640]{3,2,1,0:T(8,128)(2,1)S(1)}, bf16[2,2,64,640]{3,2,1,0:T(8,128)(2,1)S(1)}, u32[]{:S(2)}, u32[]{:S(2)}) collective-permute-start(bf16[2,2,64,640]{3,2,1,0:T(8,128)(2,1)S(1)} %pad_maximum_fusion.6.refs_0_), channel_id=1, source_target_pairs={{0,1},{1,0},{2,3},{3,2},{4,5},{5,4},{6,7},{7,6},{8,9},{9,8},{10,11... | collective-permute-start | bytes 983048 | tf_op jit(solution)/shard_map/c1/ppermute | solution.py:33
  78.0 10.4 %collective-permute-start.28 = (bf16[2,2,64,640]{3,2,1,0:T(8,128)(2,1)S(1)}, bf16[2,2,64,640]{3,2,1,0:T(8,128)(2,1)S(1)}, u32[]{:S(2)}, u32[]{:S(2)}) collective-permute-start(bf16[2,2,64,640]{3,2,1,0:T(8,128)(2,1)S(1)} %pad_maximum_fusion.6.refs_0_), channel_id=1, source_target_pairs={{0,4},{1,5},{2,6},{3,7},{4,0},{5,1},{6,2},{7,3},{8,12},{9,13},{10,... | collective-permute-start | bytes 983048 | tf_op jit(solution)/shard_map/y1/ppermute | solution.py:33
  79.3 9.2 %collective-permute-start.29 = (bf16[2,2,64,640]{3,2,1,0:T(8,128)(2,1)S(1)}, bf16[2,2,64,640]{3,2,1,0:T(8,128)(2,1)S(1)}, u32[]{:S(2)}, u32[]{:S(2)}) collective-permute-start(bf16[2,2,64,640]{3,2,1,0:T(8,128)(2,1)S(1)} %pad_maximum_fusion.7.refs_2_), channel_id=1, source_target_pairs={{0,2},{1,3},{2,0},{3,1},{4,6},{5,7},{6,4},{7,5},{8,10},{9,11},{10,... | collective-permute-start | bytes 983048 | tf_op jit(solution)/shard_map/x1/ppermute | solution.py:33
  103.0 11.2 %collective-permute-start.35 = (bf16[4,2,2,40,2048]{4,3,2,1,0:T(8,128)(2,1)S(1)}, bf16[4,2,2,40,2048]{4,3,2,1,0:T(8,128)(2,1)S(1)}, u32[]{:S(2)}, u32[]{:S(2)}) collective-permute-start(bf16[4,2,2,40,2048]{4,3,2,1,0:T(8,128)(2,1)S(1)} %get-tuple-element.237), channel_id=1, source_target_pairs={{0,1},{1,0},{2,3},{3,2},{4,5},{5,4},{6,7},{7,6},{8,9},{9,8},{10,11... | collective-permute-start | bytes 7864328 | tf_op jit(solution)/shard_map/c1/ppermute | solution.py:33
  103.5 10.8 %collective-permute-start.36 = (bf16[4,64,640]{2,1,0:T(8,128)(2,1)S(1)}, bf16[4,64,640]{2,1,0:T(8,128)(2,1)S(1)}, u32[]{:S(2)}, u32[]{:S(2)}) collective-permute-start(bf16[4,64,640]{2,1,0:T(8,128)(2,1)S(1)} %get-tuple-element.339), channel_id=1, source_target_pairs={{0,8},{1,9},{2,10},{3,11},{4,12},{5,13},{6,14},{7,15},{8,16},{9,17... | collective-permute-start | bytes 983048 | tf_op jit(solution)/shard_map/z1/ppermute | solution.py:33
  114.3 10.2 %collective-permute-start.37 = (bf16[4,64,640]{2,1,0:T(8,128)(2,1)S(1)}, bf16[4,64,640]{2,1,0:T(8,128)(2,1)S(1)}, u32[]{:S(2)}, u32[]{:S(2)}) collective-permute-start(bf16[4,64,640]{2,1,0:T(8,128)(2,1)S(1)} %get-tuple-element.246), channel_id=1, source_target_pairs={{0,24},{1,25},{2,26},{3,27},{4,28},{5,29},{6,30},{7,31},{8,0},{9,1... | collective-permute-start | bytes 983048 | tf_op jit(solution)/shard_map/z3/ppermute | solution.py:33
  116.7 15.1 %collective-permute-start.39 = (bf16[2,2,40,2048]{3,2,1,0:T(8,128)(2,1)S(1)}, bf16[2,2,40,2048]{3,2,1,0:T(8,128)(2,1)S(1)}, u32[]{:S(2)}, u32[]{:S(2)}) collective-permute-start(bf16[2,2,40,2048]{3,2,1,0:T(8,128)(2,1)S(1)} %get-tuple-element.331), channel_id=1, source_target_pairs={{0,2},{1,3},{2,0},{3,1},{4,6},{5,7},{6,4},{7,5},{8,10},{9,11},{10,... | collective-permute-start | bytes 1966088 | tf_op jit(solution)/shard_map/x1/ppermute | solution.py:33
  117.1 14.8 %collective-permute-start.38 = (bf16[2,2,40,2048]{3,2,1,0:T(8,128)(2,1)S(1)}, bf16[2,2,40,2048]{3,2,1,0:T(8,128)(2,1)S(1)}, u32[]{:S(2)}, u32[]{:S(2)}) collective-permute-start(bf16[2,2,40,2048]{3,2,1,0:T(8,128)(2,1)S(1)} %get-tuple-element.332), channel_id=1, source_target_pairs={{0,4},{1,5},{2,6},{3,7},{4,0},{5,1},{6,2},{7,3},{8,12},{9,13},{10,... | collective-permute-start | bytes 1966088 | tf_op jit(solution)/shard_map/y1/ppermute | solution.py:33
  124.5 24.0 %collective-permute-start.47 = (bf16[4,64,640]{2,1,0:T(8,128)(2,1)S(1)}, bf16[4,64,640]{2,1,0:T(8,128)(2,1)S(1)}, u32[]{:S(2)}, u32[]{:S(2)}) collective-permute-start(bf16[4,64,640]{2,1,0:T(8,128)(2,1)S(1)} %get-tuple-element.275), channel_id=1, source_target_pairs={{0,16},{1,17},{2,18},{3,19},{4,20},{5,21},{6,22},{7,23},{8,24},{9,... | collective-permute-start | bytes 983048 | tf_op jit(solution)/shard_map/z2/ppermute | solution.py:33
  131.8 13.4 %collective-permute-start.40 = (bf16[4,2,2,40,1408]{4,3,2,1,0:T(8,128)(2,1)S(1)}, bf16[4,2,2,40,1408]{4,3,2,1,0:T(8,128)(2,1)S(1)}, u32[]{:S(2)}, u32[]{:S(2)}) collective-permute-start(bf16[4,2,2,40,1408]{4,3,2,1,0:T(8,128)(2,1)S(1)} %get-tuple-element.261), channel_id=1, source_target_pairs={{0,1},{1,0},{2,3},{3,2},{4,5},{5,4},{6,7},{7,6},{8,9},{9,8},{10,11... | collective-permute-start | bytes 5406728 | tf_op jit(solution)/shard_map/c1/ppermute | solution.py:33
  134.9 9.4 %collective-permute-start.41 = (bf16[2,40,2048]{2,1,0:T(8,128)(2,1)S(1)}, bf16[2,40,2048]{2,1,0:T(8,128)(2,1)S(1)}, u32[]{:S(2)}, u32[]{:S(2)}) collective-permute-start(bf16[2,40,2048]{2,1,0:T(8,128)(2,1)S(1)} %fusion.13), channel_id=1, source_target_pairs={{0,2},{1,3},{2,0},{3,1},{4,6},{5,7},{6,4},{7,5},{8,10},{9,11},{10,... | collective-permute-start | bytes 983048 | tf_op jit(solution)/shard_map/x1/ppermute | solution.py:33
  136.2 9.1 %collective-permute-start.42 = (bf16[2,40,2048]{2,1,0:T(8,128)(2,1)S(1)}, bf16[2,40,2048]{2,1,0:T(8,128)(2,1)S(1)}, u32[]{:S(2)}, u32[]{:S(2)}) collective-permute-start(bf16[2,40,2048]{2,1,0:T(8,128)(2,1)S(1)} %fusion.14), channel_id=1, source_target_pairs={{0,4},{1,5},{2,6},{3,7},{4,0},{5,1},{6,2},{7,3},{8,12},{9,13},{10,... | collective-permute-start | bytes 983048 | tf_op jit(solution)/shard_map/y1/ppermute | solution.py:33
  147.1 10.2 %collective-permute-start.43 = (bf16[2,2,40,1408]{3,2,1,0:T(8,128)(2,1)S(1)}, bf16[2,2,40,1408]{3,2,1,0:T(8,128)(2,1)S(1)}, u32[]{:S(2)}, u32[]{:S(2)}) collective-permute-start(bf16[2,2,40,1408]{3,2,1,0:T(8,128)(2,1)S(1)} %get-tuple-element.269), channel_id=1, source_target_pairs={{0,4},{1,5},{2,6},{3,7},{4,0},{5,1},{6,2},{7,3},{8,12},{9,13},{10,... | collective-permute-start | bytes 1351688 | tf_op jit(solution)/shard_map/y1/ppermute | solution.py:33
  147.3 10.0 %collective-permute-start.44 = (bf16[2,2,40,1408]{3,2,1,0:T(8,128)(2,1)S(1)}, bf16[2,2,40,1408]{3,2,1,0:T(8,128)(2,1)S(1)}, u32[]{:S(2)}, u32[]{:S(2)}) collective-permute-start(bf16[2,2,40,1408]{3,2,1,0:T(8,128)(2,1)S(1)} %get-tuple-element.270), channel_id=1, source_target_pairs={{0,2},{1,3},{2,0},{3,1},{4,6},{5,7},{6,4},{7,5},{8,10},{9,11},{10,... | collective-permute-start | bytes 1351688 | tf_op jit(solution)/shard_map/x1/ppermute | solution.py:33
  159.1 9.3 %collective-permute-start.48 = (bf16[2,40,1408]{2,1,0:T(8,128)(2,1)S(1)}, bf16[2,40,1408]{2,1,0:T(8,128)(2,1)S(1)}, u32[]{:S(2)}, u32[]{:S(2)}) collective-permute-start(bf16[2,40,1408]{2,1,0:T(8,128)(2,1)S(1)} %fusion.18), channel_id=1, source_target_pairs={{0,2},{1,3},{2,0},{3,1},{4,6},{5,7},{6,4},{7,5},{8,10},{9,11},{10,... | collective-permute-start | bytes 675848 | tf_op jit(solution)/shard_map/x1/ppermute | solution.py:33
  161.6 13.5 %collective-permute-start.57 = (bf16[64,640]{1,0:T(8,128)(2,1)S(1)}, bf16[64,640]{1,0:T(8,128)(2,1)S(1)}, u32[]{:S(2)}, u32[]{:S(2)}) collective-permute-start(bf16[64,640]{1,0:T(8,128)(2,1)S(1)} %get-tuple-element.344), channel_id=1, source_target_pairs={{0,6},{1,7},{2,4},{3,5},{4,2},{5,3},{6,0},{7,1},{8,14},{9,15},{10,... | collective-permute-start | bytes 245768 | tf_op jit(solution)/shard_map/xy/ppermute | solution.py:531
  162.1 15.5 %collective-permute-start.56 = (bf16[64,640]{1,0:T(8,128)(2,1)S(1)}, bf16[64,640]{1,0:T(8,128)(2,1)S(1)}, u32[]{:S(2)}, u32[]{:S(2)}) collective-permute-start(bf16[64,640]{1,0:T(8,128)(2,1)S(1)} %get-tuple-element.345), channel_id=1, source_target_pairs={{0,4},{1,5},{2,6},{3,7},{4,0},{5,1},{6,2},{7,3},{8,12},{9,13},{10,... | collective-permute-start | bytes 245768 | tf_op jit(solution)/shard_map/y1/ppermute | solution.py:33
  165.1 12.5 %collective-permute-start.55 = (bf16[64,640]{1,0:T(8,128)(2,1)S(1)}, bf16[64,640]{1,0:T(8,128)(2,1)S(1)}, u32[]{:S(2)}, u32[]{:S(2)}) collective-permute-start(bf16[64,640]{1,0:T(8,128)(2,1)S(1)} %get-tuple-element.346), channel_id=1, source_target_pairs={{0,2},{1,3},{2,0},{3,1},{4,6},{5,7},{6,4},{7,5},{8,10},{9,11},{10,... | collective-permute-start | bytes 245768 | tf_op jit(solution)/shard_map/x1/ppermute | solution.py:33
  (51 other events, 294.2 us)

commit v6 on v5

--- a/solution.py
+++ b/solution.py
@@ -324,7 +324,7 @@
         dm_ref[rows, :] = pulled.astype(BF)
         return carry + fold_rows(term)
 
-    gain_ref[...] = chunks(512, 32, finish, jnp.zeros((8, 640), jnp.float32))
+    gain_ref[...] = chunks(512, 16, finish, jnp.zeros((8, 640), jnp.float32))
     for block in range(8):
         grad = dot_left_t(hidden_ref[:, 256 * block : 256 * block + 256], dm_ref[...])
         natural_ref[4 * block : 4 * block + 4] = grad.astype(BF).reshape(4, 64, 640)
@@ -385,7 +385,7 @@
         return carry[0] + fold_rows(term_one), carry[1] + fold_rows(term_two)
 
     zero = jnp.zeros((8, 640), jnp.float32)
-    gain_ref[0], gain_ref[1] = chunks(512, 32, pull, (zero, zero))
+    gain_ref[0], gain_ref[1] = chunks(512, 16, pull, (zero, zero))
 
 
 def attention_backward(
@@ -437,7 +437,7 @@
         return query_sum, key_sum + fold_rows(term)
 
     zero = jnp.zeros((8, 256), jnp.float32)
-    gain_ref[0], gain_ref[1] = chunks(512, 32, pull, (zero, zero))
+    gain_ref[0], gain_ref[1] = chunks(512, 16, pull, (zero, zero))
 
 
 def input_backward(

time: 192 us -> 194 us (1.010)
  Pallas kernels: 44.9 us -> 47 us
    ppermute x58, starting transfers between devices: 62.9 us -> 60.3 us  [shift(): return lax.ppermute(values, 'dp', shift_perm(axis, amount))]
    pallas_call x9, Pallas kernels: 44.9 us -> 47 us  [call(): pl.pallas_call(kernel, out_shape=outs, in_specs=[pl.BlockSpec(memory_spac...]
  transfers between devices with their start and end apart: 59 -> 59, of which waited for: 22 -> 23; matrix products, arithmetic and copies ran while one was open for 6% -> 5% of each run, Pallas kernels for 21% -> 21%
where the time goes in v6:
time: 194 us; the launch traced here: 191 us
  waiting for transfers between devices  64.8 us (33%)
  starting transfers between devices  61.8 us (32%)
  Pallas kernels  47 us (24%)
  other arithmetic  11.9 us (6%)
  local copies, waits for them, and re-layouts  3.79 us (2%)
    ppermute x58, waiting for transfers between devices, shift(): return lax.ppermute(values, 'dp', shift_perm(axis, amount))  64.7 us
    ppermute x58, starting transfers between devices, shift(): return lax.ppermute(values, 'dp', shift_perm(axis, amount))  60.3 us
    pallas_call x9, Pallas kernels, call(): pl.pallas_call(kernel, out_shape=outs, in_specs=[pl.BlockSpec(memory_spac...  47 us
    sub x7, other arithmetic, adam_update(): parameter - learn_rate * first_hat / (jnp.sqrt(second_hat) + adam_epsilon)  6.71 us
  transfers between devices with their start and end apart: 59, of which 23 were waited for; matrix products, arithmetic and copies ran while one was open for 5% of the time, Pallas kernels for 21%

profile of v6, /device:TPU:1, one launch (start us, length us, event | category | flops | bytes accessed | tf_op | source)
XLA Modules:
  0.0 190.8 jit_solution(3565234485802782819)
XLA Ops:
  5.3 2.6 %collective-permute-start.3 = (bf16[40,1408]{1,0:T(8,128)(2,1)S(1)}, bf16[40,1408]{1,0:T(8,128)(2,1)S(1)}, u32[]{:S(2)}, u32[]{:S(2)}) collective-permute-start(bf16[40,1408]{1,0:T(8,128)(2,1)S(1)} %fusion.31), channel_id=1, source_target_pairs={{0,8},{1,9},{2,10},{3,11},{4,12},{5,13},{6,14},{7,15},{8,16},{9,17... | collective-permute-start | bytes 337928 | tf_op jit(solution)/shard_map/z1/ppermute | solution.py:33
  7.9 2.3 %collective-permute-start.2 = (bf16[40,1408]{1,0:T(8,128)(2,1)S(1)}, bf16[40,1408]{1,0:T(8,128)(2,1)S(1)}, u32[]{:S(2)}, u32[]{:S(2)}) collective-permute-start(bf16[40,1408]{1,0:T(8,128)(2,1)S(1)} %fusion.31), channel_id=1, source_target_pairs={{0,16},{1,17},{2,18},{3,19},{4,20},{5,21},{6,22},{7,23},{8,24},{9,... | collective-permute-start | bytes 337928 | tf_op jit(solution)/shard_map/z2/ppermute | solution.py:33
  11.3 2.0 %collective-permute-done.3 = bf16[40,1408]{1,0:T(8,128)(2,1)S(1)} collective-permute-done((bf16[40,1408]{1,0:T(8,128)(2,1)S(1)}, bf16[40,1408]{1,0:T(8,128)(2,1)S(1)}, u32[]{:S(2)}, u32[]{:S(2)}) %collective-permute-start.3) | collective-permute-done | bytes 112672 | tf_op jit(solution)/shard_map/z1/ppermute | solution.py:33
  13.3 5.0 %collective-permute-done.2 = bf16[40,1408]{1,0:T(8,128)(2,1)S(1)} collective-permute-done((bf16[40,1408]{1,0:T(8,128)(2,1)S(1)}, bf16[40,1408]{1,0:T(8,128)(2,1)S(1)}, u32[]{:S(2)}, u32[]{:S(2)}) %collective-permute-start.2) | collective-permute-done | bytes 112672 | tf_op jit(solution)/shard_map/z2/ppermute | solution.py:33
  19.6 2.7 %collective-permute-start.8 = (bf16[64,640]{1,0:T(8,128)(2,1)S(1)}, bf16[64,640]{1,0:T(8,128)(2,1)S(1)}, u32[]{:S(2)}, u32[]{:S(2)}) collective-permute-start(bf16[64,640]{1,0:T(8,128)(2,1)S(1)} %convert_element_type.268), channel_id=1, source_target_pairs={{0,8},{1,9},{2,10},{3,11},{4,12},{5,13},{6,14},{7,15},{8,16},{9,17... | collective-permute-start | bytes 245768 | tf_op jit(solution)/shard_map/z1/ppermute | solution.py:33
  25.7 4.4 %collective-permute-done.5 = bf16[2,40,1408]{2,1,0:T(8,128)(2,1)S(1)} collective-permute-done((bf16[2,40,1408]{2,1,0:T(8,128)(2,1)S(1)}, bf16[2,40,1408]{2,1,0:T(8,128)(2,1)S(1)}, u32[]{:S(2)}, u32[]{:S(2)}) %collective-permute-start.5) | collective-permute-done | bytes 225312 | tf_op jit(solution)/shard_map/y1/ppermute | solution.py:33
  35.7 2.2 %collective-permute-start.11 = (bf16[40,2048]{1,0:T(8,128)(2,1)S(1)}, bf16[40,2048]{1,0:T(8,128)(2,1)S(1)}, u32[]{:S(2)}, u32[]{:S(2)}) collective-permute-start(bf16[40,2048]{1,0:T(8,128)(2,1)S(1)} %pad_maximum_fusion.11), channel_id=1, source_target_pairs={{0,24},{1,25},{2,26},{3,27},{4,28},{5,29},{6,30},{7,31},{8,0},{9,1... | collective-permute-start | bytes 491528 | tf_op jit(solution)/shard_map/z3/ppermute | solution.py:33
  38.0 2.1 %collective-permute-done.13 = bf16[40,2048]{1,0:T(8,128)(2,1)S(1)} collective-permute-done((bf16[40,2048]{1,0:T(8,128)(2,1)S(1)}, bf16[40,2048]{1,0:T(8,128)(2,1)S(1)}, u32[]{:S(2)}, u32[]{:S(2)}) %collective-permute-start.13) | collective-permute-done | bytes 163872 | tf_op jit(solution)/shard_map/z1/ppermute | solution.py:33
  40.3 8.6 %collective-permute-done.12 = bf16[40,2048]{1,0:T(8,128)(2,1)S(1)} collective-permute-done((bf16[40,2048]{1,0:T(8,128)(2,1)S(1)}, bf16[40,2048]{1,0:T(8,128)(2,1)S(1)}, u32[]{:S(2)}, u32[]{:S(2)}) %collective-permute-start.12) | collective-permute-done | bytes 163872 | tf_op jit(solution)/shard_map/z2/ppermute | solution.py:33
  51.9 5.8 %collective-permute-done.14 = bf16[2,40,2048]{2,1,0:T(8,128)(2,1)S(1)} collective-permute-done((bf16[2,40,2048]{2,1,0:T(8,128)(2,1)S(1)}, bf16[2,40,2048]{2,1,0:T(8,128)(2,1)S(1)}, u32[]{:S(2)}, u32[]{:S(2)}) %collective-permute-start.14) | collective-permute-done | bytes 327712 | tf_op jit(solution)/shard_map/x1/ppermute | solution.py:33
  61.4 3.7 %shard_map.472 = (bf16[512,640]{1,0:T(8,128)(2,1)S(1)}, f32[4,512,256]{2,1,0:T(8,128)S(1)}, f32[2,512,256]{2,1,0:T(8,128)S(1)}, bf16[4,512,256]{2,1,0:T(8,128)(2...) custom-call(s32[4]{0:T(128)S(1)} %pad_add_fusion.coords_ref, ...), custom_call_target="tpu_custom_call" | custom-call | flops 5000000000 | bytes 20000000 | tf_op jit(solution)/shard_map/pallas_call | solution.py:485
  65.2 5.0 %shard_map.473 = (bf16[4,512,384]{2,1,0:T(8,128)(2,1)S(1)}, bf16[4,512,256]{2,1,0:T(8,128)(2,1)S(1)}, f32[512,640]{1,0:T(8,128)S(1)}, f32[512,640]{1,0:T(8,128)S(1)}, bf16[512,640]{1,0:T(8,128)(2,1)S(1)}) custom-call(s32[4]{0:T(128)S(1)} %pad_add_fusion.coords_ref, bf16[512,640]{1,0:T(8,128)(2,1)S(1)} %bitcast.143, s32[1,512]{1,0:T(1,128)S(1)} %copy-done, ...), custom_call_target="tpu_custom_call" | custom-call | flops 5000000000 | bytes 20000000 | tf_op jit(solution)/shard_map/pallas_call | solution.py:485
  70.2 5.6 %collective-permute-done.18.refs_1_ = bf16[2,2,40,2048]{3,2,1,0:T(8,128)(2,1)S(1)} collective-permute-done((bf16[2,2,40,2048]{3,2,1,0:T(8,128)(2,1)S(1)}, bf16[2,2,40,2048]{3,2,1,0:T(8,128)(2,1)S(1)}, u32[]{:S(2)}, u32[]{:S(2)}) %collective-permute-start.18) | collective-permute-done | bytes 655392 | tf_op jit(solution)/shard_map/y1/ppermute | solution.py:33
  80.4 2.3 %shard_map.474 = (f32[512,2048]{1,0:T(8,128)S(1)}, bf16[640,2048]{1,0:T(8,128)(2,1)S(1)}) custom-call(s32[4]{0:T(128)S(1)} %pad_add_fusion.coords_ref, bf16[512,640]{1,0:T(8,128)(2,1)S(1)} %get-tuple-element.202.h3_ref, bf16[2,2,40,2048]{3,2,1,0:T(8,128)(2,1)S(1)} %pad_maximum_fusion.refs_0_, bf16[2,2,40,2048]{3,2,1,0:T(8,128)(2,1)S(1)} %collective-permute-done.18.refs_1_, ...), custom_call_target="tpu_custom_call" | custom-call | flops 6000000000 | bytes 20000000 | tf_op jit(solution)/shard_map/pallas_call | solution.py:485
  83.4 4.9 %shard_map.475 = (bf16[512,2048]{1,0:T(8,128)(2,1)S(1)}, bf16[512,2048]{1,0:T(8,128)(2,1)S(1)}, bf16[512,2048]{1,0:T(8,128)(2,1)S(1)}, bf16[640,2048]{1,0:T(8,128)(2,1)S(1)}) custom-call(s32[4]{0:T(128)S(1)} %pad_add_fusion.coords_ref, bf16[512,640]{1,0:T(8,128)(2,1)S(1)} %get-tuple-element.202.h3_ref, f32[512,2048]{1,0:T(8,128)S(1)} %get-tuple-element.210.own_ref, ...), custom_call_target="tpu_custom_call" | custom-call | flops 3000000000 | bytes 10000000 | tf_op jit(solution)/shard_map/pallas_call | solution.py:485
  91.1 6.1 %shard_map.476 = (bf16[512,640]{1,0:T(8,128)(2,1)}, bf16[512,640]{1,0:T(8,128)(2,1)S(1)}, f32[8,640]{1,0:T(8,128)S(1)}, bf16[32,64,640]{2,1,0:T(8,128)(2,1)S(1)}...) custom-call(s32[4]{0:T(128)S(1)} %pad_add_fusion.coords_ref, ...), custom_call_target="tpu_custom_call" | custom-call | flops 6000000000 | bytes 20000000 | tf_op jit(solution)/shard_map/pallas_call | solution.py:485
  97.6 5.4 %shard_map.477 = (bf16[2,512,2048]{2,1,0:T(8,128)(2,1)S(1)}, bf16[4,2,2,40,2048]{4,3,2,1,0:T(8,128)(2,1)S(1)}, bf16[4,2,2,40,2048]{4,3,2,1,0:T(8,128)(2,1)S(1)}) custom-call(s32[4]{0:T(128)S(1)} %pad_add_fusion.coords_ref, bf16[512,640]{1,0:T(8,128)(2,1)S(1)} %get-tuple-element.225.dm_ref, bf16[32,64,640]{2,1,0:T(8,128)(2,1)S(1)} %get-tuple-element.226.wd_ref, ...), custom_call_target="tpu_custom_call" | custom-call | flops 8000000000 | bytes 20000000 | tf_op jit(solution)/shard_map/pallas_call | solution.py:485
  103.5 3.8 %collective-permute-start.36 = (bf16[4,64,640]{2,1,0:T(8,128)(2,1)S(1)}, bf16[4,64,640]{2,1,0:T(8,128)(2,1)S(1)}, u32[]{:S(2)}, u32[]{:S(2)}) collective-permute-start(bf16[4,64,640]{2,1,0:T(8,128)(2,1)S(1)} %get-tuple-element.339), channel_id=1, source_target_pairs={{0,8},{1,9},{2,10},{3,11},{4,12},{5,13},{6,14},{7,15},{8,16},{9,17... | collective-permute-start | bytes 983048 | tf_op jit(solution)/shard_map/z1/ppermute | solution.py:33
  107.4 5.5 %shard_map.478 = (f32[512,640]{1,0:T(8,128)S(1)}, bf16[512,640]{1,0:T(8,128)(2,1)S(1)}, f32[2,8,640]{2,1,0:T(8,128)S(1)}) custom-call(s32[4]{0:T(128)S(1)} %pad_add_fusion.coords_ref, bf16[2,512,2048]{2,1,0:T(8,128)(2,1)S(1)} %get-tuple-element.232.dgu_ref, f32[512,640]{1,0:T(8,128)S(1)} %get-tuple-element.219.mid_ref, ...), custom_call_target="tpu_custom_call" | custom-call | flops 8000000000 | bytes 20000000 | tf_op jit(solution)/shard_map/pallas_call | solution.py:485
  114.3 2.1 %collective-permute-start.37 = (bf16[4,64,640]{2,1,0:T(8,128)(2,1)S(1)}, bf16[4,64,640]{2,1,0:T(8,128)(2,1)S(1)}, u32[]{:S(2)}, u32[]{:S(2)}) collective-permute-start(bf16[4,64,640]{2,1,0:T(8,128)(2,1)S(1)} %get-tuple-element.246), channel_id=1, source_target_pairs={{0,24},{1,25},{2,26},{3,27},{4,28},{5,29},{6,30},{7,31},{8,0},{9,1... | collective-permute-start | bytes 983048 | tf_op jit(solution)/shard_map/z3/ppermute | solution.py:33
  117.5 9.4 %shard_map.479 = (bf16[2,512,768]{2,1,0:T(8,128)(2,1)S(1)}, f32[2,8,256]{2,1,0:T(8,128)S(1)}, bf16[32,32,640]{2,1,0:T(8,128)(2,1)S(1)}) custom-call(s32[4]{0:T(128)S(1)} %pad_add_fusion.coords_ref, bf16[512,640]{1,0:T(8,128)(2,1)S(1)} %get-tuple-element.240.da_ref, bf16[32,32,640]{2,1,0:T(8,128)(2,1)S(1)} %get-tuple-element.198.wo_ref, ...), custom_call_target="tpu_custom_call" | custom-call | flops 6000000000 | bytes 20000000 | tf_op jit(solution)/shard_map/pallas_call | solution.py:485
  126.8 2.3 %collective-permute-start.47 = (bf16[4,64,640]{2,1,0:T(8,128)(2,1)S(1)}, bf16[4,64,640]{2,1,0:T(8,128)(2,1)S(1)}, u32[]{:S(2)}, u32[]{:S(2)}) collective-permute-start(bf16[4,64,640]{2,1,0:T(8,128)(2,1)S(1)} %get-tuple-element.275), channel_id=1, source_target_pairs={{0,16},{1,17},{2,18},{3,19},{4,20},{5,21},{6,22},{7,23},{8,24},{9,... | collective-permute-start | bytes 983048 | tf_op jit(solution)/shard_map/z2/ppermute | solution.py:33
  129.1 4.6 %shard_map.480 = (f32[512,640]{1,0:T(8,128)}, bf16[4,2,2,40,1408]{4,3,2,1,0:T(8,128)(2,1)S(1)}, bf16[4,2,2,40,1408]{4,3,2,1,0:T(8,128)(2,1)S(1)}) custom-call(s32[4]{0:T(128)S(1)} %pad_add_fusion.coords_ref, bf16[2,512,768]{2,1,0:T(8,128)(2,1)S(1)} %get-tuple-element.247.dqkv_ref, bf16[512,640]{1,0:T(8,128)(2,1)S(1)} %get-tuple-element.248.h1_ref, ...), custom_call_target="tpu_custom_call" | custom-call | flops 6000000000 | bytes 20000000 | tf_op jit(solution)/shard_map/pallas_call | solution.py:485
  133.7 2.3 %collective-permute-start.40 = (bf16[4,2,2,40,1408]{4,3,2,1,0:T(8,128)(2,1)S(1)}, bf16[4,2,2,40,1408]{4,3,2,1,0:T(8,128)(2,1)S(1)}, u32[]{:S(2)}, u32[]{:S(2)}) collective-permute-start(bf16[4,2,2,40,1408]{4,3,2,1,0:T(8,128)(2,1)S(1)} %get-tuple-element.261), channel_id=1, source_target_pairs={{0,1},{1,0},{2,3},{3,2},{4,5},{5,4},{6,7},{7,6},{8,9},{9,8},{10,11... | collective-permute-start | bytes 5406728 | tf_op jit(solution)/shard_map/c1/ppermute | solution.py:33
  138.7 7.4 %collective-permute-done.41 = bf16[2,40,2048]{2,1,0:T(8,128)(2,1)S(1)} collective-permute-done((bf16[2,40,2048]{2,1,0:T(8,128)(2,1)S(1)}, bf16[2,40,2048]{2,1,0:T(8,128)(2,1)S(1)}, u32[]{:S(2)}, u32[]{:S(2)}) %collective-permute-start.41) | collective-permute-done | bytes 327712 | tf_op jit(solution)/shard_map/x1/ppermute | solution.py:33
  151.3 4.2 %collective-permute-done.45 = bf16[40,2048]{1,0:T(8,128)(2,1)S(1)} collective-permute-done((bf16[40,2048]{1,0:T(8,128)(2,1)S(1)}, bf16[40,2048]{1,0:T(8,128)(2,1)S(1)}, u32[]{:S(2)}, u32[]{:S(2)}) %collective-permute-start.45) | collective-permute-done | bytes 163872 | tf_op jit(solution)/shard_map/z1/ppermute | solution.py:33
  155.5 3.0 %collective-permute-done.43 = bf16[2,2,40,1408]{3,2,1,0:T(8,128)(2,1)S(1)} collective-permute-done((bf16[2,2,40,1408]{3,2,1,0:T(8,128)(2,1)S(1)}, bf16[2,2,40,1408]{3,2,1,0:T(8,128)(2,1)S(1)}, u32[]{:S(2)}, u32[]{:S(2)}) %collective-permute-start.43) | collective-permute-done | bytes 450592 | tf_op jit(solution)/shard_map/y1/ppermute | solution.py:33
  163.8 5.2 %collective-permute-done.50 = bf16[40,2048]{1,0:T(8,128)(2,1)S(1)} collective-permute-done((bf16[40,2048]{1,0:T(8,128)(2,1)S(1)}, bf16[40,2048]{1,0:T(8,128)(2,1)S(1)}, u32[]{:S(2)}, u32[]{:S(2)}) %collective-permute-start.50) | collective-permute-done | bytes 163872 | tf_op jit(solution)/shard_map/z2/ppermute | solution.py:33
  170.4 2.3 %collective-permute-start.54 = (f32[20,2048]{1,0:T(8,128)S(1)}, f32[20,2048]{1,0:T(8,128)S(1)}, u32[]{:S(2)}, u32[]{:S(2)}) collective-permute-start(f32[20,2048]{1,0:T(8,128)S(1)} %slice_select_fusion), channel_id=1, source_target_pairs={{0,1},{1,0},{2,3},{3,2},{4,5},{5,4},{6,7},{7,6},{8,9},{9,8},{10,11... | collective-permute-start | bytes 491528 | tf_op jit(solution)/shard_map/c1/ppermute | solution.py:33
  174.4 2.4 %collective-permute-start.53 = (bf16[40,1408]{1,0:T(8,128)(2,1)S(1)}, bf16[40,1408]{1,0:T(8,128)(2,1)S(1)}, u32[]{:S(2)}, u32[]{:S(2)}) collective-permute-start(bf16[40,1408]{1,0:T(8,128)(2,1)S(1)} %get-tuple-element.356), channel_id=1, source_target_pairs={{0,24},{1,25},{2,26},{3,27},{4,28},{5,29},{6,30},{7,31},{8,0},{9,1... | collective-permute-start | bytes 337928 | tf_op jit(solution)/shard_map/z3/ppermute | solution.py:33
  177.3 2.3 %multiply_subtract_fusion = (f32[20,2,2048]{2,1,0:T(2,128)}, f32[20,2,2048]{2,1,0:T(2,128)}, f32[20,2,2048]{2,1,0:T(2,128)}, f32[20,2,2048]{2,1,0:T(2,128)}) fusion(f32[20,2,2048]{2,1,0:T(2,128)S(1)} %copy-done.3, f32[20,1,2048]{2,1,0:T(1,128)S(1)} %stack.174, f32[20,1,2048]{2,1,0:T(1,128)S(1)} %copy.59, f32[20,2,2048]{2,1,0:T(2,128)S(1)} %copy-done.6, ...), kind=kLoop, calls=%fused_computation.53 | loop fusion | flops 1228800 | bytes 2621440 | tf_op jit(solution)/shard_map/sub | solution.py:832
  180.7 4.2 %collective-permute-done.51 = bf16[40,1408]{1,0:T(8,128)(2,1)S(1)} collective-permute-done((bf16[40,1408]{1,0:T(8,128)(2,1)S(1)}, bf16[40,1408]{1,0:T(8,128)(2,1)S(1)}, u32[]{:S(2)}, u32[]{:S(2)}) %collective-permute-start.51) | collective-permute-done | bytes 112672 | tf_op jit(solution)/shard_map/z1/ppermute | solution.py:33
  (216 shorter events, 57.2 us)
Async XLA Ops:
  7.9 10.4 %collective-permute-start.2 = (bf16[40,1408]{1,0:T(8,128)(2,1)S(1)}, bf16[40,1408]{1,0:T(8,128)(2,1)S(1)}, u32[]{:S(2)}, u32[]{:S(2)}) collective-permute-start(bf16[40,1408]{1,0:T(8,128)(2,1)S(1)} %fusion.31), channel_id=1, source_target_pairs={{0,16},{1,17},{2,18},{3,19},{4,20},{5,21},{6,22},{7,23},{8,24},{9,... | collective-permute-start | bytes 337928 | tf_op jit(solution)/shard_map/z2/ppermute | solution.py:33
  19.6 10.5 %collective-permute-start.8 = (bf16[64,640]{1,0:T(8,128)(2,1)S(1)}, bf16[64,640]{1,0:T(8,128)(2,1)S(1)}, u32[]{:S(2)}, u32[]{:S(2)}) collective-permute-start(bf16[64,640]{1,0:T(8,128)(2,1)S(1)} %convert_element_type.268), channel_id=1, source_target_pairs={{0,8},{1,9},{2,10},{3,11},{4,12},{5,13},{6,14},{7,15},{8,16},{9,17... | collective-permute-start | bytes 245768 | tf_op jit(solution)/shard_map/z1/ppermute | solution.py:33
  30.6 18.3 %collective-permute-start.9 = (bf16[2,2,40,1408]{3,2,1,0:T(8,128)(2,1)S(1)}, bf16[2,2,40,1408]{3,2,1,0:T(8,128)(2,1)S(1)}, u32[]{:S(2)}, u32[]{:S(2)}) collective-permute-start(bf16[2,2,40,1408]{3,2,1,0:T(8,128)(2,1)S(1)} %pad_maximum_fusion.2.refs_0_), channel_id=1, source_target_pairs={{0,4},{1,5},{2,6},{3,7},{4,0},{5,1},{6,2},{7,3},{8,12},{9,13},{10,... | collective-permute-start | bytes 1351688 | tf_op jit(solution)/shard_map/y1/ppermute | solution.py:33
  31.8 17.1 %collective-permute-start.10 = (bf16[2,2,40,1408]{3,2,1,0:T(8,128)(2,1)S(1)}, bf16[2,2,40,1408]{3,2,1,0:T(8,128)(2,1)S(1)}, u32[]{:S(2)}, u32[]{:S(2)}) collective-permute-start(bf16[2,2,40,1408]{3,2,1,0:T(8,128)(2,1)S(1)} %pad_maximum_fusion.3.refs_2_), channel_id=1, source_target_pairs={{0,2},{1,3},{2,0},{3,1},{4,6},{5,7},{6,4},{7,5},{8,10},{9,11},{10,... | collective-permute-start | bytes 1351688 | tf_op jit(solution)/shard_map/x1/ppermute | solution.py:33
  35.7 13.2 %collective-permute-start.12 = (bf16[40,2048]{1,0:T(8,128)(2,1)S(1)}, bf16[40,2048]{1,0:T(8,128)(2,1)S(1)}, u32[]{:S(2)}, u32[]{:S(2)}) collective-permute-start(bf16[40,2048]{1,0:T(8,128)(2,1)S(1)} %pad_maximum_fusion.11), channel_id=1, source_target_pairs={{0,16},{1,17},{2,18},{3,19},{4,20},{5,21},{6,22},{7,23},{8,24},{9,... | collective-permute-start | bytes 491528 | tf_op jit(solution)/shard_map/z2/ppermute | solution.py:33
  35.7 13.2 %collective-permute-start.11 = (bf16[40,2048]{1,0:T(8,128)(2,1)S(1)}, bf16[40,2048]{1,0:T(8,128)(2,1)S(1)}, u32[]{:S(2)}, u32[]{:S(2)}) collective-permute-start(bf16[40,2048]{1,0:T(8,128)(2,1)S(1)} %pad_maximum_fusion.11), channel_id=1, source_target_pairs={{0,24},{1,25},{2,26},{3,27},{4,28},{5,29},{6,30},{7,31},{8,0},{9,1... | collective-permute-start | bytes 491528 | tf_op jit(solution)/shard_map/z3/ppermute | solution.py:33
  40.1 9.5 %collective-permute-start.17 = (bf16[2,64,640]{2,1,0:T(8,128)(2,1)S(1)}, bf16[2,64,640]{2,1,0:T(8,128)(2,1)S(1)}, u32[]{:S(2)}, u32[]{:S(2)}) collective-permute-start(bf16[2,64,640]{2,1,0:T(8,128)(2,1)S(1)} %get-tuple-element.361), channel_id=1, source_target_pairs={{0,4},{1,5},{2,6},{3,7},{4,0},{5,1},{6,2},{7,3},{8,12},{9,13},{10,... | collective-permute-start | bytes 491528 | tf_op jit(solution)/shard_map/y1/ppermute | solution.py:33
  49.3 9.9 %collective-permute-start.15 = (bf16[2,40,2048]{2,1,0:T(8,128)(2,1)S(1)}, bf16[2,40,2048]{2,1,0:T(8,128)(2,1)S(1)}, u32[]{:S(2)}, u32[]{:S(2)}) collective-permute-start(bf16[2,40,2048]{2,1,0:T(8,128)(2,1)S(1)} %get-tuple-element.351), channel_id=1, source_target_pairs={{0,4},{1,5},{2,6},{3,7},{4,0},{5,1},{6,2},{7,3},{8,12},{9,13},{10,... | collective-permute-start | bytes 983048 | tf_op jit(solution)/shard_map/y1/ppermute | solution.py:33
  49.7 10.0 %collective-permute-start.20 = (bf16[2,2,40,1408]{3,2,1,0:T(8,128)(2,1)S(1)}, bf16[2,2,40,1408]{3,2,1,0:T(8,128)(2,1)S(1)}, u32[]{:S(2)}, u32[]{:S(2)}) collective-permute-start(bf16[2,2,40,1408]{3,2,1,0:T(8,128)(2,1)S(1)} %pad_maximum_fusion.2.refs_0_), channel_id=1, source_target_pairs={{0,1},{1,0},{2,3},{3,2},{4,5},{5,4},{6,7},{7,6},{8,9},{9,8},{10,11... | collective-permute-start | bytes 1351688 | tf_op jit(solution)/shard_map/c1/ppermute | solution.py:33
  59.3 10.8 %collective-permute-start.24 = (bf16[2,2,40,2048]{3,2,1,0:T(8,128)(2,1)S(1)}, bf16[2,2,40,2048]{3,2,1,0:T(8,128)(2,1)S(1)}, u32[]{:S(2)}, u32[]{:S(2)}) collective-permute-start(bf16[2,2,40,2048]{3,2,1,0:T(8,128)(2,1)S(1)} %pad_maximum_fusion.refs_0_), channel_id=1, source_target_pairs={{0,1},{1,0},{2,3},{3,2},{4,5},{5,4},{6,7},{7,6},{8,9},{9,8},{10,11... | collective-permute-start | bytes 1966088 | tf_op jit(solution)/shard_map/c1/ppermute | solution.py:33
  59.7 16.1 %collective-permute-start.18 = (bf16[2,2,40,2048]{3,2,1,0:T(8,128)(2,1)S(1)}, bf16[2,2,40,2048]{3,2,1,0:T(8,128)(2,1)S(1)}, u32[]{:S(2)}, u32[]{:S(2)}) collective-permute-start(bf16[2,2,40,2048]{3,2,1,0:T(8,128)(2,1)S(1)} %pad_maximum_fusion.refs_0_), channel_id=1, source_target_pairs={{0,4},{1,5},{2,6},{3,7},{4,0},{5,1},{6,2},{7,3},{8,12},{9,13},{10,... | collective-permute-start | bytes 1966088 | tf_op jit(solution)/shard_map/y1/ppermute | solution.py:33
  59.9 15.9 %collective-permute-start.25 = (bf16[2,2,40,2048]{3,2,1,0:T(8,128)(2,1)S(1)}, bf16[2,2,40,2048]{3,2,1,0:T(8,128)(2,1)S(1)}, u32[]{:S(2)}, u32[]{:S(2)}) collective-permute-start(bf16[2,2,40,2048]{3,2,1,0:T(8,128)(2,1)S(1)} %pad_maximum_fusion.1.refs_2_), channel_id=1, source_target_pairs={{0,1},{1,0},{2,3},{3,2},{4,5},{5,4},{6,7},{7,6},{8,9},{9,8},{10,11... | collective-permute-start | bytes 1966088 | tf_op jit(solution)/shard_map/c1/ppermute | solution.py:33
  60.4 16.3 %collective-permute-start.19 = (bf16[2,2,40,2048]{3,2,1,0:T(8,128)(2,1)S(1)}, bf16[2,2,40,2048]{3,2,1,0:T(8,128)(2,1)S(1)}, u32[]{:S(2)}, u32[]{:S(2)}) collective-permute-start(bf16[2,2,40,2048]{3,2,1,0:T(8,128)(2,1)S(1)} %pad_maximum_fusion.1.refs_2_), channel_id=1, source_target_pairs={{0,2},{1,3},{2,0},{3,1},{4,6},{5,7},{6,4},{7,5},{8,10},{9,11},{10,... | collective-permute-start | bytes 1966088 | tf_op jit(solution)/shard_map/x1/ppermute | solution.py:33
  77.5 11.9 %collective-permute-start.30 = (bf16[2,2,64,640]{3,2,1,0:T(8,128)(2,1)S(1)}, bf16[2,2,64,640]{3,2,1,0:T(8,128)(2,1)S(1)}, u32[]{:S(2)}, u32[]{:S(2)}) collective-permute-start(bf16[2,2,64,640]{3,2,1,0:T(8,128)(2,1)S(1)} %pad_maximum_fusion.6.refs_0_), channel_id=1, source_target_pairs={{0,1},{1,0},{2,3},{3,2},{4,5},{5,4},{6,7},{7,6},{8,9},{9,8},{10,11... | collective-permute-start | bytes 983048 | tf_op jit(solution)/shard_map/c1/ppermute | solution.py:33
  78.0 10.2 %collective-permute-start.28 = (bf16[2,2,64,640]{3,2,1,0:T(8,128)(2,1)S(1)}, bf16[2,2,64,640]{3,2,1,0:T(8,128)(2,1)S(1)}, u32[]{:S(2)}, u32[]{:S(2)}) collective-permute-start(bf16[2,2,64,640]{3,2,1,0:T(8,128)(2,1)S(1)} %pad_maximum_fusion.6.refs_0_), channel_id=1, source_target_pairs={{0,4},{1,5},{2,6},{3,7},{4,0},{5,1},{6,2},{7,3},{8,12},{9,13},{10,... | collective-permute-start | bytes 983048 | tf_op jit(solution)/shard_map/y1/ppermute | solution.py:33
  79.3 9.0 %collective-permute-start.29 = (bf16[2,2,64,640]{3,2,1,0:T(8,128)(2,1)S(1)}, bf16[2,2,64,640]{3,2,1,0:T(8,128)(2,1)S(1)}, u32[]{:S(2)}, u32[]{:S(2)}) collective-permute-start(bf16[2,2,64,640]{3,2,1,0:T(8,128)(2,1)S(1)} %pad_maximum_fusion.7.refs_2_), channel_id=1, source_target_pairs={{0,2},{1,3},{2,0},{3,1},{4,6},{5,7},{6,4},{7,5},{8,10},{9,11},{10,... | collective-permute-start | bytes 983048 | tf_op jit(solution)/shard_map/x1/ppermute | solution.py:33
  103.0 11.3 %collective-permute-start.35 = (bf16[4,2,2,40,2048]{4,3,2,1,0:T(8,128)(2,1)S(1)}, bf16[4,2,2,40,2048]{4,3,2,1,0:T(8,128)(2,1)S(1)}, u32[]{:S(2)}, u32[]{:S(2)}) collective-permute-start(bf16[4,2,2,40,2048]{4,3,2,1,0:T(8,128)(2,1)S(1)} %get-tuple-element.237), channel_id=1, source_target_pairs={{0,1},{1,0},{2,3},{3,2},{4,5},{5,4},{6,7},{7,6},{8,9},{9,8},{10,11... | collective-permute-start | bytes 7864328 | tf_op jit(solution)/shard_map/c1/ppermute | solution.py:33
  103.5 10.8 %collective-permute-start.36 = (bf16[4,64,640]{2,1,0:T(8,128)(2,1)S(1)}, bf16[4,64,640]{2,1,0:T(8,128)(2,1)S(1)}, u32[]{:S(2)}, u32[]{:S(2)}) collective-permute-start(bf16[4,64,640]{2,1,0:T(8,128)(2,1)S(1)} %get-tuple-element.339), channel_id=1, source_target_pairs={{0,8},{1,9},{2,10},{3,11},{4,12},{5,13},{6,14},{7,15},{8,16},{9,17... | collective-permute-start | bytes 983048 | tf_op jit(solution)/shard_map/z1/ppermute | solution.py:33
  114.3 12.5 %collective-permute-start.37 = (bf16[4,64,640]{2,1,0:T(8,128)(2,1)S(1)}, bf16[4,64,640]{2,1,0:T(8,128)(2,1)S(1)}, u32[]{:S(2)}, u32[]{:S(2)}) collective-permute-start(bf16[4,64,640]{2,1,0:T(8,128)(2,1)S(1)} %get-tuple-element.246), channel_id=1, source_target_pairs={{0,24},{1,25},{2,26},{3,27},{4,28},{5,29},{6,30},{7,31},{8,0},{9,1... | collective-permute-start | bytes 983048 | tf_op jit(solution)/shard_map/z3/ppermute | solution.py:33
  116.9 16.9 %collective-permute-start.39 = (bf16[2,2,40,2048]{3,2,1,0:T(8,128)(2,1)S(1)}, bf16[2,2,40,2048]{3,2,1,0:T(8,128)(2,1)S(1)}, u32[]{:S(2)}, u32[]{:S(2)}) collective-permute-start(bf16[2,2,40,2048]{3,2,1,0:T(8,128)(2,1)S(1)} %get-tuple-element.331), channel_id=1, source_target_pairs={{0,2},{1,3},{2,0},{3,1},{4,6},{5,7},{6,4},{7,5},{8,10},{9,11},{10,... | collective-permute-start | bytes 1966088 | tf_op jit(solution)/shard_map/x1/ppermute | solution.py:33
  117.4 16.4 %collective-permute-start.38 = (bf16[2,2,40,2048]{3,2,1,0:T(8,128)(2,1)S(1)}, bf16[2,2,40,2048]{3,2,1,0:T(8,128)(2,1)S(1)}, u32[]{:S(2)}, u32[]{:S(2)}) collective-permute-start(bf16[2,2,40,2048]{3,2,1,0:T(8,128)(2,1)S(1)} %get-tuple-element.332), channel_id=1, source_target_pairs={{0,4},{1,5},{2,6},{3,7},{4,0},{5,1},{6,2},{7,3},{8,12},{9,13},{10,... | collective-permute-start | bytes 1966088 | tf_op jit(solution)/shard_map/y1/ppermute | solution.py:33
  126.8 24.0 %collective-permute-start.47 = (bf16[4,64,640]{2,1,0:T(8,128)(2,1)S(1)}, bf16[4,64,640]{2,1,0:T(8,128)(2,1)S(1)}, u32[]{:S(2)}, u32[]{:S(2)}) collective-permute-start(bf16[4,64,640]{2,1,0:T(8,128)(2,1)S(1)} %get-tuple-element.275), channel_id=1, source_target_pairs={{0,16},{1,17},{2,18},{3,19},{4,20},{5,21},{6,22},{7,23},{8,24},{9,... | collective-permute-start | bytes 983048 | tf_op jit(solution)/shard_map/z2/ppermute | solution.py:33
  133.7 12.6 %collective-permute-start.40 = (bf16[4,2,2,40,1408]{4,3,2,1,0:T(8,128)(2,1)S(1)}, bf16[4,2,2,40,1408]{4,3,2,1,0:T(8,128)(2,1)S(1)}, u32[]{:S(2)}, u32[]{:S(2)}) collective-permute-start(bf16[4,2,2,40,1408]{4,3,2,1,0:T(8,128)(2,1)S(1)} %get-tuple-element.261), channel_id=1, source_target_pairs={{0,1},{1,0},{2,3},{3,2},{4,5},{5,4},{6,7},{7,6},{8,9},{9,8},{10,11... | collective-permute-start | bytes 5406728 | tf_op jit(solution)/shard_map/c1/ppermute | solution.py:33
  136.8 9.4 %collective-permute-start.41 = (bf16[2,40,2048]{2,1,0:T(8,128)(2,1)S(1)}, bf16[2,40,2048]{2,1,0:T(8,128)(2,1)S(1)}, u32[]{:S(2)}, u32[]{:S(2)}) collective-permute-start(bf16[2,40,2048]{2,1,0:T(8,128)(2,1)S(1)} %fusion.13), channel_id=1, source_target_pairs={{0,2},{1,3},{2,0},{3,1},{4,6},{5,7},{6,4},{7,5},{8,10},{9,11},{10,... | collective-permute-start | bytes 983048 | tf_op jit(solution)/shard_map/x1/ppermute | solution.py:33
  137.3 9.1 %collective-permute-start.42 = (bf16[2,40,2048]{2,1,0:T(8,128)(2,1)S(1)}, bf16[2,40,2048]{2,1,0:T(8,128)(2,1)S(1)}, u32[]{:S(2)}, u32[]{:S(2)}) collective-permute-start(bf16[2,40,2048]{2,1,0:T(8,128)(2,1)S(1)} %fusion.14), channel_id=1, source_target_pairs={{0,4},{1,5},{2,6},{3,7},{4,0},{5,1},{6,2},{7,3},{8,12},{9,13},{10,... | collective-permute-start | bytes 983048 | tf_op jit(solution)/shard_map/y1/ppermute | solution.py:33
  148.3 10.2 %collective-permute-start.43 = (bf16[2,2,40,1408]{3,2,1,0:T(8,128)(2,1)S(1)}, bf16[2,2,40,1408]{3,2,1,0:T(8,128)(2,1)S(1)}, u32[]{:S(2)}, u32[]{:S(2)}) collective-permute-start(bf16[2,2,40,1408]{3,2,1,0:T(8,128)(2,1)S(1)} %get-tuple-element.269), channel_id=1, source_target_pairs={{0,4},{1,5},{2,6},{3,7},{4,0},{5,1},{6,2},{7,3},{8,12},{9,13},{10,... | collective-permute-start | bytes 1351688 | tf_op jit(solution)/shard_map/y1/ppermute | solution.py:33
  149.6 9.9 %collective-permute-start.44 = (bf16[2,2,40,1408]{3,2,1,0:T(8,128)(2,1)S(1)}, bf16[2,2,40,1408]{3,2,1,0:T(8,128)(2,1)S(1)}, u32[]{:S(2)}, u32[]{:S(2)}) collective-permute-start(bf16[2,2,40,1408]{3,2,1,0:T(8,128)(2,1)S(1)} %get-tuple-element.270), channel_id=1, source_target_pairs={{0,2},{1,3},{2,0},{3,1},{4,6},{5,7},{6,4},{7,5},{8,10},{9,11},{10,... | collective-permute-start | bytes 1351688 | tf_op jit(solution)/shard_map/x1/ppermute | solution.py:33
  159.9 9.2 %collective-permute-start.50 = (bf16[40,2048]{1,0:T(8,128)(2,1)S(1)}, bf16[40,2048]{1,0:T(8,128)(2,1)S(1)}, u32[]{:S(2)}, u32[]{:S(2)}) collective-permute-start(bf16[40,2048]{1,0:T(8,128)(2,1)S(1)} %fusion.26), channel_id=1, source_target_pairs={{0,16},{1,17},{2,18},{3,19},{4,20},{5,21},{6,22},{7,23},{8,24},{9,... | collective-permute-start | bytes 491528 | tf_op jit(solution)/shard_map/z2/ppermute | solution.py:33
  160.5 9.6 %collective-permute-start.48 = (bf16[2,40,1408]{2,1,0:T(8,128)(2,1)S(1)}, bf16[2,40,1408]{2,1,0:T(8,128)(2,1)S(1)}, u32[]{:S(2)}, u32[]{:S(2)}) collective-permute-start(bf16[2,40,1408]{2,1,0:T(8,128)(2,1)S(1)} %fusion.18), channel_id=1, source_target_pairs={{0,2},{1,3},{2,0},{3,1},{4,6},{5,7},{6,4},{7,5},{8,10},{9,11},{10,... | collective-permute-start | bytes 675848 | tf_op jit(solution)/shard_map/x1/ppermute | solution.py:33
  162.0 15.1 %collective-permute-start.57 = (bf16[64,640]{1,0:T(8,128)(2,1)S(1)}, bf16[64,640]{1,0:T(8,128)(2,1)S(1)}, u32[]{:S(2)}, u32[]{:S(2)}) collective-permute-start(bf16[64,640]{1,0:T(8,128)(2,1)S(1)} %get-tuple-element.344), channel_id=1, source_target_pairs={{0,6},{1,7},{2,4},{3,5},{4,2},{5,3},{6,0},{7,1},{8,14},{9,15},{10,... | collective-permute-start | bytes 245768 | tf_op jit(solution)/shard_map/xy/ppermute | solution.py:531
  163.5 16.1 %collective-permute-start.56 = (bf16[64,640]{1,0:T(8,128)(2,1)S(1)}, bf16[64,640]{1,0:T(8,128)(2,1)S(1)}, u32[]{:S(2)}, u32[]{:S(2)}) collective-permute-start(bf16[64,640]{1,0:T(8,128)(2,1)S(1)} %get-tuple-element.345), channel_id=1, source_target_pairs={{0,4},{1,5},{2,6},{3,7},{4,0},{5,1},{6,2},{7,3},{8,12},{9,13},{10,... | collective-permute-start | bytes 245768 | tf_op jit(solution)/shard_map/y1/ppermute | solution.py:33
  169.0 10.6 %collective-permute-start.55 = (bf16[64,640]{1,0:T(8,128)(2,1)S(1)}, bf16[64,640]{1,0:T(8,128)(2,1)S(1)}, u32[]{:S(2)}, u32[]{:S(2)}) collective-permute-start(bf16[64,640]{1,0:T(8,128)(2,1)S(1)} %get-tuple-element.346), channel_id=1, source_target_pairs={{0,2},{1,3},{2,0},{3,1},{4,6},{5,7},{6,4},{7,5},{8,10},{9,11},{10,... | collective-permute-start | bytes 245768 | tf_op jit(solution)/shard_map/x1/ppermute | solution.py:33
  (51 other events, 299.5 us)
